TPU v7x, 32 devices: a whole 2x2x4 slice. The times are simulated.
32 devices in a mesh: dp: 4 (over y, x), fsdp: 8 (over z, core).
Axes of the slice: x: 2, y: 2, z: 4, core: 2. Of those that a mesh axis runs over, the one named last changes fastest.
Arguments:
- tokens_in: bfloat16 [12288, 2048], P(('dp', 'fsdp')), may hold values from -6 to 6
- out_grad: bfloat16 [12288, 2048], P(('dp', 'fsdp')), may hold values from -6 to 6
- kv_grad_next: bfloat16 [12288, 256], P(('dp', 'fsdp')), may hold values from -6 to 6
- doc_ids: int32 [32, 384], P(('dp', 'fsdp')), may hold values from 0 to 5, never falling along the last dimension, each value on 1 to 192 neighbouring positions
- gains: float32 [2, 2048], P(None, ('dp', 'fsdp')), may hold values from 0.5 to 1.5
- gains_mom: float32 [2, 2048], P(None, ('dp', 'fsdp')), may hold values from -1792 to 1792
- gains_ema: float32 [2, 2048], P(None, ('dp', 'fsdp')), may hold values from 0.5 to 1.5
- w_query: float32 [2048, 2048], P(('dp', 'fsdp')), may hold values from -0.125 to 0.125
- query_mom: float32 [2048, 2048], P(('dp', 'fsdp')), may hold values from -896 to 896
- query_ema: float32 [2048, 2048], P(('dp', 'fsdp')), may hold values from -0.125 to 0.125
- w_keyval: float32 [2048, 256], P(('dp', 'fsdp')), may hold values from -0.125 to 0.125
- keyval_mom: float32 [2048, 256], P(('dp', 'fsdp')), may hold values from -4096 to 4096
- keyval_ema: float32 [2048, 256], P(('dp', 'fsdp')), may hold values from -0.125 to 0.125
- w_output: float32 [2048, 2048], P(('dp', 'fsdp')), may hold values from -0.5 to 0.5
- output_mom: float32 [2048, 2048], P(('dp', 'fsdp')), may hold values from -384 to 384
- output_ema: float32 [2048, 2048], P(('dp', 'fsdp')), may hold values from -0.5 to 0.5
- w_gate: float32 [2048, 5632], P(('dp', 'fsdp')), may hold values from -0.125 to 0.125
- gate_mom: float32 [2048, 5632], P(('dp', 'fsdp')), may hold values from -384 to 384
- gate_ema: float32 [2048, 5632], P(('dp', 'fsdp')), may hold values from -0.125 to 0.125
- w_up: float32 [2048, 5632], P(('dp', 'fsdp')), may hold values from -0.125 to 0.125
- up_mom: float32 [2048, 5632], P(('dp', 'fsdp')), may hold values from -384 to 384
- up_ema: float32 [2048, 5632], P(('dp', 'fsdp')), may hold values from -0.125 to 0.125
- w_down: float32 [5632, 2048], P(('dp', 'fsdp')), may hold values from -0.15625 to 0.15625
- down_mom: float32 [5632, 2048], P(('dp', 'fsdp')), may hold values from -320 to 320
- down_ema: float32 [5632, 2048], P(('dp', 'fsdp')), may hold values from -0.15625 to 0.15625
Outputs:
- layer_out: float32 [12288, 2048], P(('dp', 'fsdp'))
- shared_kv: float32 [12288, 256], P(('dp', 'fsdp'))
- input_grad: float32 [12288, 2048], P(('dp', 'fsdp'))
- gains_mom_new: float32 [2, 2048], P(None, ('dp', 'fsdp'))
- gains_new: float32 [2, 2048], P(None, ('dp', 'fsdp'))
- gains_ema_new: float32 [2, 2048], P(None, ('dp', 'fsdp'))
- query_mom_new: float32 [2048, 2048], P(('dp', 'fsdp'))
- query_new: float32 [2048, 2048], P(('dp', 'fsdp'))
- query_ema_new: float32 [2048, 2048], P(('dp', 'fsdp'))
- keyval_mom_new: float32 [2048, 256], P(('dp', 'fsdp'))
- keyval_new: float32 [2048, 256], P(('dp', 'fsdp'))
- keyval_ema_new: float32 [2048, 256], P(('dp', 'fsdp'))
- output_mom_new: float32 [2048, 2048], P(('dp', 'fsdp'))
- output_new: float32 [2048, 2048], P(('dp', 'fsdp'))
- output_ema_new: float32 [2048, 2048], P(('dp', 'fsdp'))
- gate_mom_new: float32 [2048, 5632], P(('dp', 'fsdp'))
- gate_new: float32 [2048, 5632], P(('dp', 'fsdp'))
- gate_ema_new: float32 [2048, 5632], P(('dp', 'fsdp'))
- up_mom_new: float32 [2048, 5632], P(('dp', 'fsdp'))
- up_new: float32 [2048, 5632], P(('dp', 'fsdp'))
- up_ema_new: float32 [2048, 5632], P(('dp', 'fsdp'))
- down_mom_new: float32 [5632, 2048], P(('dp', 'fsdp'))
- down_new: float32 [5632, 2048], P(('dp', 'fsdp'))
- down_ema_new: float32 [5632, 2048], P(('dp', 'fsdp'))
Inputs may be any that keep to these rules, and one draw needn't show every extreme that they name: `doc_ids`: each row is one sequence; document numbers start at 0 and never fall along a row; a document has 1 to 192 tokens and one in each row has exactly 192.
All inputs are finite; a program needn't handle non-finite values.
Results may differ from a plain program's by a relative error of at most 0.014.
The roundings to bfloat16 on the way count: a program that leaves them out, or rounds other values in their place, can miss the bound.
Values may be sent and summed in bfloat16 or wider, within the bound.
No kernel may reach another device: no remote copies, remote signals or barrier semaphores. Data moves between devices by JAX's collectives and lax.ppermute only.
A program may use at most 448 MiB of HBM per device.

v0:
```python
import math

import jax
import jax.numpy as jnp
from jax import lax
from jax.sharding import PartitionSpec as P

EPS = 1e-05
THETA = 10000.0
MOMENTUM = 0.9
AVERAGE = 0.75
NEG = -1e30


def positions_of(doc_ids):
    length = doc_ids.shape[-1]
    offsets = jnp.broadcast_to(jnp.arange(length, dtype=jnp.int32), doc_ids.shape)
    change = jnp.concatenate(
        [
            jnp.ones(doc_ids.shape[:-1] + (1,), dtype=jnp.bool_),
            doc_ids[..., 1:] != doc_ids[..., :-1],
        ],
        axis=-1,
    )
    starts = lax.cummax(jnp.where(change, offsets, 0), axis=doc_ids.ndim - 1)
    return offsets - starts


def rotation(positions, head_dim):
    half_dim = head_dim // 2
    inverse = THETA ** (-(jnp.arange(half_dim, dtype=jnp.float32) * 2.0) / head_dim)
    angles = positions.astype(jnp.float32)[..., None] * inverse
    return (jnp.cos(angles), jnp.sin(angles))


def rotate(values, cosine, sine_table):
    half_dim = values.shape[-1] // 2
    upper = values[..., :half_dim]
    lower = values[..., half_dim:]
    return jnp.concatenate(
        [upper * cosine - lower * sine_table, lower * cosine + upper * sine_table], axis=-1
    )


def rotate_back(grads, cosine, sine_table):
    half_dim = grads.shape[-1] // 2
    upper = grads[..., :half_dim]
    lower = grads[..., half_dim:]
    return jnp.concatenate(
        [upper * cosine + lower * sine_table, lower * cosine - upper * sine_table], axis=-1
    )


def block_masks(doc_row, block_rows):
    length = doc_row.shape[0]
    nblocks = length // block_rows
    offsets = jnp.arange(length, dtype=jnp.int32)
    return (offsets, doc_row.reshape(nblocks, block_rows), offsets.reshape(nblocks, block_rows))


def attend_forward(queries, shared, doc_row, block_rows):
    length, head_count, head_dim = queries.shape
    nblocks = length // block_rows
    key_rows = shared[:, :head_dim]
    value_rows = shared[:, head_dim:]
    offsets, id_blocks, pos_blocks = block_masks(doc_row, block_rows)

    def one_block(pieces):
        qblock, query_ids, query_pos = pieces
        scores = jnp.einsum("qhd,kd->hqk", qblock, key_rows, preferred_element_type=jnp.float32)
        allowed = (query_ids[:, None] == doc_row[None, :]) & (
            offsets[None, :] <= query_pos[:, None]
        )
        scores = jnp.where(allowed[None], scores, NEG)
        top_score = jnp.max(scores, axis=-1, keepdims=True)
        weights = jnp.exp(scores - top_score)
        totals = jnp.sum(weights, axis=-1, keepdims=True)
        probabilities = (weights / totals).astype(jnp.bfloat16)
        mixed = jnp.einsum(
            "hqk,kd->qhd", probabilities, value_rows, preferred_element_type=jnp.float32
        )
        return (mixed, (top_score + jnp.log(totals))[..., 0])

    mixed, log_totals = lax.map(
        one_block,
        (queries.reshape(nblocks, block_rows, head_count, head_dim), id_blocks, pos_blocks),
    )
    return (mixed.reshape(length, head_count, head_dim), log_totals)


def attend_backward(queries, shared, grad_mixed, log_totals, doc_row, block_rows):
    length, head_count, head_dim = queries.shape
    nblocks = length // block_rows
    key_rows = shared[:, :head_dim]
    value_rows = shared[:, head_dim:]
    offsets, id_blocks, pos_blocks = block_masks(doc_row, block_rows)

    def one_block(carry, pieces):
        qblock, gblock, lse_block, query_ids, query_pos = pieces
        scores = jnp.einsum("qhd,kd->hqk", qblock, key_rows, preferred_element_type=jnp.float32)
        allowed = (query_ids[:, None] == doc_row[None, :]) & (
            offsets[None, :] <= query_pos[:, None]
        )
        probs_full = jnp.where(
            allowed[None],
            jnp.exp(jnp.where(allowed[None], scores, NEG) - lse_block[..., None]),
            0.0,
        )
        probs_low = probs_full.astype(jnp.bfloat16)
        grad_probs = jnp.einsum(
            "qhd,kd->hqk", gblock, value_rows, preferred_element_type=jnp.float32
        )
        inner = jnp.sum(probs_full * grad_probs, axis=-1, keepdims=True)
        grad_scores = (probs_full * (grad_probs - inner)).astype(jnp.bfloat16)
        grad_query = jnp.einsum(
            "hqk,kd->qhd", grad_scores, key_rows, preferred_element_type=jnp.float32
        ).astype(jnp.bfloat16)
        grad_keys = carry[0] + jnp.einsum(
            "hqk,qhd->kd", grad_scores, qblock, preferred_element_type=jnp.float32
        )
        grad_values = carry[1] + jnp.einsum(
            "hqk,qhd->kd", probs_low, gblock, preferred_element_type=jnp.float32
        )
        return ((grad_keys, grad_values), grad_query)

    start_carry = (
        jnp.zeros((length, head_dim), jnp.float32),
        jnp.zeros((length, head_dim), jnp.float32),
    )
    blocks_in = (
        queries.reshape(nblocks, block_rows, head_count, head_dim),
        grad_mixed.reshape(nblocks, block_rows, head_count, head_dim),
        log_totals,
        id_blocks,
        pos_blocks,
    )
    carry_out, grad_blocks = lax.scan(one_block, start_carry, blocks_in)
    return (
        grad_blocks.reshape(length, head_count, head_dim),
        jnp.concatenate([carry_out[0], carry_out[1]], axis=-1),
    )


def norm_back(grad_normed, scaled, inv_rms, gain_full):
    grad_scaled = grad_normed * gain_full.astype(jnp.float32)
    grad_gain = jnp.sum(grad_normed * scaled, axis=0)
    grad_in = inv_rms * (
        grad_scaled - scaled * jnp.mean(grad_scaled * scaled, axis=-1, keepdims=True)
    )
    return (grad_gain, grad_in)


def update(weight, moment, average, grad, rate):
    moment_new = MOMENTUM * moment + grad
    weight_new = weight - rate * (grad + MOMENTUM * moment_new)
    average_new = AVERAGE * average + (1.0 - AVERAGE) * weight_new
    return (moment_new, weight_new, average_new)


def shards(
    tokens_in,
    out_grad,
    kv_grad_next,
    doc_ids,
    gains,
    gains_mom,
    gains_ema,
    w_query,
    query_mom,
    query_ema,
    w_keyval,
    keyval_mom,
    keyval_ema,
    w_output,
    output_mom,
    output_ema,
    w_gate,
    gate_mom,
    gate_ema,
    w_up,
    up_mom,
    up_ema,
    w_down,
    down_mom,
    down_ema,
):
    seq_count, length = doc_ids.shape
    width = tokens_in.shape[1]
    head_dim = w_keyval.shape[1] // 2
    head_count = w_query.shape[1] // head_dim
    hidden_units = w_gate.shape[1]
    rows = seq_count * length
    block_rows = min(512, length)
    tokens_total = rows * lax.axis_size("dp") * lax.axis_size("fsdp")
    scale_query = head_dim ** (-0.5)
    inputs = tokens_in.astype(jnp.float32)
    inv_rms = lax.rsqrt(jnp.mean(inputs * inputs, axis=-1, keepdims=True) + EPS)
    scaled = inputs * inv_rms
    gains_low = gains.astype(jnp.bfloat16)
    gain_attn = gains_low[0]
    gain_ffn = gains_low[1]
    query_low = w_query.astype(jnp.bfloat16)
    keyval_low = w_keyval.astype(jnp.bfloat16)
    output_low = w_output.astype(jnp.bfloat16)
    gate_low = w_gate.astype(jnp.bfloat16)
    up_low = w_up.astype(jnp.bfloat16)
    down_low = w_down.astype(jnp.bfloat16)

    def add_columns(left, piece):
        return jnp.dot(left, piece, preferred_element_type=jnp.float32)

    def normed_pair(source, pieces):
        piece_gain, piece_one, piece_two = pieces
        normed_cols = (source * piece_gain.astype(jnp.float32)).astype(jnp.bfloat16)
        return (
            jnp.dot(normed_cols, piece_one, preferred_element_type=jnp.float32),
            jnp.dot(normed_cols, piece_two, preferred_element_type=jnp.float32),
        )

    query_raw, keyval_raw = normed_pair(
        scaled,
        (
            lax.all_gather(gain_attn, ("dp", "fsdp"), axis=0, tiled=True),
            lax.all_gather(query_low, ("dp", "fsdp"), axis=0, tiled=True),
            lax.all_gather(keyval_low, ("dp", "fsdp"), axis=0, tiled=True),
        ),
    )
    cosine, sine_table = rotation(positions_of(doc_ids).reshape(rows), head_dim)
    queries = (
        rotate(query_raw.reshape(rows, head_count, head_dim), cosine[:, None], sine_table[:, None])
        * scale_query
    ).astype(jnp.bfloat16)
    shared = jnp.concatenate(
        [rotate(keyval_raw[:, :head_dim], cosine, sine_table), keyval_raw[:, head_dim:]], axis=-1
    ).astype(jnp.bfloat16)
    seq_queries = queries.reshape(seq_count, length, head_count, head_dim)
    seq_shared = shared.reshape(seq_count, length, 2 * head_dim)

    def run_forward(pieces):
        return attend_forward(pieces[0], pieces[1], pieces[2], block_rows)

    mixed, log_totals = lax.map(run_forward, (seq_queries, seq_shared, doc_ids))
    attended = mixed.reshape(rows, head_count * head_dim).astype(jnp.bfloat16)
    branch = add_columns(attended, lax.all_gather(output_low, ("dp", "fsdp"), axis=0, tiled=True))
    resid = inputs + branch
    inv_rms2 = lax.rsqrt(jnp.mean(resid * resid, axis=-1, keepdims=True) + EPS)
    scaled2 = resid * inv_rms2
    gate, up = normed_pair(
        scaled2,
        (
            lax.all_gather(gain_ffn, ("dp", "fsdp"), axis=0, tiled=True),
            lax.all_gather(gate_low, ("dp", "fsdp"), axis=0, tiled=True),
            lax.all_gather(up_low, ("dp", "fsdp"), axis=0, tiled=True),
        ),
    )
    sigma = jax.nn.sigmoid(gate)
    activated = gate * sigma
    hidden = (activated * up).astype(jnp.bfloat16)
    ffn_out = add_columns(hidden, lax.all_gather(down_low, ("dp", "fsdp"), axis=0, tiled=True))
    layer_out = resid + ffn_out
    attn_full, ffn_full, query_full, keyval_full, output_full, gate_full, up_full, down_full = (
        lax.all_gather(gain_attn, ("dp", "fsdp"), axis=0, tiled=True),
        lax.all_gather(gain_ffn, ("dp", "fsdp"), axis=0, tiled=True),
        lax.all_gather(query_low, ("dp", "fsdp"), axis=0, tiled=True),
        lax.all_gather(keyval_low, ("dp", "fsdp"), axis=0, tiled=True),
        lax.all_gather(output_low, ("dp", "fsdp"), axis=0, tiled=True),
        lax.all_gather(gate_low, ("dp", "fsdp"), axis=0, tiled=True),
        lax.all_gather(up_low, ("dp", "fsdp"), axis=0, tiled=True),
        lax.all_gather(down_low, ("dp", "fsdp"), axis=0, tiled=True),
    )
    normed = (scaled * attn_full.astype(jnp.float32)).astype(jnp.bfloat16)
    normed2 = (scaled2 * ffn_full.astype(jnp.float32)).astype(jnp.bfloat16)
    grad_down_w = jnp.einsum("tf,td->fd", hidden, out_grad, preferred_element_type=jnp.float32)
    grad_hidden = (
        jnp.einsum("td,fd->tf", out_grad, down_full, preferred_element_type=jnp.float32)
        .astype(jnp.bfloat16)
        .astype(jnp.float32)
    )
    grad_gate = (grad_hidden * up * (sigma * (1.0 + gate * (1.0 - sigma)))).astype(jnp.bfloat16)
    grad_up = (grad_hidden * activated).astype(jnp.bfloat16)
    grad_gate_w = jnp.einsum("td,tf->df", normed2, grad_gate, preferred_element_type=jnp.float32)
    grad_up_w = jnp.einsum("td,tf->df", normed2, grad_up, preferred_element_type=jnp.float32)
    grad_normed2 = jnp.einsum("tf,df->td", grad_gate, gate_full, preferred_element_type=jnp.float32)
    grad_normed2 = grad_normed2 + jnp.einsum(
        "tf,df->td", grad_up, up_full, preferred_element_type=jnp.float32
    )
    grad_gain_ffn, grad_through = norm_back(grad_normed2, scaled2, inv_rms2, ffn_full)
    grad_resid = out_grad.astype(jnp.float32) + grad_through
    grad_branch = grad_resid.astype(jnp.bfloat16)
    grad_output_w = jnp.einsum(
        "tj,td->jd", attended, grad_branch, preferred_element_type=jnp.float32
    )
    grad_attended = jnp.einsum(
        "td,jd->tj", grad_branch, output_full, preferred_element_type=jnp.float32
    ).astype(jnp.bfloat16)

    def run_backward(pieces):
        return attend_backward(pieces[0], pieces[1], pieces[2], pieces[3], pieces[4], block_rows)

    grad_queries, grad_shared_att = lax.map(
        run_backward,
        (
            seq_queries,
            seq_shared,
            grad_attended.reshape(seq_count, length, head_count, head_dim),
            log_totals,
            doc_ids,
        ),
    )
    grad_shared = (
        (grad_shared_att.reshape(rows, 2 * head_dim) + kv_grad_next.astype(jnp.float32))
        .astype(jnp.bfloat16)
        .astype(jnp.float32)
    )
    grad_query_raw = rotate_back(
        grad_queries.reshape(rows, head_count, head_dim).astype(jnp.float32) * scale_query,
        cosine[:, None],
        sine_table[:, None],
    )
    grad_query_raw = grad_query_raw.reshape(rows, head_count * head_dim).astype(jnp.bfloat16)
    grad_keyval_raw = jnp.concatenate(
        [rotate_back(grad_shared[:, :head_dim], cosine, sine_table), grad_shared[:, head_dim:]],
        axis=-1,
    ).astype(jnp.bfloat16)
    grad_query_w = jnp.einsum(
        "td,tj->dj", normed, grad_query_raw, preferred_element_type=jnp.float32
    )
    grad_keyval_w = jnp.einsum(
        "td,tj->dj", normed, grad_keyval_raw, preferred_element_type=jnp.float32
    )
    grad_normed = jnp.einsum(
        "tj,dj->td", grad_query_raw, query_full, preferred_element_type=jnp.float32
    )
    grad_normed = grad_normed + jnp.einsum(
        "tj,dj->td", grad_keyval_raw, keyval_full, preferred_element_type=jnp.float32
    )
    grad_gain_attn, grad_first = norm_back(grad_normed, scaled, inv_rms, attn_full)
    input_grad = grad_resid + grad_first
    attn_sum, ffn_gain_sum, query_sum, keyval_sum, output_sum, gate_sum, up_sum, down_sum = (
        lax.psum_scatter(grad_gain_attn, ("dp", "fsdp"), scatter_dimension=0, tiled=True),
        lax.psum_scatter(grad_gain_ffn, ("dp", "fsdp"), scatter_dimension=0, tiled=True),
        lax.psum_scatter(grad_query_w, ("dp", "fsdp"), scatter_dimension=0, tiled=True),
        lax.psum_scatter(grad_keyval_w, ("dp", "fsdp"), scatter_dimension=0, tiled=True),
        lax.psum_scatter(grad_output_w, ("dp", "fsdp"), scatter_dimension=0, tiled=True),
        lax.psum_scatter(grad_gate_w, ("dp", "fsdp"), scatter_dimension=0, tiled=True),
        lax.psum_scatter(grad_up_w, ("dp", "fsdp"), scatter_dimension=0, tiled=True),
        lax.psum_scatter(grad_down_w, ("dp", "fsdp"), scatter_dimension=0, tiled=True),
    )
    gains_sum = jnp.stack([attn_sum, ffn_gain_sum], axis=0)
    gains_out = update(gains, gains_mom, gains_ema, gains_sum, 0.1 / math.sqrt(tokens_total))
    query_out = update(
        w_query, query_mom, query_ema, query_sum, 0.6 / math.sqrt(width * tokens_total)
    )
    keyval_out = update(
        w_keyval, keyval_mom, keyval_ema, keyval_sum, 0.15 / math.sqrt(width * tokens_total)
    )
    output_out = update(
        w_output,
        output_mom,
        output_ema,
        output_sum,
        5.0 / math.sqrt(head_count * head_dim * tokens_total),
    )
    gate_out = update(w_gate, gate_mom, gate_ema, gate_sum, 0.6 / math.sqrt(width * tokens_total))
    up_out = update(w_up, up_mom, up_ema, up_sum, 0.6 / math.sqrt(width * tokens_total))
    down_out = update(
        w_down, down_mom, down_ema, down_sum, 1.5 / math.sqrt(hidden_units * tokens_total)
    )
    return (
        layer_out,
        shared.astype(jnp.float32),
        input_grad,
        gains_out[0],
        gains_out[1],
        gains_out[2],
        query_out[0],
        query_out[1],
        query_out[2],
        keyval_out[0],
        keyval_out[1],
        keyval_out[2],
        output_out[0],
        output_out[1],
        output_out[2],
        gate_out[0],
        gate_out[1],
        gate_out[2],
        up_out[0],
        up_out[1],
        up_out[2],
        down_out[0],
        down_out[1],
        down_out[2],
    )


def solution(mesh):
    placed = (
        P(("dp", "fsdp"), None),
        P(("dp", "fsdp"), None),
        P(("dp", "fsdp"), None),
        P(("dp", "fsdp"), None),
        P(None, ("dp", "fsdp")),
        P(None, ("dp", "fsdp")),
        P(None, ("dp", "fsdp")),
        P(("dp", "fsdp"), None),
        P(("dp", "fsdp"), None),
        P(("dp", "fsdp"), None),
        P(("dp", "fsdp"), None),
        P(("dp", "fsdp"), None),
        P(("dp", "fsdp"), None),
        P(("dp", "fsdp"), None),
        P(("dp", "fsdp"), None),
        P(("dp", "fsdp"), None),
        P(("dp", "fsdp"), None),
        P(("dp", "fsdp"), None),
        P(("dp", "fsdp"), None),
        P(("dp", "fsdp"), None),
        P(("dp", "fsdp"), None),
        P(("dp", "fsdp"), None),
        P(("dp", "fsdp"), None),
        P(("dp", "fsdp"), None),
        P(("dp", "fsdp"), None),
    )
    return jax.shard_map(
        shards,
        mesh=mesh,
        in_specs=placed,
        out_specs=(
            P(("dp", "fsdp"), None),
            P(("dp", "fsdp"), None),
            P(("dp", "fsdp"), None),
            P(None, ("dp", "fsdp")),
            P(None, ("dp", "fsdp")),
            P(None, ("dp", "fsdp")),
            P(("dp", "fsdp"), None),
            P(("dp", "fsdp"), None),
            P(("dp", "fsdp"), None),
            P(("dp", "fsdp"), None),
            P(("dp", "fsdp"), None),
            P(("dp", "fsdp"), None),
            P(("dp", "fsdp"), None),
            P(("dp", "fsdp"), None),
            P(("dp", "fsdp"), None),
            P(("dp", "fsdp"), None),
            P(("dp", "fsdp"), None),
            P(("dp", "fsdp"), None),
            P(("dp", "fsdp"), None),
            P(("dp", "fsdp"), None),
            P(("dp", "fsdp"), None),
            P(("dp", "fsdp"), None),
            P(("dp", "fsdp"), None),
            P(("dp", "fsdp"), None),
        ),
        check_vma=False,
    )
```

profile of v0, /device:TPU:0, one launch (start us, length us, event | category | flops | bytes accessed | tf_op | source)
XLA Modules:
  0.0 2804.1 jit_solution(406128494160817499)
XLA Ops:
  7.2 1.6 convert_element_type.132
  8.9 1.8 convert_element_type.134
  10.7 1.8 convert_element_type.140
  12.6 2.4 convert_element_type.146
  16.6 42.1 %all-reduce.5 = (bf16[2048]{0:T(1024)(128)(2,1)S(1)}, bf16[2048]{0:T(1024)(128)(2,1)S(1)}) all-reduce(bf16[2048]{0:T(1024)(128)(2,1)S(1)} %dynamic-update-slice, bf16[2048]{0:T(1024)(128)(2,1)S(1)} %dynamic-update-slice.1), channel_id=2, replica_groups=mesh['dp'=4,'fsdp'=8] {'dp','fsdp'}, use_global_device_ids=true, to_apply=%add | all-reduce | flops 4096 | bytes 16384
  60.3 7.9 all-gather.9.cloned.1.call-done
  68.2 2.1 fusion.69
  71.3 76.9 %all-gather.11.cloned.1.call-done = bf16[2048,2048]{1,0:T(8,128)(2,1)} async-done(((bf16[64,2048]{1,0:T(8,128)(2,1)}), bf16[2048,2048]{1,0:T(8,128)(2,1)}) %all-gather.11.cloned.1.call-update) | async-done | bytes 8388624 | tf_op jit(solution)/shard_map/all_gather | solution.py:224
  148.3 5.9 convolution_bitcast_fusion
  154.9 1.0 fusion.76
  155.9 1.8 multiply_subtract_fusion
  158.7 1.5 fusion.8
  160.2 1.6 fusion.7
  161.8 1.9 copy-done
  163.7 3.2 fusion.26
  167.0 60.9 %all-gather.13.cloned.1.call-done = bf16[2048,2048]{1,0:T(8,128)(2,1)} async-done(((bf16[64,2048]{1,0:T(8,128)(2,1)}), bf16[2048,2048]{1,0:T(8,128)(2,1)}) %all-gather.13.cloned.1.call-update) | async-done | bytes 8388624 | tf_op jit(solution)/shard_map/all_gather | solution.py:244
  227.9 6.0 multiply_reduce_fusion.2
  233.9 1.6 copy-done.3
  235.9 138.5 %all-gather.19.cloned.1.call-done = bf16[5632,2048]{1,0:T(8,128)(2,1)} async-done(((bf16[176,2048]{1,0:T(8,128)(2,1)}), bf16[5632,2048]{1,0:T(8,128)(2,1)}) %all-gather.19.cloned.1.call-update) | async-done | bytes 23068688 | tf_op jit(solution)/shard_map/all_gather | solution.py:259
  374.4 14.9 convolution_convert_fusion
  389.4 131.2 %all-gather.15.cloned.1.call-done = bf16[2048,5632]{1,0:T(8,128)(2,1)} async-done(((bf16[64,5632]{1,0:T(8,128)(2,1)}), bf16[2048,5632]{1,0:T(8,128)(2,1)}) %all-gather.15.cloned.1.call-update) | async-done | bytes 23068688 | tf_op jit(solution)/shard_map/all_gather | solution.py:252
  520.5 13.6 fusion.79
  534.1 3.3 copy-done.11
  537.4 21.0 fusion.71
  558.5 490.2 %reduce-scatter.15.cloned.1.call-done = f32[64,5632]{1,0:T(8,128)} async-done(((f32[2048,5632]{1,0:T(8,128)}), f32[64,5632]{1,0:T(8,128)}) %reduce-scatter.15.cloned.1.call-update) | async-done | bytes 1441808 | tf_op jit(solution)/shard_map/reduce_scatter | solution.py:346
  1048.6 5.4 multiply_add_fusion.4
  1054.3 141.1 %all-gather.17.cloned.1.call-done = bf16[2048,5632]{1,0:T(8,128)(2,1)} async-done(((bf16[64,5632]{1,0:T(8,128)(2,1)}), bf16[2048,5632]{1,0:T(8,128)(2,1)}) %all-gather.17.cloned.1.call-update) | async-done | bytes 23068688 | tf_op jit(solution)/shard_map/all_gather | solution.py:253
  1195.3 21.4 fusion.4
  1216.7 16.1 fusion.80
  1232.9 24.2 multiply_reduce_fusion
  1257.1 3.2 multiply_add_fusion
  1260.3 1.7 copy-done.6
  1262.0 6.9 convolution_convert_fusion.1
  1269.8 7.4 fusion
  1277.2 6.5 fusion.27
  1283.6 11.2 fusion.2
  1294.9 3.9 convolution_bitcast_fusion.1
  1299.5 2.2 fusion.54
  1301.8 4.4 multiply_bitcast_fusion
  1306.2 1.1 add_convert_fusion
  1307.4 2.0 pad_maximum_fusion
  1309.4 2.0 copy.92
  1311.4 8.4 fusion.66
  1319.9 1.3 copy-done.13
  1321.3 10.1 fusion.30
  1331.5 1.3 copy-done.8
  1332.8 20.5 fusion.82
  1353.4 1.3 copy-done.17
  1354.7 21.0 fusion.83
  1375.8 1.1 slice.110
  1378.7 6.0 fusion.81
  1384.8 3.0 fusion.23
  1387.7 38.9 %all-reduce.4 = (f32[2048]{0:T(1024)S(1)}, f32[2048]{0:T(1024)S(1)}) all-reduce(f32[2048]{0:T(1024)S(1)} %copy-done.59, f32[2048]{0:T(1024)S(1)} %get-tuple-element.232), channel_id=5, replica_groups=mesh['dp'=4,'fsdp'=8] {'dp','fsdp'}, use_global_device_ids=true, to_apply=%region_12.13.clone | all-reduce | flops 4096 | bytes 32768
  1427.3 5.5 fusion.22
  1432.9 16.1 convolution_add_fusion.2
  1449.0 1.6 multiply_add_fusion.12
  1450.6 172.1 %reduce-scatter.7.cloned.1.call-done = f32[64,2048]{1,0:T(8,128)} async-done(((f32[2048,2048]{1,0:T(8,128)}), f32[64,2048]{1,0:T(8,128)}) %reduce-scatter.7.cloned.1.call-update) | async-done | bytes 524304 | tf_op jit(solution)/shard_map/reduce_scatter | solution.py:342
  1622.7 2.3 multiply_add_fusion.10
  1625.0 184.3 %reduce-scatter.11.cloned.1.call-done = f32[64,2048]{1,0:T(8,128)} async-done(((f32[2048,2048]{1,0:T(8,128)}), f32[64,2048]{1,0:T(8,128)}) %reduce-scatter.11.cloned.1.call-update) | async-done | bytes 524304 | tf_op jit(solution)/shard_map/reduce_scatter | solution.py:344
  1809.4 2.6 multiply_add_fusion.8
  1812.0 489.4 %reduce-scatter.13.cloned.1.call-done = f32[64,5632]{1,0:T(8,128)} async-done(((f32[2048,5632]{1,0:T(8,128)}), f32[64,5632]{1,0:T(8,128)}) %reduce-scatter.13.cloned.1.call-update) | async-done | bytes 1441808 | tf_op jit(solution)/shard_map/reduce_scatter | solution.py:345
  2301.4 4.7 multiply_add_fusion.6
  2306.1 486.0 %reduce-scatter.17.cloned.1.call-done = f32[176,2048]{1,0:T(8,128)} async-done(((f32[5632,2048]{1,0:T(8,128)}), f32[176,2048]{1,0:T(8,128)}) %reduce-scatter.17.cloned.1.call-update) | async-done | bytes 1441808 | tf_op jit(solution)/shard_map/reduce_scatter | solution.py:347
  2792.2 4.9 multiply_add_fusion.2
  (192 shorter events, 10.8 us)
Async XLA Ops:
  7.2 7.9 copy-start.18
  7.2 61.0 %all-gather.9.cloned.1.call-start = ((), (), s32[]{:S(2)}) async-start(), calls=%async_computation.6 | async-start | bytes 1081344 | tf_op jit(solution)/shard_map/all_gather | solution.py:225
  8.8 139.5 %all-gather.11.cloned.1.call-start = ((), (), s32[]{:S(2)}) async-start(), calls=%async_computation.7 | async-start | bytes 8650752 | tf_op jit(solution)/shard_map/all_gather | solution.py:224
  10.7 217.2 %all-gather.13.cloned.1.call-start = ((), (), s32[]{:S(2)}) async-start(), calls=%async_computation.8 | async-start | bytes 8650752 | tf_op jit(solution)/shard_map/all_gather | solution.py:244
  12.5 3.6 copy-start.62
  12.5 46.3 %copy-start.58 = (s32[1,384]{1,0:T(1,128)S(1)}, s32[1,384]{1,0:T(1,128)}, u32[]{:S(2)}) copy-start(s32[1,384]{1,0:T(1,128)} %param.28) | copy-start | bytes 4612
  12.5 47.3 %copy-start.1 = (bf16[384,2048]{1,0:T(8,128)(2,1)S(1)}, bf16[384,2048]{1,0:T(8,128)(2,1)}, u32[]{:S(2)}) copy-start(bf16[384,2048]{1,0:T(8,128)(2,1)} %param.25) | copy-start | bytes 4718596
  12.5 361.9 %all-gather.19.cloned.1.call-start = ((), (), s32[]{:S(2)}) async-start(), calls=%async_computation.11 | async-start | bytes 23789568 | tf_op jit(solution)/shard_map/all_gather | solution.py:259
  15.0 505.5 %all-gather.15.cloned.1.call-start = ((), (), s32[]{:S(2)}) async-start(), calls=%async_computation.9 | async-start | bytes 23789568 | tf_op jit(solution)/shard_map/all_gather | solution.py:252
  16.1 1032.6 %reduce-scatter.15.cloned.1.call-start = ((), (), s32[]{:S(2)}) async-start(), calls=%async_computation.16 | async-start | bytes 47579136 | tf_op jit(solution)/shard_map/reduce_scatter | solution.py:346
  58.8 89.5 %copy-start.48 = (f32[2048]{0:T(1024)}, f32[2048]{0:T(1024)S(1)}, u32[]{:S(2)}) copy-start(f32[2048]{0:T(1024)S(1)} %convert_element_type.165) | copy-start | bytes 24580
  59.7 11.1 copy-start.60
  60.2 94.0 %copy-start.54 = (f32[384]{0:T(512)}, f32[384]{0:T(512)S(1)}, u32[]{:S(2)}) copy-start(f32[384]{0:T(512)S(1)} %add_rsqrt_fusion.1) | copy-start | bytes 4612
  60.2 94.0 %copy-start.56 = (f32[384]{0:T(512)}, f32[384]{0:T(512)S(1)}, u32[]{:S(2)}) copy-start(f32[384]{0:T(512)S(1)} %fusion.57) | copy-start | bytes 4612
  60.3 101.5 %copy-start.21 = (pred[384,384]{0,1:T(8,128)(4,1)}, pred[384,384]{0,1:T(8,128)(4,1)S(1)}, u32[]{:S(2)}) copy-start(pred[384,384]{0,1:T(8,128)(4,1)S(1)} %fusion.33) | copy-start | bytes 442372
  71.1 87.6 %copy-start.31 = (bf16[384,64]{0,1:T(8,128)(2,1)}, bf16[384,64]{0,1:T(8,128)(2,1)S(1)}, u32[]{:S(2)}) copy-start(bf16[384,64]{0,1:T(8,128)(2,1)S(1)} %get-tuple-element.272) | copy-start | bytes 147460
  71.1 87.6 %copy-start.33 = (bf16[384,64]{0,1:T(8,128)(2,1)}, bf16[384,64]{0,1:T(8,128)(2,1)S(1)}, u32[]{:S(2)}) copy-start(bf16[384,64]{0,1:T(8,128)(2,1)S(1)} %get-tuple-element.273) | copy-start | bytes 147460
  71.2 84.7 %copy-start.25 = (f32[384,64]{1,0:T(8,128)}, f32[384,64]{1,0:T(8,128)S(1)}, u32[]{:S(2)}) copy-start(f32[384,64]{1,0:T(8,128)S(1)} %copy.85) | copy-start | bytes 294916
  71.3 84.6 %copy-start.27 = (f32[384,64]{1,0:T(8,128)}, f32[384,64]{1,0:T(8,128)S(1)}, u32[]{:S(2)}) copy-start(f32[384,64]{1,0:T(8,128)S(1)} %copy.83) | copy-start | bytes 294916
  160.2 3.6 copy-start
  160.2 3.6 copy-start.36
  163.7 3.3 copy-start.50
  167.0 66.9 %copy-start.12 = (bf16[128,16,384]{2,0,1:T(8,128)(2,1)}, bf16[128,16,384]{2,0,1:T(8,128)(2,1)S(1)}, u32[]{:S(2)}) copy-start(bf16[128,16,384]{2,0,1:T(8,128)(2,1)S(1)} %fusion.26) | copy-start | bytes 4718596
  233.9 140.5 %copy-start.16 = (bf16[384,2048]{1,0:T(8,128)(2,1)S(1)}, bf16[384,2048]{1,0:T(8,128)(2,1)}, u32[]{:S(2)}) copy-start(bf16[384,2048]{1,0:T(8,128)(2,1)} %param.26) | copy-start | bytes 4718596
  235.9 959.4 %copy-start.7 = (bf16[384,2048]{1,0:T(8,128)(2,1)}, bf16[384,2048]{1,0:T(8,128)(2,1)S(1)}, u32[]{:S(2)}) copy-start(bf16[384,2048]{1,0:T(8,128)(2,1)S(1)} %multiply_convert_fusion.1) | copy-start | bytes 4718596
  534.1 3.3 copy-start.11
  558.4 490.3 %copy-start.29 = (f32[64,5632]{1,0:T(8,128)S(1)}, f32[64,5632]{1,0:T(8,128)}, u32[]{:S(2)}) copy-start(f32[64,5632]{1,0:T(8,128)} %param.46) | copy-start | bytes 4325380
  558.4 495.7 %copy-start.47 = (bf16[384,256]{1,0:T(8,128)(2,1)S(1)}, bf16[384,256]{1,0:T(8,128)(2,1)}, u32[]{:S(2)}) copy-start(bf16[384,256]{1,0:T(8,128)(2,1)} %param.27) | copy-start | bytes 589828
  558.4 495.8 %copy-start.51 = (f32[16,384]{1,0:T(8,128)S(1)}, f32[16,384]{1,0:T(8,128)}, u32[]{:S(2)}) copy-start(f32[16,384]{1,0:T(8,128)} %copy-done.50) | copy-start | bytes 73732
  558.4 636.9 %all-gather.17.cloned.1.call-start = ((), (), s32[]{:S(2)}) async-start(), calls=%async_computation.10 | async-start | bytes 23789568 | tf_op jit(solution)/shard_map/all_gather | solution.py:253
  1054.0 395.0 %reduce-scatter.9.cloned.1.call-start = ((), (), s32[]{:S(2)}) async-start(), calls=%async_computation.13 | async-start | bytes 2162688 | tf_op jit(solution)/shard_map/reduce_scatter | solution.py:343
  1216.7 16.1 copy-start.4
  1283.6 11.2 copy-start.10
  1294.9 3.9 copy-start.46
  1294.9 4.0 copy-start.57
  1294.9 4.0 copy-start.61
  1294.9 4.5 copy-start.2
  1294.9 4.5 copy-start.49
  1294.9 4.5 copy-start.55
  1301.7 4.5 copy-start.26
  1301.7 4.5 copy-start.28
  1301.7 321.0 %reduce-scatter.7.cloned.1.call-start = ((), (), s32[]{:S(2)}) async-start(), calls=%async_computation.12 | async-start | bytes 17301504 | tf_op jit(solution)/shard_map/reduce_scatter | solution.py:342
  1311.4 8.4 copy-start.14
  1319.9 489.5 %reduce-scatter.11.cloned.1.call-start = ((), (), s32[]{:S(2)}) async-start(), calls=%async_computation.14 | async-start | bytes 17301504 | tf_op jit(solution)/shard_map/reduce_scatter | solution.py:344
  1331.4 970.0 %reduce-scatter.13.cloned.1.call-start = ((), (), s32[]{:S(2)}) async-start(), calls=%async_computation.15 | async-start | bytes 47579136 | tf_op jit(solution)/shard_map/reduce_scatter | solution.py:345
  1353.4 1438.8 %reduce-scatter.17.cloned.1.call-start = ((), (), s32[]{:S(2)}) async-start(), calls=%async_computation.17 | async-start | bytes 47579136 | tf_op jit(solution)/shard_map/reduce_scatter | solution.py:347
  1378.7 6.0 copy-start.30
  1378.7 6.1 copy-start.40
  1378.7 6.1 copy-start.43
  1378.7 6.1 copy-start.45
  1384.7 3.0 copy-start.59
  1384.7 42.0 %copy-start.63 = (f32[2,64]{1,0:T(2,128)S(1)}, f32[2,64]{1,0:T(2,128)}, u32[]{:S(2)}) copy-start(f32[2,64]{1,0:T(2,128)} %param.29) | copy-start | bytes 1540
  1384.8 42.0 %copy-start.64 = (f32[2,64]{1,0:T(2,128)S(1)}, f32[2,64]{1,0:T(2,128)}, u32[]{:S(2)}) copy-start(f32[2,64]{1,0:T(2,128)} %param.31) | copy-start | bytes 1540
  1384.8 42.0 %copy-start.65 = (f32[2,64]{1,0:T(2,128)S(1)}, f32[2,64]{1,0:T(2,128)}, u32[]{:S(2)}) copy-start(f32[2,64]{1,0:T(2,128)} %param.30) | copy-start | bytes 1540
  1427.3 5.5 copy-start.5
  1432.8 16.2 copy-start.41
  1432.9 16.2 copy-start.52
  1432.9 16.2 copy-start.53
  1432.9 189.9 %copy-start.23 = (f32[64,2048]{1,0:T(8,128)S(1)}, f32[64,2048]{1,0:T(8,128)}, u32[]{:S(2)}) copy-start(f32[64,2048]{1,0:T(8,128)} %param.32) | copy-start | bytes 1572868
  1432.9 189.8 %copy-start.37 = (f32[64,2048]{1,0:T(8,128)S(1)}, f32[64,2048]{1,0:T(8,128)}, u32[]{:S(2)}) copy-start(f32[64,2048]{1,0:T(8,128)} %param.34) | copy-start | bytes 1572868
  1432.9 189.8 %copy-start.38 = (f32[64,2048]{1,0:T(8,128)S(1)}, f32[64,2048]{1,0:T(8,128)}, u32[]{:S(2)}) copy-start(f32[64,2048]{1,0:T(8,128)} %param.33) | copy-start | bytes 1572868
  1449.0 360.4 %copy-start.24 = (f32[64,2048]{1,0:T(8,128)S(1)}, f32[64,2048]{1,0:T(8,128)}, u32[]{:S(2)}) copy-start(f32[64,2048]{1,0:T(8,128)} %param.38) | copy-start | bytes 1572868
  1450.6 850.8 %copy-start.19 = (f32[64,5632]{1,0:T(8,128)S(1)}, f32[64,5632]{1,0:T(8,128)}, u32[]{:S(2)}) copy-start(f32[64,5632]{1,0:T(8,128)} %param.41) | copy-start | bytes 4325380
  1812.0 980.1 %copy-start.20 = (f32[176,2048]{1,0:T(8,128)S(1)}, f32[176,2048]{1,0:T(8,128)}, u32[]{:S(2)}) copy-start(f32[176,2048]{1,0:T(8,128)} %param.47) | copy-start | bytes 4325380
  (14 other events, 25.5 us)
Sparse Core Ops, SparseCore 0:
  11.6 56.5 all-gather.8
  71.8 76.4 all-gather.10
  151.9 75.9 all-gather.12
  231.2 143.2 all-gather.18
  377.7 142.7 all-gather.14
  558.5 490.0 reduce-scatter.14
  1054.1 141.1 all-gather.16
  1301.8 135.2 reduce-scatter.8
  1439.5 183.1 reduce-scatter.6
  1625.0 184.3 reduce-scatter.10
  1811.8 489.6 reduce-scatter.12
  2303.7 488.4 reduce-scatter.16
where the time goes:
time: 2810 us; the launch traced here: 2800 us
  waiting for transfers between devices  2380 us (85%)
  matrix products  246 us (9%)
  blocking collectives  81 us (3%)
  other arithmetic  61.3 us (2%)
    reduce_scatter x1, waiting for transfers between devices, shards(): lax.psum_scatter(grad_up_w, ('dp', 'fsdp'), scatter_dimension=0, tiled=True)  490 us
    reduce_scatter x1, waiting for transfers between devices, shards(): lax.psum_scatter(grad_gate_w, ('dp', 'fsdp'), scatter_dimension=0, tiled=...  489 us
    reduce_scatter x1, waiting for transfers between devices, shards(): lax.psum_scatter(grad_down_w, ('dp', 'fsdp'), scatter_dimension=0, tiled=...  486 us
    reduce_scatter x1, waiting for transfers between devices, shards(): lax.psum_scatter(grad_output_w, ('dp', 'fsdp'), scatter_dimension=0, tile...  184 us
    reduce_scatter x1, waiting for transfers between devices, shards(): lax.psum_scatter(grad_query_w, ('dp', 'fsdp'), scatter_dimension=0, tiled...  172 us
    all_gather x1, waiting for transfers between devices, shards(): lax.all_gather(up_low, ('dp', 'fsdp'), axis=0, tiled=True)  141 us
    all_gather x1, waiting for transfers between devices, shards(): lax.all_gather(down_low, ('dp', 'fsdp'), axis=0, tiled=True)  139 us
    all_gather x1, waiting for transfers between devices, shards(): lax.all_gather(gate_low, ('dp', 'fsdp'), axis=0, tiled=True)  131 us
  transfers between devices with their start and end apart: 12, of which 11 were waited for; matrix products, arithmetic and copies ran while one was open for 6% of the time, Pallas kernels for 0%

commit v1 on v0

v1 whole, which is shorter than its diff:
```python
import functools
import math

import jax
import jax.numpy as jnp
from jax import lax
from jax.experimental import pallas as pl
from jax.experimental.pallas import tpu as pltpu
from jax.sharding import PartitionSpec as P

EPS = 1e-05
THETA = 10000.0
MOMENTUM = 0.9
AVERAGE = 0.75
NEG = -1e30
F32 = jnp.float32
BF16 = jnp.bfloat16
BOTH = ("dp", "fsdp")
COST = 0.2
VMEM_BYTES = 60 * 1024 * 1024


def positions_of(doc_ids):
    length = doc_ids.shape[-1]
    offsets = jnp.arange(length, dtype=jnp.int32)
    same = doc_ids[..., :, None] == doc_ids[..., None, :]
    starts = jnp.min(jnp.where(same, offsets, length), axis=-1)
    return offsets - starts


def rotation(positions, head_dim):
    half_dim = head_dim // 2
    inverse = THETA ** (-(jnp.arange(half_dim, dtype=F32) * 2.0) / head_dim)
    angles = positions.astype(F32)[..., None] * inverse
    cosine, sine = jnp.cos(angles), jnp.sin(angles)
    return (
        jnp.concatenate([cosine, cosine], axis=-1),
        jnp.concatenate([-sine, sine], axis=-1),
    )


def dot(left, right, contract, kind=F32):
    return lax.dot_general(
        left, right, ((contract[:1], contract[1:]), ((), ())), preferred_element_type=F32
    ).astype(kind)


def limits(flops=0, moved=0, steps=1):
    semantics = ("arbitrary",) * steps if steps else None
    return {
        "compiler_params": pltpu.CompilerParams(
            vmem_limit_bytes=VMEM_BYTES, dimension_semantics=semantics
        ),
        "cost_estimate": pl.CostEstimate(
            flops=int(flops * COST), bytes_accessed=int(moved * COST), transcendentals=0
        ),
    }


def swap_halves(values):
    return pltpu.roll(values, values.shape[-1] // 2, values.ndim - 1)


def set_bias(bias, ids_row, ids_col):
    shape = bias.shape
    later = lax.broadcasted_iota(jnp.int32, shape, 1) > lax.broadcasted_iota(jnp.int32, shape, 0)
    apart = (ids_col[0] != ids_row[0]) | later
    bias[...] = jnp.where(apart, NEG, 0.0)


def probabilities(query, keys, bias):
    scores = dot(query, keys, (1, 1)) + bias[...]
    weights = jnp.exp(scores - jnp.max(scores, axis=-1, keepdims=True))
    return weights / jnp.sum(weights, axis=-1, keepdims=True)


def attend_kernel(
    scale, q_raw, k_raw, v_raw, cosine, sine, ids_row, ids_col, queries, attended, shared, bias
):
    head_dim = q_raw.shape[1]

    @pl.when(pl.program_id(1) == 0)
    def _():
        set_bias(bias, ids_row, ids_col)
        key = k_raw[...]
        turned = key * cosine[...] + swap_halves(key) * sine[...]
        shared[:, :head_dim] = turned.astype(BF16)
        shared[:, head_dim:] = v_raw[...].astype(BF16)

    raw = q_raw[...]
    query = ((raw * cosine[...] + swap_halves(raw) * sine[...]) * scale).astype(BF16)
    queries[...] = query
    probs = probabilities(query, shared[:, :head_dim], bias).astype(BF16)
    attended[...] = dot(probs, shared[:, head_dim:], (1, 0), BF16)


def attend(raw, cosine, sine, doc_ids, head_count, head_dim):
    seq_count, length = doc_ids.shape
    rows = seq_count * length
    column = lambda which: pl.BlockSpec((length, head_dim), which)
    whole = pl.BlockSpec((length, head_dim), lambda s, h: (s, 0))
    return pl.pallas_call(
        functools.partial(attend_kernel, head_dim ** (-0.5)),
        grid=(seq_count, head_count),
        in_specs=[
            column(lambda s, h: (s, h)),
            column(lambda s, h: (s, head_count)),
            column(lambda s, h: (s, head_count + 1)),
            whole,
            whole,
            pl.BlockSpec((1, 1, length), lambda s, h: (s, 0, 0)),
            pl.BlockSpec((1, length, 1), lambda s, h: (s, 0, 0)),
        ],
        out_specs=[
            column(lambda s, h: (s, h)),
            column(lambda s, h: (s, h)),
            pl.BlockSpec((length, 2 * head_dim), lambda s, h: (s, 0)),
        ],
        out_shape=[
            jax.ShapeDtypeStruct((rows, head_count * head_dim), BF16),
            jax.ShapeDtypeStruct((rows, head_count * head_dim), BF16),
            jax.ShapeDtypeStruct((rows, 2 * head_dim), BF16),
        ],
        scratch_shapes=[pltpu.VMEM((length, length), F32)],
        name="attend",
        **limits(6 * rows * length * head_dim * head_count, 10 * rows * head_count * head_dim, 2),
    )(raw, raw, raw, cosine, sine, doc_ids[:, None, :], doc_ids[:, :, None])


def attend_back_kernel(
    scale, head_count, query_ref, grad_ref, shared, kv_next, cosine, sine, ids_row, ids_col,
    out, bias, grad_keys, grad_values,
):
    head_dim = query_ref.shape[1]
    head = pl.program_id(1)

    def turn_back(grads):
        return grads * cosine[...] - swap_halves(grads) * sine[...]

    @pl.when(head == 0)
    def _():
        set_bias(bias, ids_row, ids_col)
        grad_keys[...] = jnp.zeros_like(grad_keys)
        grad_values[...] = jnp.zeros_like(grad_values)

    @pl.when(head < head_count)
    def _():
        query, grad = query_ref[...], grad_ref[...]
        keys, values = shared[:, :head_dim], shared[:, head_dim:]
        probs = probabilities(query, keys, bias)
        grad_probs = dot(grad, values, (1, 1))
        inner = jnp.sum(probs * grad_probs, axis=-1, keepdims=True)
        grad_scores = (probs * (grad_probs - inner)).astype(BF16)
        grad_query = dot(grad_scores, keys, (1, 0), BF16).astype(F32) * scale
        out[...] = turn_back(grad_query).astype(BF16)
        grad_keys[...] += dot(grad_scores, query, (0, 0))
        grad_values[...] += dot(probs.astype(BF16), grad, (0, 0))

    @pl.when(head == head_count)
    def _():
        grads = (grad_keys[...] + kv_next[:, :head_dim].astype(F32)).astype(BF16).astype(F32)
        out[...] = turn_back(grads).astype(BF16)

    @pl.when(head == head_count + 1)
    def _():
        out[...] = (grad_values[...] + kv_next[:, head_dim:].astype(F32)).astype(BF16)

    @pl.when(head == head_count + 2)
    def _():
        out[...] = jnp.zeros_like(out)


def attend_back(queries, grads, shared, kv_next, cosine, sine, doc_ids, head_count, head_dim):
    seq_count, length = doc_ids.shape
    rows = seq_count * length
    block = (length, head_dim)
    own = pl.BlockSpec(block, lambda s, h: (s, jnp.minimum(h, head_count - 1)))
    whole = pl.BlockSpec(block, lambda s, h: (s, 0))
    pair = pl.BlockSpec((length, 2 * head_dim), lambda s, h: (s, 0))
    return pl.pallas_call(
        functools.partial(attend_back_kernel, head_dim ** (-0.5), head_count),
        grid=(seq_count, head_count + 3),
        in_specs=[
            own,
            own,
            pair,
            pair,
            whole,
            whole,
            pl.BlockSpec((1, 1, length), lambda s, h: (s, 0, 0)),
            pl.BlockSpec((1, length, 1), lambda s, h: (s, 0, 0)),
        ],
        out_specs=pl.BlockSpec(block, lambda s, h: (s, h)),
        out_shape=jax.ShapeDtypeStruct((rows, (head_count + 3) * head_dim), BF16),
        scratch_shapes=[
            pltpu.VMEM((length, length), F32),
            pltpu.VMEM(block, F32),
            pltpu.VMEM(block, F32),
        ],
        name="attend_back",
        **limits(14 * rows * length * head_dim * head_count, 8 * rows * head_count * head_dim, 2),
    )(queries, grads, shared, kv_next, cosine, sine, doc_ids[:, None, :], doc_ids[:, :, None])


def ffn_kernel(normed, cot, gate_w, up_w, down_w, hidden, grad_gate, grad_up, grad_normed, out):
    whole = lambda ref: lambda: ref[...]
    ffn_tile(
        normed, cot, whole(gate_w), whole(up_w), whole(down_w), hidden, grad_gate, grad_up,
        grad_normed, out,
    )


def ffn_tile(normed, cot, gate_w, up_w, down_w, hidden, grad_gate, grad_up, grad_normed, out):
    gate = dot(normed[...], gate_w(), (1, 0))
    up = dot(normed[...], up_w(), (1, 0))
    sigma = 1.0 / (1.0 + jnp.exp(-gate))
    activated = gate * sigma
    hidden[...] = (activated * up).astype(BF16)
    grad_hidden = dot(cot[...], down_w(), (1, 1), BF16).astype(F32)
    grad_up[...] = (grad_hidden * activated).astype(BF16)
    grad_gate[...] = (grad_hidden * up * (sigma * (1.0 + gate * (1.0 - sigma)))).astype(BF16)
    total = dot(grad_gate[...], gate_w(), (1, 1)) + dot(grad_up[...], up_w(), (1, 1))
    grad_normed[...] = total.astype(BF16)
    out[...] = dot(hidden[...], down_w(), (1, 0), BF16)


def ffn_held_kernel(
    spot, normed, cot, held, down, hidden, grad_gate, grad_up, grad_normed, out,
    gate_w, up_w, down_w, sems,
):
    count, f_size, rows, units = gate_w.shape
    first = pl.program_id(0) == 0
    copies = [
        [
            pltpu.make_async_copy(held.at[:, k, which], buffer.at[spot[0] ^ k], sems.at[which, k])
            for k in range(count)
        ]
        for which, buffer in enumerate((gate_w, up_w))
    ]
    copies.append([pltpu.make_async_copy(down, down_w, sems.at[2, 0])])

    @pl.when(first)
    def _():
        for some in copies:
            for copy in some:
                copy.start()

    def ready(which, buffer):
        @pl.when(first)
        def _():
            for copy in copies[which]:
                copy.wait()

        return buffer

    units_of = lambda buffer: buffer[...].reshape(count * f_size * rows, units)
    seen = set()

    def weight(which, buffer, value):
        def read():
            if which not in seen:
                seen.add(which)
                ready(which, buffer)
            return value(buffer)

        return read

    ffn_tile(
        normed, cot, weight(0, gate_w, units_of), weight(1, up_w, units_of),
        weight(2, down_w, lambda ref: ref[...]), hidden, grad_gate, grad_up, grad_normed, out,
    )


def ffn_held(spot, normed, cot, held, down):
    count, width = normed.shape
    f_size, t_size, _, rows, units = held.shape
    tile = math.gcd(count, 256)
    token = pl.BlockSpec((tile, width), lambda t: (t, 0))
    inner = pl.BlockSpec((tile, units), lambda t: (t, 0))
    weights = pltpu.VMEM((t_size, f_size, rows, units), BF16)
    return pl.pallas_call(
        ffn_held_kernel,
        grid=(count // tile,),
        in_specs=[pl.BlockSpec(memory_space=pltpu.SMEM), token, token]
        + [pl.BlockSpec(memory_space=pl.ANY)] * 2,
        out_specs=[inner, inner, inner, token, token],
        out_shape=[jax.ShapeDtypeStruct((count, units), BF16)] * 3
        + [jax.ShapeDtypeStruct((count, width), BF16)] * 2,
        scratch_shapes=[
            weights,
            weights,
            pltpu.VMEM((units, width), BF16),
            pltpu.SemaphoreType.DMA((3, t_size)),
        ],
        name="ffn",
        **limits(12 * count * width * units, 6 * width * units + 8 * count * width),
    )(spot, normed, cot, held, down)


def ffn(normed, cot, gate_w, up_w, down_w):
    count, width = normed.shape
    units = gate_w.shape[1]
    tile = math.gcd(count, 256)
    token = pl.BlockSpec((tile, width), lambda t: (t, 0))
    inner = pl.BlockSpec((tile, units), lambda t: (t, 0))
    fixed = lambda shape: pl.BlockSpec(shape, lambda t: (0, 0), pipeline_mode=pl.Buffered(1))
    return pl.pallas_call(
        ffn_kernel,
        grid=(count // tile,),
        in_specs=[token, token, fixed(gate_w.shape), fixed(up_w.shape), fixed(down_w.shape)],
        out_specs=[inner, inner, inner, token, token],
        out_shape=[jax.ShapeDtypeStruct((count, units), BF16)] * 3
        + [jax.ShapeDtypeStruct((count, width), BF16)] * 2,
        name="ffn",
        **limits(12 * count * width * units, 6 * width * units + 8 * count * width),
    )(normed, cot, gate_w, up_w, down_w)


def dp_swap(value, k):
    size = lax.axis_size("dp")
    return lax.ppermute(value, "dp", [(i, i ^ k) for i in range(size)])


def z_swap(value, k):
    size = lax.axis_size("fsdp")
    return lax.ppermute(value, "fsdp", [(i, i ^ (2 * k)) for i in range(size)])


def core_swap(value):
    size = lax.axis_size("fsdp")
    return lax.ppermute(value, "fsdp", [(i, i ^ 1) for i in range(size)])


def pick(array, index, axis=0):
    return lax.dynamic_index_in_dim(array, index, axis, keepdims=False)


def put(buffer, piece, index, axis=0):
    return lax.dynamic_update_index_in_dim(buffer, piece, index, axis)


def plane_gather(value):
    size = lax.axis_size("dp")
    if size != 4:
        return [value] + [dp_swap(value, k) for k in range(1, size)]
    half = value.shape[0] // 2
    one, two = dp_swap(value, 1), dp_swap(value, 2)
    first = dp_swap(one[:half], 2)
    second = dp_swap(two[half:], 1)
    return [value, one, two, jnp.concatenate([first, second], axis=0)]


def plane_scatter(parts):
    size = len(parts)
    if size != 4:
        total = parts[0].astype(F32)
        for k in range(1, size):
            total = total + dp_swap(parts[k], k).astype(F32)
        return total
    half = parts[0].shape[0] // 2
    far_two = dp_swap(parts[3][:half], 1)
    far_one = dp_swap(parts[3][half:], 2)
    for_two = jnp.concatenate(
        [(parts[2][:half].astype(F32) + far_two.astype(F32)).astype(BF16), parts[2][half:]], axis=0
    )
    for_one = jnp.concatenate(
        [parts[1][:half], (parts[1][half:].astype(F32) + far_one.astype(F32)).astype(BF16)], axis=0
    )
    return (
        parts[0].astype(F32)
        + dp_swap(for_one, 1).astype(F32)
        + dp_swap(for_two, 2).astype(F32)
    )


def line_scatter(terms):
    count = terms.shape[0]
    size = lax.axis_size("fsdp")
    z = lax.axis_index("fsdp") // 2
    right = left = None
    for step in range(count - 1):
        out = pick(terms, jnp.clip(count - 1 - step + z, 0, count - 1))
        if right is not None:
            out = (out.astype(F32) + right.astype(F32)).astype(BF16)
        right = lax.ppermute(
            out, "fsdp", [(i, i + 2) for i in range(size - 2) if i // 2 <= step]
        )
        out = pick(terms, jnp.clip(z - (count - 1 - step), 0, count - 1))
        if left is not None:
            out = (out.astype(F32) + left.astype(F32)).astype(BF16)
        left = lax.ppermute(
            out, "fsdp", [(i, i - 2) for i in range(2, size) if count - 1 - i // 2 <= step]
        )
    return pick(terms, z).astype(F32) + right.astype(F32) + left.astype(F32)


def gather_rows(block):
    t_size, f_size = lax.axis_size("dp"), lax.axis_size("fsdp")
    z_size = f_size // 2
    dp, fs = lax.axis_index("dp"), lax.axis_index("fsdp")
    z, core = fs // 2, fs % 2
    rows, cols = block.shape
    line = jnp.zeros((z_size, rows, cols), block.dtype)
    line = put(line, block, z)
    for k in range(1, z_size):
        line = put(line, z_swap(block, k), z ^ k)
    plane = jnp.zeros((t_size, z_size, rows, cols), block.dtype)
    for k, piece in enumerate(plane_gather(line)):
        plane = put(plane, piece, dp ^ k)
    whole = jnp.zeros((t_size, z_size, 2, rows, cols), block.dtype)
    whole = put(whole, plane, core, 2)
    whole = put(whole, core_swap(plane), 1 - core, 2)
    return whole.reshape(t_size * f_size * rows, cols)


def core_sum(mine, other):
    return (mine.astype(F32) + core_swap(other).astype(F32)).astype(BF16)


def scatter_rows(grads):
    t_size, f_size = lax.axis_size("dp"), lax.axis_size("fsdp")
    z_size = f_size // 2
    dp, fs = lax.axis_index("dp"), lax.axis_index("fsdp")
    core = fs % 2
    rows = grads.shape[0] // (t_size * f_size)
    split = grads.reshape(t_size, z_size, 2, rows, grads.shape[1])
    chip = core_sum(pick(split, core, 2), pick(split, 1 - core, 2))
    line = plane_scatter([pick(chip, dp ^ k) for k in range(t_size)])
    return line_scatter(line.astype(BF16))


def scatter_fsdp(split, axis):
    f_size = lax.axis_size("fsdp")
    core = lax.axis_index("fsdp") % 2
    shape = split.shape
    pairs = split.reshape(shape[:axis] + (f_size // 2, 2) + shape[axis + 1 :])
    chip = core_sum(pick(pairs, core, axis + 1), pick(pairs, 1 - core, axis + 1))
    return line_scatter(jnp.moveaxis(chip, axis, 0))


def place():
    fs = lax.axis_index("fsdp")
    return jnp.stack([lax.axis_index("dp"), fs // 2, fs % 2]).astype(jnp.int32)


def slices_kernel(spot, gate, up, *outs):
    units = outs[0].shape[-1]
    for k, out in enumerate(outs):
        at = pl.ds(pl.multiple_of((spot[0] ^ k) * units, units), units)
        out[0] = gate[:, at].astype(BF16)
        out[1] = up[:, at].astype(BF16)


def slices(spot, gate, up, count):
    rows, units = gate.shape[0], gate.shape[1] // count
    whole = pl.BlockSpec(memory_space=pltpu.VMEM)
    return pl.pallas_call(
        slices_kernel,
        in_specs=[pl.BlockSpec(memory_space=pltpu.SMEM), whole, whole],
        out_specs=[whole] * count,
        out_shape=[jax.ShapeDtypeStruct((2, rows, units), BF16)] * count,
        name="slices",
        **limits(0, 12 * gate.size, 0),
    )(spot, gate, up)


LINE_ORDER = (0, 2, 1, 3)
PIECES = ((0, (0, 2, 1, 3)), (1, (0, 2, 1, 3)), (2, (0, 2, 1, 3)), (3, (0, 2)), (3, (1, 3)))


def fetch_rows(spot, pieces, held, sems):
    z, core = spot[1], spot[2]
    copies = [[] for _ in range(4)]
    for side in range(2):
        for (k, line), piece in zip(PIECES, pieces[side * len(PIECES) :]):
            for at, j in enumerate(line):
                slot = held.at[k, z ^ j, core ^ side]
                sem = sems.at[k, 2 * j + side]
                copies[k].append(pltpu.make_async_copy(piece.at[at], slot, sem))
    for some in copies:
        for copy in some:
            copy.start()
    return copies


def gathered_dot_kernel(back, spot, left, *refs):
    pieces, (out, held, sems) = refs[:-3], refs[-3:]
    copies = fetch_rows(spot, pieces, held, sems)
    count, z_size, cores, rows, cols = held.shape
    block = z_size * cores * rows
    for k in range(count):
        for copy in copies[k]:
            copy.wait()
        weight = held[k].reshape(block, cols)
        at = pl.ds(pl.multiple_of((spot[0] ^ k) * block, block), block)
        if back:
            out[:, at] = dot(left[...], weight, (1, 1), out.dtype)
        elif k == 0:
            out[...] = dot(left[:, at], weight, (1, 0))
        else:
            out[...] += dot(left[:, at], weight, (1, 0))


def gathered_dot(spot, left, pieces, back=False, kind=F32):
    rows, cols = pieces[0].shape[1:]
    count, width = left.shape[0], 32 * rows if back else cols
    whole = pl.BlockSpec(memory_space=pltpu.VMEM)
    return pl.pallas_call(
        functools.partial(gathered_dot_kernel, back),
        in_specs=[pl.BlockSpec(memory_space=pltpu.SMEM), whole]
        + [pl.BlockSpec(memory_space=pl.ANY)] * len(pieces),
        out_specs=whole,
        out_shape=jax.ShapeDtypeStruct((count, width), kind),
        scratch_shapes=[
            pltpu.VMEM((4, 4, 2, rows, cols), BF16),
            pltpu.SemaphoreType.DMA((4, 8)),
        ],
        name="gathered_dot",
        **limits(64 * count * rows * cols, 64 * rows * cols + 4 * count * width, 0),
    )(spot, left, *pieces)


def gather_line(block):
    two = jnp.stack([block, z_swap(block, 2)])
    return jnp.concatenate([two, z_swap(two, 1)])


def gather_plane(line):
    one, two = dp_swap(line, 1), dp_swap(line, 2)
    half = line.shape[0] // 2
    return [line, one, two, dp_swap(one[:half], 2), dp_swap(two[half:], 1)]


def spread(line):
    mine = gather_plane(line)
    return mine + [core_swap(piece) for piece in mine]


def after(value, *others):
    return lax.optimization_barrier((value, *others))[0]


def gather_gains(spot, pieces):
    dp, z, core = spot[0], spot[1], spot[2]
    rows = pieces[0].shape[1]
    ends = [piece[:, :, -128:] for piece in pieces]
    sides = []
    for side in (ends[:5], ends[5:]):
        far = jnp.concatenate(side[3:])
        sides.append(jnp.stack(side[:3] + [far]))
    got = jnp.stack(sides, axis=2)
    got = got[dp ^ jnp.arange(4)]
    line = jnp.array([0, 2, 1, 3], jnp.int32)
    got = got[:, line[z ^ jnp.arange(4)]]
    return got[:, :, core ^ jnp.arange(2)].reshape(32 * rows, 128)


def row_grads_kernel(spot, left, right, *refs):
    extra = refs[0] if len(refs) == 4 else None
    mine, other, held = refs[-3:]
    count, _, rows, cols = held.shape
    found = dot(left[...], right[...], (0, 0), BF16)
    for i in range(count):
        for core in range(2):
            at = (2 * i + core) * rows
            held[i, core, :, : found.shape[1]] = found[at : at + rows]
            if extra is not None:
                held[i, core, :, found.shape[1] :] = extra[at : at + rows]
    z, core = spot[1], spot[2]
    for half in range(2):
        for at in range(2):
            mine[half, 0, at] = held[z ^ (2 * at + half), core]
            other[half, 0, at] = held[z ^ (2 * at + half), 1 - core]


def row_grads(spot, left, right, right_cols, extra=None):
    count, width = left.shape
    rows = width // 32
    cols = right_cols + (0 if extra is None else extra.shape[1])
    turn = lambda k, spot: spot[0] ^ k ^ (k >> 1)
    out = pl.BlockSpec((2, 1, 2, rows, cols), lambda k, spot: (0, k, 0, 0, 0))
    specs = [
        pl.BlockSpec((count, width // 4), lambda k, spot: (0, turn(k, spot))),
        pl.BlockSpec((count, right_cols), lambda k, spot: (0, 0)),
    ]
    operands = [left, right]
    if extra is not None:
        specs.append(pl.BlockSpec((width // 4, extra.shape[1]), lambda k, spot: (turn(k, spot), 0)))
        operands.append(extra)
    return pl.pallas_call(
        row_grads_kernel,
        grid_spec=pltpu.PrefetchScalarGridSpec(
            num_scalar_prefetch=1,
            grid=(4,),
            in_specs=specs,
            out_specs=[out, out],
            scratch_shapes=[pltpu.VMEM((4, 2, rows, cols), BF16)],
        ),
        out_shape=[jax.ShapeDtypeStruct((2, 4, 2, rows, cols), BF16)] * 2,
        name="row_grads",
        **limits(2 * count * width * cols, 2 * width * cols + 2 * count * (width + cols)),
    )(spot, *operands)


def add_low(left, right):
    return (left.astype(F32) + right.astype(F32)).astype(BF16)


def scatter_line(terms):
    near = add_low(terms[:2], z_swap(terms[2:], 1))
    return near[0].astype(F32) + z_swap(near[1], 2).astype(F32)


def scatter_fast(mine, other):
    chip = add_low(mine, core_swap(other))
    even, odd = chip[0], chip[1]
    sent_even, sent_odd = dp_swap(even[1:3], 1), dp_swap(odd[2:4], 2)
    even_own, even_far = add_low(even[0], sent_even[0]), add_low(even[3], sent_even[1])
    odd_own, odd_far = add_low(odd[0], sent_odd[1]), add_low(odd[1], sent_odd[0])
    even = add_low(even_own, dp_swap(even_far, 2))
    odd = add_low(odd_own, dp_swap(odd_far, 1))
    return scatter_line(jnp.concatenate([even, odd]))


def unit_grads_kernel(spot, left, gate, up, mine, other, held):
    count, _, rows, units = held.shape
    z, core = spot[1], spot[2]
    for which, right in enumerate((gate, up)):
        found = dot(left[...], right[...], (0, 0), BF16)
        for i in range(count):
            for side in range(2):
                at = (2 * i + side) * rows
                held[i, side] = found[at : at + rows]
        for at, j in enumerate(LINE_ORDER):
            mine[at, 0, which] = held[z ^ j, core]
            other[at, 0, which] = held[z ^ j, 1 - core]


def unit_grads(spot, left, gate, up):
    count, width = left.shape
    units, rows = gate.shape[1], width // 32
    out = pl.BlockSpec((4, 1, 2, rows, units), lambda k, spot: (0, k, 0, 0, 0))
    right = pl.BlockSpec((count, units), lambda k, spot: (0, 0))
    return pl.pallas_call(
        unit_grads_kernel,
        grid_spec=pltpu.PrefetchScalarGridSpec(
            num_scalar_prefetch=1,
            grid=(4,),
            in_specs=[
                pl.BlockSpec((count, width // 4), lambda k, spot: (0, spot[0] ^ k)),
                right,
                right,
            ],
            out_specs=[out, out],
            scratch_shapes=[pltpu.VMEM((4, 2, rows, units), BF16)],
        ),
        out_shape=[jax.ShapeDtypeStruct((4, 4, 2, rows, units), BF16)] * 2,
        name="unit_grads",
        **limits(4 * count * width * units, 4 * width * units + 2 * count * (width + 2 * units)),
    )(spot, left, gate, up)


def down_grads_kernel(spot, left, right, mine, other, held):
    count, _, rows, cols = held.shape
    z, core = spot[1], spot[2]
    found = dot(left[...], right[...], (0, 0), BF16)
    for i in range(count):
        for side in range(2):
            at = (2 * i + side) * rows
            held[i, side] = found[at : at + rows]
    for at, j in enumerate(LINE_ORDER):
        mine[at] = held[z ^ j, core]
        other[at] = held[z ^ j, 1 - core]


def down_grads(spot, left, right):
    count, units = left.shape
    width = right.shape[1]
    rows, tile = units // 8, width // 4
    out = pl.BlockSpec((4, rows, tile), lambda n, spot: (0, 0, n))
    return pl.pallas_call(
        down_grads_kernel,
        grid_spec=pltpu.PrefetchScalarGridSpec(
            num_scalar_prefetch=1,
            grid=(4,),
            in_specs=[
                pl.BlockSpec((count, units), lambda n, spot: (0, 0)),
                pl.BlockSpec((count, tile), lambda n, spot: (0, n)),
            ],
            out_specs=[out, out],
            scratch_shapes=[pltpu.VMEM((4, 2, rows, tile), BF16)],
        ),
        out_shape=[jax.ShapeDtypeStruct((4, rows, width), BF16)] * 2,
        name="down_grads",
        **limits(2 * count * width * units, 2 * width * units + 2 * count * (width + units)),
    )(spot, left, right)


def update_units_kernel(which, rate, spot, weight, moment, average, *refs):
    pieces, outs = refs[:-3], refs[-3:]
    units = pieces[0].shape[-1]
    for k, piece in enumerate(pieces):
        at = pl.ds(pl.multiple_of((spot[0] ^ k) * units, units), units)
        results = update(
            weight[:, at], moment[:, at], average[:, at], piece[which].astype(F32), rate
        )
        for out, result in zip(outs, results):
            out[:, at] = result


def update_units(spot, weight, moment, average, pieces, which, rate):
    whole = pl.BlockSpec(memory_space=pltpu.VMEM)
    return pl.pallas_call(
        functools.partial(update_units_kernel, which, rate),
        in_specs=[pl.BlockSpec(memory_space=pltpu.SMEM)] + [whole] * (3 + len(pieces)),
        out_specs=[whole] * 3,
        out_shape=[jax.ShapeDtypeStruct(weight.shape, F32)] * 3,
        name="update_units",
        **limits(0, 32 * weight.size, 0),
    )(spot, weight, moment, average, *pieces)


def norm_back(grad_normed, scaled, inv_rms, gain_full):
    grad_scaled = grad_normed * gain_full
    grad_gain = jnp.sum(grad_normed * scaled, axis=0)
    grad_in = inv_rms * (
        grad_scaled - scaled * jnp.mean(grad_scaled * scaled, axis=-1, keepdims=True)
    )
    return (grad_gain, grad_in)


def update(weight, moment, average, grad, rate):
    moment_new = MOMENTUM * moment + grad
    weight_new = weight - rate * (grad + MOMENTUM * moment_new)
    average_new = AVERAGE * average + (1.0 - AVERAGE) * weight_new
    return (moment_new, weight_new, average_new)


def shards(
    tokens_in,
    out_grad,
    kv_grad_next,
    doc_ids,
    gains,
    gains_mom,
    gains_ema,
    w_query,
    query_mom,
    query_ema,
    w_keyval,
    keyval_mom,
    keyval_ema,
    w_output,
    output_mom,
    output_ema,
    w_gate,
    gate_mom,
    gate_ema,
    w_up,
    up_mom,
    up_ema,
    w_down,
    down_mom,
    down_ema,
):
    t_size, f_size = lax.axis_size("dp"), lax.axis_size("fsdp")
    dp = lax.axis_index("dp")
    seq_count, length = doc_ids.shape
    width = tokens_in.shape[1]
    head_dim = w_keyval.shape[1] // 2
    head_count = w_query.shape[1] // head_dim
    hidden_units = w_gate.shape[1]
    rows = seq_count * length
    heads_width = head_count * head_dim
    tokens_total = rows * t_size * f_size
    own_rows = w_query.shape[0]
    slice_units = hidden_units // t_size

    gain_cols = jnp.zeros((own_rows, 128), BF16).at[:, :2].set(gains.astype(BF16).T)
    qkv_block = jnp.concatenate([w_query.astype(BF16), w_keyval.astype(BF16), gain_cols], axis=1)
    fast = t_size == 4 and f_size == 8 and own_rows % 16 == 0
    spot = place()

    def to_slices(weight):
        split = weight.astype(BF16).reshape(own_rows, t_size, slice_units)
        held = jnp.zeros((t_size, own_rows, slice_units), BF16)
        held = put(held, pick(split, dp, 1), dp)
        for k in range(1, t_size):
            held = put(held, dp_swap(pick(split, dp ^ k, 1), k), dp ^ k)
        whole = lax.all_gather(held, "fsdp", axis=0)
        return jnp.swapaxes(whole, 0, 1).reshape(width, slice_units)

    if fast:
        qkv_line = gather_line(qkv_block)
        qkv_pieces = spread(qkv_line)
        output_line = gather_line(after(w_output.astype(BF16), qkv_line))
        output_pieces = spread(after(output_line, qkv_pieces[3], qkv_pieces[4]))
        pieces = slices(spot, w_gate, w_up, t_size)
        held = jnp.stack([pieces[0]] + [dp_swap(pieces[k], k) for k in range(1, t_size)])
        held = lax.all_gather(after(held, output_line), "fsdp", axis=0)
        gain_rows = gather_gains(spot, qkv_pieces)
        down_block = after(w_down.astype(BF16), qkv_pieces[1], qkv_pieces[2])
    else:
        qkv_full = gather_rows(qkv_block)
        output_full = gather_rows(w_output.astype(BF16))
        gate_slice = to_slices(w_gate)
        up_slice = to_slices(w_up)
        gain_rows = qkv_full[:, -128:]
        down_block = w_down.astype(BF16)
    down_slice = lax.all_gather(down_block, "fsdp", axis=0, tiled=True)
    cot_all = jnp.concatenate(plane_gather(out_grad), axis=0)

    inputs = tokens_in.astype(F32)
    inv_rms = lax.rsqrt(jnp.mean(inputs * inputs, axis=-1, keepdims=True) + EPS)
    scaled = inputs * inv_rms
    gains_full = gain_rows[:, :2].astype(F32).T
    gain_attn, gain_ffn = gains_full[0], gains_full[1]
    normed = (scaled * gain_attn).astype(BF16)
    raw = gathered_dot(spot, normed, qkv_pieces) if fast else dot(normed, qkv_full, (1, 0))
    cosine, sine = rotation(positions_of(doc_ids).reshape(rows), head_dim)
    queries, attended, shared = attend(raw, cosine, sine, doc_ids, head_count, head_dim)
    if fast:
        resid = inputs + gathered_dot(spot, attended, output_pieces)
    else:
        resid = inputs + dot(attended, output_full, (1, 0))

    inv_rms2 = lax.rsqrt(jnp.mean(resid * resid, axis=-1, keepdims=True) + EPS)
    scaled2 = resid * inv_rms2
    normed2 = (scaled2 * gain_ffn).astype(BF16)
    normed2_all = jnp.concatenate(plane_gather(normed2), axis=0)
    if fast:
        results = ffn_held(spot, normed2_all, cot_all, held, down_slice)
    else:
        results = ffn(normed2_all, cot_all, gate_slice, up_slice, down_slice)
    hidden, grad_gate, grad_up, grad_normed2_part, ffn_part = results
    grad_normed2 = plane_scatter(
        [grad_normed2_part[k * rows : (k + 1) * rows] for k in range(t_size)]
    )
    ffn_out = plane_scatter([ffn_part[k * rows : (k + 1) * rows] for k in range(t_size)])
    layer_out = resid + ffn_out
    def from_slices(grads):
        own = scatter_fsdp(grads.reshape(t_size, f_size, own_rows, slice_units), 1)
        own = own.reshape(t_size, own_rows, slice_units)
        held = jnp.zeros((own_rows, t_size, slice_units), F32)
        held = put(held, pick(own, dp), dp, 1)
        for k in range(1, t_size):
            sent = dp_swap(pick(own, dp ^ k).astype(BF16), k)
            held = put(held, sent.astype(F32), dp ^ k, 1)
        return held.reshape(own_rows, hidden_units)

    if fast:
        mine, other = down_grads(spot, hidden, cot_all)
        down_sum = scatter_line(add_low(mine, core_swap(other)))
        mine, other = unit_grads(spot, normed2_all, grad_gate, grad_up)
        unit_sum = scatter_line(add_low(mine, core_swap(other)))
        unit_pieces = [unit_sum[0]] + [
            dp_swap(unit_sum[k].astype(BF16), k) for k in range(1, t_size)
        ]
    else:
        grad_down_w = dot(hidden, cot_all, (0, 0), BF16)
        down_sum = scatter_fsdp(grad_down_w.reshape(f_size, -1, width), 0)
        gate_sum = from_slices(dot(normed2_all, grad_gate, (0, 0), BF16))
        up_sum = from_slices(dot(normed2_all, grad_up, (0, 0), BF16))

    grad_gain_ffn, grad_through = norm_back(grad_normed2, scaled2, inv_rms2, gain_ffn)
    grad_resid = out_grad.astype(F32) + grad_through
    grad_branch = grad_resid.astype(BF16)
    if fast:
        grad_attended = gathered_dot(spot, grad_branch, output_pieces, True, BF16)
    else:
        grad_attended = dot(grad_branch, output_full, (1, 1), BF16)
    if fast:
        output_sum = scatter_fast(*row_grads(spot, attended, grad_branch, width))
    else:
        output_sum = scatter_rows(dot(attended, grad_branch, (0, 0), BF16))
    grad_raw = attend_back(
        queries, grad_attended, shared, kv_grad_next, cosine, sine, doc_ids, head_count, head_dim
    )
    if fast:
        grad_normed = gathered_dot(spot, grad_raw, qkv_pieces, True)
    else:
        grad_normed = dot(grad_raw, qkv_full, (1, 1))
    grad_gain_attn, grad_first = norm_back(grad_normed, scaled, inv_rms, gain_attn)
    input_grad = grad_resid + grad_first
    gain_grads = jnp.zeros((width, 128), BF16)
    gain_grads = gain_grads.at[:, :2].set(
        jnp.stack([grad_gain_attn, grad_gain_ffn], axis=0).astype(BF16).T
    )
    if fast:
        raw_width = grad_raw.shape[1] - 128
        qkv_sum = scatter_fast(*row_grads(spot, normed, grad_raw, raw_width, gain_grads))
    else:
        qkv_sum = scatter_rows(dot(normed, grad_raw, (0, 0), BF16).at[:, -128:].set(gain_grads))
    query_sum = qkv_sum[:, :heads_width]
    keyval_sum = qkv_sum[:, heads_width : heads_width + 2 * head_dim]
    gains_sum = qkv_sum[:, -128:-126].T

    def rate(strength, fan):
        return strength / math.sqrt(fan * tokens_total)

    gains_out = update(gains, gains_mom, gains_ema, gains_sum, rate(0.1, 1))
    query_out = update(w_query, query_mom, query_ema, query_sum, rate(0.6, width))
    keyval_out = update(w_keyval, keyval_mom, keyval_ema, keyval_sum, rate(0.15, width))
    output_out = update(w_output, output_mom, output_ema, output_sum, rate(5.0, heads_width))
    if fast:
        strength = rate(0.6, width)
        gate_out = update_units(spot, w_gate, gate_mom, gate_ema, unit_pieces, 0, strength)
        up_out = update_units(spot, w_up, up_mom, up_ema, unit_pieces, 1, strength)
    else:
        gate_out = update(w_gate, gate_mom, gate_ema, gate_sum, rate(0.6, width))
        up_out = update(w_up, up_mom, up_ema, up_sum, rate(0.6, width))
    down_out = update(w_down, down_mom, down_ema, down_sum, rate(1.5, hidden_units))
    return (
        layer_out,
        shared.astype(F32),
        input_grad,
        *gains_out,
        *query_out,
        *keyval_out,
        *output_out,
        *gate_out,
        *up_out,
        *down_out,
    )


def solution(mesh):
    rows = P(BOTH, None)
    cols = P(None, BOTH)
    return jax.shard_map(
        shards,
        mesh=mesh,
        in_specs=(rows,) * 4 + (cols,) * 3 + (rows,) * 18,
        out_specs=(rows,) * 3 + (cols,) * 3 + (rows,) * 18,
        check_vma=False,
    )
```

time: 2810 us -> 868 us (0.31)
  waiting for transfers between devices: 2380 us -> 417 us
  matrix products: 246 us -> 0 us
  Pallas kernels: 0 us -> 218 us
  blocking collectives: 81 us -> 0 us
  starting transfers between devices: 0.5 us -> 71.1 us
  local copies, waits for them, and re-layouts: 20.9 us -> 50.2 us
    reduce_scatter x6 -> x0, waiting for transfers between devices: 1820 us -> none  [the longest x1 490 us: shards(): lax.psum_scatter(grad_up_w, ('dp', 'fsdp'), scatter_dimension=0, tiled=True)]
    all_gather x6 -> x2, waiting for transfers between devices: 556 us -> 0.01 us  [the longest x1 0.01 us: shards(): down_slice = lax.all_gather(down_block, 'fsdp', axis=0, tiled=True)]
    ppermute x0 -> x64, waiting for transfers between devices: none -> 417 us  [the longest x38 226 us: dp_swap(): return lax.ppermute(value, 'dp', [(i, i ^ k) for i in range(size)])]
    dot_general x24 -> x0, matrix products: 246 us -> none  [the longest x1 24.2 us: shards(): jnp.einsum('tf,df->td', grad_up, up_full, preferred_element_type=jnp.floa...]
    pallas_call x0 -> x14, Pallas kernels: none -> 218 us  [the longest x1 70.1 us: ffn_held(): pl.pallas_call(ffn_held_kernel, grid=(count // tile,), in_specs=[pl.Block...]
    unnamed x2 -> x0, blocking collectives: 81 us -> none
    ppermute x0 -> x64, starting transfers between devices: none -> 71 us  [the longest x38 40.6 us: dp_swap(): return lax.ppermute(value, 'dp', [(i, i ^ k) for i in range(size)])]
  transfers between devices with their start and end apart: 12 -> 66, of which waited for: 11 -> 31; matrix products, arithmetic and copies ran while one was open for 6% -> 14% of each run, Pallas kernels for 0% -> 16%
where the time goes in v1:
time: 868 us; the launch traced here: 859 us
  waiting for transfers between devices  417 us (48%)
  Pallas kernels  218 us (25%)
  other arithmetic  86.6 us (10%)
  starting transfers between devices  71.1 us (8%)
  local copies, waits for them, and re-layouts  50.2 us (6%)
  between operations  15.5 us (2%)
    ppermute x38, waiting for transfers between devices, dp_swap(): return lax.ppermute(value, 'dp', [(i, i ^ k) for i in range(size)])  226 us
    ppermute x12, waiting for transfers between devices, z_swap(): return lax.ppermute(value, 'fsdp', [(i, i ^ 2 * k) for i in range(size)])  191 us
    pallas_call x1, Pallas kernels, ffn_held(): pl.pallas_call(ffn_held_kernel, grid=(count // tile,), in_specs=[pl.Block...  70.1 us
    ppermute x38, starting transfers between devices, dp_swap(): return lax.ppermute(value, 'dp', [(i, i ^ k) for i in range(size)])  40.6 us
    pallas_call x4, Pallas kernels, gathered_dot(): pl.pallas_call(functools.partial(gathered_dot_kernel, back), in_specs=[pl...  37.1 us
    pallas_call x1, Pallas kernels, unit_grads(): pl.pallas_call(unit_grads_kernel, grid_spec=pltpu.PrefetchScalarGridSpec(...  27.7 us
    ppermute x12, starting transfers between devices, z_swap(): return lax.ppermute(value, 'fsdp', [(i, i ^ 2 * k) for i in range(size)])  27.6 us
    convert_element_type x12, other arithmetic, add_low(): return (left.astype(F32) + right.astype(F32)).astype(BF16)  27.3 us
  transfers between devices with their start and end apart: 66, of which 31 were waited for; matrix products, arithmetic and copies ran while one was open for 14% of the time, Pallas kernels for 16%

profile of v1, /device:TPU:0, one launch (start us, length us, event | category | flops | bytes accessed | tf_op | source)
XLA Modules:
  0.0 858.9 jit_solution(15383944843134958010)
XLA Ops:
  11.4 4.1 collective-permute-start
  15.5 14.0 %collective-permute-done = bf16[64,2432]{1,0:T(8,128)(2,1)S(1)} collective-permute-done((bf16[64,2432]{1,0:T(8,128)(2,1)S(1)}, bf16[64,2432]{1,0:T(8,128)(2,1)S(1)}, u32[]{:S(2)}, u32[]{:S(2)}) %collective-permute-start) | collective-permute-done | bytes 311328 | tf_op jit(solution)/shard_map/ppermute | solution.py:326
  30.4 14.5 %collective-permute-done.1 = bf16[2,64,2432]{2,1,0:T(8,128)(2,1)S(1)} collective-permute-done((bf16[2,64,2432]{2,1,0:T(8,128)(2,1)S(1)}, bf16[2,64,2432]{2,1,0:T(8,128)(2,1)S(1)}, u32[]{:S(2)}, u32[]{:S(2)}) %collective-permute-start.1) | collective-permute-done | bytes 622624 | tf_op jit(solution)/shard_map/ppermute | solution.py:326
  48.8 23.9 %collective-permute-done.2.refs_1_ = bf16[4,64,2432]{2,1,0:T(8,128)(2,1)S(1)} collective-permute-done((bf16[4,64,2432]{2,1,0:T(8,128)(2,1)S(1)}, bf16[4,64,2432]{2,1,0:T(8,128)(2,1)S(1)}, u32[]{:S(2)}, u32[]{:S(2)}) %collective-permute-start.2) | collective-permute-done | bytes 1245216 | tf_op jit(solution)/shard_map/ppermute | solution.py:321
  75.0 4.5 collective-permute-start.11
  80.2 3.0 slices.1
  86.7 9.8 %collective-permute-done.11 = bf16[64,2048]{1,0:T(8,128)(2,1)S(1)} collective-permute-done((bf16[64,2048]{1,0:T(8,128)(2,1)S(1)}, bf16[64,2048]{1,0:T(8,128)(2,1)S(1)}, u32[]{:S(2)}, u32[]{:S(2)}) %collective-permute-start.11) | collective-permute-done | bytes 262176 | tf_op jit(solution)/shard_map/ppermute | solution.py:326
  97.3 8.2 collective-permute-start.12
  105.6 2.4 pad_maximum_fusion.4
  108.1 36.8 %collective-permute-done.12 = bf16[2,64,2048]{2,1,0:T(8,128)(2,1)} collective-permute-done((bf16[2,64,2048]{2,1,0:T(8,128)(2,1)}, bf16[2,64,2048]{2,1,0:T(8,128)(2,1)}, u32[]{:S(2)}, u32[]{:S(2)}) %collective-permute-start.12) | collective-permute-done | bytes 524320 | tf_op jit(solution)/shard_map/ppermute | solution.py:326
  144.9 2.1 pad_maximum_fusion.6.refs_0_
  148.4 1.9 slice.400
  153.4 1.9 slice.402
  156.2 2.1 pad_maximum_fusion.10
  158.8 5.9 collective-permute-done.4.refs_3_
  166.1 6.0 collective-permute-done.5.refs_4_
  178.8 2.4 gather_fusion
  181.2 2.5 gather_fusion.2
  183.7 2.5 gather_fusion.3
  187.2 11.5 %collective-permute-done.13.refs_1_ = bf16[4,64,2048]{2,1,0:T(8,128)(2,1)S(1)} collective-permute-done((bf16[4,64,2048]{2,1,0:T(8,128)(2,1)}, bf16[4,64,2048]{2,1,0:T(8,128)(2,1)S(1)}, u32[]{:S(2)}, u32[]{:S(2)}) %collective-permute-start.13) | collective-permute-done | bytes 1048608 | tf_op jit(solution)/shard_map/ppermute | solution.py:321
  203.3 9.2 %collective-permute-done.15.refs_3_ = bf16[2,64,2048]{2,1,0:T(8,128)(2,1)S(1)} collective-permute-done((bf16[2,64,2048]{2,1,0:T(8,128)(2,1)S(1)}, bf16[2,64,2048]{2,1,0:T(8,128)(2,1)S(1)}, u32[]{:S(2)}, u32[]{:S(2)}) %collective-permute-start.15) | collective-permute-done | bytes 524320 | tf_op jit(solution)/shard_map/ppermute | solution.py:321
  215.6 9.8 %gathered_dot.4.q_raw.k_raw.v_raw = f32[384,2432]{1,0:T(8,128)} custom-call(s32[3]{0:T(128)} %pad_add_fusion.spot, bf16[384,2048]{1,0:T(8,128)(2,1)} %fusion.4.left, bf16[4,64,2432]{2,1,0:T(8,128)(2,1)} %copy-done.5, bf16[4,64,2432]{2,1,0:T(8,128)(2,1)} %copy-done.9, bf16[4,64,2432]{2,1,0:T(8,128)(2,1)} %collective-permute-done.3.refs_2_, ...), custom_call_target="tpu_custom_call" | custom-call | flops 765041024 | bytes 2739404 | tf_op jit(solution)/shard_map/gathered_dot/pallas_call | solution.py:508
  225.5 15.5 %attend.1 = (bf16[384,2048]{1,0:T(8,128)(2,1)}, bf16[384,2048]{1,0:T(8,128)(2,1)}, bf16[384,256]{1,0:T(8,128)(2,1)}) custom-call(f32[384,2432]{1,0:T(8,128)} %gathered_dot.4.q_raw.k_raw.v_raw, f32[384,2432]{1,0:T(8,128)} %gathered_dot.4.q_raw.k_raw.v_raw, f32[384,2432]{1,0:T(8,128)} %gathered_dot.4.q_raw.k_raw.v_raw, f32[384,128]{1,0:T(8,128)} %get-tuple-element.288.cosine, ...), custom_call_target="tpu_custom_call" | custom-call | flops 362387872 | bytes 1572864 | tf_op jit(solution)/shard_map/attend/pallas_call | solution.py:102
  242.8 8.7 %gathered_dot.5 = f32[384,2048]{1,0:T(8,128)} custom-call(s32[3]{0:T(128)} %pad_add_fusion.spot, bf16[384,2048]{1,0:T(8,128)(2,1)} %get-tuple-element.78.left, bf16[4,64,2048]{2,1,0:T(8,128)(2,1)} %pad_maximum_fusion.6.refs_0_, bf16[4,64,2048]{2,1,0:T(8,128)(2,1)} %copy-done.10, bf16[4,64,2048]{2,1,0:T(8,128)(2,1)} %collective-permute-done.14.refs_2_, ...), custom_call_target="tpu_custom_call" | custom-call | flops 644245120 | bytes 2306867 | tf_op jit(solution)/shard_map/gathered_dot/pallas_call | solution.py:508
  251.6 2.9 multiply_reduce_fusion.2
  258.3 20.3 %collective-permute-done.26 = bf16[384,2048]{1,0:T(8,128)(2,1)} collective-permute-done((bf16[384,2048]{1,0:T(8,128)(2,1)}, bf16[384,2048]{1,0:T(8,128)(2,1)}, u32[]{:S(2)}, u32[]{:S(2)}) %collective-permute-start.26) | collective-permute-done | bytes 1572896 | tf_op jit(solution)/shard_map/ppermute | solution.py:321
  287.4 24.8 %collective-permute-done.22 = bf16[384,2048]{1,0:T(8,128)(2,1)S(1)} collective-permute-done((bf16[384,2048]{1,0:T(8,128)(2,1)S(1)}, bf16[384,2048]{1,0:T(8,128)(2,1)S(1)}, u32[]{:S(2)}, u32[]{:S(2)}) %collective-permute-start.22) | collective-permute-done | bytes 1572896 | tf_op jit(solution)/shard_map/ppermute | solution.py:321
  313.8 16.3 %collective-permute-done.28 = bf16[192,2048]{1,0:T(8,128)(2,1)S(1)} collective-permute-done((bf16[192,2048]{1,0:T(8,128)(2,1)S(1)}, bf16[192,2048]{1,0:T(8,128)(2,1)S(1)}, u32[]{:S(2)}, u32[]{:S(2)}) %collective-permute-start.28) | collective-permute-done | bytes 786464 | tf_op jit(solution)/shard_map/ppermute | solution.py:321
  335.0 11.3 %collective-permute-done.24 = bf16[192,2048]{1,0:T(8,128)(2,1)S(1)} collective-permute-done((bf16[192,2048]{1,0:T(8,128)(2,1)S(1)}, bf16[192,2048]{1,0:T(8,128)(2,1)S(1)}, u32[]{:S(2)}, u32[]{:S(2)}) %collective-permute-start.24) | collective-permute-done | bytes 786464 | tf_op jit(solution)/shard_map/ppermute | solution.py:321
  349.5 70.1 %ffn.1 = (bf16[1536,1408]{1,0:T(8,128)(2,1)}, bf16[1536,1408]{1,0:T(8,128)(2,1)}, bf16[1536,1408]{1,0:T(8,128)(2,1)}, bf16[1536,2048]{1,0:T(8,128)(2,1)}, bf16[1536,2048]{1,0:T(8,128)(2,1)}) custom-call(s32[3]{0:T(128)} %pad_add_fusion.spot, bf16[1536,2048]{1,0:T(8,128)(2,1)} %constant_dynamic-update-slice_fusion.normed.left, bf16[1536,2048]{1,0:T(8,128)(2,1)} %copy-done.8, ...), custom_call_target="tpu_custom_call" | custom-call | flops 10630043648 | bytes 8493465 | tf_op jit(solution)/shard_map/ffn/pallas_call | solution.py:281
  419.6 2.2 fusion.31
  426.4 15.9 %collective-permute-done.37 = bf16[192,2048]{1,0:T(8,128)(2,1)S(1)} collective-permute-done((bf16[192,2048]{1,0:T(8,128)(2,1)S(1)}, bf16[192,2048]{1,0:T(8,128)(2,1)S(1)}, u32[]{:S(2)}, u32[]{:S(2)}) %collective-permute-start.37) | collective-permute-done | bytes 786464 | tf_op jit(solution)/shard_map/ppermute | solution.py:321
  443.1 2.0 add_convert_fusion.7
  449.8 9.4 %collective-permute-done.33 = bf16[192,2048]{1,0:T(8,128)(2,1)S(1)} collective-permute-done((bf16[192,2048]{1,0:T(8,128)(2,1)S(1)}, bf16[192,2048]{1,0:T(8,128)(2,1)S(1)}, u32[]{:S(2)}, u32[]{:S(2)}) %collective-permute-start.33) | collective-permute-done | bytes 786464 | tf_op jit(solution)/shard_map/ppermute | solution.py:321
  465.3 14.9 %down_grads.1 = (bf16[4,176,2048]{2,1,0:T(8,128)(2,1)}, bf16[4,176,2048]{2,1,0:T(8,128)(2,1)}) custom-call(s32[3]{0:T(128)} %pad_add_fusion.spot, bf16[1536,1408]{1,0:T(8,128)(2,1)} %get-tuple-element.105.left, bf16[1536,2048]{1,0:T(8,128)(2,1)} %copy-done.8), custom_call_target="tpu_custom_call" | custom-call | flops 1771673984 | bytes 3276800 | tf_op jit(solution)/shard_map/down_grads/pallas_call | solution.py:681
  480.2 27.7 %unit_grads.1 = (bf16[4,4,2,64,1408]{4,3,2,1,0:T(8,128)(2,1)}, bf16[4,4,2,64,1408]{4,3,2,1,0:T(8,128)(2,1)}) custom-call(s32[3]{0:T(128)} %pad_add_fusion.spot, bf16[1536,2048]{1,0:T(8,128)(2,1)} %constant_dynamic-update-slice_fusion.normed.left, bf16[1536,1408]{1,0:T(8,128)(2,1)} %get-tuple-element.95.gate, bf16[1536,1408]{1,0:T(8,128)(2,1)} %get-tuple-element.96.up), custom_call_target="tpu_custom_call" | custom-call | flops 3543347968 | bytes 5295308 | tf_op jit(solution)/shard_map/unit_grads/pallas_call | solution.py:644
  508.3 3.6 multiply_reduce_fusion
  512.0 12.4 %collective-permute-done.34 = bf16[384,2048]{1,0:T(8,128)(2,1)} collective-permute-done((bf16[384,2048]{1,0:T(8,128)(2,1)}, bf16[384,2048]{1,0:T(8,128)(2,1)}, u32[]{:S(2)}, u32[]{:S(2)}) %collective-permute-start.34) | collective-permute-done | bytes 1572896 | tf_op jit(solution)/shard_map/ppermute | solution.py:321
  524.4 7.1 fusion.30
  531.5 9.6 %row_grads.3 = (bf16[2,4,2,64,2048]{4,3,2,1,0:T(8,128)(2,1)}, bf16[2,4,2,64,2048]{4,3,2,1,0:T(8,128)(2,1)}) custom-call(s32[3]{0:T(128)} %pad_add_fusion.spot, bf16[384,2048]{1,0:T(8,128)(2,1)} %get-tuple-element.78.left, bf16[384,2048]{1,0:T(8,128)(2,1)} %get-tuple-element.249.left.right), custom_call_target="tpu_custom_call" | custom-call | flops 644245120 | bytes 2306867 | tf_op jit(solution)/shard_map/row_grads/pallas_call | solution.py:590
  541.2 8.5 gathered_dot.6.grad_ref
  549.7 19.4 %attend_back.1.left.right = bf16[384,2432]{1,0:T(8,128)(2,1)} custom-call(bf16[384,2048]{1,0:T(8,128)(2,1)} %get-tuple-element.90.query_ref, bf16[384,2048]{1,0:T(8,128)(2,1)} %gathered_dot.6.grad_ref, bf16[384,256]{1,0:T(8,128)(2,1)} %get-tuple-element.88.shared, bf16[384,256]{1,0:T(8,128)(2,1)} %kv_next.1, f32[384,128]{1,0:T(8,128)} %get-tuple-element.288.cosine, ...), custom_call_target="tpu_custom_call" | custom-call | flops 845571712 | bytes 1258291 | tf_op jit(solution)/shard_map/attend_back/pallas_call | solution.py:180
  569.1 10.0 %gathered_dot.7 = f32[384,2048]{1,0:T(8,128)} custom-call(s32[3]{0:T(128)} %pad_add_fusion.spot, bf16[384,2432]{1,0:T(8,128)(2,1)} %attend_back.1.left.right, bf16[4,64,2432]{2,1,0:T(8,128)(2,1)} %copy-done.5, bf16[4,64,2432]{2,1,0:T(8,128)(2,1)} %copy-done.9, bf16[4,64,2432]{2,1,0:T(8,128)(2,1)} %collective-permute-done.3.refs_2_, ...), custom_call_target="tpu_custom_call" | custom-call | flops 765041024 | bytes 2621440 | tf_op jit(solution)/shard_map/gathered_dot/pallas_call | solution.py:508
  579.1 2.8 fusion.9
  583.9 10.7 %row_grads.2 = (bf16[2,4,2,64,2432]{4,3,2,1,0:T(8,128)(2,1)}, bf16[2,4,2,64,2432]{4,3,2,1,0:T(8,128)(2,1)}) custom-call(s32[3]{0:T(128)} %pad_add_fusion.spot, bf16[384,2048]{1,0:T(8,128)(2,1)} %fusion.4.left, bf16[384,2432]{1,0:T(8,128)(2,1)} %attend_back.1.left.right, bf16[2048,128]{1,0:T(8,128)(2,1)} %scatter.9.refs_0_), custom_call_target="tpu_custom_call" | custom-call | flops 765041024 | bytes 2680422 | tf_op jit(solution)/shard_map/row_grads/pallas_call | solution.py:590
  595.1 3.9 add_convert_fusion.3
  602.9 5.5 fusion.8
  608.3 27.1 %collective-permute-done.62 = bf16[2,176,2048]{2,1,0:T(8,128)(2,1)S(1)} collective-permute-done((bf16[2,176,2048]{2,1,0:T(8,128)(2,1)}, bf16[2,176,2048]{2,1,0:T(8,128)(2,1)S(1)}, u32[]{:S(2)}, u32[]{:S(2)}) %collective-permute-start.62) | collective-permute-done | bytes 1441824 | tf_op jit(solution)/shard_map/ppermute | solution.py:326
  636.9 3.6 collective-permute-start.63
  640.5 6.5 add_convert_fusion
  650.6 4.1 add_convert_fusion.2
  658.9 5.4 add_convert_fusion.1
  665.1 17.5 %collective-permute-done.49 = bf16[2,2,64,2048]{3,2,1,0:T(8,128)(2,1)S(1)} collective-permute-done((bf16[2,2,64,2048]{3,2,1,0:T(8,128)(2,1)}, bf16[2,2,64,2048]{3,2,1,0:T(8,128)(2,1)S(1)}, u32[]{:S(2)}, u32[]{:S(2)}) %collective-permute-start.49) | collective-permute-done | bytes 1048608 | tf_op jit(solution)/shard_map/ppermute | solution.py:321
  686.7 3.7 multiply_add_fusion.1
  691.3 27.0 %collective-permute-done.52 = bf16[2,64,2048]{2,1,0:T(8,128)(2,1)S(1)} collective-permute-done((bf16[2,64,2048]{2,1,0:T(8,128)(2,1)S(1)}, bf16[2,64,2048]{2,1,0:T(8,128)(2,1)S(1)}, u32[]{:S(2)}, u32[]{:S(2)}) %collective-permute-start.52) | collective-permute-done | bytes 524320 | tf_op jit(solution)/shard_map/ppermute | solution.py:321
  724.1 14.3 %collective-permute-done.53 = bf16[2,64,2048]{2,1,0:T(8,128)(2,1)S(1)} collective-permute-done((bf16[2,64,2048]{2,1,0:T(8,128)(2,1)S(1)}, bf16[2,64,2048]{2,1,0:T(8,128)(2,1)S(1)}, u32[]{:S(2)}, u32[]{:S(2)}) %collective-permute-start.53) | collective-permute-done | bytes 524320 | tf_op jit(solution)/shard_map/ppermute | solution.py:326
  738.9 3.0 add_convert_fusion.4
  742.2 2.5 collective-permute-start.46
  745.3 6.0 collective-permute-done.54
  752.7 17.6 %collective-permute-done.46 = bf16[2,64,2432]{2,1,0:T(8,128)(2,1)S(1)} collective-permute-done((bf16[2,64,2432]{2,1,0:T(8,128)(2,1)S(1)}, bf16[2,64,2432]{2,1,0:T(8,128)(2,1)S(1)}, u32[]{:S(2)}, u32[]{:S(2)}) %collective-permute-start.46) | collective-permute-done | bytes 622624 | tf_op jit(solution)/shard_map/ppermute | solution.py:326
  770.7 49.1 %collective-permute-done.57 = bf16[4,2,64,1408]{3,2,1,0:T(8,128)(2,1)S(1)} collective-permute-done((bf16[4,2,64,1408]{3,2,1,0:T(8,128)(2,1)S(1)}, bf16[4,2,64,1408]{3,2,1,0:T(8,128)(2,1)S(1)}, u32[]{:S(2)}, u32[]{:S(2)}) %collective-permute-start.57) | collective-permute-done | bytes 1441824 | tf_op jit(solution)/shard_map/ppermute | solution.py:326
  831.7 7.9 collective-permute-done.59.refs_2_
  841.1 5.2 update_units.3
  846.3 5.2 update_units.2
  (296 shorter events, 122.8 us)
Async XLA Ops:
  7.2 342.3 %all-gather.4.cloned.1.call-start = ((), (), s32[]{:S(2)}) async-start(), calls=%async_computation | async-start | bytes 6488064 | tf_op jit(solution)/shard_map/all_gather | solution.py:810
  11.4 18.1 %collective-permute-start = (bf16[64,2432]{1,0:T(8,128)(2,1)S(1)}, bf16[64,2432]{1,0:T(8,128)(2,1)S(1)}, u32[]{:S(2)}, u32[]{:S(2)}) collective-permute-start(bf16[64,2432]{1,0:T(8,128)(2,1)S(1)} %get-tuple-element.282), channel_id=1, source_target_pairs={{0,4},{1,5},{2,6},{3,7},{4,0},{5,1},{6,2},{7,3},{8,12},{9,13},{10,... | collective-permute-start | bytes 933896 | tf_op jit(solution)/shard_map/ppermute | solution.py:326
  29.6 15.3 %collective-permute-start.1 = (bf16[2,64,2432]{2,1,0:T(8,128)(2,1)S(1)}, bf16[2,64,2432]{2,1,0:T(8,128)(2,1)S(1)}, u32[]{:S(2)}, u32[]{:S(2)}) collective-permute-start(bf16[2,64,2432]{2,1,0:T(8,128)(2,1)S(1)} %pad_maximum_fusion.7), channel_id=1, source_target_pairs={{0,2},{1,3},{2,0},{3,1},{4,6},{5,7},{6,4},{7,5},{8,10},{9,11},{10,... | collective-permute-start | bytes 1867784 | tf_op jit(solution)/shard_map/ppermute | solution.py:326
  45.1 27.7 %collective-permute-start.2 = (bf16[4,64,2432]{2,1,0:T(8,128)(2,1)S(1)}, bf16[4,64,2432]{2,1,0:T(8,128)(2,1)S(1)}, u32[]{:S(2)}, u32[]{:S(2)}) collective-permute-start(bf16[4,64,2432]{2,1,0:T(8,128)(2,1)S(1)} %pad_maximum_fusion.5.refs_0_), channel_id=1, source_target_pairs={{0,8},{8,0},{16,24},{24,16},{1,9},{9,1},{17,25},{25,17},{2,10},{10... | collective-permute-start | bytes 3735560 | tf_op jit(solution)/shard_map/ppermute | solution.py:321
  46.4 27.5 %collective-permute-start.3 = (bf16[4,64,2432]{2,1,0:T(8,128)(2,1)S(1)}, bf16[4,64,2432]{2,1,0:T(8,128)(2,1)}, u32[]{:S(2)}, u32[]{:S(2)}) collective-permute-start(bf16[4,64,2432]{2,1,0:T(8,128)(2,1)S(1)} %pad_maximum_fusion.5.refs_0_), channel_id=1, source_target_pairs={{0,16},{8,24},{16,0},{24,8},{1,17},{9,25},{17,1},{25,9},{2,18},{10... | collective-permute-start | bytes 3735560 | tf_op jit(solution)/shard_map/ppermute | solution.py:321
  73.9 275.6 %all-gather.6.cloned.1.call-start = ((), (), s32[]{:S(2)}) async-start(), calls=%async_computation.1 | async-start | bytes 12976128 | tf_op jit(solution)/shard_map/all_gather | solution.py:800
  75.0 21.5 %collective-permute-start.11 = (bf16[64,2048]{1,0:T(8,128)(2,1)S(1)}, bf16[64,2048]{1,0:T(8,128)(2,1)S(1)}, u32[]{:S(2)}, u32[]{:S(2)}) collective-permute-start(bf16[64,2048]{1,0:T(8,128)(2,1)S(1)} %convert_element_type.378), channel_id=1, source_target_pairs={{0,4},{1,5},{2,6},{3,7},{4,0},{5,1},{6,2},{7,3},{8,12},{9,13},{10,... | collective-permute-start | bytes 786440 | tf_op jit(solution)/shard_map/ppermute | solution.py:326
  83.2 22.4 %collective-permute-start.30 = (bf16[2,64,1408]{2,1,0:T(8,128)(2,1)}, bf16[2,64,1408]{2,1,0:T(8,128)(2,1)S(1)}, u32[]{:S(2)}, u32[]{:S(2)}) collective-permute-start(bf16[2,64,1408]{2,1,0:T(8,128)(2,1)} %get-tuple-element.82), channel_id=1, source_target_pairs={{0,8},{8,0},{16,24},{24,16},{1,9},{9,1},{17,25},{25,17},{2,10},{10... | collective-permute-start | bytes 1081352 | tf_op jit(solution)/shard_map/ppermute | solution.py:321
  83.8 21.8 %collective-permute-start.31 = (bf16[2,64,1408]{2,1,0:T(8,128)(2,1)}, bf16[2,64,1408]{2,1,0:T(8,128)(2,1)S(1)}, u32[]{:S(2)}, u32[]{:S(2)}) collective-permute-start(bf16[2,64,1408]{2,1,0:T(8,128)(2,1)} %get-tuple-element.83), channel_id=1, source_target_pairs={{0,16},{8,24},{16,0},{24,8},{1,17},{9,25},{17,1},{25,9},{2,18},{10... | collective-permute-start | bytes 1081352 | tf_op jit(solution)/shard_map/ppermute | solution.py:321
  85.3 20.3 %collective-permute-start.32 = (bf16[2,64,1408]{2,1,0:T(8,128)(2,1)}, bf16[2,64,1408]{2,1,0:T(8,128)(2,1)S(1)}, u32[]{:S(2)}, u32[]{:S(2)}) collective-permute-start(bf16[2,64,1408]{2,1,0:T(8,128)(2,1)} %get-tuple-element.84), channel_id=1, source_target_pairs={{0,24},{8,16},{16,8},{24,0},{1,25},{9,17},{17,9},{25,1},{2,26},{10... | collective-permute-start | bytes 1081352 | tf_op jit(solution)/shard_map/ppermute | solution.py:321
  97.3 47.5 %collective-permute-start.12 = (bf16[2,64,2048]{2,1,0:T(8,128)(2,1)}, bf16[2,64,2048]{2,1,0:T(8,128)(2,1)}, u32[]{:S(2)}, u32[]{:S(2)}) collective-permute-start(bf16[2,64,2048]{2,1,0:T(8,128)(2,1)} %pad_maximum_fusion.9), channel_id=1, source_target_pairs={{0,2},{1,3},{2,0},{3,1},{4,6},{5,7},{6,4},{7,5},{8,10},{9,11},{10,... | collective-permute-start | bytes 1572872 | tf_op jit(solution)/shard_map/ppermute | solution.py:326
  150.3 14.3 %collective-permute-start.4 = (bf16[2,64,2432]{2,1,0:T(8,128)(2,1)}, bf16[2,64,2432]{2,1,0:T(8,128)(2,1)S(1)}, u32[]{:S(2)}, u32[]{:S(2)}) collective-permute-start(bf16[2,64,2432]{2,1,0:T(8,128)(2,1)} %slice.400), channel_id=1, source_target_pairs={{0,16},{8,24},{16,0},{24,8},{1,17},{9,25},{17,1},{25,9},{2,18},{10... | collective-permute-start | bytes 1867784 | tf_op jit(solution)/shard_map/ppermute | solution.py:321
  151.8 21.1 %collective-permute-start.6 = (bf16[4,64,2432]{2,1,0:T(8,128)(2,1)S(1)}, bf16[4,64,2432]{2,1,0:T(8,128)(2,1)}, u32[]{:S(2)}, u32[]{:S(2)}) collective-permute-start(bf16[4,64,2432]{2,1,0:T(8,128)(2,1)S(1)} %pad_maximum_fusion.5.refs_0_), channel_id=1, source_target_pairs={{0,1},{1,0},{2,3},{3,2},{4,5},{5,4},{6,7},{7,6},{8,9},{9,8},{10,11... | collective-permute-start | bytes 3735560 | tf_op jit(solution)/shard_map/ppermute | solution.py:331
  155.3 16.8 %collective-permute-start.5 = (bf16[2,64,2432]{2,1,0:T(8,128)(2,1)}, bf16[2,64,2432]{2,1,0:T(8,128)(2,1)}, u32[]{:S(2)}, u32[]{:S(2)}) collective-permute-start(bf16[2,64,2432]{2,1,0:T(8,128)(2,1)} %slice.402), channel_id=1, source_target_pairs={{0,8},{8,0},{16,24},{24,16},{1,9},{9,1},{17,25},{25,17},{2,10},{10... | collective-permute-start | bytes 1867784 | tf_op jit(solution)/shard_map/ppermute | solution.py:321
  158.3 17.4 %collective-permute-start.8 = (bf16[4,64,2432]{2,1,0:T(8,128)(2,1)}, bf16[4,64,2432]{2,1,0:T(8,128)(2,1)S(1)}, u32[]{:S(2)}, u32[]{:S(2)}) collective-permute-start(bf16[4,64,2432]{2,1,0:T(8,128)(2,1)} %collective-permute-done.3.refs_2_), channel_id=1, source_target_pairs={{0,1},{1,0},{2,3},{3,2},{4,5},{5,4},{6,7},{7,6},{8,9},{9,8},{10,11... | collective-permute-start | bytes 3735560 | tf_op jit(solution)/shard_map/ppermute | solution.py:331
  164.7 12.1 %collective-permute-start.7 = (bf16[4,64,2432]{2,1,0:T(8,128)(2,1)}, bf16[4,64,2432]{2,1,0:T(8,128)(2,1)S(1)}, u32[]{:S(2)}, u32[]{:S(2)}) collective-permute-start(bf16[4,64,2432]{2,1,0:T(8,128)(2,1)} %copy-done.9), channel_id=1, source_target_pairs={{0,1},{1,0},{2,3},{3,2},{4,5},{5,4},{6,7},{7,6},{8,9},{9,8},{10,11... | collective-permute-start | bytes 3735560 | tf_op jit(solution)/shard_map/ppermute | solution.py:331
  172.9 25.8 %collective-permute-start.13 = (bf16[4,64,2048]{2,1,0:T(8,128)(2,1)}, bf16[4,64,2048]{2,1,0:T(8,128)(2,1)S(1)}, u32[]{:S(2)}, u32[]{:S(2)}) collective-permute-start(bf16[4,64,2048]{2,1,0:T(8,128)(2,1)} %pad_maximum_fusion.6.refs_0_), channel_id=1, source_target_pairs={{0,8},{8,0},{16,24},{24,16},{1,9},{9,1},{17,25},{25,17},{2,10},{10... | collective-permute-start | bytes 3145736 | tf_op jit(solution)/shard_map/ppermute | solution.py:321
  173.3 26.2 %collective-permute-start.14 = (bf16[4,64,2048]{2,1,0:T(8,128)(2,1)}, bf16[4,64,2048]{2,1,0:T(8,128)(2,1)}, u32[]{:S(2)}, u32[]{:S(2)}) collective-permute-start(bf16[4,64,2048]{2,1,0:T(8,128)(2,1)} %pad_maximum_fusion.6.refs_0_), channel_id=1, source_target_pairs={{0,16},{8,24},{16,0},{24,8},{1,17},{9,25},{17,1},{25,9},{2,18},{10... | collective-permute-start | bytes 3145736 | tf_op jit(solution)/shard_map/ppermute | solution.py:321
  175.6 65.4 %collective-permute-start.17 = (bf16[4,64,2048]{2,1,0:T(8,128)(2,1)}, bf16[4,64,2048]{2,1,0:T(8,128)(2,1)}, u32[]{:S(2)}, u32[]{:S(2)}) collective-permute-start(bf16[4,64,2048]{2,1,0:T(8,128)(2,1)} %pad_maximum_fusion.6.refs_0_), channel_id=1, source_target_pairs={{0,1},{1,0},{2,3},{3,2},{4,5},{5,4},{6,7},{7,6},{8,9},{9,8},{10,11... | collective-permute-start | bytes 3145736 | tf_op jit(solution)/shard_map/ppermute | solution.py:331
  198.8 13.7 %collective-permute-start.15 = (bf16[2,64,2048]{2,1,0:T(8,128)(2,1)S(1)}, bf16[2,64,2048]{2,1,0:T(8,128)(2,1)S(1)}, u32[]{:S(2)}, u32[]{:S(2)}) collective-permute-start(bf16[2,64,2048]{2,1,0:T(8,128)(2,1)S(1)} %slice.411), channel_id=1, source_target_pairs={{0,16},{8,24},{16,0},{24,8},{1,17},{9,25},{17,1},{25,9},{2,18},{10... | collective-permute-start | bytes 1572872 | tf_op jit(solution)/shard_map/ppermute | solution.py:321
  200.6 13.4 %collective-permute-start.16 = (bf16[2,64,2048]{2,1,0:T(8,128)(2,1)S(1)}, bf16[2,64,2048]{2,1,0:T(8,128)(2,1)S(1)}, u32[]{:S(2)}, u32[]{:S(2)}) collective-permute-start(bf16[2,64,2048]{2,1,0:T(8,128)(2,1)S(1)} %slice.412), channel_id=1, source_target_pairs={{0,8},{8,0},{16,24},{24,16},{1,9},{9,1},{17,25},{25,17},{2,10},{10... | collective-permute-start | bytes 1572872 | tf_op jit(solution)/shard_map/ppermute | solution.py:321
  201.8 41.0 %collective-permute-start.18 = (bf16[4,64,2048]{2,1,0:T(8,128)(2,1)S(1)}, bf16[4,64,2048]{2,1,0:T(8,128)(2,1)}, u32[]{:S(2)}, u32[]{:S(2)}) collective-permute-start(bf16[4,64,2048]{2,1,0:T(8,128)(2,1)S(1)} %collective-permute-done.13.refs_1_), channel_id=1, source_target_pairs={{0,1},{1,0},{2,3},{3,2},{4,5},{5,4},{6,7},{7,6},{8,9},{9,8},{10,11... | collective-permute-start | bytes 3145736 | tf_op jit(solution)/shard_map/ppermute | solution.py:331
  201.8 41.0 %collective-permute-start.19 = (bf16[4,64,2048]{2,1,0:T(8,128)(2,1)}, bf16[4,64,2048]{2,1,0:T(8,128)(2,1)}, u32[]{:S(2)}, u32[]{:S(2)}) collective-permute-start(bf16[4,64,2048]{2,1,0:T(8,128)(2,1)} %collective-permute-done.14.refs_2_), channel_id=1, source_target_pairs={{0,1},{1,0},{2,3},{3,2},{4,5},{5,4},{6,7},{7,6},{8,9},{9,8},{10,11... | collective-permute-start | bytes 3145736 | tf_op jit(solution)/shard_map/ppermute | solution.py:331
  212.6 29.5 %collective-permute-start.20 = (bf16[2,64,2048]{2,1,0:T(8,128)(2,1)S(1)}, bf16[2,64,2048]{2,1,0:T(8,128)(2,1)}, u32[]{:S(2)}, u32[]{:S(2)}) collective-permute-start(bf16[2,64,2048]{2,1,0:T(8,128)(2,1)S(1)} %collective-permute-done.15.refs_3_), channel_id=1, source_target_pairs={{0,1},{1,0},{2,3},{3,2},{4,5},{5,4},{6,7},{7,6},{8,9},{9,8},{10,11... | collective-permute-start | bytes 1572872 | tf_op jit(solution)/shard_map/ppermute | solution.py:331
  214.0 28.8 %collective-permute-start.21 = (bf16[2,64,2048]{2,1,0:T(8,128)(2,1)S(1)}, bf16[2,64,2048]{2,1,0:T(8,128)(2,1)}, u32[]{:S(2)}, u32[]{:S(2)}) collective-permute-start(bf16[2,64,2048]{2,1,0:T(8,128)(2,1)S(1)} %collective-permute-done.16.refs_4_), channel_id=1, source_target_pairs={{0,1},{1,0},{2,3},{3,2},{4,5},{5,4},{6,7},{7,6},{8,9},{9,8},{10,11... | collective-permute-start | bytes 1572872 | tf_op jit(solution)/shard_map/ppermute | solution.py:331
  241.0 37.6 %collective-permute-start.26 = (bf16[384,2048]{1,0:T(8,128)(2,1)}, bf16[384,2048]{1,0:T(8,128)(2,1)}, u32[]{:S(2)}, u32[]{:S(2)}) collective-permute-start(bf16[384,2048]{1,0:T(8,128)(2,1)} %param.31), channel_id=1, source_target_pairs={{0,8},{8,0},{16,24},{24,16},{1,9},{9,1},{17,25},{25,17},{2,10},{10... | collective-permute-start | bytes 4718600 | tf_op jit(solution)/shard_map/ppermute | solution.py:321
  242.1 39.2 %collective-permute-start.27 = (bf16[384,2048]{1,0:T(8,128)(2,1)}, bf16[384,2048]{1,0:T(8,128)(2,1)}, u32[]{:S(2)}, u32[]{:S(2)}) collective-permute-start(bf16[384,2048]{1,0:T(8,128)(2,1)} %param.31), channel_id=1, source_target_pairs={{0,16},{8,24},{16,0},{24,8},{1,17},{9,25},{17,1},{25,9},{2,18},{10... | collective-permute-start | bytes 4718600 | tf_op jit(solution)/shard_map/ppermute | solution.py:321
  256.0 56.2 %collective-permute-start.22 = (bf16[384,2048]{1,0:T(8,128)(2,1)S(1)}, bf16[384,2048]{1,0:T(8,128)(2,1)S(1)}, u32[]{:S(2)}, u32[]{:S(2)}) collective-permute-start(bf16[384,2048]{1,0:T(8,128)(2,1)S(1)} %get-tuple-element.252), channel_id=1, source_target_pairs={{0,8},{8,0},{16,24},{24,16},{1,9},{9,1},{17,25},{25,17},{2,10},{10... | collective-permute-start | bytes 4718600 | tf_op jit(solution)/shard_map/ppermute | solution.py:321
  257.8 72.3 %collective-permute-start.23 = (bf16[384,2048]{1,0:T(8,128)(2,1)S(1)}, bf16[384,2048]{1,0:T(8,128)(2,1)S(1)}, u32[]{:S(2)}, u32[]{:S(2)}) collective-permute-start(bf16[384,2048]{1,0:T(8,128)(2,1)S(1)} %get-tuple-element.252), channel_id=1, source_target_pairs={{0,16},{8,24},{16,0},{24,8},{1,17},{9,25},{17,1},{25,9},{2,18},{10... | collective-permute-start | bytes 4718600 | tf_op jit(solution)/shard_map/ppermute | solution.py:321
  279.8 50.3 %collective-permute-start.28 = (bf16[192,2048]{1,0:T(8,128)(2,1)S(1)}, bf16[192,2048]{1,0:T(8,128)(2,1)S(1)}, u32[]{:S(2)}, u32[]{:S(2)}) collective-permute-start(bf16[192,2048]{1,0:T(8,128)(2,1)S(1)} %slice.416), channel_id=1, source_target_pairs={{0,16},{8,24},{16,0},{24,8},{1,17},{9,25},{17,1},{25,9},{2,18},{10... | collective-permute-start | bytes 2359304 | tf_op jit(solution)/shard_map/ppermute | solution.py:321
  282.5 48.9 %collective-permute-start.29 = (bf16[192,2048]{1,0:T(8,128)(2,1)S(1)}, bf16[192,2048]{1,0:T(8,128)(2,1)S(1)}, u32[]{:S(2)}, u32[]{:S(2)}) collective-permute-start(bf16[192,2048]{1,0:T(8,128)(2,1)S(1)} %slice.417), channel_id=1, source_target_pairs={{0,8},{8,0},{16,24},{24,16},{1,9},{9,1},{17,25},{25,17},{2,10},{10... | collective-permute-start | bytes 2359304 | tf_op jit(solution)/shard_map/ppermute | solution.py:321
  312.3 34.0 %collective-permute-start.24 = (bf16[192,2048]{1,0:T(8,128)(2,1)S(1)}, bf16[192,2048]{1,0:T(8,128)(2,1)S(1)}, u32[]{:S(2)}, u32[]{:S(2)}) collective-permute-start(bf16[192,2048]{1,0:T(8,128)(2,1)S(1)} %slice.414), channel_id=1, source_target_pairs={{0,16},{8,24},{16,0},{24,8},{1,17},{9,25},{17,1},{25,9},{2,18},{10... | collective-permute-start | bytes 2359304 | tf_op jit(solution)/shard_map/ppermute | solution.py:321
  330.2 18.3 %collective-permute-start.25 = (bf16[192,2048]{1,0:T(8,128)(2,1)S(1)}, bf16[192,2048]{1,0:T(8,128)(2,1)S(1)}, u32[]{:S(2)}, u32[]{:S(2)}) collective-permute-start(bf16[192,2048]{1,0:T(8,128)(2,1)S(1)} %slice.415), channel_id=1, source_target_pairs={{0,8},{8,0},{16,24},{24,16},{1,9},{9,1},{17,25},{25,17},{2,10},{10... | collective-permute-start | bytes 2359304 | tf_op jit(solution)/shard_map/ppermute | solution.py:321
  421.8 20.5 %collective-permute-start.37 = (bf16[192,2048]{1,0:T(8,128)(2,1)S(1)}, bf16[192,2048]{1,0:T(8,128)(2,1)S(1)}, u32[]{:S(2)}, u32[]{:S(2)}) collective-permute-start(bf16[192,2048]{1,0:T(8,128)(2,1)S(1)} %get-tuple-element.258), channel_id=1, source_target_pairs={{0,16},{8,24},{16,0},{24,8},{1,17},{9,25},{17,1},{25,9},{2,18},{10... | collective-permute-start | bytes 2359304 | tf_op jit(solution)/shard_map/ppermute | solution.py:321
  422.7 20.5 %collective-permute-start.39 = (bf16[192,2048]{1,0:T(8,128)(2,1)S(1)}, bf16[192,2048]{1,0:T(8,128)(2,1)S(1)}, u32[]{:S(2)}, u32[]{:S(2)}) collective-permute-start(bf16[192,2048]{1,0:T(8,128)(2,1)S(1)} %get-tuple-element.257), channel_id=1, source_target_pairs={{0,8},{8,0},{16,24},{24,16},{1,9},{9,1},{17,25},{25,17},{2,10},{10... | collective-permute-start | bytes 2359304 | tf_op jit(solution)/shard_map/ppermute | solution.py:321
  424.7 34.5 %collective-permute-start.33 = (bf16[192,2048]{1,0:T(8,128)(2,1)S(1)}, bf16[192,2048]{1,0:T(8,128)(2,1)S(1)}, u32[]{:S(2)}, u32[]{:S(2)}) collective-permute-start(bf16[192,2048]{1,0:T(8,128)(2,1)S(1)} %get-tuple-element.264), channel_id=1, source_target_pairs={{0,16},{8,24},{16,0},{24,8},{1,17},{9,25},{17,1},{25,9},{2,18},{10... | collective-permute-start | bytes 2359304 | tf_op jit(solution)/shard_map/ppermute | solution.py:321
  425.3 34.7 %collective-permute-start.35 = (bf16[192,2048]{1,0:T(8,128)(2,1)S(1)}, bf16[192,2048]{1,0:T(8,128)(2,1)S(1)}, u32[]{:S(2)}, u32[]{:S(2)}) collective-permute-start(bf16[192,2048]{1,0:T(8,128)(2,1)S(1)} %get-tuple-element.263), channel_id=1, source_target_pairs={{0,8},{8,0},{16,24},{24,16},{1,9},{9,1},{17,25},{25,17},{2,10},{10... | collective-permute-start | bytes 2359304 | tf_op jit(solution)/shard_map/ppermute | solution.py:321
  446.4 61.5 %collective-permute-start.38 = (bf16[384,2048]{1,0:T(8,128)(2,1)}, bf16[384,2048]{1,0:T(8,128)(2,1)}, u32[]{:S(2)}, u32[]{:S(2)}) collective-permute-start(bf16[384,2048]{1,0:T(8,128)(2,1)} %pad_maximum_fusion.2), channel_id=1, source_target_pairs={{0,8},{8,0},{16,24},{24,16},{1,9},{9,1},{17,25},{25,17},{2,10},{10... | collective-permute-start | bytes 4718600 | tf_op jit(solution)/shard_map/ppermute | solution.py:321
  449.2 59.1 %collective-permute-start.40 = (bf16[384,2048]{1,0:T(8,128)(2,1)}, bf16[384,2048]{1,0:T(8,128)(2,1)}, u32[]{:S(2)}, u32[]{:S(2)}) collective-permute-start(bf16[384,2048]{1,0:T(8,128)(2,1)} %pad_maximum_fusion.3), channel_id=1, source_target_pairs={{0,16},{8,24},{16,0},{24,8},{1,17},{9,25},{17,1},{25,9},{2,18},{10... | collective-permute-start | bytes 4718600 | tf_op jit(solution)/shard_map/ppermute | solution.py:321
  461.9 62.6 %collective-permute-start.34 = (bf16[384,2048]{1,0:T(8,128)(2,1)}, bf16[384,2048]{1,0:T(8,128)(2,1)}, u32[]{:S(2)}, u32[]{:S(2)}) collective-permute-start(bf16[384,2048]{1,0:T(8,128)(2,1)} %pad_maximum_fusion), channel_id=1, source_target_pairs={{0,8},{8,0},{16,24},{24,16},{1,9},{9,1},{17,25},{25,17},{2,10},{10... | collective-permute-start | bytes 4718600 | tf_op jit(solution)/shard_map/ppermute | solution.py:321
  464.7 59.7 %collective-permute-start.36 = (bf16[384,2048]{1,0:T(8,128)(2,1)}, bf16[384,2048]{1,0:T(8,128)(2,1)}, u32[]{:S(2)}, u32[]{:S(2)}) collective-permute-start(bf16[384,2048]{1,0:T(8,128)(2,1)} %pad_maximum_fusion.1), channel_id=1, source_target_pairs={{0,16},{8,24},{16,0},{24,8},{1,17},{9,25},{17,1},{25,9},{2,18},{10... | collective-permute-start | bytes 4718600 | tf_op jit(solution)/shard_map/ppermute | solution.py:321
  480.2 115.0 %collective-permute-start.61 = (bf16[4,176,2048]{2,1,0:T(8,128)(2,1)}, bf16[4,176,2048]{2,1,0:T(8,128)(2,1)}, u32[]{:S(2)}, u32[]{:S(2)}) collective-permute-start(bf16[4,176,2048]{2,1,0:T(8,128)(2,1)} %get-tuple-element.107), channel_id=1, source_target_pairs={{0,1},{1,0},{2,3},{3,2},{4,5},{5,4},{6,7},{7,6},{8,9},{9,8},{10,11... | collective-permute-start | bytes 8650760 | tf_op jit(solution)/shard_map/ppermute | solution.py:331
  507.8 132.7 %collective-permute-start.55 = (bf16[4,4,2,64,1408]{4,3,2,1,0:T(8,128)(2,1)}, bf16[4,4,2,64,1408]{4,3,2,1,0:T(8,128)(2,1)}, u32[]{:S(2)}, u32[]{:S(2)}) collective-permute-start(bf16[4,4,2,64,1408]{4,3,2,1,0:T(8,128)(2,1)} %get-tuple-element.98), channel_id=1, source_target_pairs={{0,1},{1,0},{2,3},{3,2},{4,5},{5,4},{6,7},{7,6},{8,9},{9,8},{10,11... | collective-permute-start | bytes 17301512 | tf_op jit(solution)/shard_map/ppermute | solution.py:331
  541.1 109.5 %collective-permute-start.48 = (bf16[2,4,2,64,2048]{4,3,2,1,0:T(8,128)(2,1)}, bf16[2,4,2,64,2048]{4,3,2,1,0:T(8,128)(2,1)}, u32[]{:S(2)}, u32[]{:S(2)}) collective-permute-start(bf16[2,4,2,64,2048]{4,3,2,1,0:T(8,128)(2,1)} %get-tuple-element.94), channel_id=1, source_target_pairs={{0,1},{1,0},{2,3},{3,2},{4,5},{5,4},{6,7},{7,6},{8,9},{9,8},{10,11... | collective-permute-start | bytes 12582920 | tf_op jit(solution)/shard_map/ppermute | solution.py:331
  594.6 64.3 %collective-permute-start.41 = (bf16[2,4,2,64,2432]{4,3,2,1,0:T(8,128)(2,1)}, bf16[2,4,2,64,2432]{4,3,2,1,0:T(8,128)(2,1)}, u32[]{:S(2)}, u32[]{:S(2)}) collective-permute-start(bf16[2,4,2,64,2432]{4,3,2,1,0:T(8,128)(2,1)} %get-tuple-element.92), channel_id=1, source_target_pairs={{0,1},{1,0},{2,3},{3,2},{4,5},{5,4},{6,7},{7,6},{8,9},{9,8},{10,11... | collective-permute-start | bytes 14942216 | tf_op jit(solution)/shard_map/ppermute | solution.py:331
  601.8 33.7 %collective-permute-start.62 = (bf16[2,176,2048]{2,1,0:T(8,128)(2,1)}, bf16[2,176,2048]{2,1,0:T(8,128)(2,1)S(1)}, u32[]{:S(2)}, u32[]{:S(2)}) collective-permute-start(bf16[2,176,2048]{2,1,0:T(8,128)(2,1)} %slice.454), channel_id=1, source_target_pairs={{0,2},{1,3},{2,0},{3,1},{4,6},{5,7},{6,4},{7,5},{8,10},{9,11},{10,... | collective-permute-start | bytes 4325384 | tf_op jit(solution)/shard_map/ppermute | solution.py:326
  636.9 49.8 %collective-permute-start.63 = (bf16[176,2048]{1,0:T(8,128)(2,1)}, bf16[176,2048]{1,0:T(8,128)(2,1)}, u32[]{:S(2)}, u32[]{:S(2)}) collective-permute-start(bf16[176,2048]{1,0:T(8,128)(2,1)} %slice_bitcast_fusion.6), channel_id=1, source_target_pairs={{0,4},{1,5},{2,6},{3,7},{4,0},{5,1},{6,2},{7,3},{8,12},{9,13},{10,... | collective-permute-start | bytes 2162696 | tf_op jit(solution)/shard_map/ppermute | solution.py:326
  648.9 90.0 %collective-permute-start.56 = (bf16[2,4,2,64,1408]{4,3,2,1,0:T(8,128)(2,1)}, bf16[2,4,2,64,1408]{4,3,2,1,0:T(8,128)(2,1)}, u32[]{:S(2)}, u32[]{:S(2)}) collective-permute-start(bf16[2,4,2,64,1408]{4,3,2,1,0:T(8,128)(2,1)} %slice.446), channel_id=1, source_target_pairs={{0,2},{1,3},{2,0},{3,1},{4,6},{5,7},{6,4},{7,5},{8,10},{9,11},{10,... | collective-permute-start | bytes 8650760 | tf_op jit(solution)/shard_map/ppermute | solution.py:326
  656.3 26.3 %collective-permute-start.49 = (bf16[2,2,64,2048]{3,2,1,0:T(8,128)(2,1)}, bf16[2,2,64,2048]{3,2,1,0:T(8,128)(2,1)S(1)}, u32[]{:S(2)}, u32[]{:S(2)}) collective-permute-start(bf16[2,2,64,2048]{3,2,1,0:T(8,128)(2,1)} %get-tuple-element.275), channel_id=1, source_target_pairs={{0,8},{8,0},{16,24},{24,16},{1,9},{9,1},{17,25},{25,17},{2,10},{10... | collective-permute-start | bytes 3145736 | tf_op jit(solution)/shard_map/ppermute | solution.py:321
  657.8 25.9 %collective-permute-start.51 = (bf16[2,2,64,2048]{3,2,1,0:T(8,128)(2,1)}, bf16[2,2,64,2048]{3,2,1,0:T(8,128)(2,1)}, u32[]{:S(2)}, u32[]{:S(2)}) collective-permute-start(bf16[2,2,64,2048]{3,2,1,0:T(8,128)(2,1)} %get-tuple-element.276), channel_id=1, source_target_pairs={{0,16},{8,24},{16,0},{24,8},{1,17},{9,25},{17,1},{25,9},{2,18},{10... | collective-permute-start | bytes 3145736 | tf_op jit(solution)/shard_map/ppermute | solution.py:321
  664.6 56.5 %collective-permute-start.42 = (bf16[2,2,64,2432]{3,2,1,0:T(8,128)(2,1)S(1)}, bf16[2,2,64,2432]{3,2,1,0:T(8,128)(2,1)S(1)}, u32[]{:S(2)}, u32[]{:S(2)}) collective-permute-start(bf16[2,2,64,2432]{3,2,1,0:T(8,128)(2,1)S(1)} %get-tuple-element.269), channel_id=1, source_target_pairs={{0,8},{8,0},{16,24},{24,16},{1,9},{9,1},{17,25},{25,17},{2,10},{10... | collective-permute-start | bytes 3735560 | tf_op jit(solution)/shard_map/ppermute | solution.py:321
  682.6 38.4 %collective-permute-start.44 = (bf16[2,2,64,2432]{3,2,1,0:T(8,128)(2,1)S(1)}, bf16[2,2,64,2432]{3,2,1,0:T(8,128)(2,1)S(1)}, u32[]{:S(2)}, u32[]{:S(2)}) collective-permute-start(bf16[2,2,64,2432]{3,2,1,0:T(8,128)(2,1)S(1)} %get-tuple-element.270), channel_id=1, source_target_pairs={{0,16},{8,24},{16,0},{24,8},{1,17},{9,25},{17,1},{25,9},{2,18},{10... | collective-permute-start | bytes 3735560 | tf_op jit(solution)/shard_map/ppermute | solution.py:321
  685.1 33.2 %collective-permute-start.52 = (bf16[2,64,2048]{2,1,0:T(8,128)(2,1)S(1)}, bf16[2,64,2048]{2,1,0:T(8,128)(2,1)S(1)}, u32[]{:S(2)}, u32[]{:S(2)}) collective-permute-start(bf16[2,64,2048]{2,1,0:T(8,128)(2,1)S(1)} %get-tuple-element.274), channel_id=1, source_target_pairs={{0,8},{8,0},{16,24},{24,16},{1,9},{9,1},{17,25},{25,17},{2,10},{10... | collective-permute-start | bytes 1572872 | tf_op jit(solution)/shard_map/ppermute | solution.py:321
  690.4 33.7 %collective-permute-start.50 = (bf16[2,64,2048]{2,1,0:T(8,128)(2,1)S(1)}, bf16[2,64,2048]{2,1,0:T(8,128)(2,1)S(1)}, u32[]{:S(2)}, u32[]{:S(2)}) collective-permute-start(bf16[2,64,2048]{2,1,0:T(8,128)(2,1)S(1)} %get-tuple-element.273), channel_id=1, source_target_pairs={{0,16},{8,24},{16,0},{24,8},{1,17},{9,25},{17,1},{25,9},{2,18},{10... | collective-permute-start | bytes 1572872 | tf_op jit(solution)/shard_map/ppermute | solution.py:321
  719.5 18.9 %collective-permute-start.53 = (bf16[2,64,2048]{2,1,0:T(8,128)(2,1)S(1)}, bf16[2,64,2048]{2,1,0:T(8,128)(2,1)S(1)}, u32[]{:S(2)}, u32[]{:S(2)}) collective-permute-start(bf16[2,64,2048]{2,1,0:T(8,128)(2,1)S(1)} %add_convert_fusion.14), channel_id=1, source_target_pairs={{0,2},{1,3},{2,0},{3,1},{4,6},{5,7},{6,4},{7,5},{8,10},{9,11},{10,... | collective-permute-start | bytes 1572872 | tf_op jit(solution)/shard_map/ppermute | solution.py:326
  721.4 20.5 %collective-permute-start.45 = (bf16[2,64,2432]{2,1,0:T(8,128)(2,1)S(1)}, bf16[2,64,2432]{2,1,0:T(8,128)(2,1)S(1)}, u32[]{:S(2)}, u32[]{:S(2)}) collective-permute-start(bf16[2,64,2432]{2,1,0:T(8,128)(2,1)S(1)} %get-tuple-element.268), channel_id=1, source_target_pairs={{0,8},{8,0},{16,24},{24,16},{1,9},{9,1},{17,25},{25,17},{2,10},{10... | collective-permute-start | bytes 1867784 | tf_op jit(solution)/shard_map/ppermute | solution.py:321
  723.0 29.7 %collective-permute-start.43 = (bf16[2,64,2432]{2,1,0:T(8,128)(2,1)S(1)}, bf16[2,64,2432]{2,1,0:T(8,128)(2,1)S(1)}, u32[]{:S(2)}, u32[]{:S(2)}) collective-permute-start(bf16[2,64,2432]{2,1,0:T(8,128)(2,1)S(1)} %get-tuple-element.267), channel_id=1, source_target_pairs={{0,16},{8,24},{16,0},{24,8},{1,17},{9,25},{17,1},{25,9},{2,18},{10... | collective-permute-start | bytes 1867784 | tf_op jit(solution)/shard_map/ppermute | solution.py:321
  738.8 12.6 %collective-permute-start.54 = (bf16[64,2048]{1,0:T(8,128)(2,1)S(1)}, bf16[64,2048]{1,0:T(8,128)(2,1)S(1)}, u32[]{:S(2)}, u32[]{:S(2)}) collective-permute-start(bf16[64,2048]{1,0:T(8,128)(2,1)S(1)} %slice_bitcast_fusion.30), channel_id=1, source_target_pairs={{0,4},{1,5},{2,6},{3,7},{4,0},{5,1},{6,2},{7,3},{8,12},{9,13},{10,... | collective-permute-start | bytes 786440 | tf_op jit(solution)/shard_map/ppermute | solution.py:326
  742.2 28.1 %collective-permute-start.46 = (bf16[2,64,2432]{2,1,0:T(8,128)(2,1)S(1)}, bf16[2,64,2432]{2,1,0:T(8,128)(2,1)S(1)}, u32[]{:S(2)}, u32[]{:S(2)}) collective-permute-start(bf16[2,64,2432]{2,1,0:T(8,128)(2,1)S(1)} %add_convert_fusion.11), channel_id=1, source_target_pairs={{0,2},{1,3},{2,0},{3,1},{4,6},{5,7},{6,4},{7,5},{8,10},{9,11},{10,... | collective-permute-start | bytes 1867784 | tf_op jit(solution)/shard_map/ppermute | solution.py:326
  744.9 74.9 %collective-permute-start.57 = (bf16[4,2,64,1408]{3,2,1,0:T(8,128)(2,1)S(1)}, bf16[4,2,64,1408]{3,2,1,0:T(8,128)(2,1)S(1)}, u32[]{:S(2)}, u32[]{:S(2)}) collective-permute-start(bf16[4,2,64,1408]{3,2,1,0:T(8,128)(2,1)S(1)} %slice_bitcast_fusion), channel_id=1, source_target_pairs={{0,4},{1,5},{2,6},{3,7},{4,0},{5,1},{6,2},{7,3},{8,12},{9,13},{10,... | collective-permute-start | bytes 4325384 | tf_op jit(solution)/shard_map/ppermute | solution.py:326
  770.6 55.7 %collective-permute-start.47 = (bf16[64,2432]{1,0:T(8,128)(2,1)S(1)}, bf16[64,2432]{1,0:T(8,128)(2,1)S(1)}, u32[]{:S(2)}, u32[]{:S(2)}) collective-permute-start(bf16[64,2432]{1,0:T(8,128)(2,1)S(1)} %slice_bitcast_fusion.28), channel_id=1, source_target_pairs={{0,4},{1,5},{2,6},{3,7},{4,0},{5,1},{6,2},{7,3},{8,12},{9,13},{10,... | collective-permute-start | bytes 933896 | tf_op jit(solution)/shard_map/ppermute | solution.py:326
  820.4 11.4 %collective-permute-start.58 = (bf16[2,64,1408]{2,1,0:T(8,128)(2,1)S(1)}, bf16[2,64,1408]{2,1,0:T(8,128)(2,1)S(1)}, u32[]{:S(2)}, u32[]{:S(2)}) collective-permute-start(bf16[2,64,1408]{2,1,0:T(8,128)(2,1)S(1)} %get-tuple-element.280), channel_id=1, source_target_pairs={{0,8},{8,0},{16,24},{24,16},{1,9},{9,1},{17,25},{25,17},{2,10},{10... | collective-permute-start | bytes 1081352 | tf_op jit(solution)/shard_map/ppermute | solution.py:321
  821.9 17.7 %collective-permute-start.59 = (bf16[2,64,1408]{2,1,0:T(8,128)(2,1)S(1)}, bf16[2,64,1408]{2,1,0:T(8,128)(2,1)S(1)}, u32[]{:S(2)}, u32[]{:S(2)}) collective-permute-start(bf16[2,64,1408]{2,1,0:T(8,128)(2,1)S(1)} %get-tuple-element.279), channel_id=1, source_target_pairs={{0,16},{8,24},{16,0},{24,8},{1,17},{9,25},{17,1},{25,9},{2,18},{10... | collective-permute-start | bytes 1081352 | tf_op jit(solution)/shard_map/ppermute | solution.py:321
  823.0 16.6 %collective-permute-start.60 = (bf16[2,64,1408]{2,1,0:T(8,128)(2,1)S(1)}, bf16[2,64,1408]{2,1,0:T(8,128)(2,1)S(1)}, u32[]{:S(2)}, u32[]{:S(2)}) collective-permute-start(bf16[2,64,1408]{2,1,0:T(8,128)(2,1)S(1)} %get-tuple-element.278), channel_id=1, source_target_pairs={{0,24},{8,16},{16,8},{24,0},{1,25},{9,17},{17,9},{25,1},{2,26},{10... | collective-permute-start | bytes 1081352 | tf_op jit(solution)/shard_map/ppermute | solution.py:321
  (43 other events, 616.3 us)
Sparse Core Ops, SparseCore 0:
  74.0 75.1 all-gather.3
  151.4 108.3 all-gather.5

commit v2 on v1

--- a/solution.py
+++ b/solution.py
@@ -16,7 +16,7 @@
 F32 = jnp.float32
 BF16 = jnp.bfloat16
 BOTH = ("dp", "fsdp")
-COST = 0.2
+COST = 0.0
 VMEM_BYTES = 60 * 1024 * 1024
 
 
@@ -224,79 +224,6 @@
     out[...] = dot(hidden[...], down_w(), (1, 0), BF16)
 
 
-def ffn_held_kernel(
-    spot, normed, cot, held, down, hidden, grad_gate, grad_up, grad_normed, out,
-    gate_w, up_w, down_w, sems,
-):
-    count, f_size, rows, units = gate_w.shape
-    first = pl.program_id(0) == 0
-    copies = [
-        [
-            pltpu.make_async_copy(held.at[:, k, which], buffer.at[spot[0] ^ k], sems.at[which, k])
-            for k in range(count)
-        ]
-        for which, buffer in enumerate((gate_w, up_w))
-    ]
-    copies.append([pltpu.make_async_copy(down, down_w, sems.at[2, 0])])
-
-    @pl.when(first)
-    def _():
-        for some in copies:
-            for copy in some:
-                copy.start()
-
-    def ready(which, buffer):
-        @pl.when(first)
-        def _():
-            for copy in copies[which]:
-                copy.wait()
-
-        return buffer
-
-    units_of = lambda buffer: buffer[...].reshape(count * f_size * rows, units)
-    seen = set()
-
-    def weight(which, buffer, value):
-        def read():
-            if which not in seen:
-                seen.add(which)
-                ready(which, buffer)
-            return value(buffer)
-
-        return read
-
-    ffn_tile(
-        normed, cot, weight(0, gate_w, units_of), weight(1, up_w, units_of),
-        weight(2, down_w, lambda ref: ref[...]), hidden, grad_gate, grad_up, grad_normed, out,
-    )
-
-
-def ffn_held(spot, normed, cot, held, down):
-    count, width = normed.shape
-    f_size, t_size, _, rows, units = held.shape
-    tile = math.gcd(count, 256)
-    token = pl.BlockSpec((tile, width), lambda t: (t, 0))
-    inner = pl.BlockSpec((tile, units), lambda t: (t, 0))
-    weights = pltpu.VMEM((t_size, f_size, rows, units), BF16)
-    return pl.pallas_call(
-        ffn_held_kernel,
-        grid=(count // tile,),
-        in_specs=[pl.BlockSpec(memory_space=pltpu.SMEM), token, token]
-        + [pl.BlockSpec(memory_space=pl.ANY)] * 2,
-        out_specs=[inner, inner, inner, token, token],
-        out_shape=[jax.ShapeDtypeStruct((count, units), BF16)] * 3
-        + [jax.ShapeDtypeStruct((count, width), BF16)] * 2,
-        scratch_shapes=[
-            weights,
-            weights,
-            pltpu.VMEM((units, width), BF16),
-            pltpu.SemaphoreType.DMA((3, t_size)),
-        ],
-        name="ffn",
-        **limits(12 * count * width * units, 6 * width * units + 8 * count * width),
-    )(spot, normed, cot, held, down)
-
-
 def ffn(normed, cot, gate_w, up_w, down_w):
     count, width = normed.shape
     units = gate_w.shape[1]
@@ -438,34 +365,103 @@
     return line_scatter(jnp.moveaxis(chip, axis, 0))
 
 
+def norm_back(grad_normed, scaled, inv_rms, gain_full):
+    grad_scaled = grad_normed * gain_full
+    grad_gain = jnp.sum(grad_normed * scaled, axis=0)
+    grad_in = inv_rms * (
+        grad_scaled - scaled * jnp.mean(grad_scaled * scaled, axis=-1, keepdims=True)
+    )
+    return (grad_gain, grad_in)
+
+
+def update(weight, moment, average, grad, rate):
+    moment_new = MOMENTUM * moment + grad
+    weight_new = weight - rate * (grad + MOMENTUM * moment_new)
+    average_new = AVERAGE * average + (1.0 - AVERAGE) * weight_new
+    return (moment_new, weight_new, average_new)
+
+
+LINE_ORDER = (0, 2, 1, 3)
+PIECES = ((0, LINE_ORDER), (1, LINE_ORDER), (2, LINE_ORDER), (3, (0, 2)), (3, (1, 3)))
+SMEM = pl.BlockSpec(memory_space=pltpu.SMEM)
+VMEM = pl.BlockSpec(memory_space=pltpu.VMEM)
+ANY = pl.BlockSpec(memory_space=pl.ANY)
+
+
 def place():
     fs = lax.axis_index("fsdp")
     return jnp.stack([lax.axis_index("dp"), fs // 2, fs % 2]).astype(jnp.int32)
 
 
-def slices_kernel(spot, gate, up, *outs):
-    units = outs[0].shape[-1]
+def after(value, *others):
+    leaves, tree = jax.tree.flatten(value)
+    kept = lax.optimization_barrier((*leaves, *others))[: len(leaves)]
+    return jax.tree.unflatten(tree, kept)
+
+
+SPLIT = 96
+
+
+def slices_kernel(spot, gate, up, down, *outs):
+    outs, packed = outs[:-1], outs[-1]
+    units = packed.shape[1]
     for k, out in enumerate(outs):
         at = pl.ds(pl.multiple_of((spot[0] ^ k) * units, units), units)
         out[0] = gate[:, at].astype(BF16)
         out[1] = up[:, at].astype(BF16)
-
-
-def slices(spot, gate, up, count):
+    rows, width = down.shape
+    rest = width - units
+    packed[:rows] = down[:, :units].astype(BF16)
+    packed[rows:] = jnp.zeros((SPLIT, units), BF16)
+    packed[rows : rows + SPLIT, :rest] = down[:SPLIT, units:].astype(BF16)
+    packed[rows : 2 * rows - SPLIT, rest : 2 * rest] = down[SPLIT:, units:].astype(BF16)
+
+
+def slices(spot, gate, up, down, count):
     rows, units = gate.shape[0], gate.shape[1] // count
-    whole = pl.BlockSpec(memory_space=pltpu.VMEM)
     return pl.pallas_call(
         slices_kernel,
-        in_specs=[pl.BlockSpec(memory_space=pltpu.SMEM), whole, whole],
-        out_specs=[whole] * count,
-        out_shape=[jax.ShapeDtypeStruct((2, rows, units), BF16)] * count,
+        in_specs=[SMEM, VMEM, VMEM, VMEM],
+        out_specs=[VMEM] * (count + 1),
+        out_shape=[jax.ShapeDtypeStruct((2, rows, units), BF16)] * count
+        + [jax.ShapeDtypeStruct((down.shape[0] + SPLIT, units), BF16)],
         name="slices",
         **limits(0, 12 * gate.size, 0),
-    )(spot, gate, up)
-
-
-LINE_ORDER = (0, 2, 1, 3)
-PIECES = ((0, (0, 2, 1, 3)), (1, (0, 2, 1, 3)), (2, (0, 2, 1, 3)), (3, (0, 2)), (3, (1, 3)))
+    )(spot, gate, up, down)
+
+
+def gather_line(block):
+    two, one = z_swap(block, 2), z_swap(block, 1)
+    return jnp.stack([block, two, one, z_swap(two, 1)])
+
+
+def plane_near(value):
+    return dp_swap(value, 1), dp_swap(value, 2)
+
+
+def plane_far(one, two):
+    first, second = cut(one, 0), cut(two, 1)
+    return dp_swap(first, 2), dp_swap(second, 1)
+
+
+def cut_kernel(whole, out):
+    out[...] = whole[...]
+
+
+def cut(whole, index):
+    half = whole.shape[0] // 2
+    rest = (0,) * (whole.ndim - 1)
+    steps = 2 if whole.ndim > 2 else half // 96
+    block = (half // steps,) + whole.shape[1:]
+    return pl.pallas_call(
+        cut_kernel,
+        grid=(steps,),
+        in_specs=[pl.BlockSpec(block, lambda g: (index * steps + g,) + rest)],
+        out_specs=pl.BlockSpec(block, lambda g: (g,) + rest),
+        out_shape=jax.ShapeDtypeStruct((half,) + whole.shape[1:], whole.dtype),
+        name="cut",
+        **limits(0, 2 * whole.size),
+    )(whole)
 
 
 def fetch_rows(spot, pieces, held, sems):
@@ -483,88 +479,433 @@
     return copies
 
 
-def gathered_dot_kernel(back, spot, left, *refs):
-    pieces, (out, held, sems) = refs[:-3], refs[-3:]
-    copies = fetch_rows(spot, pieces, held, sems)
+def blocks_of(spot, copies, held):
     count, z_size, cores, rows, cols = held.shape
-    block = z_size * cores * rows
+    size = z_size * cores * rows
     for k in range(count):
         for copy in copies[k]:
             copy.wait()
-        weight = held[k].reshape(block, cols)
-        at = pl.ds(pl.multiple_of((spot[0] ^ k) * block, block), block)
-        if back:
-            out[:, at] = dot(left[...], weight, (1, 1), out.dtype)
-        elif k == 0:
-            out[...] = dot(left[:, at], weight, (1, 0))
-        else:
-            out[...] += dot(left[:, at], weight, (1, 0))
-
-
-def gathered_dot(spot, left, pieces, back=False, kind=F32):
+        at = pl.ds(pl.multiple_of((spot[0] ^ k) * size, size), size)
+        yield k, at, held[k].reshape(size, cols)
+
+
+def held_shapes(pieces):
     rows, cols = pieces[0].shape[1:]
-    count, width = left.shape[0], 32 * rows if back else cols
-    whole = pl.BlockSpec(memory_space=pltpu.VMEM)
-    return pl.pallas_call(
-        functools.partial(gathered_dot_kernel, back),
-        in_specs=[pl.BlockSpec(memory_space=pltpu.SMEM), whole]
-        + [pl.BlockSpec(memory_space=pl.ANY)] * len(pieces),
-        out_specs=whole,
-        out_shape=jax.ShapeDtypeStruct((count, width), kind),
+    return [pltpu.VMEM((4, 4, 2, rows, cols), BF16), pltpu.SemaphoreType.DMA((4, 8))]
+
+
+def inverse_rms(values):
+    return lax.rsqrt(jnp.mean(values * values, axis=-1, keepdims=True) + EPS)
+
+
+def enter_kernel(spot, tokens, *refs):
+    pieces, (raw, normed, gains, held, sems) = refs[:-5], refs[-5:]
+    copies = fetch_rows(spot, pieces, held, sems)
+    values = tokens[...].astype(F32)
+    inv_rms = inverse_rms(values)
+    cols = raw.shape[1]
+    for k, at, weight in blocks_of(spot, copies, held):
+        turned = weight[:, cols:].astype(F32).T
+        gains[:, at] = turned[: gains.shape[0]]
+        scaled = tokens[:, at].astype(F32) * inv_rms
+        normed[:, at] = (scaled * turned[:1]).astype(BF16)
+        found = dot(normed[:, at], weight[:, :cols], (1, 0))
+        raw[...] = found if k == 0 else raw[...] + found
+
+
+def enter(spot, tokens, pieces):
+    count, width = tokens.shape
+    cols = pieces[0].shape[2] - 128
+    return pl.pallas_call(
+        enter_kernel,
+        in_specs=[SMEM, VMEM] + [ANY] * len(pieces),
+        out_specs=[VMEM] * 3,
+        out_shape=[
+            jax.ShapeDtypeStruct((count, cols), F32),
+            jax.ShapeDtypeStruct((count, width), BF16),
+            jax.ShapeDtypeStruct((8, width), F32),
+        ],
+        scratch_shapes=held_shapes(pieces),
+        name="enter",
+        **limits(2 * count * width * cols, 2 * width * cols, 0),
+    )(spot, tokens, *pieces)
+
+
+def leave_kernel(spot, attended, tokens, gains, *refs):
+    pieces, (resid, normed, held, sems) = refs[:-4], refs[-4:]
+    copies = fetch_rows(spot, pieces, held, sems)
+    resid[...] = tokens[...].astype(F32)
+    for _, at, weight in blocks_of(spot, copies, held):
+        resid[...] += dot(attended[:, at], weight, (1, 0))
+    values = resid[...]
+    normed[...] = (values * inverse_rms(values) * gains[1:2]).astype(BF16)
+
+
+def leave(spot, attended, tokens, gains, pieces):
+    count, width = tokens.shape
+    return pl.pallas_call(
+        leave_kernel,
+        in_specs=[SMEM] + [VMEM] * 3 + [ANY] * len(pieces),
+        out_specs=[VMEM] * 2,
+        out_shape=[
+            jax.ShapeDtypeStruct((count, width), F32),
+            jax.ShapeDtypeStruct((count, width), BF16),
+        ],
+        scratch_shapes=held_shapes(pieces),
+        name="leave",
+        **limits(2 * count * width * width, 2 * width * width, 0),
+    )(spot, attended, tokens, gains, *pieces)
+
+
+def leave_back_kernel(spot, grads, *refs):
+    pieces, (out, held, sems) = refs[:-3], refs[-3:]
+    copies = fetch_rows(spot, pieces, held, sems)
+    for _, at, weight in blocks_of(spot, copies, held):
+        out[:, at] = dot(grads[...], weight, (1, 1), BF16)
+
+
+def leave_back(spot, grads, pieces):
+    count, width = grads.shape
+    return pl.pallas_call(
+        leave_back_kernel,
+        in_specs=[SMEM, VMEM] + [ANY] * len(pieces),
+        out_specs=VMEM,
+        out_shape=jax.ShapeDtypeStruct((count, width), BF16),
+        scratch_shapes=held_shapes(pieces),
+        name="leave_back",
+        **limits(2 * count * width * width, 2 * width * width, 0),
+    )(spot, grads, *pieces)
+
+
+def enter_back_kernel(spot, grads, tokens, gains, grad_resid, *refs):
+    pieces, (out, grad_gain, held, sems) = refs[:-4], refs[-4:]
+    copies = fetch_rows(spot, pieces, held, sems)
+    for _, at, weight in blocks_of(spot, copies, held):
+        out[:, at] = dot(grads[...], weight, (1, 1))
+    values = tokens[...].astype(F32)
+    inv_rms = inverse_rms(values)
+    total, through = norm_back(out[...], values * inv_rms, inv_rms, gains[:1])
+    grad_gain[...] = jnp.broadcast_to(total[None], grad_gain.shape)
+    out[...] = grad_resid[...] + through
+
+
+def enter_back(spot, grads, tokens, gains, grad_resid, pieces):
+    count, width = tokens.shape
+    return pl.pallas_call(
+        enter_back_kernel,
+        in_specs=[SMEM] + [VMEM] * 4 + [ANY] * len(pieces),
+        out_specs=[VMEM] * 2,
+        out_shape=[
+            jax.ShapeDtypeStruct((count, width), F32),
+            jax.ShapeDtypeStruct((8, width), F32),
+        ],
+        scratch_shapes=held_shapes(pieces),
+        name="enter_back",
+        **limits(2 * count * width * width, 2 * width * width, 0),
+    )(spot, grads, tokens, gains, grad_resid, *pieces)
+
+
+TOKEN_ORDER = (1, 3, 2, 0)
+
+
+def ffn_all_kernel(spot, *refs):
+    ins, held_in = (refs[:5], refs[5:10]), refs[10]
+    wholes, (hidden, grad_gate, grad_up, sums, out) = refs[11:13], refs[13:18]
+    gate_w, up_w, down_w, tiles, grad_tile, out_tile, sems, in_sems, out_sems = refs[18:]
+    count, f_size, rows, units = gate_w.shape
+    step = pl.program_id(0)
+    first = step == 0
+    size = tiles.shape[2]
+    half = size // 2
+    copies = [
+        [
+            pltpu.make_async_copy(
+                held_in.at[:, pl.ds((2 * k + which) * rows, rows)], buffer.at[spot[0] ^ k],
+                sems.at[which, k],
+            )
+            for k in range(count)
+        ]
+        for which, buffer in enumerate((gate_w, up_w))
+    ]
+    above, (low, width) = 2 * count * rows, down_w.shape[1:]
+    rest = width - units
+    copies.append(
+        [
+            pltpu.make_async_copy(
+                held_in.at[:, pl.ds(above, low)], down_w.at[:, :, pl.ds(0, units)], sems.at[2, 0]
+            ),
+            pltpu.make_async_copy(
+                held_in.at[:, pl.ds(above + low, SPLIT), pl.ds(0, rest)],
+                down_w.at[:, pl.ds(0, SPLIT), pl.ds(units, rest)],
+                sems.at[2, 1],
+            ),
+            pltpu.make_async_copy(
+                held_in.at[:, pl.ds(above + low, low - SPLIT), pl.ds(rest, rest)],
+                down_w.at[:, pl.ds(SPLIT, low - SPLIT), pl.ds(units, rest)],
+                sems.at[2, 2],
+            ),
+        ]
+    )
+
+    def brought(at):
+        k, some = TOKEN_ORDER[at], []
+        for which, pieces in enumerate(ins):
+            slot = tiles.at[at % 2, which]
+            parts = pieces[k : k + 1] if k < 3 else pieces[3:]
+            for i, piece in enumerate(parts):
+                target = slot.at[pl.ds(i * half, half)] if k == 3 else slot
+                some.append(pltpu.make_async_copy(piece, target, in_sems.at[at % 2, which, i]))
+        return some
+
+    def kept(at):
+        return [
+            pltpu.make_async_copy(
+                tiles.at[at % 2, which], whole.at[pl.ds(at * size, size)], out_sems.at[at % 2, which]
+            )
+            for which, whole in enumerate(wholes)
+        ]
+
+    for at in range(4):
+
+        @pl.when(step == at)
+        def _():
+            if at == 0:
+                for copy in brought(0):
+                    copy.start()
+                for held in copies:
+                    for copy in held:
+                        copy.start()
+            for copy in brought(at):
+                copy.wait()
+            if at > 0:
+                for copy in kept(at - 1):
+                    copy.wait()
+            for copy in kept(at):
+                copy.start()
+            if at < 3:
+                for copy in brought(at + 1):
+                    copy.start()
+
+    normed, cot = tiles.at[step % 2, 0], tiles.at[step % 2, 1]
+
+    def weight(which, buffer):
+        waited = []
+
+        def read():
+            if not waited:
+                waited.append(True)
+
+                @pl.when(first)
+                def _():
+                    for copy in copies[which]:
+                        copy.wait()
+
+            return buffer[...].reshape(-1, buffer.shape[-1])
+
+        return read
+
+    ffn_tile(
+        normed, cot, weight(0, gate_w), weight(1, up_w), weight(2, down_w),
+        hidden, grad_gate, grad_up, grad_tile, out_tile,
+    )
+    for i in range(2):
+        sums[i, 0] = grad_tile[i * half : (i + 1) * half]
+        out[i, 0] = out_tile[i * half : (i + 1) * half]
+
+    @pl.when(step == 3)
+    def _():
+        for copy in kept(3):
+            copy.wait()
+
+
+def ffn_all(spot, normed, cot, held_in, t_size, low):
+    count, width = normed[0].shape
+    half = count // 2
+    f_size, above, units = held_in.shape
+    rows = (above - low - SPLIT) // (2 * t_size)
+    inner = pl.BlockSpec((count, units), lambda t: (t, 0))
+    sums = pl.BlockSpec((2, 1, half, width), lambda t: (0, t, 0, 0))
+    weights = pltpu.VMEM((t_size, f_size, rows, units), BF16)
+    total = 4 * count
+    return pl.pallas_call(
+        ffn_all_kernel,
+        grid=(4,),
+        in_specs=[SMEM] + [ANY] * 11,
+        out_specs=[ANY, ANY, inner, inner, inner, sums, sums],
         scratch_shapes=[
-            pltpu.VMEM((4, 4, 2, rows, cols), BF16),
-            pltpu.SemaphoreType.DMA((4, 8)),
+            weights,
+            weights,
+            pltpu.VMEM((f_size, low, width), BF16),
+            pltpu.VMEM((2, 2, count, width), BF16),
+            pltpu.VMEM((count, width), BF16),
+            pltpu.VMEM((count, width), BF16),
+            pltpu.SemaphoreType.DMA((3, t_size)),
+            pltpu.SemaphoreType.DMA((2, 2, 2)),
+            pltpu.SemaphoreType.DMA((2, 2)),
         ],
-        name="gathered_dot",
-        **limits(64 * count * rows * cols, 64 * rows * cols + 4 * count * width, 0),
-    )(spot, left, *pieces)
-
-
-def gather_line(block):
-    two = jnp.stack([block, z_swap(block, 2)])
-    return jnp.concatenate([two, z_swap(two, 1)])
-
-
-def gather_plane(line):
-    one, two = dp_swap(line, 1), dp_swap(line, 2)
-    half = line.shape[0] // 2
-    return [line, one, two, dp_swap(one[:half], 2), dp_swap(two[half:], 1)]
-
-
-def spread(line):
-    mine = gather_plane(line)
-    return mine + [core_swap(piece) for piece in mine]
-
-
-def after(value, *others):
-    return lax.optimization_barrier((value, *others))[0]
-
-
-def gather_gains(spot, pieces):
-    dp, z, core = spot[0], spot[1], spot[2]
-    rows = pieces[0].shape[1]
-    ends = [piece[:, :, -128:] for piece in pieces]
-    sides = []
-    for side in (ends[:5], ends[5:]):
-        far = jnp.concatenate(side[3:])
-        sides.append(jnp.stack(side[:3] + [far]))
-    got = jnp.stack(sides, axis=2)
-    got = got[dp ^ jnp.arange(4)]
-    line = jnp.array([0, 2, 1, 3], jnp.int32)
-    got = got[:, line[z ^ jnp.arange(4)]]
-    return got[:, :, core ^ jnp.arange(2)].reshape(32 * rows, 128)
+        out_shape=[jax.ShapeDtypeStruct((total, width), BF16)] * 2
+        + [jax.ShapeDtypeStruct((total, units), BF16)] * 3
+        + [jax.ShapeDtypeStruct((2, 4, half, width), BF16)] * 2,
+        name="ffn_all",
+        **limits(12 * total * width * units, 6 * width * units + 8 * total * width),
+    )(spot, *normed, *cot, held_in)
+
+
+class TokenSum:
+    def __init__(self, terms):
+        self.own = terms
+        self.sent = add([[(terms, 0)], [(terms, 5)]], 2)
+        self.a, self.b = dp_swap(self.sent[0], 1), dp_swap(self.sent[1], 2)
+
+    def cross(self):
+        self.crossed = add([[(self.own, 2), (self.a, 1)], [(self.own, 4), (self.b, 0)]], 1)
+        self.last_a, self.last_b = dp_swap(self.crossed[0], 2), dp_swap(self.crossed[1], 1)
+
+    def parts(self):
+        return [
+            [(flat(self.own), 3), (self.a, 0), (self.last_a, 0)],
+            [(flat(self.own), 7), (self.b, 1), (self.last_b, 0)],
+        ]
+
+
+def add_kernel(counts, *refs):
+    outs = refs[len(refs) - len(counts) :]
+    at = 0
+    for count, out in zip(counts, outs):
+        total = refs[at][...].astype(F32)
+        for ref in refs[at + 1 : at + count]:
+            total = total + ref[...].astype(F32)
+        out[...] = total.astype(out.dtype)
+        at += count
+
+
+def flat(array):
+    return array.reshape((-1,) + array.shape[-2:])
+
+
+def add(jobs, count, group=1):
+    operands = [flat(array) for job in jobs for array, _ in job]
+    starts = [start for job in jobs for _, start in job]
+    block = (group,) + operands[0].shape[1:]
+    spec = lambda start: pl.BlockSpec(block, lambda g: (g + start // group, 0, 0))
+    return pl.pallas_call(
+        functools.partial(add_kernel, [len(job) for job in jobs]),
+        grid=(count // group,),
+        in_specs=[spec(start) for start in starts],
+        out_specs=[spec(0)] * len(jobs),
+        out_shape=[jax.ShapeDtypeStruct((count,) + block[1:], BF16)] * len(jobs),
+        name="add",
+        **limits(0, 2 * (len(starts) + len(jobs)) * count * block[1] * block[2]),
+    )(*operands)
+
+
+def turns(step):
+    return jnp.minimum(step, 2), jnp.maximum(step - 3, 0)
+
+
+def half_specs(parts, rows):
+    specs = []
+    for side, terms in enumerate(parts):
+        for array, start in terms:
+            shape = (1, rows, array.shape[-1])
+            specs.append(
+                pl.BlockSpec(shape, lambda t, side=side, start=start: (start, turns(t)[side], 0))
+            )
+    return specs
+
+
+def half_total(refs, side):
+    some = refs[side * 3 : side * 3 + 3]
+    return some[0][0].astype(F32) + some[1][0].astype(F32) + some[2][0].astype(F32)
+
+
+def branch_kernel(resid, cot, gains, *refs):
+    terms, (grad_resid, grad_branch, grad_gain) = refs[:6], refs[6:]
+    step = pl.program_id(0)
+
+    def finish(grads):
+        inv_rms = inverse_rms(resid[...])
+        total, through = norm_back(grads, resid[...] * inv_rms, inv_rms, gains[1:2])
+        sums = jnp.broadcast_to(total[None], grad_gain.shape)
+
+        @pl.when(step == 0)
+        def _():
+            grad_gain[...] = sums
+
+        @pl.when(step > 0)
+        def _():
+            grad_gain[...] += sums
+
+        grads = cot[...].astype(F32) + through
+        grad_resid[...] = grads
+        grad_branch[...] = grads.astype(BF16)
+
+    for side in range(2):
+
+        @pl.when(step // 3 == side)
+        def _():
+            finish(half_total(terms, side))
+
+
+def branch(resid, cot, gains, parts):
+    count, width = resid.shape
+    rows = count // 6
+    token = pl.BlockSpec((rows, width), lambda t: (t, 0))
+    fixed = pl.BlockSpec((8, width), lambda t: (0, 0))
+    return pl.pallas_call(
+        branch_kernel,
+        grid=(6,),
+        in_specs=[token, token, fixed] + half_specs(parts, rows),
+        out_specs=[token, token, fixed],
+        out_shape=[
+            jax.ShapeDtypeStruct((count, width), F32),
+            jax.ShapeDtypeStruct((count, width), BF16),
+            jax.ShapeDtypeStruct((8, width), F32),
+        ],
+        name="branch",
+        **limits(0, 18 * count * width),
+    )(resid, cot, gains, *[array for terms in parts for array, _ in terms])
+
+
+def layer_out_kernel(resid, *refs):
+    terms, out = refs[:6], refs[6]
+    for side in range(2):
+
+        @pl.when(pl.program_id(0) // 3 == side)
+        def _():
+            out[...] = resid[...] + half_total(terms, side)
+
+
+def layer_out_of(resid, parts):
+    count, width = resid.shape
+    rows = count // 6
+    token = pl.BlockSpec((rows, width), lambda t: (t, 0))
+    return pl.pallas_call(
+        layer_out_kernel,
+        grid=(6,),
+        in_specs=[token] + half_specs(parts, rows),
+        out_specs=token,
+        out_shape=jax.ShapeDtypeStruct((count, width), F32),
+        name="layer_out",
+        **limits(0, 14 * count * width),
+    )(resid, *[array for terms in parts for array, _ in terms])
 
 
 def row_grads_kernel(spot, left, right, *refs):
-    extra = refs[0] if len(refs) == 4 else None
+    gains = refs[:-3]
     mine, other, held = refs[-3:]
     count, _, rows, cols = held.shape
     found = dot(left[...], right[...], (0, 0), BF16)
+    if gains:
+        shape = (128, left.shape[1])
+        which = lax.broadcasted_iota(jnp.int32, shape, 0)
+        one, two = gains[0][:1], gains[1][:1]
+        extra = jnp.where(which == 0, one, jnp.where(which == 1, two, 0.0)).T.astype(BF16)
     for i in range(count):
         for core in range(2):
             at = (2 * i + core) * rows
             held[i, core, :, : found.shape[1]] = found[at : at + rows]
-            if extra is not None:
+            if gains:
                 held[i, core, :, found.shape[1] :] = extra[at : at + rows]
     z, core = spot[1], spot[2]
     for half in range(2):
@@ -573,170 +914,226 @@
             other[half, 0, at] = held[z ^ (2 * at + half), 1 - core]
 
 
-def row_grads(spot, left, right, right_cols, extra=None):
+def row_grads(spot, left, right, right_cols, gains=()):
     count, width = left.shape
     rows = width // 32
-    cols = right_cols + (0 if extra is None else extra.shape[1])
+    cols = right_cols + (128 if gains else 0)
     turn = lambda k, spot: spot[0] ^ k ^ (k >> 1)
     out = pl.BlockSpec((2, 1, 2, rows, cols), lambda k, spot: (0, k, 0, 0, 0))
-    specs = [
-        pl.BlockSpec((count, width // 4), lambda k, spot: (0, turn(k, spot))),
-        pl.BlockSpec((count, right_cols), lambda k, spot: (0, 0)),
-    ]
-    operands = [left, right]
-    if extra is not None:
-        specs.append(pl.BlockSpec((width // 4, extra.shape[1]), lambda k, spot: (turn(k, spot), 0)))
-        operands.append(extra)
+    gain = pl.BlockSpec((8, width // 4), lambda k, spot: (0, turn(k, spot)))
     return pl.pallas_call(
         row_grads_kernel,
         grid_spec=pltpu.PrefetchScalarGridSpec(
             num_scalar_prefetch=1,
             grid=(4,),
-            in_specs=specs,
+            in_specs=[
+                pl.BlockSpec((count, width // 4), lambda k, spot: (0, turn(k, spot))),
+                pl.BlockSpec((count, right_cols), lambda k, spot: (0, 0)),
+            ]
+            + [gain] * len(gains),
             out_specs=[out, out],
             scratch_shapes=[pltpu.VMEM((4, 2, rows, cols), BF16)],
         ),
         out_shape=[jax.ShapeDtypeStruct((2, 4, 2, rows, cols), BF16)] * 2,
         name="row_grads",
         **limits(2 * count * width * cols, 2 * width * cols + 2 * count * (width + cols)),
-    )(spot, *operands)
-
-
-def add_low(left, right):
-    return (left.astype(F32) + right.astype(F32)).astype(BF16)
-
-
-def scatter_line(terms):
-    near = add_low(terms[:2], z_swap(terms[2:], 1))
-    return near[0].astype(F32) + z_swap(near[1], 2).astype(F32)
-
-
-def scatter_fast(mine, other):
-    chip = add_low(mine, core_swap(other))
-    even, odd = chip[0], chip[1]
-    sent_even, sent_odd = dp_swap(even[1:3], 1), dp_swap(odd[2:4], 2)
-    even_own, even_far = add_low(even[0], sent_even[0]), add_low(even[3], sent_even[1])
-    odd_own, odd_far = add_low(odd[0], sent_odd[1]), add_low(odd[1], sent_odd[0])
-    even = add_low(even_own, dp_swap(even_far, 2))
-    odd = add_low(odd_own, dp_swap(odd_far, 1))
-    return scatter_line(jnp.concatenate([even, odd]))
-
-
-def unit_grads_kernel(spot, left, gate, up, mine, other, held):
-    count, _, rows, units = held.shape
-    z, core = spot[1], spot[2]
-    for which, right in enumerate((gate, up)):
-        found = dot(left[...], right[...], (0, 0), BF16)
-        for i in range(count):
-            for side in range(2):
-                at = (2 * i + side) * rows
-                held[i, side] = found[at : at + rows]
-        for at, j in enumerate(LINE_ORDER):
-            mine[at, 0, which] = held[z ^ j, core]
-            other[at, 0, which] = held[z ^ j, 1 - core]
-
-
-def unit_grads(spot, left, gate, up):
-    count, width = left.shape
-    units, rows = gate.shape[1], width // 32
-    out = pl.BlockSpec((4, 1, 2, rows, units), lambda k, spot: (0, k, 0, 0, 0))
-    right = pl.BlockSpec((count, units), lambda k, spot: (0, 0))
-    return pl.pallas_call(
-        unit_grads_kernel,
-        grid_spec=pltpu.PrefetchScalarGridSpec(
-            num_scalar_prefetch=1,
-            grid=(4,),
-            in_specs=[
-                pl.BlockSpec((count, width // 4), lambda k, spot: (0, spot[0] ^ k)),
-                right,
-                right,
+    )(spot, left, right, *gains)
+
+
+class RowSum:
+    def __init__(self, mine, other):
+        self.mine, self.other = mine, core_swap(other)
+
+    def plane(self):
+        pair = lambda start: [(self.mine, start), (self.other, start)]
+        a, b = self.sent = add([pair(2), pair(12)], 4, 2)
+        self.a, self.b = dp_swap(a, 1), dp_swap(b, 2)
+
+    def cross(self):
+        a, b = self.crossed = add(
+            [
+                [(self.mine, 6), (self.other, 6), (self.a, 2)],
+                [(self.mine, 10), (self.other, 10), (self.b, 0)],
             ],
-            out_specs=[out, out],
-            scratch_shapes=[pltpu.VMEM((4, 2, rows, units), BF16)],
-        ),
-        out_shape=[jax.ShapeDtypeStruct((4, 4, 2, rows, units), BF16)] * 2,
-        name="unit_grads",
-        **limits(4 * count * width * units, 4 * width * units + 2 * count * (width + 2 * units)),
-    )(spot, left, gate, up)
-
-
-def down_grads_kernel(spot, left, right, mine, other, held):
-    count, _, rows, cols = held.shape
-    z, core = spot[1], spot[2]
-    found = dot(left[...], right[...], (0, 0), BF16)
+            2,
+        )
+        self.last_a, self.last_b = dp_swap(a, 2), dp_swap(b, 1)
+
+    def near(self):
+        terms = [(self.mine, 8), (self.other, 8), (self.b, 2), (self.last_b, 0)]
+        self.odd = add([terms], 2)[0]
+        self.line = z_swap(self.odd, 1)
+
+    def terms(self, at):
+        return [(x, at) for x in (self.mine, self.other, self.a, self.last_a, self.line)]
+
+    def far(self):
+        self.rest = add([self.terms(1)], 1)[0]
+        self.last = z_swap(self.rest, 2)
+
+    def final(self):
+        return self.terms(0) + [(self.last, 0)]
+
+
+class LineSum:
+    def __init__(self, mine, other):
+        self.mine, self.other = mine, core_swap(other)
+
+    def line(self):
+        blocks = self.mine.shape[0]
+        count = flat(self.mine).shape[0]
+        self.chip = add([[(self.mine, 0), (self.other, 0)]], count, count // blocks)[0]
+        size = lax.axis_size("fsdp")
+        groups = [list(range(core, size, 2)) for core in range(2)]
+        self.total = lax.psum_scatter(
+            self.chip, "fsdp", scatter_dimension=0, axis_index_groups=groups, tiled=True
+        )
+
+
+def chunk_dot(lefts, rights):
+    found = dot(lefts[0][...], rights[0][...], (0, 0))
+    for left, right in zip(lefts[1:], rights[1:]):
+        found = found + dot(left[...], right[...], (0, 0))
+    return found.astype(BF16)
+
+
+def place_line(spot, found, held, mine, other):
+    count, _, rows, _ = held.shape
+    core = spot[2]
     for i in range(count):
         for side in range(2):
             at = (2 * i + side) * rows
             held[i, side] = found[at : at + rows]
-    for at, j in enumerate(LINE_ORDER):
-        mine[at] = held[z ^ j, core]
-        other[at] = held[z ^ j, 1 - core]
-
-
-def down_grads(spot, left, right):
-    count, units = left.shape
-    width = right.shape[1]
-    rows, tile = units // 8, width // 4
-    out = pl.BlockSpec((4, rows, tile), lambda n, spot: (0, 0, n))
-    return pl.pallas_call(
-        down_grads_kernel,
+    for at in range(count):
+        mine[at] = held[at, core].reshape(mine.shape[1:])
+        other[at] = held[at, 1 - core].reshape(other.shape[1:])
+
+
+def line_grads_kernel(spot, *refs):
+    mine, other, held = refs[-3:]
+    chunks = (len(refs) - 3) // 2
+    found = chunk_dot(refs[:chunks], refs[chunks : 2 * chunks])
+    place_line(spot, found, held, mine, other)
+
+
+def unit_grads(spot, lefts, rights):
+    count, width = lefts[0].shape
+    units, rows = rights[0].shape[1], width // 32
+    out = pl.BlockSpec((4, 1, rows, units), lambda k, spot: (0, k, 0, 0))
+    left = pl.BlockSpec((count, width // 4), lambda k, spot: (0, spot[0] ^ k))
+    right = pl.BlockSpec((count, units), lambda k, spot: (0, 0), pipeline_mode=pl.Buffered(1))
+    total = count * len(lefts)
+    return pl.pallas_call(
+        line_grads_kernel,
         grid_spec=pltpu.PrefetchScalarGridSpec(
             num_scalar_prefetch=1,
             grid=(4,),
-            in_specs=[
-                pl.BlockSpec((count, units), lambda n, spot: (0, 0)),
-                pl.BlockSpec((count, tile), lambda n, spot: (0, n)),
-            ],
+            in_specs=[left] * len(lefts) + [right] * len(rights),
+            out_specs=[out, out],
+            scratch_shapes=[pltpu.VMEM((4, 2, rows, units), BF16)],
+        ),
+        out_shape=[jax.ShapeDtypeStruct((4, 4, rows, units), BF16)] * 2,
+        name="unit_grads",
+        **limits(2 * total * width * units, 2 * width * units + 2 * total * (width + units)),
+    )(spot, *lefts, *rights)
+
+
+def down_grads(spot, lefts, rights):
+    count, units = lefts[0].shape
+    width = rights[0].shape[1]
+    rows, tile = units // 8, width // 4
+    out = pl.BlockSpec((4, rows, tile), lambda n, spot: (0, 0, n))
+    left = pl.BlockSpec((count, units), lambda n, spot: (0, 0), pipeline_mode=pl.Buffered(1))
+    right = pl.BlockSpec((count, tile), lambda n, spot: (0, n))
+    total = count * len(lefts)
+    return pl.pallas_call(
+        line_grads_kernel,
+        grid_spec=pltpu.PrefetchScalarGridSpec(
+            num_scalar_prefetch=1,
+            grid=(4,),
+            in_specs=[left] * len(lefts) + [right] * len(rights),
             out_specs=[out, out],
             scratch_shapes=[pltpu.VMEM((4, 2, rows, tile), BF16)],
         ),
         out_shape=[jax.ShapeDtypeStruct((4, rows, width), BF16)] * 2,
         name="down_grads",
-        **limits(2 * count * width * units, 2 * width * units + 2 * count * (width + units)),
-    )(spot, left, right)
-
-
-def update_units_kernel(which, rate, spot, weight, moment, average, *refs):
-    pieces, outs = refs[:-3], refs[-3:]
+        **limits(2 * total * width * units, 2 * width * units + 2 * total * (width + units)),
+    )(spot, *lefts, *rights)
+
+
+def sum_of(refs):
+    total = refs[0][0].astype(F32)
+    for ref in refs[1:]:
+        total = total + ref[0].astype(F32)
+    return total
+
+
+def update_rows_kernel(rates, count, *refs):
+    terms, rest = refs[:count], refs[count:]
+    held = 3 * len(rates)
+    ins, outs = rest[:held], rest[held:]
+    grads = sum_of(terms)
+    at = 0
+    for i, rate in enumerate(rates):
+        own = ins[3 * i : 3 * i + 3]
+        cols = own[0].shape[1]
+        piece = grads[:, at : at + cols]
+        at += cols
+        results = update(*[ref[...] for ref in own], piece, rate)
+        for out, result in zip(outs[3 * i :], results):
+            out[...] = result
+    if at < grads.shape[1]:
+        outs[-1][...] = grads[:, at:]
+
+
+def update_rows(terms, weights, rates):
+    operands = [flat(array) for array, _ in terms]
+    block = (1,) + operands[0].shape[1:]
+    left = block[2] - sum(w[0].shape[1] for w in weights)
+    arrays = [array for some in weights for array in some]
+    shapes = [jax.ShapeDtypeStruct(array.shape, F32) for array in arrays]
+    if left:
+        shapes.append(jax.ShapeDtypeStruct((block[1], left), F32))
+    whole = lambda shape: pl.BlockSpec(shape, lambda g: (0, 0))
+    return pl.pallas_call(
+        functools.partial(update_rows_kernel, rates, len(terms)),
+        grid=(1,),
+        in_specs=[pl.BlockSpec(block, lambda g, start=start: (start, 0, 0)) for _, start in terms]
+        + [whole(array.shape) for array in arrays],
+        out_specs=[whole(shape.shape) for shape in shapes],
+        out_shape=shapes,
+        name="update_rows",
+        **limits(0, 32 * arrays[0].size),
+    )(*operands, *arrays)
+
+
+def update_units_kernel(rate, spot, weight, moment, average, *refs):
+    pieces, outs = refs[:4], refs[4:]
     units = pieces[0].shape[-1]
-    for k, piece in enumerate(pieces):
+    for k in range(4):
+        grads = pieces[k][0].astype(F32)
         at = pl.ds(pl.multiple_of((spot[0] ^ k) * units, units), units)
-        results = update(
-            weight[:, at], moment[:, at], average[:, at], piece[which].astype(F32), rate
-        )
+        results = update(weight[:, at], moment[:, at], average[:, at], grads, rate)
         for out, result in zip(outs, results):
             out[:, at] = result
 
 
-def update_units(spot, weight, moment, average, pieces, which, rate):
-    whole = pl.BlockSpec(memory_space=pltpu.VMEM)
-    return pl.pallas_call(
-        functools.partial(update_units_kernel, which, rate),
-        in_specs=[pl.BlockSpec(memory_space=pltpu.SMEM)] + [whole] * (3 + len(pieces)),
+def update_units(spot, weight, moment, average, pieces, rate):
+    block = (1,) + pieces[0].shape[1:]
+    first = pl.BlockSpec(block, lambda g: (0, 0, 0))
+    whole = pl.BlockSpec(weight.shape, lambda g: (0, 0))
+    return pl.pallas_call(
+        functools.partial(update_units_kernel, rate),
+        grid=(1,),
+        in_specs=[SMEM] + [whole] * 3 + [first] * 4,
         out_specs=[whole] * 3,
         out_shape=[jax.ShapeDtypeStruct(weight.shape, F32)] * 3,
         name="update_units",
-        **limits(0, 32 * weight.size, 0),
+        **limits(0, 32 * weight.size),
     )(spot, weight, moment, average, *pieces)
 
 
-def norm_back(grad_normed, scaled, inv_rms, gain_full):
-    grad_scaled = grad_normed * gain_full
-    grad_gain = jnp.sum(grad_normed * scaled, axis=0)
-    grad_in = inv_rms * (
-        grad_scaled - scaled * jnp.mean(grad_scaled * scaled, axis=-1, keepdims=True)
-    )
-    return (grad_gain, grad_in)
-
-
-def update(weight, moment, average, grad, rate):
-    moment_new = MOMENTUM * moment + grad
-    weight_new = weight - rate * (grad + MOMENTUM * moment_new)
-    average_new = AVERAGE * average + (1.0 - AVERAGE) * weight_new
-    return (moment_new, weight_new, average_new)
-
-
-def shards(
+def shards_any(
     tokens_in,
     out_grad,
     kv_grad_next,
@@ -778,8 +1175,6 @@
 
     gain_cols = jnp.zeros((own_rows, 128), BF16).at[:, :2].set(gains.astype(BF16).T)
     qkv_block = jnp.concatenate([w_query.astype(BF16), w_keyval.astype(BF16), gain_cols], axis=1)
-    fast = t_size == 4 and f_size == 8 and own_rows % 16 == 0
-    spot = place()
 
     def to_slices(weight):
         split = weight.astype(BF16).reshape(own_rows, t_size, slice_units)
@@ -790,23 +1185,12 @@
         whole = lax.all_gather(held, "fsdp", axis=0)
         return jnp.swapaxes(whole, 0, 1).reshape(width, slice_units)
 
-    if fast:
-        qkv_line = gather_line(qkv_block)
-        qkv_pieces = spread(qkv_line)
-        output_line = gather_line(after(w_output.astype(BF16), qkv_line))
-        output_pieces = spread(after(output_line, qkv_pieces[3], qkv_pieces[4]))
-        pieces = slices(spot, w_gate, w_up, t_size)
-        held = jnp.stack([pieces[0]] + [dp_swap(pieces[k], k) for k in range(1, t_size)])
-        held = lax.all_gather(after(held, output_line), "fsdp", axis=0)
-        gain_rows = gather_gains(spot, qkv_pieces)
-        down_block = after(w_down.astype(BF16), qkv_pieces[1], qkv_pieces[2])
-    else:
-        qkv_full = gather_rows(qkv_block)
-        output_full = gather_rows(w_output.astype(BF16))
-        gate_slice = to_slices(w_gate)
-        up_slice = to_slices(w_up)
-        gain_rows = qkv_full[:, -128:]
-        down_block = w_down.astype(BF16)
+    qkv_full = gather_rows(qkv_block)
+    output_full = gather_rows(w_output.astype(BF16))
+    gate_slice = to_slices(w_gate)
+    up_slice = to_slices(w_up)
+    gain_rows = qkv_full[:, -128:]
+    down_block = w_down.astype(BF16)
     down_slice = lax.all_gather(down_block, "fsdp", axis=0, tiled=True)
     cot_all = jnp.concatenate(plane_gather(out_grad), axis=0)
 
@@ -816,22 +1200,16 @@
     gains_full = gain_rows[:, :2].astype(F32).T
     gain_attn, gain_ffn = gains_full[0], gains_full[1]
     normed = (scaled * gain_attn).astype(BF16)
-    raw = gathered_dot(spot, normed, qkv_pieces) if fast else dot(normed, qkv_full, (1, 0))
+    raw = dot(normed, qkv_full, (1, 0))
     cosine, sine = rotation(positions_of(doc_ids).reshape(rows), head_dim)
     queries, attended, shared = attend(raw, cosine, sine, doc_ids, head_count, head_dim)
-    if fast:
-        resid = inputs + gathered_dot(spot, attended, output_pieces)
-    else:
-        resid = inputs + dot(attended, output_full, (1, 0))
+    resid = inputs + dot(attended, output_full, (1, 0))
 
     inv_rms2 = lax.rsqrt(jnp.mean(resid * resid, axis=-1, keepdims=True) + EPS)
     scaled2 = resid * inv_rms2
     normed2 = (scaled2 * gain_ffn).astype(BF16)
     normed2_all = jnp.concatenate(plane_gather(normed2), axis=0)
-    if fast:
-        results = ffn_held(spot, normed2_all, cot_all, held, down_slice)
-    else:
-        results = ffn(normed2_all, cot_all, gate_slice, up_slice, down_slice)
+    results = ffn(normed2_all, cot_all, gate_slice, up_slice, down_slice)
     hidden, grad_gate, grad_up, grad_normed2_part, ffn_part = results
     grad_normed2 = plane_scatter(
         [grad_normed2_part[k * rows : (k + 1) * rows] for k in range(t_size)]
@@ -848,49 +1226,27 @@
             held = put(held, sent.astype(F32), dp ^ k, 1)
         return held.reshape(own_rows, hidden_units)
 
-    if fast:
-        mine, other = down_grads(spot, hidden, cot_all)
-        down_sum = scatter_line(add_low(mine, core_swap(other)))
-        mine, other = unit_grads(spot, normed2_all, grad_gate, grad_up)
-        unit_sum = scatter_line(add_low(mine, core_swap(other)))
-        unit_pieces = [unit_sum[0]] + [
-            dp_swap(unit_sum[k].astype(BF16), k) for k in range(1, t_size)
-        ]
-    else:
-        grad_down_w = dot(hidden, cot_all, (0, 0), BF16)
-        down_sum = scatter_fsdp(grad_down_w.reshape(f_size, -1, width), 0)
-        gate_sum = from_slices(dot(normed2_all, grad_gate, (0, 0), BF16))
-        up_sum = from_slices(dot(normed2_all, grad_up, (0, 0), BF16))
+    grad_down_w = dot(hidden, cot_all, (0, 0), BF16)
+    down_sum = scatter_fsdp(grad_down_w.reshape(f_size, -1, width), 0)
+    gate_sum = from_slices(dot(normed2_all, grad_gate, (0, 0), BF16))
+    up_sum = from_slices(dot(normed2_all, grad_up, (0, 0), BF16))
 
     grad_gain_ffn, grad_through = norm_back(grad_normed2, scaled2, inv_rms2, gain_ffn)
     grad_resid = out_grad.astype(F32) + grad_through
     grad_branch = grad_resid.astype(BF16)
-    if fast:
-        grad_attended = gathered_dot(spot, grad_branch, output_pieces, True, BF16)
-    else:
-        grad_attended = dot(grad_branch, output_full, (1, 1), BF16)
-    if fast:
-        output_sum = scatter_fast(*row_grads(spot, attended, grad_branch, width))
-    else:
-        output_sum = scatter_rows(dot(attended, grad_branch, (0, 0), BF16))
+    grad_attended = dot(grad_branch, output_full, (1, 1), BF16)
+    output_sum = scatter_rows(dot(attended, grad_branch, (0, 0), BF16))
     grad_raw = attend_back(
         queries, grad_attended, shared, kv_grad_next, cosine, sine, doc_ids, head_count, head_dim
     )
-    if fast:
-        grad_normed = gathered_dot(spot, grad_raw, qkv_pieces, True)
-    else:
-        grad_normed = dot(grad_raw, qkv_full, (1, 1))
+    grad_normed = dot(grad_raw, qkv_full, (1, 1))
     grad_gain_attn, grad_first = norm_back(grad_normed, scaled, inv_rms, gain_attn)
     input_grad = grad_resid + grad_first
     gain_grads = jnp.zeros((width, 128), BF16)
     gain_grads = gain_grads.at[:, :2].set(
         jnp.stack([grad_gain_attn, grad_gain_ffn], axis=0).astype(BF16).T
     )
-    if fast:
-        raw_width = grad_raw.shape[1] - 128
-        qkv_sum = scatter_fast(*row_grads(spot, normed, grad_raw, raw_width, gain_grads))
-    else:
-        qkv_sum = scatter_rows(dot(normed, grad_raw, (0, 0), BF16).at[:, -128:].set(gain_grads))
+    qkv_sum = scatter_rows(dot(normed, grad_raw, (0, 0), BF16).at[:, -128:].set(gain_grads))
     query_sum = qkv_sum[:, :heads_width]
     keyval_sum = qkv_sum[:, heads_width : heads_width + 2 * head_dim]
     gains_sum = qkv_sum[:, -128:-126].T
@@ -902,13 +1258,8 @@
     query_out = update(w_query, query_mom, query_ema, query_sum, rate(0.6, width))
     keyval_out = update(w_keyval, keyval_mom, keyval_ema, keyval_sum, rate(0.15, width))
     output_out = update(w_output, output_mom, output_ema, output_sum, rate(5.0, heads_width))
-    if fast:
-        strength = rate(0.6, width)
-        gate_out = update_units(spot, w_gate, gate_mom, gate_ema, unit_pieces, 0, strength)
-        up_out = update_units(spot, w_up, up_mom, up_ema, unit_pieces, 1, strength)
-    else:
-        gate_out = update(w_gate, gate_mom, gate_ema, gate_sum, rate(0.6, width))
-        up_out = update(w_up, up_mom, up_ema, up_sum, rate(0.6, width))
+    gate_out = update(w_gate, gate_mom, gate_ema, gate_sum, rate(0.6, width))
+    up_out = update(w_up, up_mom, up_ema, up_sum, rate(0.6, width))
     down_out = update(w_down, down_mom, down_ema, down_sum, rate(1.5, hidden_units))
     return (
         layer_out,
@@ -924,8 +1275,173 @@
     )
 
 
+def shards_fast(
+    tokens_in,
+    out_grad,
+    kv_grad_next,
+    doc_ids,
+    gains,
+    gains_mom,
+    gains_ema,
+    w_query,
+    query_mom,
+    query_ema,
+    w_keyval,
+    keyval_mom,
+    keyval_ema,
+    w_output,
+    output_mom,
+    output_ema,
+    w_gate,
+    gate_mom,
+    gate_ema,
+    w_up,
+    up_mom,
+    up_ema,
+    w_down,
+    down_mom,
+    down_ema,
+):
+    t_size, f_size = lax.axis_size("dp"), lax.axis_size("fsdp")
+    seq_count, length = doc_ids.shape
+    width = tokens_in.shape[1]
+    head_dim = w_keyval.shape[1] // 2
+    head_count = w_query.shape[1] // head_dim
+    hidden_units = w_gate.shape[1]
+    rows = seq_count * length
+    half = rows // 2
+    heads_width = head_count * head_dim
+    raw_width = heads_width + 2 * head_dim
+    tokens_total = rows * t_size * f_size
+    own_rows = w_query.shape[0]
+    spot = place()
+
+    gain_cols = jnp.zeros((own_rows, 128), BF16).at[:, :2].set(gains.astype(BF16).T)
+    qkv_block = jnp.concatenate([w_query.astype(BF16), w_keyval.astype(BF16), gain_cols], axis=1)
+    qkv_line = gather_line(qkv_block)
+
+    *sent, packed = slices(spot, w_gate, w_up, w_down, t_size)
+    got = [sent[0]] + [dp_swap(sent[k], k) for k in range(1, t_size)]
+    packed = jnp.concatenate([flat(piece).reshape(-1, piece.shape[-1]) for piece in got] + [packed])
+    output_line = gather_line(after(w_output.astype(BF16), qkv_line))
+    units_all = lax.all_gather(after(packed, output_line), "fsdp", axis=0)
+
+    qkv_near = plane_near(qkv_line)
+    qkv_far = plane_far(*qkv_near)
+    qkv_mine = [qkv_line, *qkv_near, *qkv_far]
+    qkv_pieces = qkv_mine + [core_swap(piece) for piece in qkv_mine]
+    output_near = plane_near(after(output_line, *qkv_far))
+    cot_near = plane_near(after(out_grad, *qkv_pieces[8:]))
+
+    raw, normed, gains_full = enter(spot, after(tokens_in, output_line), qkv_pieces)
+    cosine, sine = rotation(positions_of(doc_ids).reshape(rows), head_dim)
+    queries, attended, shared = attend(raw, cosine, sine, doc_ids, head_count, head_dim)
+    output_mine = [output_line, *output_near, *plane_far(*after(output_near, attended))]
+    output_pieces = output_mine + [core_swap(piece) for piece in output_mine]
+    cot = [out_grad, *cot_near, *plane_far(*cot_near)]
+    resid, normed2 = leave(spot, after(attended, *cot_near), tokens_in, gains_full, output_pieces)
+
+    normed2_near = plane_near(normed2)
+    normed2_all = [normed2, *normed2_near, *plane_far(*normed2_near)]
+    tokens2, cots, hidden, grad_gate, grad_up, grad_terms, out_terms = ffn_all(
+        spot, normed2_all, cot, units_all, t_size, w_down.shape[0]
+    )
+    normed2_sum = TokenSum(grad_terms)
+    down = LineSum(*down_grads(spot, [after(hidden, *normed2_sum.sent)], [cots]))
+    gate = LineSum(*unit_grads(spot, [after(tokens2, down.mine)], [grad_gate]))
+    up = LineSum(*unit_grads(spot, [after(tokens2, gate.mine)], [grad_up]))
+    normed2_sum.a, normed2_sum.b = after((normed2_sum.a, normed2_sum.b), up.mine)
+    normed2_sum.cross()
+    down.other = after(down.other, *normed2_sum.crossed)
+    down.line()
+    grad_resid, grad_branch, grad_gain_ffn = branch(
+        after(resid, down.chip), out_grad, gains_full, normed2_sum.parts()
+    )
+    out_sum = TokenSum(after(out_terms, grad_branch))
+
+    grad_attended = leave_back(spot, after(grad_branch, *out_sum.sent), output_pieces)
+    gate.other = after(gate.other, grad_attended)
+    gate.line()
+    output = RowSum(*row_grads(spot, attended, after(grad_branch, grad_attended), width))
+    grad_raw = attend_back(
+        queries, after(grad_attended, output.mine, gate.chip), shared, kv_grad_next, cosine, sine,
+        doc_ids, head_count, head_dim,
+    )
+    output.other, up.other = after((output.other, up.other), grad_raw)
+    output.plane()
+    up.line()
+    grad_raw = after(grad_raw, up.chip, *output.sent, down.total)
+    input_grad, grad_gain_attn = enter_back(
+        spot, grad_raw, tokens_in, gains_full, grad_resid, qkv_pieces
+    )
+    out_sum.a, out_sum.b = after((out_sum.a, out_sum.b), input_grad)
+    out_sum.cross()
+    mine, other = row_grads(
+        spot, after(normed, *out_sum.crossed), grad_raw, raw_width,
+        (grad_gain_attn, grad_gain_ffn),
+    )
+    qkv = RowSum(mine, other)
+    output.a, output.b = after((output.a, output.b), mine)
+    output.cross()
+    qkv.other = after(qkv.other, gate.total, *output.crossed)
+    qkv.plane()
+
+    def rate(strength, fan):
+        return strength / math.sqrt(fan * tokens_total)
+
+    def exchange(total):
+        pieces = [total[k : k + 1] for k in range(t_size)]
+        return pieces[:1] + [dp_swap(pieces[k], k) for k in range(1, t_size)]
+
+    gate_pieces = exchange(flat(after(gate.total, *qkv.sent)))
+    output.last_a, output.last_b, out_sum.last_a, out_sum.last_b, down.total = after(
+        (output.last_a, output.last_b, out_sum.last_a, out_sum.last_b, down.total), *qkv.sent
+    )
+    output.near()
+    layer_out = layer_out_of(resid, out_sum.parts())
+    down_out = update_rows(
+        [(down.total, 0)], [(w_down, down_mom, down_ema)], [rate(1.5, hidden_units)]
+    )
+    qkv.a, qkv.b = after((qkv.a, qkv.b), output.odd, layer_out, down_out[0])
+    qkv.cross()
+    output.line, gate_pieces = after((output.line, gate_pieces), *qkv.crossed)
+    output.far()
+    gate_out = update_units(spot, w_gate, gate_mom, gate_ema, gate_pieces, rate(0.6, width))
+    qkv.last_a, qkv.last_b = after((qkv.last_a, qkv.last_b), output.rest, gate_out[0])
+    qkv.near()
+    up_pieces = exchange(flat(after(up.total, qkv.odd)))
+    output_out = update_rows(
+        [(after(x, qkv.odd), at) for x, at in output.final()], [(w_output, output_mom, output_ema)],
+        [rate(5.0, heads_width)],
+    )
+    qkv.line = after(qkv.line, output_out[0])
+    qkv.far()
+    up_out = update_units(
+        spot, w_up, up_mom, up_ema, after(up_pieces, qkv.rest), rate(0.6, width)
+    )
+    qkv.last = after(qkv.last, up_out[0])
+    *qkv_out, left_over = update_rows(
+        qkv.final(),
+        [(w_query, query_mom, query_ema), (w_keyval, keyval_mom, keyval_ema)],
+        [rate(0.6, width), rate(0.15, width)],
+    )
+    gains_out = update(gains, gains_mom, gains_ema, left_over[:, :2].T, rate(0.1, 1))
+    return (
+        layer_out,
+        shared.astype(F32),
+        input_grad,
+        *gains_out,
+        *qkv_out,
+        *output_out,
+        *gate_out,
+        *up_out,
+        *down_out,
+    )
+
+
 def solution(mesh):
     rows = P(BOTH, None)
+    shards = shards_fast if dict(mesh.shape) == {"dp": 4, "fsdp": 8} else shards_any
     cols = P(None, BOTH)
     return jax.shard_map(
         shards,

time: 868 us -> 743 us (0.86)
  waiting for transfers between devices: 417 us -> 293 us
  Pallas kernels: 218 us -> 320 us
  other arithmetic: 86.6 us -> 8.39 us
  local copies, waits for them, and re-layouts: 50.2 us -> 28.9 us
    ppermute x12 -> x10, waiting for transfers between devices: 191 us -> 35.1 us  [z_swap(): return lax.ppermute(value, 'fsdp', [(i, i ^ 2 * k) for i in range(size)])]
    pallas_call x10 -> x39, Pallas kernels: 163 us -> 265 us  [the longest x1 72.4 us: ffn_all(): pl.pallas_call(ffn_all_kernel, grid=(4,), in_specs=[SMEM] + [ANY] * 11, o...]
    convert_element_type x21 -> x4, other arithmetic: 43.4 us -> 2.72 us  [the longest x1 1.07 us: shards_fast(): w_query.astype(BF16)]
    ppermute x38 -> x41, waiting for transfers between devices: 226 us -> 253 us  [dp_swap(): return lax.ppermute(value, 'dp', [(i, i ^ k) for i in range(size)])]
    slice x19 -> x2, local copies, waits for them, and re-layouts: 16.7 us -> 1.46 us  [exchange(): pieces = [total[k:k + 1] for k in range(t_size)]]
    ppermute x12 -> x10, starting transfers between devices: 27.6 us -> 16.9 us  [z_swap(): return lax.ppermute(value, 'fsdp', [(i, i ^ 2 * k) for i in range(size)])]
    reduce_sum x4 -> x0, other arithmetic: 9.73 us -> none  [the longest x2 6.44 us: norm_back(): grad_gain = jnp.sum(grad_normed * scaled, axis=0)]
    gather x5 -> x0, local copies, waits for them, and re-layouts: 9.09 us -> none  [the longest x2 3.53 us: gather_gains(): return got[:, :, core ^ jnp.arange(2)].reshape(32 * rows, 128)]
  transfers between devices with their start and end apart: 66 -> 70, of which waited for: 31 -> 30; matrix products, arithmetic and copies ran while one was open for 14% -> 2% of each run, Pallas kernels for 16% -> 30%
where the time goes in v2:
time: 743 us; the launch traced here: 731 us
  Pallas kernels  320 us (43%)
  waiting for transfers between devices  293 us (39%)
  starting transfers between devices  67 us (9%)
  local copies, waits for them, and re-layouts  28.9 us (4%)
  between operations  14.7 us (2%)
  other arithmetic  8.39 us (1%)
    ppermute x41, waiting for transfers between devices, dp_swap(): return lax.ppermute(value, 'dp', [(i, i ^ k) for i in range(size)])  253 us
    pallas_call x1, Pallas kernels, ffn_all(): pl.pallas_call(ffn_all_kernel, grid=(4,), in_specs=[SMEM] + [ANY] * 11, o...  72.4 us
    pallas_call x15, Pallas kernels, add(): pl.pallas_call(functools.partial(add_kernel, [len(job) for job in jobs]),...  50.1 us
    ppermute x41, starting transfers between devices, dp_swap(): return lax.ppermute(value, 'dp', [(i, i ^ k) for i in range(size)])  47.3 us
    ppermute x10, waiting for transfers between devices, z_swap(): return lax.ppermute(value, 'fsdp', [(i, i ^ 2 * k) for i in range(size)])  35.1 us
    pallas_call x2, Pallas kernels, unit_grads(): pl.pallas_call(line_grads_kernel, grid_spec=pltpu.PrefetchScalarGridSpec(...  31.1 us
    unnamed x118, local copies, waits for them, and re-layouts  25.4 us
    pallas_call x2, Pallas kernels, row_grads(): pl.pallas_call(row_grads_kernel, grid_spec=pltpu.PrefetchScalarGridSpec(n...  19.7 us
  transfers between devices with their start and end apart: 70, of which 30 were waited for; matrix products, arithmetic and copies ran while one was open for 2% of the time, Pallas kernels for 30%

profile of v2, /device:TPU:0, one launch (start us, length us, event | category | flops | bytes accessed | tf_op | source)
XLA Modules:
  0.0 731.4 jit_solution(18166161400179143194)
XLA Ops:
  11.3 4.1 collective-permute-start
  17.0 12.6 %collective-permute-done = bf16[64,2432]{1,0:T(8,128)(2,1)S(1)} collective-permute-done((bf16[64,2432]{1,0:T(8,128)(2,1)S(1)}, bf16[64,2432]{1,0:T(8,128)(2,1)S(1)}, u32[]{:S(2)}, u32[]{:S(2)}) %collective-permute-start) | collective-permute-done | bytes 311328 | tf_op jit(solution)/shard_map/ppermute | solution.py:253
  30.8 3.8 slices.1
  40.1 3.4 collective-permute-start.3
  43.5 2.6 collective-permute-done.32
  46.9 6.9 collective-permute-done.33
  58.3 4.2 collective-permute-done.4
  62.5 2.8 collective-permute-done.5
  66.5 2.1 collective-permute-start.7
  68.6 23.3 %collective-permute-done.6.whole.refs_1_ = bf16[4,64,2432]{2,1,0:T(8,128)(2,1)S(1)} collective-permute-done((bf16[4,64,2432]{2,1,0:T(8,128)(2,1)S(1)}, bf16[4,64,2432]{2,1,0:T(8,128)(2,1)S(1)}, u32[]{:S(2)}, u32[]{:S(2)}) %collective-permute-start.6) | collective-permute-done | bytes 1245216 | tf_op jit(solution)/shard_map/ppermute | solution.py:248
  100.1 7.0 collective-permute-done.8.refs_3_
  107.1 2.9 collective-permute-done.9.refs_4_
  120.5 10.2 %enter.1 = (f32[384,2304]{1,0:T(8,128)}, bf16[384,2048]{1,0:T(8,128)(2,1)}, f32[8,2048]{1,0:T(8,128)}) custom-call(s32[3]{0:T(128)} %pad_add_fusion.spot, bf16[384,2048]{1,0:T(8,128)(2,1)} %tokens.4, bf16[4,64,2432]{2,1,0:T(8,128)(2,1)} %copy-done, bf16[4,64,2432]{2,1,0:T(8,128)(2,1)} %copy-done.1, ...), custom_call_target="tpu_custom_call" | custom-call | tf_op jit(solution)/shard_map/enter/pallas_call | solution.py:519
  130.6 15.3 %attend.1 = (bf16[384,2048]{1,0:T(8,128)(2,1)}, bf16[384,2048]{1,0:T(8,128)(2,1)}, bf16[384,256]{1,0:T(8,128)(2,1)}) custom-call(f32[384,2304]{1,0:T(8,128)} %get-tuple-element.165.q_raw.k_raw.v_raw, f32[384,2304]{1,0:T(8,128)} %get-tuple-element.165.q_raw.k_raw.v_raw, f32[384,2304]{1,0:T(8,128)} %get-tuple-element.165.q_raw.k_raw.v_raw, ...), custom_call_target="tpu_custom_call" | custom-call | tf_op jit(solution)/shard_map/attend/pallas_call | solution.py:102
  151.1 32.8 %collective-permute-done.19.refs_3_ = bf16[2,64,2048]{2,1,0:T(8,128)(2,1)S(1)} collective-permute-done((bf16[2,64,2048]{2,1,0:T(8,128)(2,1)}, bf16[2,64,2048]{2,1,0:T(8,128)(2,1)S(1)}, u32[]{:S(2)}, u32[]{:S(2)}) %collective-permute-start.19) | collective-permute-done | bytes 524320 | tf_op jit(solution)/shard_map/ppermute | solution.py:248
  186.1 2.1 collective-permute-done.24.refs_8_
  190.8 9.7 %leave.1 = (f32[384,2048]{1,0:T(8,128)}, bf16[384,2048]{1,0:T(8,128)(2,1)}) custom-call(s32[3]{0:T(128)} %pad_add_fusion.spot, bf16[384,2048]{1,0:T(8,128)(2,1)} %get-tuple-element.168.attended.left, bf16[384,2048]{1,0:T(8,128)(2,1)} %tokens.4, f32[8,2048]{1,0:T(8,128)} %get-tuple-element.169.gains, bf16[4,64,2048]{2,1,0:T(8,128)(2,1)} %copy-done.4, ...), custom_call_target="tpu_custom_call" | custom-call | tf_op jit(solution)/shard_map/leave/pallas_call | solution.py:546
  206.3 1.9 cut.15
  208.5 29.6 %collective-permute-done.26.whole.refs_1_ = bf16[384,2048]{1,0:T(8,128)(2,1)S(1)} collective-permute-done((bf16[384,2048]{1,0:T(8,128)(2,1)}, bf16[384,2048]{1,0:T(8,128)(2,1)S(1)}, u32[]{:S(2)}, u32[]{:S(2)}) %collective-permute-start.26) | collective-permute-done | bytes 1572896 | tf_op jit(solution)/shard_map/ppermute | solution.py:248
  243.7 1.9 cut.13
  247.3 9.4 %collective-permute-done.30.refs_8_ = bf16[192,2048]{1,0:T(8,128)(2,1)S(1)} collective-permute-done((bf16[192,2048]{1,0:T(8,128)(2,1)}, bf16[192,2048]{1,0:T(8,128)(2,1)S(1)}, u32[]{:S(2)}, u32[]{:S(2)}) %collective-permute-start.30) | collective-permute-done | bytes 786464 | tf_op jit(solution)/shard_map/ppermute | solution.py:248
  256.7 15.7 %collective-permute-done.28.refs_3_ = bf16[192,2048]{1,0:T(8,128)(2,1)S(1)} collective-permute-done((bf16[192,2048]{1,0:T(8,128)(2,1)}, bf16[192,2048]{1,0:T(8,128)(2,1)S(1)}, u32[]{:S(2)}, u32[]{:S(2)}) %collective-permute-start.28) | collective-permute-done | bytes 786464 | tf_op jit(solution)/shard_map/ppermute | solution.py:248
  273.6 72.4 %ffn_all.1 = (bf16[1536,2048]{1,0:T(8,128)(2,1)}, bf16[1536,2048]{1,0:T(8,128)(2,1)}, bf16[1536,1408]{1,0:T(8,128)(2,1)}, bf16[1536,1408]{1,0:T(8,128)(2,1)}, bf...) custom-call(s32[3]{0:T(128)} %pad_add_fusion.spot, ...), custom_call_target="tpu_custom_call" | custom-call | tf_op jit(solution)/shard_map/ffn_all/pallas_call | solution.py:730
  346.0 3.2 add.60
  349.2 14.9 %down_grads.1 = (bf16[4,176,2048]{2,1,0:T(8,128)(2,1)}, bf16[4,176,2048]{2,1,0:T(8,128)(2,1)}) custom-call(s32[3]{0:T(128)} %pad_add_fusion.spot, bf16[1536,1408]{1,0:T(8,128)(2,1)} %get-tuple-element.186.refs_0_, bf16[1536,2048]{1,0:T(8,128)(2,1)} %get-tuple-element.187.refs_1_), custom_call_target="tpu_custom_call" | custom-call | tf_op jit(solution)/shard_map/down_grads/pallas_call | solution.py:1049
  365.8 15.5 %unit_grads.2 = (bf16[4,4,64,1408]{3,2,1,0:T(8,128)(2,1)}, bf16[4,4,64,1408]{3,2,1,0:T(8,128)(2,1)}) custom-call(s32[3]{0:T(128)} %pad_add_fusion.spot, bf16[1536,2048]{1,0:T(8,128)(2,1)} %get-tuple-element.194.refs_0_, bf16[1536,1408]{1,0:T(8,128)(2,1)} %get-tuple-element.192.refs_1_), custom_call_target="tpu_custom_call" | custom-call | tf_op jit(solution)/shard_map/unit_grads/pallas_call | solution.py:1026
  381.3 15.6 %unit_grads.3 = (bf16[4,4,64,1408]{3,2,1,0:T(8,128)(2,1)}, bf16[4,4,64,1408]{3,2,1,0:T(8,128)(2,1)}) custom-call(s32[3]{0:T(128)} %pad_add_fusion.spot, bf16[1536,2048]{1,0:T(8,128)(2,1)} %get-tuple-element.194.refs_0_, bf16[1536,1408]{1,0:T(8,128)(2,1)} %get-tuple-element.195.refs_1_), custom_call_target="tpu_custom_call" | custom-call | tf_op jit(solution)/shard_map/unit_grads/pallas_call | solution.py:1026
  396.9 4.2 collective-permute-done.36.refs_1_
  402.8 3.2 add.61
  405.9 5.0 add.62
  413.8 17.5 %collective-permute-done.38.refs_2_ = bf16[1,192,2048]{2,1,0:T(8,128)(2,1)S(1)} collective-permute-done((bf16[1,192,2048]{2,1,0:T(8,128)(2,1)}, bf16[1,192,2048]{2,1,0:T(8,128)(2,1)S(1)}, u32[]{:S(2)}, u32[]{:S(2)}) %collective-permute-start.38) | collective-permute-done | bytes 786464 | tf_op jit(solution)/shard_map/ppermute | solution.py:248
  432.4 8.7 %branch.1 = (f32[384,2048]{1,0:T(8,128)}, bf16[384,2048]{1,0:T(8,128)(2,1)}, f32[8,2048]{1,0:T(8,128)}) custom-call(f32[384,2048]{1,0:T(8,128)} %get-tuple-element.202.resid, bf16[384,2048]{1,0:T(8,128)(2,1)} %cot.1, f32[8,2048]{1,0:T(8,128)} %get-tuple-element.169.gains, bf16[8,192,2048]{2,1,0:T(8,128)(2,1)} %bitcast.58, bf16[2,192,2048]{2,1,0:T(8,128)(2,1)} %copy-done.10, ...), custom_call_target="tpu_custom_call" | custom-call | tf_op jit(solution)/shard_map/branch/pallas_call | solution.py:855
  441.1 3.2 add.63
  444.3 8.5 %leave_back.1.grad_ref = bf16[384,2048]{1,0:T(8,128)(2,1)} custom-call(s32[3]{0:T(128)} %pad_add_fusion.spot, bf16[384,2048]{1,0:T(8,128)(2,1)} %get-tuple-element.209.grads.right, bf16[4,64,2048]{2,1,0:T(8,128)(2,1)} %copy-done.4, bf16[4,64,2048]{2,1,0:T(8,128)(2,1)} %collective-permute-done.17.whole.refs_1_, ...), custom_call_target="tpu_custom_call" | custom-call | tf_op jit(solution)/shard_map/leave_back/pallas_call | solution.py:569
  452.8 9.3 %row_grads.2 = (bf16[2,4,2,64,2048]{4,3,2,1,0:T(8,128)(2,1)}, bf16[2,4,2,64,2048]{4,3,2,1,0:T(8,128)(2,1)}) custom-call(s32[3]{0:T(128)} %pad_add_fusion.spot, bf16[384,2048]{1,0:T(8,128)(2,1)} %get-tuple-element.168.attended.left, bf16[384,2048]{1,0:T(8,128)(2,1)} %get-tuple-element.209.grads.right), custom_call_target="tpu_custom_call" | custom-call | tf_op jit(solution)/shard_map/row_grads/pallas_call | solution.py:924
  463.7 4.9 add.64
  471.7 19.7 %attend_back.1.grads.right = bf16[384,2432]{1,0:T(8,128)(2,1)} custom-call(bf16[384,2048]{1,0:T(8,128)(2,1)} %get-tuple-element.207.query_ref, bf16[384,2048]{1,0:T(8,128)(2,1)} %leave_back.1.grad_ref, bf16[384,256]{1,0:T(8,128)(2,1)} %get-tuple-element.214.shared, bf16[384,256]{1,0:T(8,128)(2,1)} %kv_next.1, f32[384,128]{1,0:T(8,128)} %get-tuple-element.402.cosine, ...), custom_call_target="tpu_custom_call" | custom-call | tf_op jit(solution)/shard_map/attend_back/pallas_call | solution.py:180
  491.4 4.9 add.65
  496.3 3.4 add.66
  499.7 13.1 %enter_back.1 = (f32[384,2048]{1,0:T(8,128)}, f32[8,2048]{1,0:T(8,128)}) custom-call(s32[3]{0:T(128)} %pad_add_fusion.spot, bf16[384,2432]{1,0:T(8,128)(2,1)} %attend_back.1.grads.right, bf16[384,2048]{1,0:T(8,128)(2,1)} %tokens.4, f32[8,2048]{1,0:T(8,128)} %get-tuple-element.169.gains, f32[384,2048]{1,0:T(8,128)} %get-tuple-element.222.grad_resid, ...), custom_call_target="tpu_custom_call" | custom-call | tf_op jit(solution)/shard_map/enter_back/pallas_call | solution.py:594
  513.9 3.2 add.67
  517.1 10.4 %row_grads.3 = (bf16[2,4,2,64,2432]{4,3,2,1,0:T(8,128)(2,1)}, bf16[2,4,2,64,2432]{4,3,2,1,0:T(8,128)(2,1)}) custom-call(s32[3]{0:T(128)} %pad_add_fusion.spot, bf16[384,2048]{1,0:T(8,128)(2,1)} %get-tuple-element.229.left, bf16[384,2432]{1,0:T(8,128)(2,1)} %attend_back.1.grads.right, f32[8,2048]{1,0:T(8,128)} %get-tuple-element.230.refs_0_, ...), custom_call_target="tpu_custom_call" | custom-call | tf_op jit(solution)/shard_map/row_grads/pallas_call | solution.py:924
  529.5 23.8 %collective-permute-done.45.refs_2_ = bf16[4,64,2048]{2,1,0:T(8,128)(2,1)S(1)} collective-permute-done((bf16[4,64,2048]{2,1,0:T(8,128)(2,1)}, bf16[4,64,2048]{2,1,0:T(8,128)(2,1)S(1)}, u32[]{:S(2)}, u32[]{:S(2)}) %collective-permute-start.45) | collective-permute-done | bytes 1048608 | tf_op jit(solution)/shard_map/ppermute | solution.py:248
  554.7 2.8 add.68
  557.5 3.8 add.69
  566.1 38.1 %collective-permute-done.47.refs_3_ = bf16[2,64,2048]{2,1,0:T(8,128)(2,1)S(1)} collective-permute-done((bf16[2,64,2048]{2,1,0:T(8,128)(2,1)S(1)}, bf16[2,64,2048]{2,1,0:T(8,128)(2,1)S(1)}, u32[]{:S(2)}, u32[]{:S(2)}) %collective-permute-start.47) | collective-permute-done | bytes 524320 | tf_op jit(solution)/shard_map/ppermute | solution.py:248
  605.1 13.6 %collective-permute-done.48.refs_3_ = bf16[2,64,2048]{2,1,0:T(8,128)(2,1)S(1)} collective-permute-done((bf16[2,64,2048]{2,1,0:T(8,128)(2,1)S(1)}, bf16[2,64,2048]{2,1,0:T(8,128)(2,1)S(1)}, u32[]{:S(2)}, u32[]{:S(2)}) %collective-permute-start.48) | collective-permute-done | bytes 524320 | tf_op jit(solution)/shard_map/ppermute | solution.py:248
  619.5 2.3 add.70
  621.8 6.5 layer_out.1
  628.3 4.9 update_rows.3
  634.7 3.2 add.71
  642.8 14.8 %collective-permute-done.57.refs_1_ = bf16[1,64,1408]{2,1,0:T(8,128)(2,1)S(1)} collective-permute-done((bf16[1,64,1408]{2,1,0:T(8,128)(2,1)S(1)}, bf16[1,64,1408]{2,1,0:T(8,128)(2,1)S(1)}, u32[]{:S(2)}, u32[]{:S(2)}) %collective-permute-start.57) | collective-permute-done | bytes 180256 | tf_op jit(solution)/shard_map/ppermute | solution.py:248
  658.9 5.1 collective-permute-done.59.refs_3_
  664.8 2.1 add.72
  666.9 4.9 update_units.2
  672.8 2.5 add.73
  677.2 15.5 %collective-permute-done.61.refs_5_ = bf16[1,64,2048]{2,1,0:T(8,128)(2,1)S(1)} collective-permute-done((bf16[1,64,2048]{2,1,0:T(8,128)(2,1)S(1)}, bf16[1,64,2048]{2,1,0:T(8,128)(2,1)S(1)}, u32[]{:S(2)}, u32[]{:S(2)}) %collective-permute-start.61) | collective-permute-done | bytes 262176 | tf_op jit(solution)/shard_map/ppermute | solution.py:253
  693.4 3.3 update_rows.4
  697.5 2.3 add.74
  699.9 3.4 collective-permute-start.62
  705.4 2.1 collective-permute-start.65
  709.7 2.3 collective-permute-done.65.refs_3_
  712.7 4.9 update_units.3
  718.3 3.4 update_rows.5
  (267 shorter events, 106.2 us)
Async XLA Ops:
  7.2 265.3 %all-gather.3.cloned.1.call-start = ((), (), s32[]{:S(2)}) async-start(), calls=%async_computation.6 | async-start | bytes 19869696 | tf_op jit(solution)/shard_map/all_gather | solution.py:1327
  11.3 18.2 %collective-permute-start = (bf16[64,2432]{1,0:T(8,128)(2,1)S(1)}, bf16[64,2432]{1,0:T(8,128)(2,1)S(1)}, u32[]{:S(2)}, u32[]{:S(2)}) collective-permute-start(bf16[64,2432]{1,0:T(8,128)(2,1)S(1)} %get-tuple-element.398), channel_id=1, source_target_pairs={{0,4},{1,5},{2,6},{3,7},{4,0},{5,1},{6,2},{7,3},{8,12},{9,13},{10,... | collective-permute-start | bytes 933896 | tf_op jit(solution)/shard_map/ppermute | solution.py:253
  15.4 24.4 %collective-permute-start.1 = (bf16[64,2432]{1,0:T(8,128)(2,1)S(1)}, bf16[64,2432]{1,0:T(8,128)(2,1)S(1)}, u32[]{:S(2)}, u32[]{:S(2)}) collective-permute-start(bf16[64,2432]{1,0:T(8,128)(2,1)S(1)} %get-tuple-element.398), channel_id=1, source_target_pairs={{0,2},{1,3},{2,0},{3,1},{4,6},{5,7},{6,4},{7,5},{8,10},{9,11},{10,... | collective-permute-start | bytes 933896 | tf_op jit(solution)/shard_map/ppermute | solution.py:253
  29.5 10.3 %collective-permute-start.2 = (bf16[64,2432]{1,0:T(8,128)(2,1)S(1)}, bf16[64,2432]{1,0:T(8,128)(2,1)S(1)}, u32[]{:S(2)}, u32[]{:S(2)}) collective-permute-start(bf16[64,2432]{1,0:T(8,128)(2,1)S(1)} %collective-permute-done), channel_id=1, source_target_pairs={{0,2},{1,3},{2,0},{3,1},{4,6},{5,7},{6,4},{7,5},{8,10},{9,11},{10,... | collective-permute-start | bytes 933896 | tf_op jit(solution)/shard_map/ppermute | solution.py:253
  34.6 11.5 %collective-permute-start.32 = (bf16[2,64,1408]{2,1,0:T(8,128)(2,1)}, bf16[2,64,1408]{2,1,0:T(8,128)(2,1)S(1)}, u32[]{:S(2)}, u32[]{:S(2)}) collective-permute-start(bf16[2,64,1408]{2,1,0:T(8,128)(2,1)} %get-tuple-element.176), channel_id=1, source_target_pairs={{0,8},{8,0},{16,24},{24,16},{1,9},{9,1},{17,25},{25,17},{2,10},{10... | collective-permute-start | bytes 1081352 | tf_op jit(solution)/shard_map/ppermute | solution.py:248
  36.1 17.7 %collective-permute-start.33 = (bf16[2,64,1408]{2,1,0:T(8,128)(2,1)}, bf16[2,64,1408]{2,1,0:T(8,128)(2,1)S(1)}, u32[]{:S(2)}, u32[]{:S(2)}) collective-permute-start(bf16[2,64,1408]{2,1,0:T(8,128)(2,1)} %get-tuple-element.177), channel_id=1, source_target_pairs={{0,16},{8,24},{16,0},{24,8},{1,17},{9,25},{17,1},{25,9},{2,18},{10... | collective-permute-start | bytes 1081352 | tf_op jit(solution)/shard_map/ppermute | solution.py:248
  37.6 19.0 %collective-permute-start.34 = (bf16[2,64,1408]{2,1,0:T(8,128)(2,1)}, bf16[2,64,1408]{2,1,0:T(8,128)(2,1)S(1)}, u32[]{:S(2)}, u32[]{:S(2)}) collective-permute-start(bf16[2,64,1408]{2,1,0:T(8,128)(2,1)} %get-tuple-element.178), channel_id=1, source_target_pairs={{0,24},{8,16},{16,8},{24,0},{1,25},{9,17},{17,9},{25,1},{2,26},{10... | collective-permute-start | bytes 1081352 | tf_op jit(solution)/shard_map/ppermute | solution.py:248
  40.1 14.8 %collective-permute-start.3 = (bf16[64,2048]{1,0:T(8,128)(2,1)S(1)}, bf16[64,2048]{1,0:T(8,128)(2,1)S(1)}, u32[]{:S(2)}, u32[]{:S(2)}) collective-permute-start(bf16[64,2048]{1,0:T(8,128)(2,1)S(1)} %convert_element_type.22), channel_id=1, source_target_pairs={{0,4},{1,5},{2,6},{3,7},{4,0},{5,1},{6,2},{7,3},{8,12},{9,13},{10,... | collective-permute-start | bytes 786440 | tf_op jit(solution)/shard_map/ppermute | solution.py:253
  54.5 8.0 %collective-permute-start.4 = (bf16[64,2048]{1,0:T(8,128)(2,1)S(1)}, bf16[64,2048]{1,0:T(8,128)(2,1)S(1)}, u32[]{:S(2)}, u32[]{:S(2)}) collective-permute-start(bf16[64,2048]{1,0:T(8,128)(2,1)S(1)} %convert_element_type.22), channel_id=1, source_target_pairs={{0,2},{1,3},{2,0},{3,1},{4,6},{5,7},{6,4},{7,5},{8,10},{9,11},{10,... | collective-permute-start | bytes 786440 | tf_op jit(solution)/shard_map/ppermute | solution.py:253
  54.9 10.4 %collective-permute-start.5 = (bf16[64,2048]{1,0:T(8,128)(2,1)S(1)}, bf16[64,2048]{1,0:T(8,128)(2,1)S(1)}, u32[]{:S(2)}, u32[]{:S(2)}) collective-permute-start(bf16[64,2048]{1,0:T(8,128)(2,1)S(1)} %collective-permute-done.3), channel_id=1, source_target_pairs={{0,2},{1,3},{2,0},{3,1},{4,6},{5,7},{6,4},{7,5},{8,10},{9,11},{10,... | collective-permute-start | bytes 786440 | tf_op jit(solution)/shard_map/ppermute | solution.py:253
  65.5 434.2 %reduce-scatter.4.cloned.1.call-start = ((), (), s32[]{:S(2)}) async-start(), calls=%async_computation.3 | async-start | bytes 3604480 | tf_op jit(solution)/shard_map/reduce_scatter | solution.py:988
  65.5 26.3 %collective-permute-start.6 = (bf16[4,64,2432]{2,1,0:T(8,128)(2,1)S(1)}, bf16[4,64,2432]{2,1,0:T(8,128)(2,1)S(1)}, u32[]{:S(2)}, u32[]{:S(2)}) collective-permute-start(bf16[4,64,2432]{2,1,0:T(8,128)(2,1)S(1)} %pad_maximum_fusion.refs_0_), channel_id=1, source_target_pairs={{0,8},{8,0},{16,24},{24,16},{1,9},{9,1},{17,25},{25,17},{2,10},{10... | collective-permute-start | bytes 3735560 | tf_op jit(solution)/shard_map/ppermute | solution.py:248
  66.5 29.5 %collective-permute-start.7 = (bf16[4,64,2432]{2,1,0:T(8,128)(2,1)S(1)}, bf16[4,64,2432]{2,1,0:T(8,128)(2,1)}, u32[]{:S(2)}, u32[]{:S(2)}) collective-permute-start(bf16[4,64,2432]{2,1,0:T(8,128)(2,1)S(1)} %pad_maximum_fusion.refs_0_), channel_id=1, source_target_pairs={{0,16},{8,24},{16,0},{24,8},{1,17},{9,25},{17,1},{25,9},{2,18},{10... | collective-permute-start | bytes 3735560 | tf_op jit(solution)/shard_map/ppermute | solution.py:248
  94.7 12.4 %collective-permute-start.8 = (bf16[2,64,2432]{2,1,0:T(8,128)(2,1)}, bf16[2,64,2432]{2,1,0:T(8,128)(2,1)}, u32[]{:S(2)}, u32[]{:S(2)}) collective-permute-start(bf16[2,64,2432]{2,1,0:T(8,128)(2,1)} %cut.8), channel_id=1, source_target_pairs={{0,16},{8,24},{16,0},{24,8},{1,17},{9,25},{17,1},{25,9},{2,18},{10... | collective-permute-start | bytes 1867784 | tf_op jit(solution)/shard_map/ppermute | solution.py:248
  97.9 12.2 %collective-permute-start.9 = (bf16[2,64,2432]{2,1,0:T(8,128)(2,1)}, bf16[2,64,2432]{2,1,0:T(8,128)(2,1)S(1)}, u32[]{:S(2)}, u32[]{:S(2)}) collective-permute-start(bf16[2,64,2432]{2,1,0:T(8,128)(2,1)} %cut.9), channel_id=1, source_target_pairs={{0,8},{8,0},{16,24},{24,16},{1,9},{9,1},{17,25},{25,17},{2,10},{10... | collective-permute-start | bytes 1867784 | tf_op jit(solution)/shard_map/ppermute | solution.py:248
  99.6 15.8 %collective-permute-start.10 = (bf16[4,64,2432]{2,1,0:T(8,128)(2,1)S(1)}, bf16[4,64,2432]{2,1,0:T(8,128)(2,1)}, u32[]{:S(2)}, u32[]{:S(2)}) collective-permute-start(bf16[4,64,2432]{2,1,0:T(8,128)(2,1)S(1)} %pad_maximum_fusion.refs_0_), channel_id=1, source_target_pairs={{0,1},{1,0},{2,3},{3,2},{4,5},{5,4},{6,7},{7,6},{8,9},{9,8},{10,11... | collective-permute-start | bytes 3735560 | tf_op jit(solution)/shard_map/ppermute | solution.py:258
  99.6 17.7 %collective-permute-start.11 = (bf16[4,64,2432]{2,1,0:T(8,128)(2,1)S(1)}, bf16[4,64,2432]{2,1,0:T(8,128)(2,1)}, u32[]{:S(2)}, u32[]{:S(2)}) collective-permute-start(bf16[4,64,2432]{2,1,0:T(8,128)(2,1)S(1)} %copy-done.2), channel_id=1, source_target_pairs={{0,1},{1,0},{2,3},{3,2},{4,5},{5,4},{6,7},{7,6},{8,9},{9,8},{10,11... | collective-permute-start | bytes 3735560 | tf_op jit(solution)/shard_map/ppermute | solution.py:258
  110.0 10.4 %collective-permute-start.12 = (bf16[4,64,2432]{2,1,0:T(8,128)(2,1)}, bf16[4,64,2432]{2,1,0:T(8,128)(2,1)}, u32[]{:S(2)}, u32[]{:S(2)}) collective-permute-start(bf16[4,64,2432]{2,1,0:T(8,128)(2,1)} %collective-permute-done.7.whole.refs_2_), channel_id=1, source_target_pairs={{0,1},{1,0},{2,3},{3,2},{4,5},{5,4},{6,7},{7,6},{8,9},{9,8},{10,11... | collective-permute-start | bytes 3735560 | tf_op jit(solution)/shard_map/ppermute | solution.py:258
  110.5 35.4 %collective-permute-start.17 = (bf16[4,64,2048]{2,1,0:T(8,128)(2,1)S(1)}, bf16[4,64,2048]{2,1,0:T(8,128)(2,1)}, u32[]{:S(2)}, u32[]{:S(2)}) collective-permute-start(bf16[4,64,2048]{2,1,0:T(8,128)(2,1)S(1)} %pad_maximum_fusion.1.refs_0_), channel_id=1, source_target_pairs={{0,8},{8,0},{16,24},{24,16},{1,9},{9,1},{17,25},{25,17},{2,10},{10... | collective-permute-start | bytes 3145736 | tf_op jit(solution)/shard_map/ppermute | solution.py:248
  113.8 32.1 %collective-permute-start.18 = (bf16[4,64,2048]{2,1,0:T(8,128)(2,1)S(1)}, bf16[4,64,2048]{2,1,0:T(8,128)(2,1)}, u32[]{:S(2)}, u32[]{:S(2)}) collective-permute-start(bf16[4,64,2048]{2,1,0:T(8,128)(2,1)S(1)} %pad_maximum_fusion.1.refs_0_), channel_id=1, source_target_pairs={{0,16},{8,24},{16,0},{24,8},{1,17},{9,25},{17,1},{25,9},{2,18},{10... | collective-permute-start | bytes 3145736 | tf_op jit(solution)/shard_map/ppermute | solution.py:248
  115.5 69.0 %collective-permute-start.15 = (bf16[384,2048]{1,0:T(8,128)(2,1)}, bf16[384,2048]{1,0:T(8,128)(2,1)}, u32[]{:S(2)}, u32[]{:S(2)}) collective-permute-start(bf16[384,2048]{1,0:T(8,128)(2,1)} %cot.1), channel_id=1, source_target_pairs={{0,8},{8,0},{16,24},{24,16},{1,9},{9,1},{17,25},{25,17},{2,10},{10... | collective-permute-start | bytes 4718600 | tf_op jit(solution)/shard_map/ppermute | solution.py:248
  117.3 67.3 %collective-permute-start.16 = (bf16[384,2048]{1,0:T(8,128)(2,1)}, bf16[384,2048]{1,0:T(8,128)(2,1)S(1)}, u32[]{:S(2)}, u32[]{:S(2)}) collective-permute-start(bf16[384,2048]{1,0:T(8,128)(2,1)} %cot.1), channel_id=1, source_target_pairs={{0,16},{8,24},{16,0},{24,8},{1,17},{9,25},{17,1},{25,9},{2,18},{10... | collective-permute-start | bytes 4718600 | tf_op jit(solution)/shard_map/ppermute | solution.py:248
  147.7 36.2 %collective-permute-start.19 = (bf16[2,64,2048]{2,1,0:T(8,128)(2,1)}, bf16[2,64,2048]{2,1,0:T(8,128)(2,1)S(1)}, u32[]{:S(2)}, u32[]{:S(2)}) collective-permute-start(bf16[2,64,2048]{2,1,0:T(8,128)(2,1)} %cut.10), channel_id=1, source_target_pairs={{0,16},{8,24},{16,0},{24,8},{1,17},{9,25},{17,1},{25,9},{2,18},{10... | collective-permute-start | bytes 1572872 | tf_op jit(solution)/shard_map/ppermute | solution.py:248
  150.8 33.2 %collective-permute-start.20 = (bf16[2,64,2048]{2,1,0:T(8,128)(2,1)}, bf16[2,64,2048]{2,1,0:T(8,128)(2,1)S(1)}, u32[]{:S(2)}, u32[]{:S(2)}) collective-permute-start(bf16[2,64,2048]{2,1,0:T(8,128)(2,1)} %cut.11), channel_id=1, source_target_pairs={{0,8},{8,0},{16,24},{24,16},{1,9},{9,1},{17,25},{25,17},{2,10},{10... | collective-permute-start | bytes 1572872 | tf_op jit(solution)/shard_map/ppermute | solution.py:248
  151.1 33.9 %collective-permute-start.21 = (bf16[4,64,2048]{2,1,0:T(8,128)(2,1)S(1)}, bf16[4,64,2048]{2,1,0:T(8,128)(2,1)S(1)}, u32[]{:S(2)}, u32[]{:S(2)}) collective-permute-start(bf16[4,64,2048]{2,1,0:T(8,128)(2,1)S(1)} %pad_maximum_fusion.1.refs_0_), channel_id=1, source_target_pairs={{0,1},{1,0},{2,3},{3,2},{4,5},{5,4},{6,7},{7,6},{8,9},{9,8},{10,11... | collective-permute-start | bytes 3145736 | tf_op jit(solution)/shard_map/ppermute | solution.py:258
  184.0 6.1 collective-permute-start.22
  184.0 6.8 collective-permute-start.23
  200.5 37.5 %collective-permute-start.26 = (bf16[384,2048]{1,0:T(8,128)(2,1)}, bf16[384,2048]{1,0:T(8,128)(2,1)S(1)}, u32[]{:S(2)}, u32[]{:S(2)}) collective-permute-start(bf16[384,2048]{1,0:T(8,128)(2,1)} %get-tuple-element.174.refs_0_), channel_id=1, source_target_pairs={{0,8},{8,0},{16,24},{24,16},{1,9},{9,1},{17,25},{25,17},{2,10},{10... | collective-permute-start | bytes 4718600 | tf_op jit(solution)/shard_map/ppermute | solution.py:248
  202.4 40.1 %collective-permute-start.27 = (bf16[384,2048]{1,0:T(8,128)(2,1)}, bf16[384,2048]{1,0:T(8,128)(2,1)S(1)}, u32[]{:S(2)}, u32[]{:S(2)}) collective-permute-start(bf16[384,2048]{1,0:T(8,128)(2,1)} %get-tuple-element.174.refs_0_), channel_id=1, source_target_pairs={{0,16},{8,24},{16,0},{24,8},{1,17},{9,25},{17,1},{25,9},{2,18},{10... | collective-permute-start | bytes 4718600 | tf_op jit(solution)/shard_map/ppermute | solution.py:248
  205.6 51.1 %collective-permute-start.30 = (bf16[192,2048]{1,0:T(8,128)(2,1)}, bf16[192,2048]{1,0:T(8,128)(2,1)S(1)}, u32[]{:S(2)}, u32[]{:S(2)}) collective-permute-start(bf16[192,2048]{1,0:T(8,128)(2,1)} %cut.14), channel_id=1, source_target_pairs={{0,16},{8,24},{16,0},{24,8},{1,17},{9,25},{17,1},{25,9},{2,18},{10... | collective-permute-start | bytes 2359304 | tf_op jit(solution)/shard_map/ppermute | solution.py:248
  208.2 48.5 %collective-permute-start.31 = (bf16[192,2048]{1,0:T(8,128)(2,1)}, bf16[192,2048]{1,0:T(8,128)(2,1)}, u32[]{:S(2)}, u32[]{:S(2)}) collective-permute-start(bf16[192,2048]{1,0:T(8,128)(2,1)} %cut.15), channel_id=1, source_target_pairs={{0,8},{8,0},{16,24},{24,16},{1,9},{9,1},{17,25},{25,17},{2,10},{10... | collective-permute-start | bytes 2359304 | tf_op jit(solution)/shard_map/ppermute | solution.py:248
  241.1 31.3 %collective-permute-start.28 = (bf16[192,2048]{1,0:T(8,128)(2,1)}, bf16[192,2048]{1,0:T(8,128)(2,1)S(1)}, u32[]{:S(2)}, u32[]{:S(2)}) collective-permute-start(bf16[192,2048]{1,0:T(8,128)(2,1)} %cut.12), channel_id=1, source_target_pairs={{0,16},{8,24},{16,0},{24,8},{1,17},{9,25},{17,1},{25,9},{2,18},{10... | collective-permute-start | bytes 2359304 | tf_op jit(solution)/shard_map/ppermute | solution.py:248
  245.6 26.9 %collective-permute-start.29 = (bf16[192,2048]{1,0:T(8,128)(2,1)}, bf16[192,2048]{1,0:T(8,128)(2,1)S(1)}, u32[]{:S(2)}, u32[]{:S(2)}) collective-permute-start(bf16[192,2048]{1,0:T(8,128)(2,1)} %cut.13), channel_id=1, source_target_pairs={{0,8},{8,0},{16,24},{24,16},{1,9},{9,1},{17,25},{25,17},{2,10},{10... | collective-permute-start | bytes 2359304 | tf_op jit(solution)/shard_map/ppermute | solution.py:248
  364.1 41.9 %collective-permute-start.35 = (bf16[4,176,2048]{2,1,0:T(8,128)(2,1)}, bf16[4,176,2048]{2,1,0:T(8,128)(2,1)}, u32[]{:S(2)}, u32[]{:S(2)}) collective-permute-start(bf16[4,176,2048]{2,1,0:T(8,128)(2,1)} %get-tuple-element.189), channel_id=1, source_target_pairs={{0,1},{1,0},{2,3},{3,2},{4,5},{5,4},{6,7},{7,6},{8,9},{9,8},{10,11... | collective-permute-start | bytes 8650760 | tf_op jit(solution)/shard_map/ppermute | solution.py:258
  364.1 37.0 %collective-permute-start.36 = (bf16[2,192,2048]{2,1,0:T(8,128)(2,1)}, bf16[2,192,2048]{2,1,0:T(8,128)(2,1)S(1)}, u32[]{:S(2)}, u32[]{:S(2)}) collective-permute-start(bf16[2,192,2048]{2,1,0:T(8,128)(2,1)} %get-tuple-element.184), channel_id=1, source_target_pairs={{0,8},{8,0},{16,24},{24,16},{1,9},{9,1},{17,25},{25,17},{2,10},{10... | collective-permute-start | bytes 4718600 | tf_op jit(solution)/shard_map/ppermute | solution.py:248
  364.5 36.7 %collective-permute-start.37 = (bf16[2,192,2048]{2,1,0:T(8,128)(2,1)}, bf16[2,192,2048]{2,1,0:T(8,128)(2,1)S(1)}, u32[]{:S(2)}, u32[]{:S(2)}) collective-permute-start(bf16[2,192,2048]{2,1,0:T(8,128)(2,1)} %get-tuple-element.185), channel_id=1, source_target_pairs={{0,16},{8,24},{16,0},{24,8},{1,17},{9,25},{17,1},{25,9},{2,18},{10... | collective-permute-start | bytes 4718600 | tf_op jit(solution)/shard_map/ppermute | solution.py:248
  410.9 146.6 %reduce-scatter.6.cloned.1.call-start = ((), (), s32[]{:S(2)}) async-start(), calls=%async_computation.4 | async-start | bytes 3604480 | tf_op jit(solution)/shard_map/reduce_scatter | solution.py:988
  411.0 51.1 %collective-permute-start.42 = (bf16[4,4,64,1408]{3,2,1,0:T(8,128)(2,1)}, bf16[4,4,64,1408]{3,2,1,0:T(8,128)(2,1)S(1)}, u32[]{:S(2)}, u32[]{:S(2)}) collective-permute-start(bf16[4,4,64,1408]{3,2,1,0:T(8,128)(2,1)} %get-tuple-element.211), channel_id=1, source_target_pairs={{0,1},{1,0},{2,3},{3,2},{4,5},{5,4},{6,7},{7,6},{8,9},{9,8},{10,11... | collective-permute-start | bytes 8650760 | tf_op jit(solution)/shard_map/ppermute | solution.py:258
  411.1 20.2 %collective-permute-start.38 = (bf16[1,192,2048]{2,1,0:T(8,128)(2,1)}, bf16[1,192,2048]{2,1,0:T(8,128)(2,1)S(1)}, u32[]{:S(2)}, u32[]{:S(2)}) collective-permute-start(bf16[1,192,2048]{2,1,0:T(8,128)(2,1)} %get-tuple-element.199), channel_id=1, source_target_pairs={{0,16},{8,24},{16,0},{24,8},{1,17},{9,25},{17,1},{25,9},{2,18},{10... | collective-permute-start | bytes 2359304 | tf_op jit(solution)/shard_map/ppermute | solution.py:248
  412.5 19.9 %collective-permute-start.39 = (bf16[1,192,2048]{2,1,0:T(8,128)(2,1)}, bf16[1,192,2048]{2,1,0:T(8,128)(2,1)}, u32[]{:S(2)}, u32[]{:S(2)}) collective-permute-start(bf16[1,192,2048]{2,1,0:T(8,128)(2,1)} %get-tuple-element.200), channel_id=1, source_target_pairs={{0,8},{8,0},{16,24},{24,16},{1,9},{9,1},{17,25},{25,17},{2,10},{10... | collective-permute-start | bytes 2359304 | tf_op jit(solution)/shard_map/ppermute | solution.py:248
  462.1 29.3 %collective-permute-start.43 = (bf16[2,4,2,64,2048]{4,3,2,1,0:T(8,128)(2,1)}, bf16[2,4,2,64,2048]{4,3,2,1,0:T(8,128)(2,1)}, u32[]{:S(2)}, u32[]{:S(2)}) collective-permute-start(bf16[2,4,2,64,2048]{4,3,2,1,0:T(8,128)(2,1)} %get-tuple-element.215), channel_id=1, source_target_pairs={{0,1},{1,0},{2,3},{3,2},{4,5},{5,4},{6,7},{7,6},{8,9},{9,8},{10,11... | collective-permute-start | bytes 12582920 | tf_op jit(solution)/shard_map/ppermute | solution.py:258
  468.7 224.1 %reduce-scatter.8.cloned.1.call-start = ((), (), s32[]{:S(2)}) async-start(), calls=%async_computation.5 | async-start | bytes 3604480 | tf_op jit(solution)/shard_map/reduce_scatter | solution.py:988
  468.7 22.6 %collective-permute-start.44 = (bf16[4,4,64,1408]{3,2,1,0:T(8,128)(2,1)}, bf16[4,4,64,1408]{3,2,1,0:T(8,128)(2,1)}, u32[]{:S(2)}, u32[]{:S(2)}) collective-permute-start(bf16[4,4,64,1408]{3,2,1,0:T(8,128)(2,1)} %get-tuple-element.216), channel_id=1, source_target_pairs={{0,1},{1,0},{2,3},{3,2},{4,5},{5,4},{6,7},{7,6},{8,9},{9,8},{10,11... | collective-permute-start | bytes 8650760 | tf_op jit(solution)/shard_map/ppermute | solution.py:258
  469.3 43.4 %collective-permute-start.40 = (bf16[2,192,2048]{2,1,0:T(8,128)(2,1)}, bf16[2,192,2048]{2,1,0:T(8,128)(2,1)S(1)}, u32[]{:S(2)}, u32[]{:S(2)}) collective-permute-start(bf16[2,192,2048]{2,1,0:T(8,128)(2,1)} %get-tuple-element.205), channel_id=1, source_target_pairs={{0,8},{8,0},{16,24},{24,16},{1,9},{9,1},{17,25},{25,17},{2,10},{10... | collective-permute-start | bytes 4718600 | tf_op jit(solution)/shard_map/ppermute | solution.py:248
  470.6 42.2 %collective-permute-start.41 = (bf16[2,192,2048]{2,1,0:T(8,128)(2,1)S(1)}, bf16[2,192,2048]{2,1,0:T(8,128)(2,1)}, u32[]{:S(2)}, u32[]{:S(2)}) collective-permute-start(bf16[2,192,2048]{2,1,0:T(8,128)(2,1)S(1)} %copy-done.51), channel_id=1, source_target_pairs={{0,16},{8,24},{16,0},{24,8},{1,17},{9,25},{17,1},{25,9},{2,18},{10... | collective-permute-start | bytes 4718600 | tf_op jit(solution)/shard_map/ppermute | solution.py:248
  527.5 30.0 %collective-permute-start.51 = (bf16[2,4,2,64,2432]{4,3,2,1,0:T(8,128)(2,1)}, bf16[2,4,2,64,2432]{4,3,2,1,0:T(8,128)(2,1)}, u32[]{:S(2)}, u32[]{:S(2)}) collective-permute-start(bf16[2,4,2,64,2432]{4,3,2,1,0:T(8,128)(2,1)} %get-tuple-element.237), channel_id=1, source_target_pairs={{0,1},{1,0},{2,3},{3,2},{4,5},{5,4},{6,7},{7,6},{8,9},{9,8},{10,11... | collective-permute-start | bytes 14942216 | tf_op jit(solution)/shard_map/ppermute | solution.py:258
  527.5 25.8 %collective-permute-start.45 = (bf16[4,64,2048]{2,1,0:T(8,128)(2,1)}, bf16[4,64,2048]{2,1,0:T(8,128)(2,1)S(1)}, u32[]{:S(2)}, u32[]{:S(2)}) collective-permute-start(bf16[4,64,2048]{2,1,0:T(8,128)(2,1)} %get-tuple-element.219), channel_id=1, source_target_pairs={{0,8},{8,0},{16,24},{24,16},{1,9},{9,1},{17,25},{25,17},{2,10},{10... | collective-permute-start | bytes 3145736 | tf_op jit(solution)/shard_map/ppermute | solution.py:248
  528.7 24.7 %collective-permute-start.46 = (bf16[4,64,2048]{2,1,0:T(8,128)(2,1)S(1)}, bf16[4,64,2048]{2,1,0:T(8,128)(2,1)S(1)}, u32[]{:S(2)}, u32[]{:S(2)}) collective-permute-start(bf16[4,64,2048]{2,1,0:T(8,128)(2,1)S(1)} %copy-done.52), channel_id=1, source_target_pairs={{0,16},{8,24},{16,0},{24,8},{1,17},{9,25},{17,1},{25,9},{2,18},{10... | collective-permute-start | bytes 3145736 | tf_op jit(solution)/shard_map/ppermute | solution.py:248
  561.3 71.9 %collective-permute-start.52 = (bf16[4,64,2432]{2,1,0:T(8,128)(2,1)}, bf16[4,64,2432]{2,1,0:T(8,128)(2,1)S(1)}, u32[]{:S(2)}, u32[]{:S(2)}) collective-permute-start(bf16[4,64,2432]{2,1,0:T(8,128)(2,1)} %get-tuple-element.239), channel_id=1, source_target_pairs={{0,8},{8,0},{16,24},{24,16},{1,9},{9,1},{17,25},{25,17},{2,10},{10... | collective-permute-start | bytes 3735560 | tf_op jit(solution)/shard_map/ppermute | solution.py:248
  562.4 70.9 %collective-permute-start.53 = (bf16[4,64,2432]{2,1,0:T(8,128)(2,1)}, bf16[4,64,2432]{2,1,0:T(8,128)(2,1)S(1)}, u32[]{:S(2)}, u32[]{:S(2)}) collective-permute-start(bf16[4,64,2432]{2,1,0:T(8,128)(2,1)} %get-tuple-element.240), channel_id=1, source_target_pairs={{0,16},{8,24},{16,0},{24,8},{1,17},{9,25},{17,1},{25,9},{2,18},{10... | collective-permute-start | bytes 3735560 | tf_op jit(solution)/shard_map/ppermute | solution.py:248
  563.2 40.9 %collective-permute-start.47 = (bf16[2,64,2048]{2,1,0:T(8,128)(2,1)S(1)}, bf16[2,64,2048]{2,1,0:T(8,128)(2,1)S(1)}, u32[]{:S(2)}, u32[]{:S(2)}) collective-permute-start(bf16[2,64,2048]{2,1,0:T(8,128)(2,1)S(1)} %copy-done.54), channel_id=1, source_target_pairs={{0,16},{8,24},{16,0},{24,8},{1,17},{9,25},{17,1},{25,9},{2,18},{10... | collective-permute-start | bytes 1572872 | tf_op jit(solution)/shard_map/ppermute | solution.py:248
  564.4 54.9 %collective-permute-start.49 = (bf16[1,192,2048]{2,1,0:T(8,128)(2,1)}, bf16[1,192,2048]{2,1,0:T(8,128)(2,1)}, u32[]{:S(2)}, u32[]{:S(2)}) collective-permute-start(bf16[1,192,2048]{2,1,0:T(8,128)(2,1)} %get-tuple-element.227), channel_id=1, source_target_pairs={{0,16},{8,24},{16,0},{24,8},{1,17},{9,25},{17,1},{25,9},{2,18},{10... | collective-permute-start | bytes 2359304 | tf_op jit(solution)/shard_map/ppermute | solution.py:248
  565.2 54.1 %collective-permute-start.50 = (bf16[1,192,2048]{2,1,0:T(8,128)(2,1)}, bf16[1,192,2048]{2,1,0:T(8,128)(2,1)}, u32[]{:S(2)}, u32[]{:S(2)}) collective-permute-start(bf16[1,192,2048]{2,1,0:T(8,128)(2,1)} %get-tuple-element.228), channel_id=1, source_target_pairs={{0,8},{8,0},{16,24},{24,16},{1,9},{9,1},{17,25},{25,17},{2,10},{10... | collective-permute-start | bytes 2359304 | tf_op jit(solution)/shard_map/ppermute | solution.py:248
  604.2 14.5 %collective-permute-start.48 = (bf16[2,64,2048]{2,1,0:T(8,128)(2,1)S(1)}, bf16[2,64,2048]{2,1,0:T(8,128)(2,1)S(1)}, u32[]{:S(2)}, u32[]{:S(2)}) collective-permute-start(bf16[2,64,2048]{2,1,0:T(8,128)(2,1)S(1)} %copy-done.53), channel_id=1, source_target_pairs={{0,8},{8,0},{16,24},{24,16},{1,9},{9,1},{17,25},{25,17},{2,10},{10... | collective-permute-start | bytes 1572872 | tf_op jit(solution)/shard_map/ppermute | solution.py:248
  621.8 42.2 %collective-permute-start.56 = (bf16[2,64,2048]{2,1,0:T(8,128)(2,1)}, bf16[2,64,2048]{2,1,0:T(8,128)(2,1)S(1)}, u32[]{:S(2)}, u32[]{:S(2)}) collective-permute-start(bf16[2,64,2048]{2,1,0:T(8,128)(2,1)} %add.70), channel_id=1, source_target_pairs={{0,2},{1,3},{2,0},{3,1},{4,6},{5,7},{6,4},{7,5},{8,10},{9,11},{10,... | collective-permute-start | bytes 1572872 | tf_op jit(solution)/shard_map/ppermute | solution.py:253
  638.0 33.9 %collective-permute-start.54 = (bf16[2,64,2432]{2,1,0:T(8,128)(2,1)}, bf16[2,64,2432]{2,1,0:T(8,128)(2,1)S(1)}, u32[]{:S(2)}, u32[]{:S(2)}) collective-permute-start(bf16[2,64,2432]{2,1,0:T(8,128)(2,1)} %get-tuple-element.248), channel_id=1, source_target_pairs={{0,16},{8,24},{16,0},{24,8},{1,17},{9,25},{17,1},{25,9},{2,18},{10... | collective-permute-start | bytes 1867784 | tf_op jit(solution)/shard_map/ppermute | solution.py:248
  638.9 33.0 %collective-permute-start.55 = (bf16[2,64,2432]{2,1,0:T(8,128)(2,1)}, bf16[2,64,2432]{2,1,0:T(8,128)(2,1)S(1)}, u32[]{:S(2)}, u32[]{:S(2)}) collective-permute-start(bf16[2,64,2432]{2,1,0:T(8,128)(2,1)} %get-tuple-element.249), channel_id=1, source_target_pairs={{0,8},{8,0},{16,24},{24,16},{1,9},{9,1},{17,25},{25,17},{2,10},{10... | collective-permute-start | bytes 1867784 | tf_op jit(solution)/shard_map/ppermute | solution.py:248
  640.7 16.9 %collective-permute-start.57 = (bf16[1,64,1408]{2,1,0:T(8,128)(2,1)S(1)}, bf16[1,64,1408]{2,1,0:T(8,128)(2,1)S(1)}, u32[]{:S(2)}, u32[]{:S(2)}) collective-permute-start(bf16[1,64,1408]{2,1,0:T(8,128)(2,1)S(1)} %get-tuple-element.395), channel_id=1, source_target_pairs={{0,8},{8,0},{16,24},{24,16},{1,9},{9,1},{17,25},{25,17},{2,10},{10... | collective-permute-start | bytes 540680 | tf_op jit(solution)/shard_map/ppermute | solution.py:248
  641.6 17.2 %collective-permute-start.58 = (bf16[1,64,1408]{2,1,0:T(8,128)(2,1)S(1)}, bf16[1,64,1408]{2,1,0:T(8,128)(2,1)S(1)}, u32[]{:S(2)}, u32[]{:S(2)}) collective-permute-start(bf16[1,64,1408]{2,1,0:T(8,128)(2,1)S(1)} %get-tuple-element.394), channel_id=1, source_target_pairs={{0,16},{8,24},{16,0},{24,8},{1,17},{9,25},{17,1},{25,9},{2,18},{10... | collective-permute-start | bytes 540680 | tf_op jit(solution)/shard_map/ppermute | solution.py:248
  657.6 6.4 collective-permute-start.59
  675.3 21.4 %collective-permute-start.60 = (bf16[2,64,2432]{2,1,0:T(8,128)(2,1)}, bf16[2,64,2432]{2,1,0:T(8,128)(2,1)S(1)}, u32[]{:S(2)}, u32[]{:S(2)}) collective-permute-start(bf16[2,64,2432]{2,1,0:T(8,128)(2,1)} %add.73), channel_id=1, source_target_pairs={{0,2},{1,3},{2,0},{3,1},{4,6},{5,7},{6,4},{7,5},{8,10},{9,11},{10,... | collective-permute-start | bytes 1867784 | tf_op jit(solution)/shard_map/ppermute | solution.py:253
  677.0 15.7 %collective-permute-start.61 = (bf16[1,64,2048]{2,1,0:T(8,128)(2,1)S(1)}, bf16[1,64,2048]{2,1,0:T(8,128)(2,1)S(1)}, u32[]{:S(2)}, u32[]{:S(2)}) collective-permute-start(bf16[1,64,2048]{2,1,0:T(8,128)(2,1)S(1)} %copy-done.40), channel_id=1, source_target_pairs={{0,4},{1,5},{2,6},{3,7},{4,0},{5,1},{6,2},{7,3},{8,12},{9,13},{10,... | collective-permute-start | bytes 786440 | tf_op jit(solution)/shard_map/ppermute | solution.py:253
  699.9 17.7 %collective-permute-start.62 = (bf16[1,64,2432]{2,1,0:T(8,128)(2,1)}, bf16[1,64,2432]{2,1,0:T(8,128)(2,1)S(1)}, u32[]{:S(2)}, u32[]{:S(2)}) collective-permute-start(bf16[1,64,2432]{2,1,0:T(8,128)(2,1)} %add.74), channel_id=1, source_target_pairs={{0,4},{1,5},{2,6},{3,7},{4,0},{5,1},{6,2},{7,3},{8,12},{9,13},{10,... | collective-permute-start | bytes 933896 | tf_op jit(solution)/shard_map/ppermute | solution.py:253
  705.4 6.6 collective-permute-start.65
  (61 other events, 471.2 us)
Sparse Core Ops, SparseCore 0:
  65.6 157.3 all-gather.2
  411.1 54.0 reduce-scatter.3
  468.8 54.6 reduce-scatter.5
  527.6 54.0 reduce-scatter.7

commit v3 on v2

--- a/solution.py
+++ b/solution.py
@@ -16,7 +16,7 @@
 F32 = jnp.float32
 BF16 = jnp.bfloat16
 BOTH = ("dp", "fsdp")
-COST = 0.0
+COST = 40.0
 VMEM_BYTES = 60 * 1024 * 1024
 
 
@@ -1323,11 +1323,17 @@
     *sent, packed = slices(spot, w_gate, w_up, w_down, t_size)
     got = [sent[0]] + [dp_swap(sent[k], k) for k in range(1, t_size)]
     packed = jnp.concatenate([flat(piece).reshape(-1, piece.shape[-1]) for piece in got] + [packed])
-    output_line = gather_line(after(w_output.astype(BF16), qkv_line))
-    units_all = lax.all_gather(after(packed, output_line), "fsdp", axis=0)
-
-    qkv_near = plane_near(qkv_line)
-    qkv_far = plane_far(*qkv_near)
+    output_block = after(w_output.astype(BF16), qkv_line)
+    output_two, output_one = z_swap(output_block, 2), z_swap(output_block, 1)
+    output_last = z_swap(output_two, 1)
+    output_line = [output_block, output_two, output_one, output_last]
+    units_all = lax.all_gather(
+        after(packed, output_line[1], output_line[3]), "fsdp", axis=0
+    )
+    output_line = jnp.stack(output_line)
+
+    qkv_near = plane_near(after(qkv_line, packed))
+    qkv_far = plane_far(*after(qkv_near, output_last))
     qkv_mine = [qkv_line, *qkv_near, *qkv_far]
     qkv_pieces = qkv_mine + [core_swap(piece) for piece in qkv_mine]
     output_near = plane_near(after(output_line, *qkv_far))
@@ -1338,10 +1344,11 @@
     queries, attended, shared = attend(raw, cosine, sine, doc_ids, head_count, head_dim)
     output_mine = [output_line, *output_near, *plane_far(*after(output_near, attended))]
     output_pieces = output_mine + [core_swap(piece) for piece in output_mine]
-    cot = [out_grad, *cot_near, *plane_far(*cot_near)]
-    resid, normed2 = leave(spot, after(attended, *cot_near), tokens_in, gains_full, output_pieces)
-
-    normed2_near = plane_near(normed2)
+    cot_first, cot_second = cut(cot_near[0], 0), cut(cot_near[1], 1)
+    cot = [out_grad, *cot_near, dp_swap(cot_first, 2), dp_swap(cot_second, 1)]
+    resid, normed2 = leave(spot, after(attended, cot_first, cot_second), tokens_in, gains_full, output_pieces)
+
+    normed2_near = plane_near(after(normed2, *cot[3:]))
     normed2_all = [normed2, *normed2_near, *plane_far(*normed2_near)]
     tokens2, cots, hidden, grad_gate, grad_up, grad_terms, out_terms = ffn_all(
         spot, normed2_all, cot, units_all, t_size, w_down.shape[0]
@@ -1349,41 +1356,44 @@
     normed2_sum = TokenSum(grad_terms)
     down = LineSum(*down_grads(spot, [after(hidden, *normed2_sum.sent)], [cots]))
     gate = LineSum(*unit_grads(spot, [after(tokens2, down.mine)], [grad_gate]))
-    up = LineSum(*unit_grads(spot, [after(tokens2, gate.mine)], [grad_up]))
-    normed2_sum.a, normed2_sum.b = after((normed2_sum.a, normed2_sum.b), up.mine)
+    down.other = after(down.other, gate.mine)
+    down.line()
+    normed2_sum.a, normed2_sum.b = after((normed2_sum.a, normed2_sum.b), down.chip)
     normed2_sum.cross()
-    down.other = after(down.other, *normed2_sum.crossed)
-    down.line()
+    up = LineSum(*unit_grads(spot, [after(tokens2, *normed2_sum.crossed)], [grad_up]))
     grad_resid, grad_branch, grad_gain_ffn = branch(
-        after(resid, down.chip), out_grad, gains_full, normed2_sum.parts()
+        after(resid, up.mine), out_grad, gains_full, normed2_sum.parts()
     )
     out_sum = TokenSum(after(out_terms, grad_branch))
 
-    grad_attended = leave_back(spot, after(grad_branch, *out_sum.sent), output_pieces)
-    gate.other = after(gate.other, grad_attended)
+    output = RowSum(*row_grads(spot, attended, after(grad_branch, *out_sum.sent), width))
+    grad_attended = leave_back(spot, after(grad_branch, output.mine), output_pieces)
+    gate.other, output.other = after((gate.other, output.other), grad_attended)
+    output.plane()
     gate.line()
-    output = RowSum(*row_grads(spot, attended, after(grad_branch, grad_attended), width))
     grad_raw = attend_back(
-        queries, after(grad_attended, output.mine, gate.chip), shared, kv_grad_next, cosine, sine,
+        queries, after(grad_attended, gate.chip, *output.sent), shared, kv_grad_next, cosine, sine,
         doc_ids, head_count, head_dim,
     )
-    output.other, up.other = after((output.other, up.other), grad_raw)
-    output.plane()
-    up.line()
-    grad_raw = after(grad_raw, up.chip, *output.sent, down.total)
     input_grad, grad_gain_attn = enter_back(
         spot, grad_raw, tokens_in, gains_full, grad_resid, qkv_pieces
     )
-    out_sum.a, out_sum.b = after((out_sum.a, out_sum.b), input_grad)
-    out_sum.cross()
-    mine, other = row_grads(
-        spot, after(normed, *out_sum.crossed), grad_raw, raw_width,
-        (grad_gain_attn, grad_gain_ffn),
-    )
-    qkv = RowSum(mine, other)
-    output.a, output.b = after((output.a, output.b), mine)
+    out_sum.a, out_sum.b, output.a, output.b = after(
+        (out_sum.a, out_sum.b, output.a, output.b), input_grad
+    )
     output.cross()
-    qkv.other = after(qkv.other, gate.total, *output.crossed)
+    qkv = RowSum(
+        *row_grads(
+            spot, after(normed, *output.crossed, down.total), grad_raw, raw_width,
+            (grad_gain_attn, grad_gain_ffn),
+        )
+    )
+    output.last_a, output.last_b = after((output.last_a, output.last_b), qkv.mine)
+    output.near()
+    up.other = after(up.other, output.odd)
+    up.line()
+    gate.total = after(gate.total, up.chip)
+    qkv.other = after(qkv.other, gate.total)
     qkv.plane()
 
     def rate(strength, fan):
@@ -1393,33 +1403,37 @@
         pieces = [total[k : k + 1] for k in range(t_size)]
         return pieces[:1] + [dp_swap(pieces[k], k) for k in range(1, t_size)]
 
-    gate_pieces = exchange(flat(after(gate.total, *qkv.sent)))
-    output.last_a, output.last_b, out_sum.last_a, out_sum.last_b, down.total = after(
-        (output.last_a, output.last_b, out_sum.last_a, out_sum.last_b, down.total), *qkv.sent
-    )
-    output.near()
+    down_out = update_rows(
+        [(after(down.total, *qkv.sent), 0)], [(w_down, down_mom, down_ema)],
+        [rate(1.5, hidden_units)],
+    )
+    out_sum.a, out_sum.b = after((out_sum.a, out_sum.b), *qkv.sent)
+    out_sum.cross()
+    qkv.a, qkv.b = after((qkv.a, qkv.b), down_out[0], *out_sum.crossed)
+    qkv.cross()
+    gate_pieces = exchange(flat(after(gate.total, *qkv.crossed)))
+    output.line = after(output.line, *qkv.crossed)
+    output.far()
+    qkv.last_a, qkv.last_b = after((qkv.last_a, qkv.last_b), output.rest)
+    qkv.near()
+    out_sum.last_a, out_sum.last_b, gate_pieces = after(
+        (out_sum.last_a, out_sum.last_b, gate_pieces), qkv.odd
+    )
     layer_out = layer_out_of(resid, out_sum.parts())
-    down_out = update_rows(
-        [(down.total, 0)], [(w_down, down_mom, down_ema)], [rate(1.5, hidden_units)]
-    )
-    qkv.a, qkv.b = after((qkv.a, qkv.b), output.odd, layer_out, down_out[0])
-    qkv.cross()
-    output.line, gate_pieces = after((output.line, gate_pieces), *qkv.crossed)
-    output.far()
-    gate_out = update_units(spot, w_gate, gate_mom, gate_ema, gate_pieces, rate(0.6, width))
-    qkv.last_a, qkv.last_b = after((qkv.last_a, qkv.last_b), output.rest, gate_out[0])
-    qkv.near()
+    gate_out = update_units(
+        spot, w_gate, gate_mom, gate_ema, gate_pieces, rate(0.6, width)
+    )
     up_pieces = exchange(flat(after(up.total, qkv.odd)))
+    qkv.line = after(qkv.line, layer_out, gate_out[0])
+    qkv.far()
     output_out = update_rows(
-        [(after(x, qkv.odd), at) for x, at in output.final()], [(w_output, output_mom, output_ema)],
-        [rate(5.0, heads_width)],
-    )
-    qkv.line = after(qkv.line, output_out[0])
-    qkv.far()
+        [(after(x, qkv.rest), at) for x, at in output.final()],
+        [(w_output, output_mom, output_ema)], [rate(5.0, heads_width)],
+    )
     up_out = update_units(
         spot, w_up, up_mom, up_ema, after(up_pieces, qkv.rest), rate(0.6, width)
     )
-    qkv.last = after(qkv.last, up_out[0])
+    qkv.last = after(qkv.last, up_out[0], output_out[0])
     *qkv_out, left_over = update_rows(
         qkv.final(),
         [(w_query, query_mom, query_ema), (w_keyval, keyval_mom, keyval_ema)],

time: 743 us -> 642 us (0.86)
  waiting for transfers between devices: 293 us -> 212 us
  local copies, waits for them, and re-layouts: 28.9 us -> 18 us
    ppermute x41, waiting for transfers between devices: 253 us -> 153 us  [dp_swap(): return lax.ppermute(value, 'dp', [(i, i ^ k) for i in range(size)])]
    ppermute x10, waiting for transfers between devices: 35.1 us -> 56.4 us  [z_swap(): return lax.ppermute(value, 'fsdp', [(i, i ^ 2 * k) for i in range(size)])]
    unnamed x118 -> x102, local copies, waits for them, and re-layouts: 25.4 us -> 13.5 us
  transfers between devices with their start and end apart: 70 -> 70, of which waited for: 30 -> 26; matrix products, arithmetic and copies ran while one was open for 2% -> 2% of each run, Pallas kernels for 30% -> 37%
where the time goes in v3:
time: 642 us; the launch traced here: 637 us
  Pallas kernels  321 us (50%)
  waiting for transfers between devices  212 us (33%)
  starting transfers between devices  62.3 us (10%)
  local copies, waits for them, and re-layouts  18 us (3%)
  between operations  14.6 us (2%)
  other arithmetic  8.61 us (1%)
    ppermute x41, waiting for transfers between devices, dp_swap(): return lax.ppermute(value, 'dp', [(i, i ^ k) for i in range(size)])  153 us
    pallas_call x1, Pallas kernels, ffn_all(): pl.pallas_call(ffn_all_kernel, grid=(4,), in_specs=[SMEM] + [ANY] * 11, o...  72.3 us
    ppermute x10, waiting for transfers between devices, z_swap(): return lax.ppermute(value, 'fsdp', [(i, i ^ 2 * k) for i in range(size)])  56.4 us
    pallas_call x15, Pallas kernels, add(): pl.pallas_call(functools.partial(add_kernel, [len(job) for job in jobs]),...  50.1 us
    ppermute x41, starting transfers between devices, dp_swap(): return lax.ppermute(value, 'dp', [(i, i ^ k) for i in range(size)])  44.1 us
    pallas_call x2, Pallas kernels, unit_grads(): pl.pallas_call(line_grads_kernel, grid_spec=pltpu.PrefetchScalarGridSpec(...  31.1 us
    pallas_call x2, Pallas kernels, row_grads(): pl.pallas_call(row_grads_kernel, grid_spec=pltpu.PrefetchScalarGridSpec(n...  20 us
    pallas_call x1, Pallas kernels, attend_back(): pl.pallas_call(functools.partial(attend_back_kernel, head_dim ** (-0.5),...  19.6 us
  transfers between devices with their start and end apart: 70, of which 26 were waited for; matrix products, arithmetic and copies ran while one was open for 2% of the time, Pallas kernels for 37%

profile of v3, /device:TPU:0, one launch (start us, length us, event | category | flops | bytes accessed | tf_op | source)
XLA Modules:
  0.0 637.0 jit_solution(12956729366567250071)
XLA Ops:
  7.9 3.8 slices.1
  11.7 2.9 collective-permute-start.6
  16.9 2.6 collective-permute-start
  23.1 10.6 %collective-permute-done = bf16[64,2432]{1,0:T(8,128)(2,1)} collective-permute-done((bf16[64,2432]{1,0:T(8,128)(2,1)}, bf16[64,2432]{1,0:T(8,128)(2,1)}, u32[]{:S(2)}, u32[]{:S(2)}) %collective-permute-start) | collective-permute-done | bytes 311328 | tf_op jit(solution)/shard_map/ppermute | solution.py:253
  34.3 4.0 collective-permute-done.7
  38.5 3.5 collective-permute-done.2
  45.5 3.4 collective-permute-start.3
  48.9 11.0 %collective-permute-done.3 = bf16[64,2048]{1,0:T(8,128)(2,1)S(1)} collective-permute-done((bf16[64,2048]{1,0:T(8,128)(2,1)S(1)}, bf16[64,2048]{1,0:T(8,128)(2,1)S(1)}, u32[]{:S(2)}, u32[]{:S(2)}) %collective-permute-start.3) | collective-permute-done | bytes 262176 | tf_op jit(solution)/shard_map/ppermute | solution.py:253
  62.0 7.2 %collective-permute-done.5 = bf16[64,2048]{1,0:T(8,128)(2,1)S(1)} collective-permute-done((bf16[64,2048]{1,0:T(8,128)(2,1)S(1)}, bf16[64,2048]{1,0:T(8,128)(2,1)S(1)}, u32[]{:S(2)}, u32[]{:S(2)}) %collective-permute-start.5) | collective-permute-done | bytes 262176 | tf_op jit(solution)/shard_map/ppermute | solution.py:253
  69.2 2.0 collective-permute-done.9.whole.refs_1_
  72.2 1.9 cut.8
  79.8 8.2 %collective-permute-done.11.refs_3_ = bf16[2,64,2432]{2,1,0:T(8,128)(2,1)} collective-permute-done((bf16[2,64,2432]{2,1,0:T(8,128)(2,1)}, bf16[2,64,2432]{2,1,0:T(8,128)(2,1)}, u32[]{:S(2)}, u32[]{:S(2)}) %collective-permute-start.11) | collective-permute-done | bytes 622624 | tf_op jit(solution)/shard_map/ppermute | solution.py:248
  88.0 3.0 collective-permute-done.12.refs_4_
  99.5 10.6 %enter.1 = (f32[384,2304]{1,0:T(8,128)}, bf16[384,2048]{1,0:T(8,128)(2,1)}, f32[8,2048]{1,0:T(8,128)}) custom-call(s32[3]{0:T(128)} %pad_add_fusion.spot, bf16[384,2048]{1,0:T(8,128)(2,1)} %tokens.4, bf16[4,64,2432]{2,1,0:T(8,128)(2,1)} %copy-done.11, bf16[4,64,2432]{2,1,0:T(8,128)(2,1)} %copy-done.13, ...), custom_call_target="tpu_custom_call" | custom-call | flops 144955146240 | bytes 377487360 | tf_op jit(solution)/shard_map/enter/pallas_call | solution.py:519
  110.1 15.2 %attend.1 = (bf16[384,2048]{1,0:T(8,128)(2,1)}, bf16[384,2048]{1,0:T(8,128)(2,1)}, bf16[384,256]{1,0:T(8,128)(2,1)}) custom-call(f32[384,2304]{1,0:T(8,128)} %get-tuple-element.179.q_raw.k_raw.v_raw, f32[384,2304]{1,0:T(8,128)} %get-tuple-element.179.q_raw.k_raw.v_raw, f32[384,2304]{1,0:T(8,128)} %get-tuple-element.179.q_raw.k_raw.v_raw, ...), custom_call_target="tpu_custom_call" | custom-call | flops 72477573120 | bytes 314572800 | tf_op jit(solution)/shard_map/attend/pallas_call | solution.py:102
  130.0 36.5 %collective-permute-done.22.refs_3_ = bf16[2,64,2048]{2,1,0:T(8,128)(2,1)} collective-permute-done((bf16[2,64,2048]{2,1,0:T(8,128)(2,1)}, bf16[2,64,2048]{2,1,0:T(8,128)(2,1)}, u32[]{:S(2)}, u32[]{:S(2)}) %collective-permute-start.22) | collective-permute-done | bytes 524320 | tf_op jit(solution)/shard_map/ppermute | solution.py:248
  169.4 2.0 cut.11
  174.8 9.8 %leave.1 = (f32[384,2048]{1,0:T(8,128)}, bf16[384,2048]{1,0:T(8,128)(2,1)}) custom-call(s32[3]{0:T(128)} %pad_add_fusion.spot, bf16[384,2048]{1,0:T(8,128)(2,1)} %get-tuple-element.182.attended.left, bf16[384,2048]{1,0:T(8,128)(2,1)} %tokens.4, f32[8,2048]{1,0:T(8,128)} %get-tuple-element.183.gains, bf16[4,64,2048]{2,1,0:T(8,128)(2,1)} %pad_maximum_fusion.1.refs_0_, ...), custom_call_target="tpu_custom_call" | custom-call | flops 128849018880 | bytes 335544320 | tf_op jit(solution)/shard_map/leave/pallas_call | solution.py:546
  184.6 6.5 %collective-permute-done.29.refs_8_ = bf16[192,2048]{1,0:T(8,128)(2,1)} collective-permute-done((bf16[192,2048]{1,0:T(8,128)(2,1)S(1)}, bf16[192,2048]{1,0:T(8,128)(2,1)}, u32[]{:S(2)}, u32[]{:S(2)}) %collective-permute-start.29) | collective-permute-done | bytes 786464 | tf_op jit(solution)/shard_map/ppermute | solution.py:248
  194.5 32.4 %collective-permute-done.31.whole.refs_1_ = bf16[384,2048]{1,0:T(8,128)(2,1)S(1)} collective-permute-done((bf16[384,2048]{1,0:T(8,128)(2,1)}, bf16[384,2048]{1,0:T(8,128)(2,1)S(1)}, u32[]{:S(2)}, u32[]{:S(2)}) %collective-permute-start.31) | collective-permute-done | bytes 1572896 | tf_op jit(solution)/shard_map/ppermute | solution.py:248
  232.7 1.9 cut.15
  236.1 11.7 %collective-permute-done.33.refs_3_ = bf16[192,2048]{1,0:T(8,128)(2,1)S(1)} collective-permute-done((bf16[192,2048]{1,0:T(8,128)(2,1)}, bf16[192,2048]{1,0:T(8,128)(2,1)S(1)}, u32[]{:S(2)}, u32[]{:S(2)}) %collective-permute-start.33) | collective-permute-done | bytes 786464 | tf_op jit(solution)/shard_map/ppermute | solution.py:248
  247.8 4.3 collective-permute-done.34.refs_4_
  252.1 2.9 all-gather.3.cloned.1.call-done
  255.1 72.3 %ffn_all.1 = (bf16[1536,2048]{1,0:T(8,128)(2,1)}, bf16[1536,2048]{1,0:T(8,128)(2,1)}, bf16[1536,1408]{1,0:T(8,128)(2,1)}, bf16[1536,1408]{1,0:T(8,128)(2,1)}, bf...) custom-call(s32[3]{0:T(128)} %pad_add_fusion.spot, ...), custom_call_target="tpu_custom_call" | custom-call | flops 2126008811520 | bytes 1698693120 | tf_op jit(solution)/shard_map/ffn_all/pallas_call | solution.py:730
  327.4 3.3 add.60
  333.6 15.1 %down_grads.1 = (bf16[4,176,2048]{2,1,0:T(8,128)(2,1)}, bf16[4,176,2048]{2,1,0:T(8,128)(2,1)}) custom-call(s32[3]{0:T(128)} %pad_add_fusion.spot, bf16[1536,1408]{1,0:T(8,128)(2,1)} %get-tuple-element.197.refs_0_, bf16[1536,2048]{1,0:T(8,128)(2,1)} %get-tuple-element.198.refs_1_), custom_call_target="tpu_custom_call" | custom-call | flops 354334801920 | bytes 655360000 | tf_op jit(solution)/shard_map/down_grads/pallas_call | solution.py:1049
  348.7 15.5 %unit_grads.2 = (bf16[4,4,64,1408]{3,2,1,0:T(8,128)(2,1)}, bf16[4,4,64,1408]{3,2,1,0:T(8,128)(2,1)}) custom-call(s32[3]{0:T(128)} %pad_add_fusion.spot, bf16[1536,2048]{1,0:T(8,128)(2,1)} %get-tuple-element.209.refs_0_, bf16[1536,1408]{1,0:T(8,128)(2,1)} %get-tuple-element.202.refs_1_), custom_call_target="tpu_custom_call" | custom-call | flops 354334801920 | bytes 655360000 | tf_op jit(solution)/shard_map/unit_grads/pallas_call | solution.py:1026
  364.7 4.9 add.61
  369.6 3.2 add.62
  374.0 15.6 %unit_grads.3 = (bf16[4,4,64,1408]{3,2,1,0:T(8,128)(2,1)}, bf16[4,4,64,1408]{3,2,1,0:T(8,128)(2,1)}) custom-call(s32[3]{0:T(128)} %pad_add_fusion.spot, bf16[1536,2048]{1,0:T(8,128)(2,1)} %get-tuple-element.209.refs_0_, bf16[1536,1408]{1,0:T(8,128)(2,1)} %get-tuple-element.210.refs_1_), custom_call_target="tpu_custom_call" | custom-call | flops 354334801920 | bytes 655360000 | tf_op jit(solution)/shard_map/unit_grads/pallas_call | solution.py:1026
  389.6 3.0 collective-permute-done.38.refs_2_
  392.9 8.7 %branch.1 = (f32[384,2048]{1,0:T(8,128)}, bf16[384,2048]{1,0:T(8,128)(2,1)}, f32[8,2048]{1,0:T(8,128)}) custom-call(f32[384,2048]{1,0:T(8,128)} %get-tuple-element.212.resid, bf16[384,2048]{1,0:T(8,128)(2,1)} %cot.1, f32[8,2048]{1,0:T(8,128)} %get-tuple-element.183.gains, bf16[8,192,2048]{2,1,0:T(8,128)(2,1)} %bitcast.58, ...), custom_call_target="tpu_custom_call" | custom-call | bytes 566231040 | tf_op jit(solution)/shard_map/branch/pallas_call | solution.py:855
  401.5 3.2 add.63
  406.8 9.4 %row_grads.2 = (bf16[2,4,2,64,2048]{4,3,2,1,0:T(8,128)(2,1)}, bf16[2,4,2,64,2048]{4,3,2,1,0:T(8,128)(2,1)}) custom-call(s32[3]{0:T(128)} %pad_add_fusion.spot, bf16[384,2048]{1,0:T(8,128)(2,1)} %get-tuple-element.182.attended.left, bf16[384,2048]{1,0:T(8,128)(2,1)} %get-tuple-element.221.right.grads), custom_call_target="tpu_custom_call" | custom-call | flops 128849018880 | bytes 461373440 | tf_op jit(solution)/shard_map/row_grads/pallas_call | solution.py:924
  416.2 8.4 %leave_back.1.grad_ref = bf16[384,2048]{1,0:T(8,128)(2,1)} custom-call(s32[3]{0:T(128)} %pad_add_fusion.spot, bf16[384,2048]{1,0:T(8,128)(2,1)} %get-tuple-element.221.right.grads, bf16[4,64,2048]{2,1,0:T(8,128)(2,1)} %pad_maximum_fusion.1.refs_0_, bf16[4,64,2048]{2,1,0:T(8,128)(2,1)} %collective-permute-done.20.whole.refs_1_, ...), custom_call_target="tpu_custom_call" | custom-call | flops 128849018880 | bytes 335544320 | tf_op jit(solution)/shard_map/leave_back/pallas_call | solution.py:569
  424.6 3.3 add.64
  429.9 4.9 add.65
  434.9 19.6 %attend_back.1.grads.right = bf16[384,2432]{1,0:T(8,128)(2,1)} custom-call(bf16[384,2048]{1,0:T(8,128)(2,1)} %get-tuple-element.225.query_ref, bf16[384,2048]{1,0:T(8,128)(2,1)} %leave_back.1.grad_ref, bf16[384,256]{1,0:T(8,128)(2,1)} %get-tuple-element.228.shared, bf16[384,256]{1,0:T(8,128)(2,1)} %kv_next.1, f32[384,128]{1,0:T(8,128)} %get-tuple-element.414.cosine, ...), custom_call_target="tpu_custom_call" | custom-call | flops 169114337280 | bytes 251658240 | tf_op jit(solution)/shard_map/attend_back/pallas_call | solution.py:180
  454.5 13.1 %enter_back.1 = (f32[384,2048]{1,0:T(8,128)}, f32[8,2048]{1,0:T(8,128)}) custom-call(s32[3]{0:T(128)} %pad_add_fusion.spot, bf16[384,2432]{1,0:T(8,128)(2,1)} %attend_back.1.grads.right, bf16[384,2048]{1,0:T(8,128)(2,1)} %tokens.4, f32[8,2048]{1,0:T(8,128)} %get-tuple-element.183.gains, f32[384,2048]{1,0:T(8,128)} %get-tuple-element.229.grad_resid, ...), custom_call_target="tpu_custom_call" | custom-call | flops 128849018880 | bytes 335544320 | tf_op jit(solution)/shard_map/enter_back/pallas_call | solution.py:594
  467.6 2.8 add.66
  470.5 10.6 %row_grads.3 = (bf16[2,4,2,64,2432]{4,3,2,1,0:T(8,128)(2,1)}, bf16[2,4,2,64,2432]{4,3,2,1,0:T(8,128)(2,1)}) custom-call(s32[3]{0:T(128)} %pad_add_fusion.spot, bf16[384,2048]{1,0:T(8,128)(2,1)} %get-tuple-element.238.left, bf16[384,2432]{1,0:T(8,128)(2,1)} %attend_back.1.grads.right, f32[8,2048]{1,0:T(8,128)} %get-tuple-element.239.refs_0_, ...), custom_call_target="tpu_custom_call" | custom-call | flops 153008209920 | bytes 536084480 | tf_op jit(solution)/shard_map/row_grads/pallas_call | solution.py:924
  483.1 12.3 %collective-permute-done.48.refs_3_ = bf16[2,64,2048]{2,1,0:T(8,128)(2,1)S(1)} collective-permute-done((bf16[2,64,2048]{2,1,0:T(8,128)(2,1)S(1)}, bf16[2,64,2048]{2,1,0:T(8,128)(2,1)S(1)}, u32[]{:S(2)}, u32[]{:S(2)}) %collective-permute-start.48) | collective-permute-done | bytes 524320 | tf_op jit(solution)/shard_map/ppermute | solution.py:248
  497.4 2.3 add.67
  499.7 4.9 add.68
  504.7 3.7 add.69
  509.4 3.7 add.70
  513.1 4.9 update_rows.3
  518.0 19.2 %collective-permute-done.52.refs_2_ = bf16[4,64,2432]{2,1,0:T(8,128)(2,1)S(1)} collective-permute-done((bf16[4,64,2432]{2,1,0:T(8,128)(2,1)}, bf16[4,64,2432]{2,1,0:T(8,128)(2,1)S(1)}, u32[]{:S(2)}, u32[]{:S(2)}) %collective-permute-start.52) | collective-permute-done | bytes 1245216 | tf_op jit(solution)/shard_map/ppermute | solution.py:248
  538.6 3.0 add.71
  545.9 24.1 %collective-permute-done.59.refs_4_ = bf16[2,64,2048]{2,1,0:T(8,128)(2,1)S(1)} collective-permute-done((bf16[2,64,2048]{2,1,0:T(8,128)(2,1)}, bf16[2,64,2048]{2,1,0:T(8,128)(2,1)S(1)}, u32[]{:S(2)}, u32[]{:S(2)}) %collective-permute-start.59) | collective-permute-done | bytes 524320 | tf_op jit(solution)/shard_map/ppermute | solution.py:253
  570.8 2.2 add.72
  573.8 2.5 add.73
  576.3 1.9 fusion.8
  582.4 2.1 collective-permute-start.65
  585.7 2.3 collective-permute-done.55.refs_2_
  588.1 6.7 %layer_out.1 = f32[384,2048]{1,0:T(8,128)} custom-call(f32[384,2048]{1,0:T(8,128)} %get-tuple-element.212.resid, bf16[8,192,2048]{2,1,0:T(8,128)(2,1)} %bitcast.52, bf16[2,192,2048]{2,1,0:T(8,128)(2,1)} %collective-permute-done.40.refs_1_, bf16[1,192,2048]{2,1,0:T(8,128)(2,1)} %copy-done.15, bf16[8,192,2048]{2,1,0:T(8,128)(2,1)} %bitcast.53, ...), custom_call_target="tpu_custom_call" | custom-call | bytes 440401920 | tf_op jit(solution)/shard_map/layer_out/pallas_call | solution.py:883
  594.8 4.9 update_units.2
  600.6 2.3 add.74
  602.9 2.2 collective-permute-start.61
  611.8 2.5 collective-permute-done.63.refs_2_
  615.1 5.0 update_units.3
  620.1 3.3 update_rows.4
  624.1 3.5 update_rows.5
  (251 shorter events, 88.0 us)
Async XLA Ops:
  7.2 247.9 %all-gather.3.cloned.1.call-start = ((), (), s32[]{:S(2)}) async-start(), calls=%async_computation.6 | async-start | bytes 19869696 | tf_op jit(solution)/shard_map/all_gather | solution.py:1330
  11.7 22.6 %collective-permute-start.6 = (bf16[2,64,1408]{2,1,0:T(8,128)(2,1)}, bf16[2,64,1408]{2,1,0:T(8,128)(2,1)S(1)}, u32[]{:S(2)}, u32[]{:S(2)}) collective-permute-start(bf16[2,64,1408]{2,1,0:T(8,128)(2,1)} %get-tuple-element.172), channel_id=1, source_target_pairs={{0,8},{8,0},{16,24},{24,16},{1,9},{9,1},{17,25},{25,17},{2,10},{10... | collective-permute-start | bytes 1081352 | tf_op jit(solution)/shard_map/ppermute | solution.py:248
  16.9 16.8 %collective-permute-start = (bf16[64,2432]{1,0:T(8,128)(2,1)}, bf16[64,2432]{1,0:T(8,128)(2,1)}, u32[]{:S(2)}, u32[]{:S(2)}) collective-permute-start(bf16[64,2432]{1,0:T(8,128)(2,1)} %get-tuple-element.410), channel_id=1, source_target_pairs={{0,4},{1,5},{2,6},{3,7},{4,0},{5,1},{6,2},{7,3},{8,12},{9,13},{10,... | collective-permute-start | bytes 933896 | tf_op jit(solution)/shard_map/ppermute | solution.py:253
  19.5 19.1 %collective-permute-start.1 = (bf16[64,2432]{1,0:T(8,128)(2,1)}, bf16[64,2432]{1,0:T(8,128)(2,1)}, u32[]{:S(2)}, u32[]{:S(2)}) collective-permute-start(bf16[64,2432]{1,0:T(8,128)(2,1)} %get-tuple-element.410), channel_id=1, source_target_pairs={{0,2},{1,3},{2,0},{3,1},{4,6},{5,7},{6,4},{7,5},{8,10},{9,11},{10,... | collective-permute-start | bytes 933896 | tf_op jit(solution)/shard_map/ppermute | solution.py:253
  21.1 17.2 %collective-permute-start.7 = (bf16[2,64,1408]{2,1,0:T(8,128)(2,1)}, bf16[2,64,1408]{2,1,0:T(8,128)(2,1)S(1)}, u32[]{:S(2)}, u32[]{:S(2)}) collective-permute-start(bf16[2,64,1408]{2,1,0:T(8,128)(2,1)} %get-tuple-element.173), channel_id=1, source_target_pairs={{0,16},{8,24},{16,0},{24,8},{1,17},{9,25},{17,1},{25,9},{2,18},{10... | collective-permute-start | bytes 1081352 | tf_op jit(solution)/shard_map/ppermute | solution.py:248
  22.6 15.8 %collective-permute-start.8 = (bf16[2,64,1408]{2,1,0:T(8,128)(2,1)}, bf16[2,64,1408]{2,1,0:T(8,128)(2,1)S(1)}, u32[]{:S(2)}, u32[]{:S(2)}) collective-permute-start(bf16[2,64,1408]{2,1,0:T(8,128)(2,1)} %get-tuple-element.174), channel_id=1, source_target_pairs={{0,24},{8,16},{16,8},{24,0},{1,25},{9,17},{17,9},{25,1},{2,26},{10... | collective-permute-start | bytes 1081352 | tf_op jit(solution)/shard_map/ppermute | solution.py:248
  33.7 8.4 %collective-permute-start.2 = (bf16[64,2432]{1,0:T(8,128)(2,1)}, bf16[64,2432]{1,0:T(8,128)(2,1)S(1)}, u32[]{:S(2)}, u32[]{:S(2)}) collective-permute-start(bf16[64,2432]{1,0:T(8,128)(2,1)} %collective-permute-done), channel_id=1, source_target_pairs={{0,2},{1,3},{2,0},{3,1},{4,6},{5,7},{6,4},{7,5},{8,10},{9,11},{10,... | collective-permute-start | bytes 933896 | tf_op jit(solution)/shard_map/ppermute | solution.py:253
  43.3 27.8 %collective-permute-start.9 = (bf16[4,64,2432]{2,1,0:T(8,128)(2,1)S(1)}, bf16[4,64,2432]{2,1,0:T(8,128)(2,1)S(1)}, u32[]{:S(2)}, u32[]{:S(2)}) collective-permute-start(bf16[4,64,2432]{2,1,0:T(8,128)(2,1)S(1)} %pad_maximum_fusion.refs_0_), channel_id=1, source_target_pairs={{0,8},{8,0},{16,24},{24,16},{1,9},{9,1},{17,25},{25,17},{2,10},{10... | collective-permute-start | bytes 3735560 | tf_op jit(solution)/shard_map/ppermute | solution.py:248
  43.9 28.3 %collective-permute-start.10 = (bf16[4,64,2432]{2,1,0:T(8,128)(2,1)S(1)}, bf16[4,64,2432]{2,1,0:T(8,128)(2,1)}, u32[]{:S(2)}, u32[]{:S(2)}) collective-permute-start(bf16[4,64,2432]{2,1,0:T(8,128)(2,1)S(1)} %pad_maximum_fusion.refs_0_), channel_id=1, source_target_pairs={{0,16},{8,24},{16,0},{24,8},{1,17},{9,25},{17,1},{25,9},{2,18},{10... | collective-permute-start | bytes 3735560 | tf_op jit(solution)/shard_map/ppermute | solution.py:248
  45.5 14.4 %collective-permute-start.3 = (bf16[64,2048]{1,0:T(8,128)(2,1)S(1)}, bf16[64,2048]{1,0:T(8,128)(2,1)S(1)}, u32[]{:S(2)}, u32[]{:S(2)}) collective-permute-start(bf16[64,2048]{1,0:T(8,128)(2,1)S(1)} %convert_element_type.22), channel_id=1, source_target_pairs={{0,4},{1,5},{2,6},{3,7},{4,0},{5,1},{6,2},{7,3},{8,12},{9,13},{10,... | collective-permute-start | bytes 786440 | tf_op jit(solution)/shard_map/ppermute | solution.py:253
  59.9 9.3 %collective-permute-start.5 = (bf16[64,2048]{1,0:T(8,128)(2,1)S(1)}, bf16[64,2048]{1,0:T(8,128)(2,1)S(1)}, u32[]{:S(2)}, u32[]{:S(2)}) collective-permute-start(bf16[64,2048]{1,0:T(8,128)(2,1)S(1)} %collective-permute-done.3), channel_id=1, source_target_pairs={{0,2},{1,3},{2,0},{3,1},{4,6},{5,7},{6,4},{7,5},{8,10},{9,11},{10,... | collective-permute-start | bytes 786440 | tf_op jit(solution)/shard_map/ppermute | solution.py:253
  60.6 18.2 %collective-permute-start.4 = (bf16[64,2048]{1,0:T(8,128)(2,1)S(1)}, bf16[64,2048]{1,0:T(8,128)(2,1)S(1)}, u32[]{:S(2)}, u32[]{:S(2)}) collective-permute-start(bf16[64,2048]{1,0:T(8,128)(2,1)S(1)} %convert_element_type.22), channel_id=1, source_target_pairs={{0,2},{1,3},{2,0},{3,1},{4,6},{5,7},{6,4},{7,5},{8,10},{9,11},{10,... | collective-permute-start | bytes 786440 | tf_op jit(solution)/shard_map/ppermute | solution.py:253
  74.1 13.9 %collective-permute-start.11 = (bf16[2,64,2432]{2,1,0:T(8,128)(2,1)}, bf16[2,64,2432]{2,1,0:T(8,128)(2,1)}, u32[]{:S(2)}, u32[]{:S(2)}) collective-permute-start(bf16[2,64,2432]{2,1,0:T(8,128)(2,1)} %cut.8), channel_id=1, source_target_pairs={{0,16},{8,24},{16,0},{24,8},{1,17},{9,25},{17,1},{25,9},{2,18},{10... | collective-permute-start | bytes 1867784 | tf_op jit(solution)/shard_map/ppermute | solution.py:248
  77.4 13.6 %collective-permute-start.12 = (bf16[2,64,2432]{2,1,0:T(8,128)(2,1)}, bf16[2,64,2432]{2,1,0:T(8,128)(2,1)}, u32[]{:S(2)}, u32[]{:S(2)}) collective-permute-start(bf16[2,64,2432]{2,1,0:T(8,128)(2,1)} %cut.9), channel_id=1, source_target_pairs={{0,8},{8,0},{16,24},{24,16},{1,9},{9,1},{17,25},{25,17},{2,10},{10... | collective-permute-start | bytes 1867784 | tf_op jit(solution)/shard_map/ppermute | solution.py:248
  78.3 18.2 %collective-permute-start.13 = (bf16[4,64,2432]{2,1,0:T(8,128)(2,1)S(1)}, bf16[4,64,2432]{2,1,0:T(8,128)(2,1)}, u32[]{:S(2)}, u32[]{:S(2)}) collective-permute-start(bf16[4,64,2432]{2,1,0:T(8,128)(2,1)S(1)} %copy-done.12), channel_id=1, source_target_pairs={{0,1},{1,0},{2,3},{3,2},{4,5},{5,4},{6,7},{7,6},{8,9},{9,8},{10,11... | collective-permute-start | bytes 3735560 | tf_op jit(solution)/shard_map/ppermute | solution.py:258
  78.3 19.7 %collective-permute-start.14 = (bf16[4,64,2432]{2,1,0:T(8,128)(2,1)S(1)}, bf16[4,64,2432]{2,1,0:T(8,128)(2,1)}, u32[]{:S(2)}, u32[]{:S(2)}) collective-permute-start(bf16[4,64,2432]{2,1,0:T(8,128)(2,1)S(1)} %copy-done.14), channel_id=1, source_target_pairs={{0,1},{1,0},{2,3},{3,2},{4,5},{5,4},{6,7},{7,6},{8,9},{9,8},{10,11... | collective-permute-start | bytes 3735560 | tf_op jit(solution)/shard_map/ppermute | solution.py:258
  79.5 20.0 %collective-permute-start.15 = (bf16[4,64,2432]{2,1,0:T(8,128)(2,1)}, bf16[4,64,2432]{2,1,0:T(8,128)(2,1)}, u32[]{:S(2)}, u32[]{:S(2)}) collective-permute-start(bf16[4,64,2432]{2,1,0:T(8,128)(2,1)} %collective-permute-done.10.whole.refs_2_), channel_id=1, source_target_pairs={{0,1},{1,0},{2,3},{3,2},{4,5},{5,4},{6,7},{7,6},{8,9},{9,8},{10,11... | collective-permute-start | bytes 3735560 | tf_op jit(solution)/shard_map/ppermute | solution.py:258
  88.0 7.3 %collective-permute-start.16 = (bf16[2,64,2432]{2,1,0:T(8,128)(2,1)}, bf16[2,64,2432]{2,1,0:T(8,128)(2,1)}, u32[]{:S(2)}, u32[]{:S(2)}) collective-permute-start(bf16[2,64,2432]{2,1,0:T(8,128)(2,1)} %collective-permute-done.11.refs_3_), channel_id=1, source_target_pairs={{0,1},{1,0},{2,3},{3,2},{4,5},{5,4},{6,7},{7,6},{8,9},{9,8},{10,11... | collective-permute-start | bytes 1867784 | tf_op jit(solution)/shard_map/ppermute | solution.py:258
  94.8 375.7 %reduce-scatter.4.cloned.1.call-start = ((), (), s32[]{:S(2)}) async-start(), calls=%async_computation.3 | async-start | bytes 3604480 | tf_op jit(solution)/shard_map/reduce_scatter | solution.py:988
  95.3 30.0 %collective-permute-start.20 = (bf16[4,64,2048]{2,1,0:T(8,128)(2,1)}, bf16[4,64,2048]{2,1,0:T(8,128)(2,1)}, u32[]{:S(2)}, u32[]{:S(2)}) collective-permute-start(bf16[4,64,2048]{2,1,0:T(8,128)(2,1)} %pad_maximum_fusion.1.refs_0_), channel_id=1, source_target_pairs={{0,8},{8,0},{16,24},{24,16},{1,9},{9,1},{17,25},{25,17},{2,10},{10... | collective-permute-start | bytes 3145736 | tf_op jit(solution)/shard_map/ppermute | solution.py:248
  95.9 29.4 %collective-permute-start.21 = (bf16[4,64,2048]{2,1,0:T(8,128)(2,1)}, bf16[4,64,2048]{2,1,0:T(8,128)(2,1)}, u32[]{:S(2)}, u32[]{:S(2)}) collective-permute-start(bf16[4,64,2048]{2,1,0:T(8,128)(2,1)} %pad_maximum_fusion.1.refs_0_), channel_id=1, source_target_pairs={{0,16},{8,24},{16,0},{24,8},{1,17},{9,25},{17,1},{25,9},{2,18},{10... | collective-permute-start | bytes 3145736 | tf_op jit(solution)/shard_map/ppermute | solution.py:248
  96.5 70.5 %collective-permute-start.18 = (bf16[384,2048]{1,0:T(8,128)(2,1)}, bf16[384,2048]{1,0:T(8,128)(2,1)}, u32[]{:S(2)}, u32[]{:S(2)}) collective-permute-start(bf16[384,2048]{1,0:T(8,128)(2,1)} %cot.1), channel_id=1, source_target_pairs={{0,8},{8,0},{16,24},{24,16},{1,9},{9,1},{17,25},{25,17},{2,10},{10... | collective-permute-start | bytes 4718600 | tf_op jit(solution)/shard_map/ppermute | solution.py:248
  97.9 69.1 %collective-permute-start.19 = (bf16[384,2048]{1,0:T(8,128)(2,1)}, bf16[384,2048]{1,0:T(8,128)(2,1)}, u32[]{:S(2)}, u32[]{:S(2)}) collective-permute-start(bf16[384,2048]{1,0:T(8,128)(2,1)} %cot.1), channel_id=1, source_target_pairs={{0,16},{8,24},{16,0},{24,8},{1,17},{9,25},{17,1},{25,9},{2,18},{10... | collective-permute-start | bytes 4718600 | tf_op jit(solution)/shard_map/ppermute | solution.py:248
  127.1 39.4 %collective-permute-start.22 = (bf16[2,64,2048]{2,1,0:T(8,128)(2,1)}, bf16[2,64,2048]{2,1,0:T(8,128)(2,1)}, u32[]{:S(2)}, u32[]{:S(2)}) collective-permute-start(bf16[2,64,2048]{2,1,0:T(8,128)(2,1)} %cut.12), channel_id=1, source_target_pairs={{0,16},{8,24},{16,0},{24,8},{1,17},{9,25},{17,1},{25,9},{2,18},{10... | collective-permute-start | bytes 1572872 | tf_op jit(solution)/shard_map/ppermute | solution.py:248
  129.3 37.2 %collective-permute-start.23 = (bf16[2,64,2048]{2,1,0:T(8,128)(2,1)}, bf16[2,64,2048]{2,1,0:T(8,128)(2,1)}, u32[]{:S(2)}, u32[]{:S(2)}) collective-permute-start(bf16[2,64,2048]{2,1,0:T(8,128)(2,1)} %cut.13), channel_id=1, source_target_pairs={{0,8},{8,0},{16,24},{24,16},{1,9},{9,1},{17,25},{25,17},{2,10},{10... | collective-permute-start | bytes 1572872 | tf_op jit(solution)/shard_map/ppermute | solution.py:248
  130.0 41.4 %collective-permute-start.24 = (bf16[4,64,2048]{2,1,0:T(8,128)(2,1)}, bf16[4,64,2048]{2,1,0:T(8,128)(2,1)S(1)}, u32[]{:S(2)}, u32[]{:S(2)}) collective-permute-start(bf16[4,64,2048]{2,1,0:T(8,128)(2,1)} %pad_maximum_fusion.1.refs_0_), channel_id=1, source_target_pairs={{0,1},{1,0},{2,3},{3,2},{4,5},{5,4},{6,7},{7,6},{8,9},{9,8},{10,11... | collective-permute-start | bytes 3145736 | tf_op jit(solution)/shard_map/ppermute | solution.py:258
  166.5 7.0 %collective-permute-start.26 = (bf16[4,64,2048]{2,1,0:T(8,128)(2,1)}, bf16[4,64,2048]{2,1,0:T(8,128)(2,1)S(1)}, u32[]{:S(2)}, u32[]{:S(2)}) collective-permute-start(bf16[4,64,2048]{2,1,0:T(8,128)(2,1)} %collective-permute-done.21.whole.refs_2_), channel_id=1, source_target_pairs={{0,1},{1,0},{2,3},{3,2},{4,5},{5,4},{6,7},{7,6},{8,9},{9,8},{10,11... | collective-permute-start | bytes 3145736 | tf_op jit(solution)/shard_map/ppermute | solution.py:258
  171.4 19.7 %collective-permute-start.29 = (bf16[192,2048]{1,0:T(8,128)(2,1)S(1)}, bf16[192,2048]{1,0:T(8,128)(2,1)}, u32[]{:S(2)}, u32[]{:S(2)}) collective-permute-start(bf16[192,2048]{1,0:T(8,128)(2,1)S(1)} %copy-done.17), channel_id=1, source_target_pairs={{0,16},{8,24},{16,0},{24,8},{1,17},{9,25},{17,1},{25,9},{2,18},{10... | collective-permute-start | bytes 2359304 | tf_op jit(solution)/shard_map/ppermute | solution.py:248
  172.0 19.6 %collective-permute-start.30 = (bf16[192,2048]{1,0:T(8,128)(2,1)}, bf16[192,2048]{1,0:T(8,128)(2,1)}, u32[]{:S(2)}, u32[]{:S(2)}) collective-permute-start(bf16[192,2048]{1,0:T(8,128)(2,1)} %cut.11), channel_id=1, source_target_pairs={{0,8},{8,0},{16,24},{24,16},{1,9},{9,1},{17,25},{25,17},{2,10},{10... | collective-permute-start | bytes 2359304 | tf_op jit(solution)/shard_map/ppermute | solution.py:248
  191.6 35.4 %collective-permute-start.31 = (bf16[384,2048]{1,0:T(8,128)(2,1)}, bf16[384,2048]{1,0:T(8,128)(2,1)S(1)}, u32[]{:S(2)}, u32[]{:S(2)}) collective-permute-start(bf16[384,2048]{1,0:T(8,128)(2,1)} %get-tuple-element.189.refs_0_), channel_id=1, source_target_pairs={{0,8},{8,0},{16,24},{24,16},{1,9},{9,1},{17,25},{25,17},{2,10},{10... | collective-permute-start | bytes 4718600 | tf_op jit(solution)/shard_map/ppermute | solution.py:248
  193.0 38.5 %collective-permute-start.32 = (bf16[384,2048]{1,0:T(8,128)(2,1)}, bf16[384,2048]{1,0:T(8,128)(2,1)S(1)}, u32[]{:S(2)}, u32[]{:S(2)}) collective-permute-start(bf16[384,2048]{1,0:T(8,128)(2,1)} %get-tuple-element.189.refs_0_), channel_id=1, source_target_pairs={{0,16},{8,24},{16,0},{24,8},{1,17},{9,25},{17,1},{25,9},{2,18},{10... | collective-permute-start | bytes 4718600 | tf_op jit(solution)/shard_map/ppermute | solution.py:248
  230.0 17.8 %collective-permute-start.33 = (bf16[192,2048]{1,0:T(8,128)(2,1)}, bf16[192,2048]{1,0:T(8,128)(2,1)S(1)}, u32[]{:S(2)}, u32[]{:S(2)}) collective-permute-start(bf16[192,2048]{1,0:T(8,128)(2,1)} %cut.14), channel_id=1, source_target_pairs={{0,16},{8,24},{16,0},{24,8},{1,17},{9,25},{17,1},{25,9},{2,18},{10... | collective-permute-start | bytes 2359304 | tf_op jit(solution)/shard_map/ppermute | solution.py:248
  234.6 17.5 %collective-permute-start.34 = (bf16[192,2048]{1,0:T(8,128)(2,1)}, bf16[192,2048]{1,0:T(8,128)(2,1)S(1)}, u32[]{:S(2)}, u32[]{:S(2)}) collective-permute-start(bf16[192,2048]{1,0:T(8,128)(2,1)} %cut.15), channel_id=1, source_target_pairs={{0,8},{8,0},{16,24},{24,16},{1,9},{9,1},{17,25},{25,17},{2,10},{10... | collective-permute-start | bytes 2359304 | tf_op jit(solution)/shard_map/ppermute | solution.py:248
  330.7 39.0 %collective-permute-start.35 = (bf16[2,192,2048]{2,1,0:T(8,128)(2,1)}, bf16[2,192,2048]{2,1,0:T(8,128)(2,1)}, u32[]{:S(2)}, u32[]{:S(2)}) collective-permute-start(bf16[2,192,2048]{2,1,0:T(8,128)(2,1)} %get-tuple-element.194), channel_id=1, source_target_pairs={{0,8},{8,0},{16,24},{24,16},{1,9},{9,1},{17,25},{25,17},{2,10},{10... | collective-permute-start | bytes 4718600 | tf_op jit(solution)/shard_map/ppermute | solution.py:248
  332.1 37.5 %collective-permute-start.36 = (bf16[2,192,2048]{2,1,0:T(8,128)(2,1)}, bf16[2,192,2048]{2,1,0:T(8,128)(2,1)}, u32[]{:S(2)}, u32[]{:S(2)}) collective-permute-start(bf16[2,192,2048]{2,1,0:T(8,128)(2,1)} %get-tuple-element.195), channel_id=1, source_target_pairs={{0,16},{8,24},{16,0},{24,8},{1,17},{9,25},{17,1},{25,9},{2,18},{10... | collective-permute-start | bytes 4718600 | tf_op jit(solution)/shard_map/ppermute | solution.py:248
  348.7 16.0 %collective-permute-start.37 = (bf16[4,176,2048]{2,1,0:T(8,128)(2,1)}, bf16[4,176,2048]{2,1,0:T(8,128)(2,1)}, u32[]{:S(2)}, u32[]{:S(2)}) collective-permute-start(bf16[4,176,2048]{2,1,0:T(8,128)(2,1)} %get-tuple-element.200), channel_id=1, source_target_pairs={{0,1},{1,0},{2,3},{3,2},{4,5},{5,4},{6,7},{7,6},{8,9},{9,8},{10,11... | collective-permute-start | bytes 8650760 | tf_op jit(solution)/shard_map/ppermute | solution.py:258
  364.2 60.4 %collective-permute-start.42 = (bf16[4,4,64,1408]{3,2,1,0:T(8,128)(2,1)}, bf16[4,4,64,1408]{3,2,1,0:T(8,128)(2,1)}, u32[]{:S(2)}, u32[]{:S(2)}) collective-permute-start(bf16[4,4,64,1408]{3,2,1,0:T(8,128)(2,1)} %get-tuple-element.219), channel_id=1, source_target_pairs={{0,1},{1,0},{2,3},{3,2},{4,5},{5,4},{6,7},{7,6},{8,9},{9,8},{10,11... | collective-permute-start | bytes 8650760 | tf_op jit(solution)/shard_map/ppermute | solution.py:258
  372.8 19.8 %collective-permute-start.38 = (bf16[1,192,2048]{2,1,0:T(8,128)(2,1)}, bf16[1,192,2048]{2,1,0:T(8,128)(2,1)}, u32[]{:S(2)}, u32[]{:S(2)}) collective-permute-start(bf16[1,192,2048]{2,1,0:T(8,128)(2,1)} %get-tuple-element.207), channel_id=1, source_target_pairs={{0,16},{8,24},{16,0},{24,8},{1,17},{9,25},{17,1},{25,9},{2,18},{10... | collective-permute-start | bytes 2359304 | tf_op jit(solution)/shard_map/ppermute | solution.py:248
  373.4 19.5 %collective-permute-start.39 = (bf16[1,192,2048]{2,1,0:T(8,128)(2,1)}, bf16[1,192,2048]{2,1,0:T(8,128)(2,1)}, u32[]{:S(2)}, u32[]{:S(2)}) collective-permute-start(bf16[1,192,2048]{2,1,0:T(8,128)(2,1)} %get-tuple-element.208), channel_id=1, source_target_pairs={{0,8},{8,0},{16,24},{24,16},{1,9},{9,1},{17,25},{25,17},{2,10},{10... | collective-permute-start | bytes 2359304 | tf_op jit(solution)/shard_map/ppermute | solution.py:248
  373.9 130.7 %reduce-scatter.6.cloned.1.call-start = ((), (), s32[]{:S(2)}) async-start(), calls=%async_computation.4 | async-start | bytes 3604480 | tf_op jit(solution)/shard_map/reduce_scatter | solution.py:988
  389.6 110.2 %collective-permute-start.47 = (bf16[4,4,64,1408]{3,2,1,0:T(8,128)(2,1)}, bf16[4,4,64,1408]{3,2,1,0:T(8,128)(2,1)}, u32[]{:S(2)}, u32[]{:S(2)}) collective-permute-start(bf16[4,4,64,1408]{3,2,1,0:T(8,128)(2,1)} %get-tuple-element.243), channel_id=1, source_target_pairs={{0,1},{1,0},{2,3},{3,2},{4,5},{5,4},{6,7},{7,6},{8,9},{9,8},{10,11... | collective-permute-start | bytes 8650760 | tf_op jit(solution)/shard_map/ppermute | solution.py:258
  404.7 62.9 %collective-permute-start.40 = (bf16[2,192,2048]{2,1,0:T(8,128)(2,1)}, bf16[2,192,2048]{2,1,0:T(8,128)(2,1)}, u32[]{:S(2)}, u32[]{:S(2)}) collective-permute-start(bf16[2,192,2048]{2,1,0:T(8,128)(2,1)} %get-tuple-element.215), channel_id=1, source_target_pairs={{0,8},{8,0},{16,24},{24,16},{1,9},{9,1},{17,25},{25,17},{2,10},{10... | collective-permute-start | bytes 4718600 | tf_op jit(solution)/shard_map/ppermute | solution.py:248
  405.3 62.3 %collective-permute-start.41 = (bf16[2,192,2048]{2,1,0:T(8,128)(2,1)}, bf16[2,192,2048]{2,1,0:T(8,128)(2,1)}, u32[]{:S(2)}, u32[]{:S(2)}) collective-permute-start(bf16[2,192,2048]{2,1,0:T(8,128)(2,1)} %get-tuple-element.216), channel_id=1, source_target_pairs={{0,16},{8,24},{16,0},{24,8},{1,17},{9,25},{17,1},{25,9},{2,18},{10... | collective-permute-start | bytes 4718600 | tf_op jit(solution)/shard_map/ppermute | solution.py:248
  416.2 8.5 %collective-permute-start.43 = (bf16[2,4,2,64,2048]{4,3,2,1,0:T(8,128)(2,1)}, bf16[2,4,2,64,2048]{4,3,2,1,0:T(8,128)(2,1)}, u32[]{:S(2)}, u32[]{:S(2)}) collective-permute-start(bf16[2,4,2,64,2048]{4,3,2,1,0:T(8,128)(2,1)} %get-tuple-element.220), channel_id=1, source_target_pairs={{0,1},{1,0},{2,3},{3,2},{4,5},{5,4},{6,7},{7,6},{8,9},{9,8},{10,11... | collective-permute-start | bytes 12582920 | tf_op jit(solution)/shard_map/ppermute | solution.py:258
  427.9 39.7 %collective-permute-start.44 = (bf16[4,64,2048]{2,1,0:T(8,128)(2,1)}, bf16[4,64,2048]{2,1,0:T(8,128)(2,1)}, u32[]{:S(2)}, u32[]{:S(2)}) collective-permute-start(bf16[4,64,2048]{2,1,0:T(8,128)(2,1)} %get-tuple-element.223), channel_id=1, source_target_pairs={{0,8},{8,0},{16,24},{24,16},{1,9},{9,1},{17,25},{25,17},{2,10},{10... | collective-permute-start | bytes 3145736 | tf_op jit(solution)/shard_map/ppermute | solution.py:248
  429.3 38.3 %collective-permute-start.45 = (bf16[4,64,2048]{2,1,0:T(8,128)(2,1)}, bf16[4,64,2048]{2,1,0:T(8,128)(2,1)}, u32[]{:S(2)}, u32[]{:S(2)}) collective-permute-start(bf16[4,64,2048]{2,1,0:T(8,128)(2,1)} %get-tuple-element.224), channel_id=1, source_target_pairs={{0,16},{8,24},{16,0},{24,8},{1,17},{9,25},{17,1},{25,9},{2,18},{10... | collective-permute-start | bytes 3145736 | tf_op jit(solution)/shard_map/ppermute | solution.py:248
  434.8 153.2 %reduce-scatter.8.cloned.1.call-start = ((), (), s32[]{:S(2)}) async-start(), calls=%async_computation.5 | async-start | bytes 3604480 | tf_op jit(solution)/shard_map/reduce_scatter | solution.py:988
  481.1 23.6 %collective-permute-start.46 = (bf16[2,4,2,64,2432]{4,3,2,1,0:T(8,128)(2,1)}, bf16[2,4,2,64,2432]{4,3,2,1,0:T(8,128)(2,1)}, u32[]{:S(2)}, u32[]{:S(2)}) collective-permute-start(bf16[2,4,2,64,2432]{4,3,2,1,0:T(8,128)(2,1)} %get-tuple-element.242), channel_id=1, source_target_pairs={{0,1},{1,0},{2,3},{3,2},{4,5},{5,4},{6,7},{7,6},{8,9},{9,8},{10,11... | collective-permute-start | bytes 14942216 | tf_op jit(solution)/shard_map/ppermute | solution.py:258
  481.1 14.3 %collective-permute-start.48 = (bf16[2,64,2048]{2,1,0:T(8,128)(2,1)S(1)}, bf16[2,64,2048]{2,1,0:T(8,128)(2,1)S(1)}, u32[]{:S(2)}, u32[]{:S(2)}) collective-permute-start(bf16[2,64,2048]{2,1,0:T(8,128)(2,1)S(1)} %copy-done.46), channel_id=1, source_target_pairs={{0,16},{8,24},{16,0},{24,8},{1,17},{9,25},{17,1},{25,9},{2,18},{10... | collective-permute-start | bytes 1572872 | tf_op jit(solution)/shard_map/ppermute | solution.py:248
  482.6 14.0 %collective-permute-start.49 = (bf16[2,64,2048]{2,1,0:T(8,128)(2,1)S(1)}, bf16[2,64,2048]{2,1,0:T(8,128)(2,1)S(1)}, u32[]{:S(2)}, u32[]{:S(2)}) collective-permute-start(bf16[2,64,2048]{2,1,0:T(8,128)(2,1)S(1)} %copy-done.45), channel_id=1, source_target_pairs={{0,8},{8,0},{16,24},{24,16},{1,9},{9,1},{17,25},{25,17},{2,10},{10... | collective-permute-start | bytes 1572872 | tf_op jit(solution)/shard_map/ppermute | solution.py:248
  508.4 28.8 %collective-permute-start.52 = (bf16[4,64,2432]{2,1,0:T(8,128)(2,1)}, bf16[4,64,2432]{2,1,0:T(8,128)(2,1)S(1)}, u32[]{:S(2)}, u32[]{:S(2)}) collective-permute-start(bf16[4,64,2432]{2,1,0:T(8,128)(2,1)} %get-tuple-element.248), channel_id=1, source_target_pairs={{0,8},{8,0},{16,24},{24,16},{1,9},{9,1},{17,25},{25,17},{2,10},{10... | collective-permute-start | bytes 3735560 | tf_op jit(solution)/shard_map/ppermute | solution.py:248
  508.9 28.5 %collective-permute-start.53 = (bf16[4,64,2432]{2,1,0:T(8,128)(2,1)}, bf16[4,64,2432]{2,1,0:T(8,128)(2,1)S(1)}, u32[]{:S(2)}, u32[]{:S(2)}) collective-permute-start(bf16[4,64,2432]{2,1,0:T(8,128)(2,1)} %get-tuple-element.249), channel_id=1, source_target_pairs={{0,16},{8,24},{16,0},{24,8},{1,17},{9,25},{17,1},{25,9},{2,18},{10... | collective-permute-start | bytes 3735560 | tf_op jit(solution)/shard_map/ppermute | solution.py:248
  541.6 31.3 %collective-permute-start.57 = (bf16[2,64,2432]{2,1,0:T(8,128)(2,1)}, bf16[2,64,2432]{2,1,0:T(8,128)(2,1)S(1)}, u32[]{:S(2)}, u32[]{:S(2)}) collective-permute-start(bf16[2,64,2432]{2,1,0:T(8,128)(2,1)} %get-tuple-element.258), channel_id=1, source_target_pairs={{0,16},{8,24},{16,0},{24,8},{1,17},{9,25},{17,1},{25,9},{2,18},{10... | collective-permute-start | bytes 1867784 | tf_op jit(solution)/shard_map/ppermute | solution.py:248
  542.3 30.6 %collective-permute-start.58 = (bf16[2,64,2432]{2,1,0:T(8,128)(2,1)}, bf16[2,64,2432]{2,1,0:T(8,128)(2,1)S(1)}, u32[]{:S(2)}, u32[]{:S(2)}) collective-permute-start(bf16[2,64,2432]{2,1,0:T(8,128)(2,1)} %get-tuple-element.259), channel_id=1, source_target_pairs={{0,8},{8,0},{16,24},{24,16},{1,9},{9,1},{17,25},{25,17},{2,10},{10... | collective-permute-start | bytes 1867784 | tf_op jit(solution)/shard_map/ppermute | solution.py:248
  543.6 26.3 %collective-permute-start.59 = (bf16[2,64,2048]{2,1,0:T(8,128)(2,1)}, bf16[2,64,2048]{2,1,0:T(8,128)(2,1)S(1)}, u32[]{:S(2)}, u32[]{:S(2)}) collective-permute-start(bf16[2,64,2048]{2,1,0:T(8,128)(2,1)} %add.67), channel_id=1, source_target_pairs={{0,2},{1,3},{2,0},{3,1},{4,6},{5,7},{6,4},{7,5},{8,10},{9,11},{10,... | collective-permute-start | bytes 1572872 | tf_op jit(solution)/shard_map/ppermute | solution.py:253
  544.5 35.8 %collective-permute-start.50 = (bf16[1,192,2048]{2,1,0:T(8,128)(2,1)}, bf16[1,192,2048]{2,1,0:T(8,128)(2,1)S(1)}, u32[]{:S(2)}, u32[]{:S(2)}) collective-permute-start(bf16[1,192,2048]{2,1,0:T(8,128)(2,1)} %get-tuple-element.252), channel_id=1, source_target_pairs={{0,16},{8,24},{16,0},{24,8},{1,17},{9,25},{17,1},{25,9},{2,18},{10... | collective-permute-start | bytes 2359304 | tf_op jit(solution)/shard_map/ppermute | solution.py:248
  545.1 37.3 %collective-permute-start.51 = (bf16[1,192,2048]{2,1,0:T(8,128)(2,1)}, bf16[1,192,2048]{2,1,0:T(8,128)(2,1)S(1)}, u32[]{:S(2)}, u32[]{:S(2)}) collective-permute-start(bf16[1,192,2048]{2,1,0:T(8,128)(2,1)} %get-tuple-element.253), channel_id=1, source_target_pairs={{0,8},{8,0},{16,24},{24,16},{1,9},{9,1},{17,25},{25,17},{2,10},{10... | collective-permute-start | bytes 2359304 | tf_op jit(solution)/shard_map/ppermute | solution.py:248
  576.3 23.4 %collective-permute-start.60 = (bf16[2,64,2432]{2,1,0:T(8,128)(2,1)}, bf16[2,64,2432]{2,1,0:T(8,128)(2,1)S(1)}, u32[]{:S(2)}, u32[]{:S(2)}) collective-permute-start(bf16[2,64,2432]{2,1,0:T(8,128)(2,1)} %add.73), channel_id=1, source_target_pairs={{0,2},{1,3},{2,0},{3,1},{4,6},{5,7},{6,4},{7,5},{8,10},{9,11},{10,... | collective-permute-start | bytes 1867784 | tf_op jit(solution)/shard_map/ppermute | solution.py:253
  578.2 7.5 %collective-permute-start.54 = (bf16[1,64,1408]{2,1,0:T(8,128)(2,1)S(1)}, bf16[1,64,1408]{2,1,0:T(8,128)(2,1)S(1)}, u32[]{:S(2)}, u32[]{:S(2)}) collective-permute-start(bf16[1,64,1408]{2,1,0:T(8,128)(2,1)S(1)} %get-tuple-element.407), channel_id=1, source_target_pairs={{0,8},{8,0},{16,24},{24,16},{1,9},{9,1},{17,25},{25,17},{2,10},{10... | collective-permute-start | bytes 540680 | tf_op jit(solution)/shard_map/ppermute | solution.py:248
  579.6 8.5 %collective-permute-start.55 = (bf16[1,64,1408]{2,1,0:T(8,128)(2,1)S(1)}, bf16[1,64,1408]{2,1,0:T(8,128)(2,1)}, u32[]{:S(2)}, u32[]{:S(2)}) collective-permute-start(bf16[1,64,1408]{2,1,0:T(8,128)(2,1)S(1)} %get-tuple-element.406), channel_id=1, source_target_pairs={{0,16},{8,24},{16,0},{24,8},{1,17},{9,25},{17,1},{25,9},{2,18},{10... | collective-permute-start | bytes 540680 | tf_op jit(solution)/shard_map/ppermute | solution.py:248
  580.3 7.7 %collective-permute-start.56 = (bf16[1,64,1408]{2,1,0:T(8,128)(2,1)S(1)}, bf16[1,64,1408]{2,1,0:T(8,128)(2,1)}, u32[]{:S(2)}, u32[]{:S(2)}) collective-permute-start(bf16[1,64,1408]{2,1,0:T(8,128)(2,1)S(1)} %get-tuple-element.405), channel_id=1, source_target_pairs={{0,24},{8,16},{16,8},{24,0},{1,25},{9,17},{17,9},{25,1},{2,26},{10... | collective-permute-start | bytes 540680 | tf_op jit(solution)/shard_map/ppermute | solution.py:248
  582.4 31.9 %collective-permute-start.65 = (bf16[1,64,2048]{2,1,0:T(8,128)(2,1)S(1)}, bf16[1,64,2048]{2,1,0:T(8,128)(2,1)S(1)}, u32[]{:S(2)}, u32[]{:S(2)}) collective-permute-start(bf16[1,64,2048]{2,1,0:T(8,128)(2,1)S(1)} %copy-done.28), channel_id=1, source_target_pairs={{0,4},{1,5},{2,6},{3,7},{4,0},{5,1},{6,2},{7,3},{8,12},{9,13},{10,... | collective-permute-start | bytes 786440 | tf_op jit(solution)/shard_map/ppermute | solution.py:253
  602.9 20.4 %collective-permute-start.61 = (bf16[1,64,2432]{2,1,0:T(8,128)(2,1)}, bf16[1,64,2432]{2,1,0:T(8,128)(2,1)S(1)}, u32[]{:S(2)}, u32[]{:S(2)}) collective-permute-start(bf16[1,64,2432]{2,1,0:T(8,128)(2,1)} %add.74), channel_id=1, source_target_pairs={{0,4},{1,5},{2,6},{3,7},{4,0},{5,1},{6,2},{7,3},{8,12},{9,13},{10,... | collective-permute-start | bytes 933896 | tf_op jit(solution)/shard_map/ppermute | solution.py:253
  606.9 7.4 %collective-permute-start.63 = (bf16[1,64,1408]{2,1,0:T(8,128)(2,1)S(1)}, bf16[1,64,1408]{2,1,0:T(8,128)(2,1)S(1)}, u32[]{:S(2)}, u32[]{:S(2)}) collective-permute-start(bf16[1,64,1408]{2,1,0:T(8,128)(2,1)S(1)} %get-tuple-element.402), channel_id=1, source_target_pairs={{0,16},{8,24},{16,0},{24,8},{1,17},{9,25},{17,1},{25,9},{2,18},{10... | collective-permute-start | bytes 540680 | tf_op jit(solution)/shard_map/ppermute | solution.py:248
  (53 other events, 309.7 us)
Sparse Core Ops, SparseCore 0:
  94.9 160.1 all-gather.2
  374.1 56.6 reduce-scatter.3
  435.0 55.8 reduce-scatter.5
  504.8 66.4 reduce-scatter.7

commit v4 on v3

--- a/solution.py
+++ b/solution.py
@@ -611,7 +611,8 @@
 def ffn_all_kernel(spot, *refs):
     ins, held_in = (refs[:5], refs[5:10]), refs[10]
     wholes, (hidden, grad_gate, grad_up, sums, out) = refs[11:13], refs[13:18]
-    gate_w, up_w, down_w, tiles, grad_tile, out_tile, sems, in_sems, out_sems = refs[18:]
+    sent_a, sent_b = refs[18:20]
+    gate_w, up_w, down_w, tiles, grad_tile, out_tile, sems, in_sems, out_sems = refs[20:]
     count, f_size, rows, units = gate_w.shape
     step = pl.program_id(0)
     first = step == 0
@@ -712,6 +713,14 @@
         sums[i, 0] = grad_tile[i * half : (i + 1) * half]
         out[i, 0] = out_tile[i * half : (i + 1) * half]
 
+    @pl.when(step < 2)
+    def _():
+        sent_a[0] = grad_tile[:half]
+
+    @pl.when((step > 0) & (step < 3))
+    def _():
+        sent_b[0] = grad_tile[half:]
+
     @pl.when(step == 3)
     def _():
         for copy in kept(3):
@@ -725,13 +734,16 @@
     rows = (above - low - SPLIT) // (2 * t_size)
     inner = pl.BlockSpec((count, units), lambda t: (t, 0))
     sums = pl.BlockSpec((2, 1, half, width), lambda t: (0, t, 0, 0))
+    sent = lambda low: pl.BlockSpec(
+        (1, half, width), lambda t: (jnp.clip(t - low, 0, 1), 0, 0)
+    )
     weights = pltpu.VMEM((t_size, f_size, rows, units), BF16)
     total = 4 * count
     return pl.pallas_call(
         ffn_all_kernel,
         grid=(4,),
         in_specs=[SMEM] + [ANY] * 11,
-        out_specs=[ANY, ANY, inner, inner, inner, sums, sums],
+        out_specs=[ANY, ANY, inner, inner, inner, sums, sums, sent(0), sent(1)],
         scratch_shapes=[
             weights,
             weights,
@@ -745,16 +757,17 @@
         ],
         out_shape=[jax.ShapeDtypeStruct((total, width), BF16)] * 2
         + [jax.ShapeDtypeStruct((total, units), BF16)] * 3
-        + [jax.ShapeDtypeStruct((2, 4, half, width), BF16)] * 2,
+        + [jax.ShapeDtypeStruct((2, 4, half, width), BF16)] * 2
+        + [jax.ShapeDtypeStruct((2, half, width), BF16)] * 2,
         name="ffn_all",
         **limits(12 * total * width * units, 6 * width * units + 8 * total * width),
     )(spot, *normed, *cot, held_in)
 
 
 class TokenSum:
-    def __init__(self, terms):
+    def __init__(self, terms, sent=None):
         self.own = terms
-        self.sent = add([[(terms, 0)], [(terms, 5)]], 2)
+        self.sent = sent or add([[(terms, 0)], [(terms, 5)]], 2)
         self.a, self.b = dp_swap(self.sent[0], 1), dp_swap(self.sent[1], 2)
 
     def cross(self):
@@ -1118,9 +1131,9 @@
             out[:, at] = result
 
 
-def update_units(spot, weight, moment, average, pieces, rate):
+def update_units(spot, weight, moment, average, pieces, which, rate):
     block = (1,) + pieces[0].shape[1:]
-    first = pl.BlockSpec(block, lambda g: (0, 0, 0))
+    first = pl.BlockSpec(block, lambda g: (which, 0, 0))
     whole = pl.BlockSpec(weight.shape, lambda g: (0, 0))
     return pl.pallas_call(
         functools.partial(update_units_kernel, rate),
@@ -1350,11 +1363,11 @@
 
     normed2_near = plane_near(after(normed2, *cot[3:]))
     normed2_all = [normed2, *normed2_near, *plane_far(*normed2_near)]
-    tokens2, cots, hidden, grad_gate, grad_up, grad_terms, out_terms = ffn_all(
+    tokens2, cots, hidden, grad_gate, grad_up, grad_terms, out_terms, *grads_sent = ffn_all(
         spot, normed2_all, cot, units_all, t_size, w_down.shape[0]
     )
-    normed2_sum = TokenSum(grad_terms)
-    down = LineSum(*down_grads(spot, [after(hidden, *normed2_sum.sent)], [cots]))
+    normed2_sum = TokenSum(grad_terms, grads_sent)
+    down = LineSum(*down_grads(spot, [hidden], [cots]))
     gate = LineSum(*unit_grads(spot, [after(tokens2, down.mine)], [grad_gate]))
     down.other = after(down.other, gate.mine)
     down.line()
@@ -1388,19 +1401,20 @@
             (grad_gain_attn, grad_gain_ffn),
         )
     )
-    output.last_a, output.last_b = after((output.last_a, output.last_b), qkv.mine)
+    up.other = after(up.other, qkv.mine)
+    up.line()
+    output.last_a, output.last_b = after((output.last_a, output.last_b), up.chip)
     output.near()
-    up.other = after(up.other, output.odd)
-    up.line()
-    gate.total = after(gate.total, up.chip)
+    gate.total = after(gate.total, output.odd)
     qkv.other = after(qkv.other, gate.total)
     qkv.plane()
 
     def rate(strength, fan):
         return strength / math.sqrt(fan * tokens_total)
 
-    def exchange(total):
-        pieces = [total[k : k + 1] for k in range(t_size)]
+    def exchange(*totals):
+        totals = [flat(total) for total in totals]
+        pieces = [jnp.stack([total[k] for total in totals]) for k in range(t_size)]
         return pieces[:1] + [dp_swap(pieces[k], k) for k in range(1, t_size)]
 
     down_out = update_rows(
@@ -1411,29 +1425,22 @@
     out_sum.cross()
     qkv.a, qkv.b = after((qkv.a, qkv.b), down_out[0], *out_sum.crossed)
     qkv.cross()
-    gate_pieces = exchange(flat(after(gate.total, *qkv.crossed)))
-    output.line = after(output.line, *qkv.crossed)
+    qkv.near()
+    pieces = exchange(after(gate.total, qkv.odd), after(up.total, qkv.odd))
+    output.line = after(output.line, qkv.odd)
     output.far()
-    qkv.last_a, qkv.last_b = after((qkv.last_a, qkv.last_b), output.rest)
-    qkv.near()
-    out_sum.last_a, out_sum.last_b, gate_pieces = after(
-        (out_sum.last_a, out_sum.last_b, gate_pieces), qkv.odd
-    )
+    qkv.line = after(qkv.line, output.rest)
+    qkv.far()
+    out_sum.last_a, out_sum.last_b = after((out_sum.last_a, out_sum.last_b), qkv.rest)
     layer_out = layer_out_of(resid, out_sum.parts())
-    gate_out = update_units(
-        spot, w_gate, gate_mom, gate_ema, gate_pieces, rate(0.6, width)
-    )
-    up_pieces = exchange(flat(after(up.total, qkv.odd)))
-    qkv.line = after(qkv.line, layer_out, gate_out[0])
-    qkv.far()
+    pieces = after(pieces, qkv.rest)
+    gate_out = update_units(spot, w_gate, gate_mom, gate_ema, pieces, 0, rate(0.6, width))
+    up_out = update_units(spot, w_up, up_mom, up_ema, pieces, 1, rate(0.6, width))
     output_out = update_rows(
         [(after(x, qkv.rest), at) for x, at in output.final()],
         [(w_output, output_mom, output_ema)], [rate(5.0, heads_width)],
     )
-    up_out = update_units(
-        spot, w_up, up_mom, up_ema, after(up_pieces, qkv.rest), rate(0.6, width)
-    )
-    qkv.last = after(qkv.last, up_out[0], output_out[0])
+    qkv.last = after(qkv.last, gate_out[0], layer_out)
     *qkv_out, left_over = update_rows(
         qkv.final(),
         [(w_query, query_mom, query_ema), (w_keyval, keyval_mom, keyval_ema)],

time: 642 us -> 633 us (0.986)
    ppermute x10, waiting for transfers between devices: 56.4 us -> 41.1 us  [z_swap(): return lax.ppermute(value, 'fsdp', [(i, i ^ 2 * k) for i in range(size)])]
    ppermute x41 -> x38, waiting for transfers between devices: 153 us -> 164 us  [dp_swap(): return lax.ppermute(value, 'dp', [(i, i ^ k) for i in range(size)])]
    pallas_call x15 -> x14, Pallas kernels: 50.1 us -> 46.5 us  [add(): pl.pallas_call(functools.partial(add_kernel, [len(job) for job in jobs]),...]
    ppermute x41 -> x38, starting transfers between devices: 44.1 us -> 42.1 us  [dp_swap(): return lax.ppermute(value, 'dp', [(i, i ^ k) for i in range(size)])]
    unnamed x102 -> x90, local copies, waits for them, and re-layouts: 13.5 us -> 12.3 us
  transfers between devices with their start and end apart: 70 -> 67, of which waited for: 26 -> 25; matrix products, arithmetic and copies ran while one was open for 2% -> 2% of each run, Pallas kernels for 37% -> 38%
where the time goes in v4:
time: 633 us; the launch traced here: 627 us
  Pallas kernels  318 us (50%)
  waiting for transfers between devices  208 us (33%)
  starting transfers between devices  57.8 us (9%)
  local copies, waits for them, and re-layouts  16.1 us (3%)
  between operations  14.5 us (2%)
  other arithmetic  12.6 us (2%)
    ppermute x38, waiting for transfers between devices, dp_swap(): return lax.ppermute(value, 'dp', [(i, i ^ k) for i in range(size)])  164 us
    pallas_call x1, Pallas kernels, ffn_all(): pl.pallas_call(ffn_all_kernel, grid=(4,), in_specs=[SMEM] + [ANY] * 11, o...  73.1 us
    pallas_call x14, Pallas kernels, add(): pl.pallas_call(functools.partial(add_kernel, [len(job) for job in jobs]),...  46.5 us
    ppermute x38, starting transfers between devices, dp_swap(): return lax.ppermute(value, 'dp', [(i, i ^ k) for i in range(size)])  42.1 us
    ppermute x10, waiting for transfers between devices, z_swap(): return lax.ppermute(value, 'fsdp', [(i, i ^ 2 * k) for i in range(size)])  41.1 us
    pallas_call x2, Pallas kernels, unit_grads(): pl.pallas_call(line_grads_kernel, grid_spec=pltpu.PrefetchScalarGridSpec(...  31.1 us
    pallas_call x1, Pallas kernels, attend_back(): pl.pallas_call(functools.partial(attend_back_kernel, head_dim ** (-0.5),...  19.9 us
    pallas_call x2, Pallas kernels, row_grads(): pl.pallas_call(row_grads_kernel, grid_spec=pltpu.PrefetchScalarGridSpec(n...  19.9 us
  transfers between devices with their start and end apart: 67, of which 25 were waited for; matrix products, arithmetic and copies ran while one was open for 2% of the time, Pallas kernels for 38%

profile of v4, /device:TPU:0, one launch (start us, length us, event | category | flops | bytes accessed | tf_op | source)
XLA Modules:
  0.0 627.1 jit_solution(6406402870072679686)
XLA Ops:
  7.8 3.8 slices.1
  11.6 2.9 collective-permute-start.6
  16.8 2.6 collective-permute-start
  23.0 10.6 %collective-permute-done = bf16[64,2432]{1,0:T(8,128)(2,1)} collective-permute-done((bf16[64,2432]{1,0:T(8,128)(2,1)}, bf16[64,2432]{1,0:T(8,128)(2,1)}, u32[]{:S(2)}, u32[]{:S(2)}) %collective-permute-start) | collective-permute-done | bytes 311328 | tf_op jit(solution)/shard_map/ppermute | solution.py:253
  34.2 4.0 collective-permute-done.7
  38.5 3.5 collective-permute-done.2
  45.4 3.4 collective-permute-start.3
  48.8 11.0 %collective-permute-done.3 = bf16[64,2048]{1,0:T(8,128)(2,1)S(1)} collective-permute-done((bf16[64,2048]{1,0:T(8,128)(2,1)S(1)}, bf16[64,2048]{1,0:T(8,128)(2,1)S(1)}, u32[]{:S(2)}, u32[]{:S(2)}) %collective-permute-start.3) | collective-permute-done | bytes 262176 | tf_op jit(solution)/shard_map/ppermute | solution.py:253
  61.9 7.2 %collective-permute-done.5 = bf16[64,2048]{1,0:T(8,128)(2,1)S(1)} collective-permute-done((bf16[64,2048]{1,0:T(8,128)(2,1)S(1)}, bf16[64,2048]{1,0:T(8,128)(2,1)S(1)}, u32[]{:S(2)}, u32[]{:S(2)}) %collective-permute-start.5) | collective-permute-done | bytes 262176 | tf_op jit(solution)/shard_map/ppermute | solution.py:253
  69.1 2.0 collective-permute-done.9.whole.refs_1_
  72.1 1.9 cut.8
  79.7 8.2 %collective-permute-done.11.refs_3_ = bf16[2,64,2432]{2,1,0:T(8,128)(2,1)} collective-permute-done((bf16[2,64,2432]{2,1,0:T(8,128)(2,1)}, bf16[2,64,2432]{2,1,0:T(8,128)(2,1)}, u32[]{:S(2)}, u32[]{:S(2)}) %collective-permute-start.11) | collective-permute-done | bytes 622624 | tf_op jit(solution)/shard_map/ppermute | solution.py:248
  88.0 3.0 collective-permute-done.12.refs_4_
  99.4 10.6 %enter.1 = (f32[384,2304]{1,0:T(8,128)}, bf16[384,2048]{1,0:T(8,128)(2,1)}, f32[8,2048]{1,0:T(8,128)}) custom-call(s32[3]{0:T(128)} %pad_add_fusion.spot, bf16[384,2048]{1,0:T(8,128)(2,1)} %tokens.4, bf16[4,64,2432]{2,1,0:T(8,128)(2,1)} %copy-done.14, bf16[4,64,2432]{2,1,0:T(8,128)(2,1)} %copy-done.16, ...), custom_call_target="tpu_custom_call" | custom-call | flops 144955146240 | bytes 377487360 | tf_op jit(solution)/shard_map/enter/pallas_call | solution.py:519
  110.0 15.2 %attend.1 = (bf16[384,2048]{1,0:T(8,128)(2,1)}, bf16[384,2048]{1,0:T(8,128)(2,1)}, bf16[384,256]{1,0:T(8,128)(2,1)}) custom-call(f32[384,2304]{1,0:T(8,128)} %get-tuple-element.172.q_raw.k_raw.v_raw, f32[384,2304]{1,0:T(8,128)} %get-tuple-element.172.q_raw.k_raw.v_raw, f32[384,2304]{1,0:T(8,128)} %get-tuple-element.172.q_raw.k_raw.v_raw, ...), custom_call_target="tpu_custom_call" | custom-call | flops 72477573120 | bytes 314572800 | tf_op jit(solution)/shard_map/attend/pallas_call | solution.py:102
  129.9 36.5 %collective-permute-done.22.refs_3_ = bf16[2,64,2048]{2,1,0:T(8,128)(2,1)} collective-permute-done((bf16[2,64,2048]{2,1,0:T(8,128)(2,1)}, bf16[2,64,2048]{2,1,0:T(8,128)(2,1)}, u32[]{:S(2)}, u32[]{:S(2)}) %collective-permute-start.22) | collective-permute-done | bytes 524320 | tf_op jit(solution)/shard_map/ppermute | solution.py:248
  167.4 1.9 cut.10
  169.3 2.0 cut.11
  174.7 9.8 %leave.1 = (f32[384,2048]{1,0:T(8,128)}, bf16[384,2048]{1,0:T(8,128)(2,1)}) custom-call(s32[3]{0:T(128)} %pad_add_fusion.spot, bf16[384,2048]{1,0:T(8,128)(2,1)} %get-tuple-element.175.attended.left, bf16[384,2048]{1,0:T(8,128)(2,1)} %tokens.4, f32[8,2048]{1,0:T(8,128)} %get-tuple-element.176.gains, bf16[4,64,2048]{2,1,0:T(8,128)(2,1)} %pad_maximum_fusion.1.refs_0_, ...), custom_call_target="tpu_custom_call" | custom-call | flops 128849018880 | bytes 335544320 | tf_op jit(solution)/shard_map/leave/pallas_call | solution.py:546
  184.6 6.5 %collective-permute-done.29.refs_8_ = bf16[192,2048]{1,0:T(8,128)(2,1)} collective-permute-done((bf16[192,2048]{1,0:T(8,128)(2,1)S(1)}, bf16[192,2048]{1,0:T(8,128)(2,1)}, u32[]{:S(2)}, u32[]{:S(2)}) %collective-permute-start.29) | collective-permute-done | bytes 786464 | tf_op jit(solution)/shard_map/ppermute | solution.py:248
  194.5 32.4 %collective-permute-done.31.whole.refs_1_ = bf16[384,2048]{1,0:T(8,128)(2,1)S(1)} collective-permute-done((bf16[384,2048]{1,0:T(8,128)(2,1)}, bf16[384,2048]{1,0:T(8,128)(2,1)S(1)}, u32[]{:S(2)}, u32[]{:S(2)}) %collective-permute-start.31) | collective-permute-done | bytes 1572896 | tf_op jit(solution)/shard_map/ppermute | solution.py:248
  228.1 1.9 cut.14
  232.7 1.9 cut.15
  236.0 11.7 %collective-permute-done.33.refs_3_ = bf16[192,2048]{1,0:T(8,128)(2,1)S(1)} collective-permute-done((bf16[192,2048]{1,0:T(8,128)(2,1)}, bf16[192,2048]{1,0:T(8,128)(2,1)S(1)}, u32[]{:S(2)}, u32[]{:S(2)}) %collective-permute-start.33) | collective-permute-done | bytes 786464 | tf_op jit(solution)/shard_map/ppermute | solution.py:248
  247.7 4.3 collective-permute-done.34.refs_4_
  252.0 2.9 all-gather.3.cloned.1.call-done
  255.0 73.1 %ffn_all.1 = (bf16[1536,2048]{1,0:T(8,128)(2,1)}, bf16[1536,2048]{1,0:T(8,128)(2,1)}, bf16[1536,1408]{1,0:T(8,128)(2,1)}, bf16[1536,1408]{1,0:T(8,128)(2,1)}, bf...) custom-call(s32[3]{0:T(128)} %pad_add_fusion.spot, ...), custom_call_target="tpu_custom_call" | custom-call | flops 2126008811520 | bytes 1698693120 | tf_op jit(solution)/shard_map/ffn_all/pallas_call | solution.py:742
  331.1 14.9 %down_grads.1 = (bf16[4,176,2048]{2,1,0:T(8,128)(2,1)}, bf16[4,176,2048]{2,1,0:T(8,128)(2,1)}) custom-call(s32[3]{0:T(128)} %pad_add_fusion.spot, bf16[1536,1408]{1,0:T(8,128)(2,1)} %get-tuple-element.189.refs_0_, bf16[1536,2048]{1,0:T(8,128)(2,1)} %get-tuple-element.190.refs_1_), custom_call_target="tpu_custom_call" | custom-call | flops 354334801920 | bytes 655360000 | tf_op jit(solution)/shard_map/down_grads/pallas_call | solution.py:1062
  346.0 15.5 %unit_grads.2 = (bf16[4,4,64,1408]{3,2,1,0:T(8,128)(2,1)}, bf16[4,4,64,1408]{3,2,1,0:T(8,128)(2,1)}) custom-call(s32[3]{0:T(128)} %pad_add_fusion.spot, bf16[1536,2048]{1,0:T(8,128)(2,1)} %get-tuple-element.201.refs_0_, bf16[1536,1408]{1,0:T(8,128)(2,1)} %get-tuple-element.194.refs_1_), custom_call_target="tpu_custom_call" | custom-call | flops 354334801920 | bytes 655360000 | tf_op jit(solution)/shard_map/unit_grads/pallas_call | solution.py:1039
  362.0 4.9 add.59
  366.9 3.2 add.60
  371.5 15.5 %unit_grads.3 = (bf16[4,4,64,1408]{3,2,1,0:T(8,128)(2,1)}, bf16[4,4,64,1408]{3,2,1,0:T(8,128)(2,1)}) custom-call(s32[3]{0:T(128)} %pad_add_fusion.spot, bf16[1536,2048]{1,0:T(8,128)(2,1)} %get-tuple-element.201.refs_0_, bf16[1536,1408]{1,0:T(8,128)(2,1)} %get-tuple-element.202.refs_1_), custom_call_target="tpu_custom_call" | custom-call | flops 354334801920 | bytes 655360000 | tf_op jit(solution)/shard_map/unit_grads/pallas_call | solution.py:1039
  387.0 2.9 collective-permute-done.38.refs_2_
  390.1 8.7 %branch.1 = (f32[384,2048]{1,0:T(8,128)}, bf16[384,2048]{1,0:T(8,128)(2,1)}, f32[8,2048]{1,0:T(8,128)}) custom-call(f32[384,2048]{1,0:T(8,128)} %get-tuple-element.204.resid, bf16[384,2048]{1,0:T(8,128)(2,1)} %cot.1, f32[8,2048]{1,0:T(8,128)} %get-tuple-element.176.gains, bf16[8,192,2048]{2,1,0:T(8,128)(2,1)} %bitcast.63, ...), custom_call_target="tpu_custom_call" | custom-call | bytes 566231040 | tf_op jit(solution)/shard_map/branch/pallas_call | solution.py:868
  398.8 3.2 add.61
  404.0 9.4 %row_grads.2 = (bf16[2,4,2,64,2048]{4,3,2,1,0:T(8,128)(2,1)}, bf16[2,4,2,64,2048]{4,3,2,1,0:T(8,128)(2,1)}) custom-call(s32[3]{0:T(128)} %pad_add_fusion.spot, bf16[384,2048]{1,0:T(8,128)(2,1)} %get-tuple-element.175.attended.left, bf16[384,2048]{1,0:T(8,128)(2,1)} %get-tuple-element.213.right.grads), custom_call_target="tpu_custom_call" | custom-call | flops 128849018880 | bytes 461373440 | tf_op jit(solution)/shard_map/row_grads/pallas_call | solution.py:937
  413.4 8.5 %leave_back.1.grad_ref = bf16[384,2048]{1,0:T(8,128)(2,1)} custom-call(s32[3]{0:T(128)} %pad_add_fusion.spot, bf16[384,2048]{1,0:T(8,128)(2,1)} %get-tuple-element.213.right.grads, bf16[4,64,2048]{2,1,0:T(8,128)(2,1)} %pad_maximum_fusion.1.refs_0_, bf16[4,64,2048]{2,1,0:T(8,128)(2,1)} %collective-permute-done.20.whole.refs_1_, ...), custom_call_target="tpu_custom_call" | custom-call | flops 128849018880 | bytes 335544320 | tf_op jit(solution)/shard_map/leave_back/pallas_call | solution.py:569
  421.9 3.3 add.62
  427.2 4.9 add.63
  432.2 19.9 %attend_back.1.grads.right = bf16[384,2432]{1,0:T(8,128)(2,1)} custom-call(bf16[384,2048]{1,0:T(8,128)(2,1)} %get-tuple-element.217.query_ref, bf16[384,2048]{1,0:T(8,128)(2,1)} %leave_back.1.grad_ref, bf16[384,256]{1,0:T(8,128)(2,1)} %get-tuple-element.220.shared, bf16[384,256]{1,0:T(8,128)(2,1)} %kv_next.1, f32[384,128]{1,0:T(8,128)} %get-tuple-element.400.cosine, ...), custom_call_target="tpu_custom_call" | custom-call | flops 169114337280 | bytes 251658240 | tf_op jit(solution)/shard_map/attend_back/pallas_call | solution.py:180
  452.1 13.1 %enter_back.1 = (f32[384,2048]{1,0:T(8,128)}, f32[8,2048]{1,0:T(8,128)}) custom-call(s32[3]{0:T(128)} %pad_add_fusion.spot, bf16[384,2432]{1,0:T(8,128)(2,1)} %attend_back.1.grads.right, bf16[384,2048]{1,0:T(8,128)(2,1)} %tokens.4, f32[8,2048]{1,0:T(8,128)} %get-tuple-element.176.gains, f32[384,2048]{1,0:T(8,128)} %get-tuple-element.221.grad_resid, ...), custom_call_target="tpu_custom_call" | custom-call | flops 128849018880 | bytes 335544320 | tf_op jit(solution)/shard_map/enter_back/pallas_call | solution.py:594
  465.2 2.8 add.64
  468.1 10.5 %row_grads.3 = (bf16[2,4,2,64,2432]{4,3,2,1,0:T(8,128)(2,1)}, bf16[2,4,2,64,2432]{4,3,2,1,0:T(8,128)(2,1)}) custom-call(s32[3]{0:T(128)} %pad_add_fusion.spot, bf16[384,2048]{1,0:T(8,128)(2,1)} %get-tuple-element.230.left, bf16[384,2432]{1,0:T(8,128)(2,1)} %attend_back.1.grads.right, f32[8,2048]{1,0:T(8,128)} %get-tuple-element.231.refs_0_, ...), custom_call_target="tpu_custom_call" | custom-call | flops 153008209920 | bytes 536084480 | tf_op jit(solution)/shard_map/row_grads/pallas_call | solution.py:937
  478.5 4.9 add.65
  486.5 12.3 %collective-permute-done.47.refs_3_ = bf16[2,64,2048]{2,1,0:T(8,128)(2,1)S(1)} collective-permute-done((bf16[2,64,2048]{2,1,0:T(8,128)(2,1)S(1)}, bf16[2,64,2048]{2,1,0:T(8,128)(2,1)S(1)}, u32[]{:S(2)}, u32[]{:S(2)}) %collective-permute-start.47) | collective-permute-done | bytes 524320 | tf_op jit(solution)/shard_map/ppermute | solution.py:248
  500.7 2.3 add.66
  503.1 3.7 add.67
  507.8 3.2 add.68
  511.0 5.0 update_rows.3
  516.0 19.7 %collective-permute-done.52.refs_2_ = bf16[4,64,2432]{2,1,0:T(8,128)(2,1)S(1)} collective-permute-done((bf16[4,64,2432]{2,1,0:T(8,128)(2,1)}, bf16[4,64,2432]{2,1,0:T(8,128)(2,1)S(1)}, u32[]{:S(2)}, u32[]{:S(2)}) %collective-permute-start.52) | collective-permute-done | bytes 1245216 | tf_op jit(solution)/shard_map/ppermute | solution.py:248
  537.1 3.0 add.69
  544.3 13.0 %collective-permute-done.55.refs_3_ = bf16[2,64,2432]{2,1,0:T(8,128)(2,1)S(1)} collective-permute-done((bf16[2,64,2432]{2,1,0:T(8,128)(2,1)}, bf16[2,64,2432]{2,1,0:T(8,128)(2,1)S(1)}, u32[]{:S(2)}, u32[]{:S(2)}) %collective-permute-start.55) | collective-permute-done | bytes 622624 | tf_op jit(solution)/shard_map/ppermute | solution.py:248
  558.1 2.6 add.70
  565.6 2.1 add.71
  569.3 5.6 collective-permute-done.56.refs_4_
  574.9 2.3 collective-permute-start.62
  579.1 2.3 add.72
  585.3 5.4 collective-permute-done.60.refs_2_
  590.7 3.1 collective-permute-done.62.refs_5_
  593.8 6.6 %layer_out.1 = f32[384,2048]{1,0:T(8,128)} custom-call(f32[384,2048]{1,0:T(8,128)} %get-tuple-element.204.resid, bf16[8,192,2048]{2,1,0:T(8,128)(2,1)} %bitcast.52, bf16[2,192,2048]{2,1,0:T(8,128)(2,1)} %collective-permute-done.40.refs_1_, bf16[1,192,2048]{2,1,0:T(8,128)(2,1)} %copy-done.18, bf16[8,192,2048]{2,1,0:T(8,128)(2,1)} %bitcast.53, ...), custom_call_target="tpu_custom_call" | custom-call | bytes 440401920 | tf_op jit(solution)/shard_map/layer_out/pallas_call | solution.py:896
  600.4 4.9 update_units.2
  605.3 4.9 update_units.3
  610.2 3.3 update_rows.5
  614.2 3.4 update_rows.4
  (236 shorter events, 82.8 us)
Async XLA Ops:
  7.2 247.8 %all-gather.3.cloned.1.call-start = ((), (), s32[]{:S(2)}) async-start(), calls=%async_computation.6 | async-start | bytes 19869696 | tf_op jit(solution)/shard_map/all_gather | solution.py:1343
  11.6 22.6 %collective-permute-start.6 = (bf16[2,64,1408]{2,1,0:T(8,128)(2,1)}, bf16[2,64,1408]{2,1,0:T(8,128)(2,1)S(1)}, u32[]{:S(2)}, u32[]{:S(2)}) collective-permute-start(bf16[2,64,1408]{2,1,0:T(8,128)(2,1)} %get-tuple-element.165), channel_id=1, source_target_pairs={{0,8},{8,0},{16,24},{24,16},{1,9},{9,1},{17,25},{25,17},{2,10},{10... | collective-permute-start | bytes 1081352 | tf_op jit(solution)/shard_map/ppermute | solution.py:248
  16.8 16.8 %collective-permute-start = (bf16[64,2432]{1,0:T(8,128)(2,1)}, bf16[64,2432]{1,0:T(8,128)(2,1)}, u32[]{:S(2)}, u32[]{:S(2)}) collective-permute-start(bf16[64,2432]{1,0:T(8,128)(2,1)} %get-tuple-element.396), channel_id=1, source_target_pairs={{0,4},{1,5},{2,6},{3,7},{4,0},{5,1},{6,2},{7,3},{8,12},{9,13},{10,... | collective-permute-start | bytes 933896 | tf_op jit(solution)/shard_map/ppermute | solution.py:253
  19.4 19.1 %collective-permute-start.1 = (bf16[64,2432]{1,0:T(8,128)(2,1)}, bf16[64,2432]{1,0:T(8,128)(2,1)}, u32[]{:S(2)}, u32[]{:S(2)}) collective-permute-start(bf16[64,2432]{1,0:T(8,128)(2,1)} %get-tuple-element.396), channel_id=1, source_target_pairs={{0,2},{1,3},{2,0},{3,1},{4,6},{5,7},{6,4},{7,5},{8,10},{9,11},{10,... | collective-permute-start | bytes 933896 | tf_op jit(solution)/shard_map/ppermute | solution.py:253
  21.0 17.2 %collective-permute-start.7 = (bf16[2,64,1408]{2,1,0:T(8,128)(2,1)}, bf16[2,64,1408]{2,1,0:T(8,128)(2,1)S(1)}, u32[]{:S(2)}, u32[]{:S(2)}) collective-permute-start(bf16[2,64,1408]{2,1,0:T(8,128)(2,1)} %get-tuple-element.166), channel_id=1, source_target_pairs={{0,16},{8,24},{16,0},{24,8},{1,17},{9,25},{17,1},{25,9},{2,18},{10... | collective-permute-start | bytes 1081352 | tf_op jit(solution)/shard_map/ppermute | solution.py:248
  22.5 15.8 %collective-permute-start.8 = (bf16[2,64,1408]{2,1,0:T(8,128)(2,1)}, bf16[2,64,1408]{2,1,0:T(8,128)(2,1)S(1)}, u32[]{:S(2)}, u32[]{:S(2)}) collective-permute-start(bf16[2,64,1408]{2,1,0:T(8,128)(2,1)} %get-tuple-element.167), channel_id=1, source_target_pairs={{0,24},{8,16},{16,8},{24,0},{1,25},{9,17},{17,9},{25,1},{2,26},{10... | collective-permute-start | bytes 1081352 | tf_op jit(solution)/shard_map/ppermute | solution.py:248
  33.6 8.4 %collective-permute-start.2 = (bf16[64,2432]{1,0:T(8,128)(2,1)}, bf16[64,2432]{1,0:T(8,128)(2,1)S(1)}, u32[]{:S(2)}, u32[]{:S(2)}) collective-permute-start(bf16[64,2432]{1,0:T(8,128)(2,1)} %collective-permute-done), channel_id=1, source_target_pairs={{0,2},{1,3},{2,0},{3,1},{4,6},{5,7},{6,4},{7,5},{8,10},{9,11},{10,... | collective-permute-start | bytes 933896 | tf_op jit(solution)/shard_map/ppermute | solution.py:253
  43.2 27.8 %collective-permute-start.9 = (bf16[4,64,2432]{2,1,0:T(8,128)(2,1)S(1)}, bf16[4,64,2432]{2,1,0:T(8,128)(2,1)S(1)}, u32[]{:S(2)}, u32[]{:S(2)}) collective-permute-start(bf16[4,64,2432]{2,1,0:T(8,128)(2,1)S(1)} %pad_maximum_fusion.refs_0_), channel_id=1, source_target_pairs={{0,8},{8,0},{16,24},{24,16},{1,9},{9,1},{17,25},{25,17},{2,10},{10... | collective-permute-start | bytes 3735560 | tf_op jit(solution)/shard_map/ppermute | solution.py:248
  43.8 28.3 %collective-permute-start.10 = (bf16[4,64,2432]{2,1,0:T(8,128)(2,1)S(1)}, bf16[4,64,2432]{2,1,0:T(8,128)(2,1)}, u32[]{:S(2)}, u32[]{:S(2)}) collective-permute-start(bf16[4,64,2432]{2,1,0:T(8,128)(2,1)S(1)} %pad_maximum_fusion.refs_0_), channel_id=1, source_target_pairs={{0,16},{8,24},{16,0},{24,8},{1,17},{9,25},{17,1},{25,9},{2,18},{10... | collective-permute-start | bytes 3735560 | tf_op jit(solution)/shard_map/ppermute | solution.py:248
  45.4 14.4 %collective-permute-start.3 = (bf16[64,2048]{1,0:T(8,128)(2,1)S(1)}, bf16[64,2048]{1,0:T(8,128)(2,1)S(1)}, u32[]{:S(2)}, u32[]{:S(2)}) collective-permute-start(bf16[64,2048]{1,0:T(8,128)(2,1)S(1)} %convert_element_type.22), channel_id=1, source_target_pairs={{0,4},{1,5},{2,6},{3,7},{4,0},{5,1},{6,2},{7,3},{8,12},{9,13},{10,... | collective-permute-start | bytes 786440 | tf_op jit(solution)/shard_map/ppermute | solution.py:253
  59.8 9.3 %collective-permute-start.5 = (bf16[64,2048]{1,0:T(8,128)(2,1)S(1)}, bf16[64,2048]{1,0:T(8,128)(2,1)S(1)}, u32[]{:S(2)}, u32[]{:S(2)}) collective-permute-start(bf16[64,2048]{1,0:T(8,128)(2,1)S(1)} %collective-permute-done.3), channel_id=1, source_target_pairs={{0,2},{1,3},{2,0},{3,1},{4,6},{5,7},{6,4},{7,5},{8,10},{9,11},{10,... | collective-permute-start | bytes 786440 | tf_op jit(solution)/shard_map/ppermute | solution.py:253
  60.5 18.2 %collective-permute-start.4 = (bf16[64,2048]{1,0:T(8,128)(2,1)S(1)}, bf16[64,2048]{1,0:T(8,128)(2,1)S(1)}, u32[]{:S(2)}, u32[]{:S(2)}) collective-permute-start(bf16[64,2048]{1,0:T(8,128)(2,1)S(1)} %convert_element_type.22), channel_id=1, source_target_pairs={{0,2},{1,3},{2,0},{3,1},{4,6},{5,7},{6,4},{7,5},{8,10},{9,11},{10,... | collective-permute-start | bytes 786440 | tf_op jit(solution)/shard_map/ppermute | solution.py:253
  74.0 13.9 %collective-permute-start.11 = (bf16[2,64,2432]{2,1,0:T(8,128)(2,1)}, bf16[2,64,2432]{2,1,0:T(8,128)(2,1)}, u32[]{:S(2)}, u32[]{:S(2)}) collective-permute-start(bf16[2,64,2432]{2,1,0:T(8,128)(2,1)} %cut.8), channel_id=1, source_target_pairs={{0,16},{8,24},{16,0},{24,8},{1,17},{9,25},{17,1},{25,9},{2,18},{10... | collective-permute-start | bytes 1867784 | tf_op jit(solution)/shard_map/ppermute | solution.py:248
  77.4 13.6 %collective-permute-start.12 = (bf16[2,64,2432]{2,1,0:T(8,128)(2,1)}, bf16[2,64,2432]{2,1,0:T(8,128)(2,1)}, u32[]{:S(2)}, u32[]{:S(2)}) collective-permute-start(bf16[2,64,2432]{2,1,0:T(8,128)(2,1)} %cut.9), channel_id=1, source_target_pairs={{0,8},{8,0},{16,24},{24,16},{1,9},{9,1},{17,25},{25,17},{2,10},{10... | collective-permute-start | bytes 1867784 | tf_op jit(solution)/shard_map/ppermute | solution.py:248
  78.2 18.2 %collective-permute-start.13 = (bf16[4,64,2432]{2,1,0:T(8,128)(2,1)S(1)}, bf16[4,64,2432]{2,1,0:T(8,128)(2,1)}, u32[]{:S(2)}, u32[]{:S(2)}) collective-permute-start(bf16[4,64,2432]{2,1,0:T(8,128)(2,1)S(1)} %copy-done.15), channel_id=1, source_target_pairs={{0,1},{1,0},{2,3},{3,2},{4,5},{5,4},{6,7},{7,6},{8,9},{9,8},{10,11... | collective-permute-start | bytes 3735560 | tf_op jit(solution)/shard_map/ppermute | solution.py:258
  78.2 19.7 %collective-permute-start.14 = (bf16[4,64,2432]{2,1,0:T(8,128)(2,1)S(1)}, bf16[4,64,2432]{2,1,0:T(8,128)(2,1)}, u32[]{:S(2)}, u32[]{:S(2)}) collective-permute-start(bf16[4,64,2432]{2,1,0:T(8,128)(2,1)S(1)} %copy-done.17), channel_id=1, source_target_pairs={{0,1},{1,0},{2,3},{3,2},{4,5},{5,4},{6,7},{7,6},{8,9},{9,8},{10,11... | collective-permute-start | bytes 3735560 | tf_op jit(solution)/shard_map/ppermute | solution.py:258
  79.4 20.0 %collective-permute-start.15 = (bf16[4,64,2432]{2,1,0:T(8,128)(2,1)}, bf16[4,64,2432]{2,1,0:T(8,128)(2,1)}, u32[]{:S(2)}, u32[]{:S(2)}) collective-permute-start(bf16[4,64,2432]{2,1,0:T(8,128)(2,1)} %collective-permute-done.10.whole.refs_2_), channel_id=1, source_target_pairs={{0,1},{1,0},{2,3},{3,2},{4,5},{5,4},{6,7},{7,6},{8,9},{9,8},{10,11... | collective-permute-start | bytes 3735560 | tf_op jit(solution)/shard_map/ppermute | solution.py:258
  88.0 7.3 %collective-permute-start.16 = (bf16[2,64,2432]{2,1,0:T(8,128)(2,1)}, bf16[2,64,2432]{2,1,0:T(8,128)(2,1)}, u32[]{:S(2)}, u32[]{:S(2)}) collective-permute-start(bf16[2,64,2432]{2,1,0:T(8,128)(2,1)} %collective-permute-done.11.refs_3_), channel_id=1, source_target_pairs={{0,1},{1,0},{2,3},{3,2},{4,5},{5,4},{6,7},{7,6},{8,9},{9,8},{10,11... | collective-permute-start | bytes 1867784 | tf_op jit(solution)/shard_map/ppermute | solution.py:258
  94.7 373.4 %reduce-scatter.4.cloned.1.call-start = ((), (), s32[]{:S(2)}) async-start(), calls=%async_computation.3 | async-start | bytes 3604480 | tf_op jit(solution)/shard_map/reduce_scatter | solution.py:1001
  95.3 30.0 %collective-permute-start.20 = (bf16[4,64,2048]{2,1,0:T(8,128)(2,1)}, bf16[4,64,2048]{2,1,0:T(8,128)(2,1)}, u32[]{:S(2)}, u32[]{:S(2)}) collective-permute-start(bf16[4,64,2048]{2,1,0:T(8,128)(2,1)} %pad_maximum_fusion.1.refs_0_), channel_id=1, source_target_pairs={{0,8},{8,0},{16,24},{24,16},{1,9},{9,1},{17,25},{25,17},{2,10},{10... | collective-permute-start | bytes 3145736 | tf_op jit(solution)/shard_map/ppermute | solution.py:248
  95.9 29.4 %collective-permute-start.21 = (bf16[4,64,2048]{2,1,0:T(8,128)(2,1)}, bf16[4,64,2048]{2,1,0:T(8,128)(2,1)}, u32[]{:S(2)}, u32[]{:S(2)}) collective-permute-start(bf16[4,64,2048]{2,1,0:T(8,128)(2,1)} %pad_maximum_fusion.1.refs_0_), channel_id=1, source_target_pairs={{0,16},{8,24},{16,0},{24,8},{1,17},{9,25},{17,1},{25,9},{2,18},{10... | collective-permute-start | bytes 3145736 | tf_op jit(solution)/shard_map/ppermute | solution.py:248
  96.4 70.5 %collective-permute-start.18 = (bf16[384,2048]{1,0:T(8,128)(2,1)}, bf16[384,2048]{1,0:T(8,128)(2,1)}, u32[]{:S(2)}, u32[]{:S(2)}) collective-permute-start(bf16[384,2048]{1,0:T(8,128)(2,1)} %cot.1), channel_id=1, source_target_pairs={{0,8},{8,0},{16,24},{24,16},{1,9},{9,1},{17,25},{25,17},{2,10},{10... | collective-permute-start | bytes 4718600 | tf_op jit(solution)/shard_map/ppermute | solution.py:248
  97.9 69.1 %collective-permute-start.19 = (bf16[384,2048]{1,0:T(8,128)(2,1)}, bf16[384,2048]{1,0:T(8,128)(2,1)}, u32[]{:S(2)}, u32[]{:S(2)}) collective-permute-start(bf16[384,2048]{1,0:T(8,128)(2,1)} %cot.1), channel_id=1, source_target_pairs={{0,16},{8,24},{16,0},{24,8},{1,17},{9,25},{17,1},{25,9},{2,18},{10... | collective-permute-start | bytes 4718600 | tf_op jit(solution)/shard_map/ppermute | solution.py:248
  127.0 39.4 %collective-permute-start.22 = (bf16[2,64,2048]{2,1,0:T(8,128)(2,1)}, bf16[2,64,2048]{2,1,0:T(8,128)(2,1)}, u32[]{:S(2)}, u32[]{:S(2)}) collective-permute-start(bf16[2,64,2048]{2,1,0:T(8,128)(2,1)} %cut.12), channel_id=1, source_target_pairs={{0,16},{8,24},{16,0},{24,8},{1,17},{9,25},{17,1},{25,9},{2,18},{10... | collective-permute-start | bytes 1572872 | tf_op jit(solution)/shard_map/ppermute | solution.py:248
  129.3 37.1 %collective-permute-start.23 = (bf16[2,64,2048]{2,1,0:T(8,128)(2,1)}, bf16[2,64,2048]{2,1,0:T(8,128)(2,1)}, u32[]{:S(2)}, u32[]{:S(2)}) collective-permute-start(bf16[2,64,2048]{2,1,0:T(8,128)(2,1)} %cut.13), channel_id=1, source_target_pairs={{0,8},{8,0},{16,24},{24,16},{1,9},{9,1},{17,25},{25,17},{2,10},{10... | collective-permute-start | bytes 1572872 | tf_op jit(solution)/shard_map/ppermute | solution.py:248
  129.9 41.4 %collective-permute-start.24 = (bf16[4,64,2048]{2,1,0:T(8,128)(2,1)}, bf16[4,64,2048]{2,1,0:T(8,128)(2,1)S(1)}, u32[]{:S(2)}, u32[]{:S(2)}) collective-permute-start(bf16[4,64,2048]{2,1,0:T(8,128)(2,1)} %pad_maximum_fusion.1.refs_0_), channel_id=1, source_target_pairs={{0,1},{1,0},{2,3},{3,2},{4,5},{5,4},{6,7},{7,6},{8,9},{9,8},{10,11... | collective-permute-start | bytes 3145736 | tf_op jit(solution)/shard_map/ppermute | solution.py:258
  166.4 7.0 %collective-permute-start.25 = (bf16[4,64,2048]{2,1,0:T(8,128)(2,1)}, bf16[4,64,2048]{2,1,0:T(8,128)(2,1)S(1)}, u32[]{:S(2)}, u32[]{:S(2)}) collective-permute-start(bf16[4,64,2048]{2,1,0:T(8,128)(2,1)} %collective-permute-done.20.whole.refs_1_), channel_id=1, source_target_pairs={{0,1},{1,0},{2,3},{3,2},{4,5},{5,4},{6,7},{7,6},{8,9},{9,8},{10,11... | collective-permute-start | bytes 3145736 | tf_op jit(solution)/shard_map/ppermute | solution.py:258
  166.4 7.0 %collective-permute-start.26 = (bf16[4,64,2048]{2,1,0:T(8,128)(2,1)}, bf16[4,64,2048]{2,1,0:T(8,128)(2,1)S(1)}, u32[]{:S(2)}, u32[]{:S(2)}) collective-permute-start(bf16[4,64,2048]{2,1,0:T(8,128)(2,1)} %collective-permute-done.21.whole.refs_2_), channel_id=1, source_target_pairs={{0,1},{1,0},{2,3},{3,2},{4,5},{5,4},{6,7},{7,6},{8,9},{9,8},{10,11... | collective-permute-start | bytes 3145736 | tf_op jit(solution)/shard_map/ppermute | solution.py:258
  171.3 19.7 %collective-permute-start.29 = (bf16[192,2048]{1,0:T(8,128)(2,1)S(1)}, bf16[192,2048]{1,0:T(8,128)(2,1)}, u32[]{:S(2)}, u32[]{:S(2)}) collective-permute-start(bf16[192,2048]{1,0:T(8,128)(2,1)S(1)} %copy-done.19), channel_id=1, source_target_pairs={{0,16},{8,24},{16,0},{24,8},{1,17},{9,25},{17,1},{25,9},{2,18},{10... | collective-permute-start | bytes 2359304 | tf_op jit(solution)/shard_map/ppermute | solution.py:248
  171.9 19.6 %collective-permute-start.30 = (bf16[192,2048]{1,0:T(8,128)(2,1)}, bf16[192,2048]{1,0:T(8,128)(2,1)}, u32[]{:S(2)}, u32[]{:S(2)}) collective-permute-start(bf16[192,2048]{1,0:T(8,128)(2,1)} %cut.11), channel_id=1, source_target_pairs={{0,8},{8,0},{16,24},{24,16},{1,9},{9,1},{17,25},{25,17},{2,10},{10... | collective-permute-start | bytes 2359304 | tf_op jit(solution)/shard_map/ppermute | solution.py:248
  191.5 35.4 %collective-permute-start.31 = (bf16[384,2048]{1,0:T(8,128)(2,1)}, bf16[384,2048]{1,0:T(8,128)(2,1)S(1)}, u32[]{:S(2)}, u32[]{:S(2)}) collective-permute-start(bf16[384,2048]{1,0:T(8,128)(2,1)} %get-tuple-element.182.refs_0_), channel_id=1, source_target_pairs={{0,8},{8,0},{16,24},{24,16},{1,9},{9,1},{17,25},{25,17},{2,10},{10... | collective-permute-start | bytes 4718600 | tf_op jit(solution)/shard_map/ppermute | solution.py:248
  192.9 38.5 %collective-permute-start.32 = (bf16[384,2048]{1,0:T(8,128)(2,1)}, bf16[384,2048]{1,0:T(8,128)(2,1)S(1)}, u32[]{:S(2)}, u32[]{:S(2)}) collective-permute-start(bf16[384,2048]{1,0:T(8,128)(2,1)} %get-tuple-element.182.refs_0_), channel_id=1, source_target_pairs={{0,16},{8,24},{16,0},{24,8},{1,17},{9,25},{17,1},{25,9},{2,18},{10... | collective-permute-start | bytes 4718600 | tf_op jit(solution)/shard_map/ppermute | solution.py:248
  230.0 17.8 %collective-permute-start.33 = (bf16[192,2048]{1,0:T(8,128)(2,1)}, bf16[192,2048]{1,0:T(8,128)(2,1)S(1)}, u32[]{:S(2)}, u32[]{:S(2)}) collective-permute-start(bf16[192,2048]{1,0:T(8,128)(2,1)} %cut.14), channel_id=1, source_target_pairs={{0,16},{8,24},{16,0},{24,8},{1,17},{9,25},{17,1},{25,9},{2,18},{10... | collective-permute-start | bytes 2359304 | tf_op jit(solution)/shard_map/ppermute | solution.py:248
  234.6 17.5 %collective-permute-start.34 = (bf16[192,2048]{1,0:T(8,128)(2,1)}, bf16[192,2048]{1,0:T(8,128)(2,1)S(1)}, u32[]{:S(2)}, u32[]{:S(2)}) collective-permute-start(bf16[192,2048]{1,0:T(8,128)(2,1)} %cut.15), channel_id=1, source_target_pairs={{0,8},{8,0},{16,24},{24,16},{1,9},{9,1},{17,25},{25,17},{2,10},{10... | collective-permute-start | bytes 2359304 | tf_op jit(solution)/shard_map/ppermute | solution.py:248
  328.1 38.8 %collective-permute-start.35 = (bf16[2,192,2048]{2,1,0:T(8,128)(2,1)}, bf16[2,192,2048]{2,1,0:T(8,128)(2,1)}, u32[]{:S(2)}, u32[]{:S(2)}) collective-permute-start(bf16[2,192,2048]{2,1,0:T(8,128)(2,1)} %get-tuple-element.187), channel_id=1, source_target_pairs={{0,8},{8,0},{16,24},{24,16},{1,9},{9,1},{17,25},{25,17},{2,10},{10... | collective-permute-start | bytes 4718600 | tf_op jit(solution)/shard_map/ppermute | solution.py:248
  329.6 37.3 %collective-permute-start.36 = (bf16[2,192,2048]{2,1,0:T(8,128)(2,1)}, bf16[2,192,2048]{2,1,0:T(8,128)(2,1)}, u32[]{:S(2)}, u32[]{:S(2)}) collective-permute-start(bf16[2,192,2048]{2,1,0:T(8,128)(2,1)} %get-tuple-element.188), channel_id=1, source_target_pairs={{0,16},{8,24},{16,0},{24,8},{1,17},{9,25},{17,1},{25,9},{2,18},{10... | collective-permute-start | bytes 4718600 | tf_op jit(solution)/shard_map/ppermute | solution.py:248
  346.0 16.0 %collective-permute-start.37 = (bf16[4,176,2048]{2,1,0:T(8,128)(2,1)}, bf16[4,176,2048]{2,1,0:T(8,128)(2,1)}, u32[]{:S(2)}, u32[]{:S(2)}) collective-permute-start(bf16[4,176,2048]{2,1,0:T(8,128)(2,1)} %get-tuple-element.192), channel_id=1, source_target_pairs={{0,1},{1,0},{2,3},{3,2},{4,5},{5,4},{6,7},{7,6},{8,9},{9,8},{10,11... | collective-permute-start | bytes 8650760 | tf_op jit(solution)/shard_map/ppermute | solution.py:258
  361.5 60.4 %collective-permute-start.42 = (bf16[4,4,64,1408]{3,2,1,0:T(8,128)(2,1)}, bf16[4,4,64,1408]{3,2,1,0:T(8,128)(2,1)}, u32[]{:S(2)}, u32[]{:S(2)}) collective-permute-start(bf16[4,4,64,1408]{3,2,1,0:T(8,128)(2,1)} %get-tuple-element.211), channel_id=1, source_target_pairs={{0,1},{1,0},{2,3},{3,2},{4,5},{5,4},{6,7},{7,6},{8,9},{9,8},{10,11... | collective-permute-start | bytes 8650760 | tf_op jit(solution)/shard_map/ppermute | solution.py:258
  370.1 19.8 %collective-permute-start.38 = (bf16[1,192,2048]{2,1,0:T(8,128)(2,1)}, bf16[1,192,2048]{2,1,0:T(8,128)(2,1)}, u32[]{:S(2)}, u32[]{:S(2)}) collective-permute-start(bf16[1,192,2048]{2,1,0:T(8,128)(2,1)} %get-tuple-element.199), channel_id=1, source_target_pairs={{0,16},{8,24},{16,0},{24,8},{1,17},{9,25},{17,1},{25,9},{2,18},{10... | collective-permute-start | bytes 2359304 | tf_op jit(solution)/shard_map/ppermute | solution.py:248
  370.8 19.3 %collective-permute-start.39 = (bf16[1,192,2048]{2,1,0:T(8,128)(2,1)}, bf16[1,192,2048]{2,1,0:T(8,128)(2,1)}, u32[]{:S(2)}, u32[]{:S(2)}) collective-permute-start(bf16[1,192,2048]{2,1,0:T(8,128)(2,1)} %get-tuple-element.200), channel_id=1, source_target_pairs={{0,8},{8,0},{16,24},{24,16},{1,9},{9,1},{17,25},{25,17},{2,10},{10... | collective-permute-start | bytes 2359304 | tf_op jit(solution)/shard_map/ppermute | solution.py:248
  371.4 131.7 %reduce-scatter.6.cloned.1.call-start = ((), (), s32[]{:S(2)}) async-start(), calls=%async_computation.4 | async-start | bytes 3604480 | tf_op jit(solution)/shard_map/reduce_scatter | solution.py:1001
  387.0 91.5 %collective-permute-start.49 = (bf16[4,4,64,1408]{3,2,1,0:T(8,128)(2,1)}, bf16[4,4,64,1408]{3,2,1,0:T(8,128)(2,1)}, u32[]{:S(2)}, u32[]{:S(2)}) collective-permute-start(bf16[4,4,64,1408]{3,2,1,0:T(8,128)(2,1)} %get-tuple-element.235), channel_id=1, source_target_pairs={{0,1},{1,0},{2,3},{3,2},{4,5},{5,4},{6,7},{7,6},{8,9},{9,8},{10,11... | collective-permute-start | bytes 8650760 | tf_op jit(solution)/shard_map/ppermute | solution.py:258
  402.0 63.2 %collective-permute-start.40 = (bf16[2,192,2048]{2,1,0:T(8,128)(2,1)}, bf16[2,192,2048]{2,1,0:T(8,128)(2,1)}, u32[]{:S(2)}, u32[]{:S(2)}) collective-permute-start(bf16[2,192,2048]{2,1,0:T(8,128)(2,1)} %get-tuple-element.207), channel_id=1, source_target_pairs={{0,8},{8,0},{16,24},{24,16},{1,9},{9,1},{17,25},{25,17},{2,10},{10... | collective-permute-start | bytes 4718600 | tf_op jit(solution)/shard_map/ppermute | solution.py:248
  402.5 62.6 %collective-permute-start.41 = (bf16[2,192,2048]{2,1,0:T(8,128)(2,1)}, bf16[2,192,2048]{2,1,0:T(8,128)(2,1)}, u32[]{:S(2)}, u32[]{:S(2)}) collective-permute-start(bf16[2,192,2048]{2,1,0:T(8,128)(2,1)} %get-tuple-element.208), channel_id=1, source_target_pairs={{0,16},{8,24},{16,0},{24,8},{1,17},{9,25},{17,1},{25,9},{2,18},{10... | collective-permute-start | bytes 4718600 | tf_op jit(solution)/shard_map/ppermute | solution.py:248
  413.4 8.5 %collective-permute-start.43 = (bf16[2,4,2,64,2048]{4,3,2,1,0:T(8,128)(2,1)}, bf16[2,4,2,64,2048]{4,3,2,1,0:T(8,128)(2,1)}, u32[]{:S(2)}, u32[]{:S(2)}) collective-permute-start(bf16[2,4,2,64,2048]{4,3,2,1,0:T(8,128)(2,1)} %get-tuple-element.212), channel_id=1, source_target_pairs={{0,1},{1,0},{2,3},{3,2},{4,5},{5,4},{6,7},{7,6},{8,9},{9,8},{10,11... | collective-permute-start | bytes 12582920 | tf_op jit(solution)/shard_map/ppermute | solution.py:258
  425.2 40.0 %collective-permute-start.44 = (bf16[4,64,2048]{2,1,0:T(8,128)(2,1)}, bf16[4,64,2048]{2,1,0:T(8,128)(2,1)}, u32[]{:S(2)}, u32[]{:S(2)}) collective-permute-start(bf16[4,64,2048]{2,1,0:T(8,128)(2,1)} %get-tuple-element.215), channel_id=1, source_target_pairs={{0,8},{8,0},{16,24},{24,16},{1,9},{9,1},{17,25},{25,17},{2,10},{10... | collective-permute-start | bytes 3145736 | tf_op jit(solution)/shard_map/ppermute | solution.py:248
  426.6 38.6 %collective-permute-start.45 = (bf16[4,64,2048]{2,1,0:T(8,128)(2,1)}, bf16[4,64,2048]{2,1,0:T(8,128)(2,1)}, u32[]{:S(2)}, u32[]{:S(2)}) collective-permute-start(bf16[4,64,2048]{2,1,0:T(8,128)(2,1)} %get-tuple-element.216), channel_id=1, source_target_pairs={{0,16},{8,24},{16,0},{24,8},{1,17},{9,25},{17,1},{25,9},{2,18},{10... | collective-permute-start | bytes 3145736 | tf_op jit(solution)/shard_map/ppermute | solution.py:248
  432.2 128.8 %reduce-scatter.8.cloned.1.call-start = ((), (), s32[]{:S(2)}) async-start(), calls=%async_computation.5 | async-start | bytes 3604480 | tf_op jit(solution)/shard_map/reduce_scatter | solution.py:1001
  478.5 24.6 %collective-permute-start.46 = (bf16[2,4,2,64,2432]{4,3,2,1,0:T(8,128)(2,1)}, bf16[2,4,2,64,2432]{4,3,2,1,0:T(8,128)(2,1)}, u32[]{:S(2)}, u32[]{:S(2)}) collective-permute-start(bf16[2,4,2,64,2432]{4,3,2,1,0:T(8,128)(2,1)} %get-tuple-element.234), channel_id=1, source_target_pairs={{0,1},{1,0},{2,3},{3,2},{4,5},{5,4},{6,7},{7,6},{8,9},{9,8},{10,11... | collective-permute-start | bytes 14942216 | tf_op jit(solution)/shard_map/ppermute | solution.py:258
  484.5 14.3 %collective-permute-start.47 = (bf16[2,64,2048]{2,1,0:T(8,128)(2,1)S(1)}, bf16[2,64,2048]{2,1,0:T(8,128)(2,1)S(1)}, u32[]{:S(2)}, u32[]{:S(2)}) collective-permute-start(bf16[2,64,2048]{2,1,0:T(8,128)(2,1)S(1)} %copy-done.40), channel_id=1, source_target_pairs={{0,16},{8,24},{16,0},{24,8},{1,17},{9,25},{17,1},{25,9},{2,18},{10... | collective-permute-start | bytes 1572872 | tf_op jit(solution)/shard_map/ppermute | solution.py:248
  485.9 14.0 %collective-permute-start.48 = (bf16[2,64,2048]{2,1,0:T(8,128)(2,1)S(1)}, bf16[2,64,2048]{2,1,0:T(8,128)(2,1)S(1)}, u32[]{:S(2)}, u32[]{:S(2)}) collective-permute-start(bf16[2,64,2048]{2,1,0:T(8,128)(2,1)S(1)} %copy-done.39), channel_id=1, source_target_pairs={{0,8},{8,0},{16,24},{24,16},{1,9},{9,1},{17,25},{25,17},{2,10},{10... | collective-permute-start | bytes 1572872 | tf_op jit(solution)/shard_map/ppermute | solution.py:248
  506.8 28.9 %collective-permute-start.52 = (bf16[4,64,2432]{2,1,0:T(8,128)(2,1)}, bf16[4,64,2432]{2,1,0:T(8,128)(2,1)S(1)}, u32[]{:S(2)}, u32[]{:S(2)}) collective-permute-start(bf16[4,64,2432]{2,1,0:T(8,128)(2,1)} %get-tuple-element.240), channel_id=1, source_target_pairs={{0,8},{8,0},{16,24},{24,16},{1,9},{9,1},{17,25},{25,17},{2,10},{10... | collective-permute-start | bytes 3735560 | tf_op jit(solution)/shard_map/ppermute | solution.py:248
  507.3 28.5 %collective-permute-start.53 = (bf16[4,64,2432]{2,1,0:T(8,128)(2,1)}, bf16[4,64,2432]{2,1,0:T(8,128)(2,1)S(1)}, u32[]{:S(2)}, u32[]{:S(2)}) collective-permute-start(bf16[4,64,2432]{2,1,0:T(8,128)(2,1)} %get-tuple-element.241), channel_id=1, source_target_pairs={{0,16},{8,24},{16,0},{24,8},{1,17},{9,25},{17,1},{25,9},{2,18},{10... | collective-permute-start | bytes 3735560 | tf_op jit(solution)/shard_map/ppermute | solution.py:248
  540.1 17.2 %collective-permute-start.55 = (bf16[2,64,2432]{2,1,0:T(8,128)(2,1)}, bf16[2,64,2432]{2,1,0:T(8,128)(2,1)S(1)}, u32[]{:S(2)}, u32[]{:S(2)}) collective-permute-start(bf16[2,64,2432]{2,1,0:T(8,128)(2,1)} %get-tuple-element.251), channel_id=1, source_target_pairs={{0,8},{8,0},{16,24},{24,16},{1,9},{9,1},{17,25},{25,17},{2,10},{10... | collective-permute-start | bytes 1867784 | tf_op jit(solution)/shard_map/ppermute | solution.py:248
  541.5 22.0 %collective-permute-start.57 = (bf16[2,64,2048]{2,1,0:T(8,128)(2,1)}, bf16[2,64,2048]{2,1,0:T(8,128)(2,1)S(1)}, u32[]{:S(2)}, u32[]{:S(2)}) collective-permute-start(bf16[2,64,2048]{2,1,0:T(8,128)(2,1)} %add.66), channel_id=1, source_target_pairs={{0,2},{1,3},{2,0},{3,1},{4,6},{5,7},{6,4},{7,5},{8,10},{9,11},{10,... | collective-permute-start | bytes 1572872 | tf_op jit(solution)/shard_map/ppermute | solution.py:253
  541.5 39.8 %collective-permute-start.50 = (bf16[1,192,2048]{2,1,0:T(8,128)(2,1)}, bf16[1,192,2048]{2,1,0:T(8,128)(2,1)S(1)}, u32[]{:S(2)}, u32[]{:S(2)}) collective-permute-start(bf16[1,192,2048]{2,1,0:T(8,128)(2,1)} %get-tuple-element.244), channel_id=1, source_target_pairs={{0,16},{8,24},{16,0},{24,8},{1,17},{9,25},{17,1},{25,9},{2,18},{10... | collective-permute-start | bytes 2359304 | tf_op jit(solution)/shard_map/ppermute | solution.py:248
  542.9 39.4 %collective-permute-start.51 = (bf16[1,192,2048]{2,1,0:T(8,128)(2,1)}, bf16[1,192,2048]{2,1,0:T(8,128)(2,1)}, u32[]{:S(2)}, u32[]{:S(2)}) collective-permute-start(bf16[1,192,2048]{2,1,0:T(8,128)(2,1)} %get-tuple-element.245), channel_id=1, source_target_pairs={{0,8},{8,0},{16,24},{24,16},{1,9},{9,1},{17,25},{25,17},{2,10},{10... | collective-permute-start | bytes 2359304 | tf_op jit(solution)/shard_map/ppermute | solution.py:248
  543.6 33.6 %collective-permute-start.54 = (bf16[2,64,2432]{2,1,0:T(8,128)(2,1)}, bf16[2,64,2432]{2,1,0:T(8,128)(2,1)S(1)}, u32[]{:S(2)}, u32[]{:S(2)}) collective-permute-start(bf16[2,64,2432]{2,1,0:T(8,128)(2,1)} %get-tuple-element.250), channel_id=1, source_target_pairs={{0,16},{8,24},{16,0},{24,8},{1,17},{9,25},{17,1},{25,9},{2,18},{10... | collective-permute-start | bytes 1867784 | tf_op jit(solution)/shard_map/ppermute | solution.py:248
  560.8 14.2 %collective-permute-start.56 = (bf16[2,64,2432]{2,1,0:T(8,128)(2,1)}, bf16[2,64,2432]{2,1,0:T(8,128)(2,1)S(1)}, u32[]{:S(2)}, u32[]{:S(2)}) collective-permute-start(bf16[2,64,2432]{2,1,0:T(8,128)(2,1)} %add.70), channel_id=1, source_target_pairs={{0,2},{1,3},{2,0},{3,1},{4,6},{5,7},{6,4},{7,5},{8,10},{9,11},{10,... | collective-permute-start | bytes 1867784 | tf_op jit(solution)/shard_map/ppermute | solution.py:253
  564.3 21.0 %collective-permute-start.59 = (bf16[2,64,1408]{2,1,0:T(8,128)(2,1)}, bf16[2,64,1408]{2,1,0:T(8,128)(2,1)S(1)}, u32[]{:S(2)}, u32[]{:S(2)}) collective-permute-start(bf16[2,64,1408]{2,1,0:T(8,128)(2,1)} %pad_maximum_fusion.3), channel_id=1, source_target_pairs={{0,8},{8,0},{16,24},{24,16},{1,9},{9,1},{17,25},{25,17},{2,10},{10... | collective-permute-start | bytes 1081352 | tf_op jit(solution)/shard_map/ppermute | solution.py:248
  574.9 18.8 %collective-permute-start.62 = (bf16[1,64,2048]{2,1,0:T(8,128)(2,1)}, bf16[1,64,2048]{2,1,0:T(8,128)(2,1)S(1)}, u32[]{:S(2)}, u32[]{:S(2)}) collective-permute-start(bf16[1,64,2048]{2,1,0:T(8,128)(2,1)} %add.71), channel_id=1, source_target_pairs={{0,4},{1,5},{2,6},{3,7},{4,0},{5,1},{6,2},{7,3},{8,12},{9,13},{10,... | collective-permute-start | bytes 786440 | tf_op jit(solution)/shard_map/ppermute | solution.py:253
  577.2 13.5 %collective-permute-start.60 = (bf16[2,64,1408]{2,1,0:T(8,128)(2,1)}, bf16[2,64,1408]{2,1,0:T(8,128)(2,1)S(1)}, u32[]{:S(2)}, u32[]{:S(2)}) collective-permute-start(bf16[2,64,1408]{2,1,0:T(8,128)(2,1)} %pad_maximum_fusion.4), channel_id=1, source_target_pairs={{0,16},{8,24},{16,0},{24,8},{1,17},{9,25},{17,1},{25,9},{2,18},{10... | collective-permute-start | bytes 1081352 | tf_op jit(solution)/shard_map/ppermute | solution.py:248
  581.3 9.4 %collective-permute-start.61 = (bf16[2,64,1408]{2,1,0:T(8,128)(2,1)}, bf16[2,64,1408]{2,1,0:T(8,128)(2,1)S(1)}, u32[]{:S(2)}, u32[]{:S(2)}) collective-permute-start(bf16[2,64,1408]{2,1,0:T(8,128)(2,1)} %pad_maximum_fusion.5), channel_id=1, source_target_pairs={{0,24},{8,16},{16,8},{24,0},{1,25},{9,17},{17,9},{25,1},{2,26},{10... | collective-permute-start | bytes 1081352 | tf_op jit(solution)/shard_map/ppermute | solution.py:248
  582.3 31.2 %collective-permute-start.58 = (bf16[1,64,2432]{2,1,0:T(8,128)(2,1)}, bf16[1,64,2432]{2,1,0:T(8,128)(2,1)S(1)}, u32[]{:S(2)}, u32[]{:S(2)}) collective-permute-start(bf16[1,64,2432]{2,1,0:T(8,128)(2,1)} %add.72), channel_id=1, source_target_pairs={{0,4},{1,5},{2,6},{3,7},{4,0},{5,1},{6,2},{7,3},{8,12},{9,13},{10,... | collective-permute-start | bytes 933896 | tf_op jit(solution)/shard_map/ppermute | solution.py:253
  (44 other events, 278.2 us)
Sparse Core Ops, SparseCore 0:
  94.8 160.1 all-gather.2
  371.5 56.4 reduce-scatter.3
  432.3 55.8 reduce-scatter.5
  490.9 56.5 reduce-scatter.7

commit v5 on v4

--- a/solution.py
+++ b/solution.py
@@ -611,8 +611,8 @@
 def ffn_all_kernel(spot, *refs):
     ins, held_in = (refs[:5], refs[5:10]), refs[10]
     wholes, (hidden, grad_gate, grad_up, sums, out) = refs[11:13], refs[13:18]
-    sent_a, sent_b = refs[18:20]
-    gate_w, up_w, down_w, tiles, grad_tile, out_tile, sems, in_sems, out_sems = refs[20:]
+    sent_a, sent_b, out_a, out_b = refs[18:22]
+    gate_w, up_w, down_w, tiles, grad_tile, out_tile, sems, in_sems, out_sems = refs[22:]
     count, f_size, rows, units = gate_w.shape
     step = pl.program_id(0)
     first = step == 0
@@ -716,10 +716,12 @@
     @pl.when(step < 2)
     def _():
         sent_a[0] = grad_tile[:half]
+        out_a[0] = out_tile[:half]
 
     @pl.when((step > 0) & (step < 3))
     def _():
         sent_b[0] = grad_tile[half:]
+        out_b[0] = out_tile[half:]
 
     @pl.when(step == 3)
     def _():
@@ -743,7 +745,8 @@
         ffn_all_kernel,
         grid=(4,),
         in_specs=[SMEM] + [ANY] * 11,
-        out_specs=[ANY, ANY, inner, inner, inner, sums, sums, sent(0), sent(1)],
+        out_specs=[ANY, ANY, inner, inner, inner, sums, sums]
+        + [sent(0), sent(1)] * 2,
         scratch_shapes=[
             weights,
             weights,
@@ -758,7 +761,7 @@
         out_shape=[jax.ShapeDtypeStruct((total, width), BF16)] * 2
         + [jax.ShapeDtypeStruct((total, units), BF16)] * 3
         + [jax.ShapeDtypeStruct((2, 4, half, width), BF16)] * 2
-        + [jax.ShapeDtypeStruct((2, half, width), BF16)] * 2,
+        + [jax.ShapeDtypeStruct((2, half, width), BF16)] * 4,
         name="ffn_all",
         **limits(12 * total * width * units, 6 * width * units + 8 * total * width),
     )(spot, *normed, *cot, held_in)
@@ -1366,7 +1369,7 @@
     tokens2, cots, hidden, grad_gate, grad_up, grad_terms, out_terms, *grads_sent = ffn_all(
         spot, normed2_all, cot, units_all, t_size, w_down.shape[0]
     )
-    normed2_sum = TokenSum(grad_terms, grads_sent)
+    normed2_sum = TokenSum(grad_terms, grads_sent[:2])
     down = LineSum(*down_grads(spot, [hidden], [cots]))
     gate = LineSum(*unit_grads(spot, [after(tokens2, down.mine)], [grad_gate]))
     down.other = after(down.other, gate.mine)
@@ -1377,7 +1380,7 @@
     grad_resid, grad_branch, grad_gain_ffn = branch(
         after(resid, up.mine), out_grad, gains_full, normed2_sum.parts()
     )
-    out_sum = TokenSum(after(out_terms, grad_branch))
+    out_sum = TokenSum(out_terms, after(grads_sent[2:], grad_branch))
 
     output = RowSum(*row_grads(spot, attended, after(grad_branch, *out_sum.sent), width))
     grad_attended = leave_back(spot, after(grad_branch, output.mine), output_pieces)

time: 633 us -> 630 us (level)
    pallas_call x14 -> x13, Pallas kernels: 46.5 us -> 43.2 us  [add(): pl.pallas_call(functools.partial(add_kernel, [len(job) for job in jobs]),...]
  transfers between devices with their start and end apart: 67 -> 67, of which waited for: 25 -> 25; matrix products, arithmetic and copies ran while one was open for 2% -> 2% of each run, Pallas kernels for 38% -> 37%
where the time goes in v5:
time: 630 us; the launch traced here: 625 us
  Pallas kernels  315 us (50%)
  waiting for transfers between devices  207 us (33%)
  starting transfers between devices  59.8 us (9%)
  local copies, waits for them, and re-layouts  15.8 us (3%)
  between operations  14.5 us (2%)
  other arithmetic  12.7 us (2%)
    ppermute x38, waiting for transfers between devices, dp_swap(): return lax.ppermute(value, 'dp', [(i, i ^ k) for i in range(size)])  164 us
    pallas_call x1, Pallas kernels, ffn_all(): pl.pallas_call(ffn_all_kernel, grid=(4,), in_specs=[SMEM] + [ANY] * 11, o...  73.9 us
    pallas_call x13, Pallas kernels, add(): pl.pallas_call(functools.partial(add_kernel, [len(job) for job in jobs]),...  43.2 us
    ppermute x38, starting transfers between devices, dp_swap(): return lax.ppermute(value, 'dp', [(i, i ^ k) for i in range(size)])  41.9 us
    ppermute x10, waiting for transfers between devices, z_swap(): return lax.ppermute(value, 'fsdp', [(i, i ^ 2 * k) for i in range(size)])  39.7 us
    pallas_call x2, Pallas kernels, unit_grads(): pl.pallas_call(line_grads_kernel, grid_spec=pltpu.PrefetchScalarGridSpec(...  31.1 us
    pallas_call x1, Pallas kernels, attend_back(): pl.pallas_call(functools.partial(attend_back_kernel, head_dim ** (-0.5),...  19.9 us
    pallas_call x2, Pallas kernels, row_grads(): pl.pallas_call(row_grads_kernel, grid_spec=pltpu.PrefetchScalarGridSpec(n...  19.8 us
  transfers between devices with their start and end apart: 67, of which 25 were waited for; matrix products, arithmetic and copies ran while one was open for 2% of the time, Pallas kernels for 37%

profile of v5, /device:TPU:0, one launch (start us, length us, event | category | flops | bytes accessed | tf_op | source)
XLA Modules:
  0.0 624.9 jit_solution(14451811842922091330)
XLA Ops:
  7.9 3.8 slices.1
  11.7 2.9 collective-permute-start.6
  16.9 2.6 collective-permute-start
  23.1 10.6 %collective-permute-done = bf16[64,2432]{1,0:T(8,128)(2,1)} collective-permute-done((bf16[64,2432]{1,0:T(8,128)(2,1)}, bf16[64,2432]{1,0:T(8,128)(2,1)}, u32[]{:S(2)}, u32[]{:S(2)}) %collective-permute-start) | collective-permute-done | bytes 311328 | tf_op jit(solution)/shard_map/ppermute | solution.py:253
  34.3 4.0 collective-permute-done.7
  38.6 3.5 collective-permute-done.2
  45.5 3.4 collective-permute-start.3
  48.9 11.0 %collective-permute-done.3 = bf16[64,2048]{1,0:T(8,128)(2,1)S(1)} collective-permute-done((bf16[64,2048]{1,0:T(8,128)(2,1)S(1)}, bf16[64,2048]{1,0:T(8,128)(2,1)S(1)}, u32[]{:S(2)}, u32[]{:S(2)}) %collective-permute-start.3) | collective-permute-done | bytes 262176 | tf_op jit(solution)/shard_map/ppermute | solution.py:253
  62.0 7.2 %collective-permute-done.5 = bf16[64,2048]{1,0:T(8,128)(2,1)S(1)} collective-permute-done((bf16[64,2048]{1,0:T(8,128)(2,1)S(1)}, bf16[64,2048]{1,0:T(8,128)(2,1)S(1)}, u32[]{:S(2)}, u32[]{:S(2)}) %collective-permute-start.5) | collective-permute-done | bytes 262176 | tf_op jit(solution)/shard_map/ppermute | solution.py:253
  69.2 2.0 collective-permute-done.9.whole.refs_1_
  72.2 1.9 cut.8
  75.7 1.8 cut.9
  79.8 8.2 %collective-permute-done.11.refs_3_ = bf16[2,64,2432]{2,1,0:T(8,128)(2,1)} collective-permute-done((bf16[2,64,2432]{2,1,0:T(8,128)(2,1)}, bf16[2,64,2432]{2,1,0:T(8,128)(2,1)}, u32[]{:S(2)}, u32[]{:S(2)}) %collective-permute-start.11) | collective-permute-done | bytes 622624 | tf_op jit(solution)/shard_map/ppermute | solution.py:248
  88.1 3.0 collective-permute-done.12.refs_4_
  99.5 10.6 %enter.1 = (f32[384,2304]{1,0:T(8,128)}, bf16[384,2048]{1,0:T(8,128)(2,1)}, f32[8,2048]{1,0:T(8,128)}) custom-call(s32[3]{0:T(128)} %pad_add_fusion.spot, bf16[384,2048]{1,0:T(8,128)(2,1)} %tokens.4, bf16[4,64,2432]{2,1,0:T(8,128)(2,1)} %copy-done.14, bf16[4,64,2432]{2,1,0:T(8,128)(2,1)} %copy-done.16, ...), custom_call_target="tpu_custom_call" | custom-call | flops 144955146240 | bytes 377487360 | tf_op jit(solution)/shard_map/enter/pallas_call | solution.py:519
  110.1 15.2 %attend.1 = (bf16[384,2048]{1,0:T(8,128)(2,1)}, bf16[384,2048]{1,0:T(8,128)(2,1)}, bf16[384,256]{1,0:T(8,128)(2,1)}) custom-call(f32[384,2304]{1,0:T(8,128)} %get-tuple-element.173.q_raw.k_raw.v_raw, f32[384,2304]{1,0:T(8,128)} %get-tuple-element.173.q_raw.k_raw.v_raw, f32[384,2304]{1,0:T(8,128)} %get-tuple-element.173.q_raw.k_raw.v_raw, ...), custom_call_target="tpu_custom_call" | custom-call | flops 72477573120 | bytes 314572800 | tf_op jit(solution)/shard_map/attend/pallas_call | solution.py:102
  130.0 36.5 %collective-permute-done.22.refs_3_ = bf16[2,64,2048]{2,1,0:T(8,128)(2,1)} collective-permute-done((bf16[2,64,2048]{2,1,0:T(8,128)(2,1)}, bf16[2,64,2048]{2,1,0:T(8,128)(2,1)}, u32[]{:S(2)}, u32[]{:S(2)}) %collective-permute-start.22) | collective-permute-done | bytes 524320 | tf_op jit(solution)/shard_map/ppermute | solution.py:248
  167.5 1.9 cut.10
  169.4 2.0 cut.11
  174.8 9.8 %leave.1 = (f32[384,2048]{1,0:T(8,128)}, bf16[384,2048]{1,0:T(8,128)(2,1)}) custom-call(s32[3]{0:T(128)} %pad_add_fusion.spot, bf16[384,2048]{1,0:T(8,128)(2,1)} %get-tuple-element.176.attended.left, bf16[384,2048]{1,0:T(8,128)(2,1)} %tokens.4, f32[8,2048]{1,0:T(8,128)} %get-tuple-element.177.gains, bf16[4,64,2048]{2,1,0:T(8,128)(2,1)} %pad_maximum_fusion.1.refs_0_, ...), custom_call_target="tpu_custom_call" | custom-call | flops 128849018880 | bytes 335544320 | tf_op jit(solution)/shard_map/leave/pallas_call | solution.py:546
  184.7 6.5 %collective-permute-done.29.refs_8_ = bf16[192,2048]{1,0:T(8,128)(2,1)} collective-permute-done((bf16[192,2048]{1,0:T(8,128)(2,1)S(1)}, bf16[192,2048]{1,0:T(8,128)(2,1)}, u32[]{:S(2)}, u32[]{:S(2)}) %collective-permute-start.29) | collective-permute-done | bytes 786464 | tf_op jit(solution)/shard_map/ppermute | solution.py:248
  194.6 32.4 %collective-permute-done.31.whole.refs_1_ = bf16[384,2048]{1,0:T(8,128)(2,1)S(1)} collective-permute-done((bf16[384,2048]{1,0:T(8,128)(2,1)}, bf16[384,2048]{1,0:T(8,128)(2,1)S(1)}, u32[]{:S(2)}, u32[]{:S(2)}) %collective-permute-start.31) | collective-permute-done | bytes 1572896 | tf_op jit(solution)/shard_map/ppermute | solution.py:248
  228.3 1.9 cut.14
  232.8 1.9 cut.15
  236.2 11.7 %collective-permute-done.33.refs_3_ = bf16[192,2048]{1,0:T(8,128)(2,1)S(1)} collective-permute-done((bf16[192,2048]{1,0:T(8,128)(2,1)}, bf16[192,2048]{1,0:T(8,128)(2,1)S(1)}, u32[]{:S(2)}, u32[]{:S(2)}) %collective-permute-start.33) | collective-permute-done | bytes 786464 | tf_op jit(solution)/shard_map/ppermute | solution.py:248
  247.9 4.3 collective-permute-done.34.refs_4_
  252.2 2.9 all-gather.3.cloned.1.call-done
  255.1 73.9 %ffn_all.1 = (bf16[1536,2048]{1,0:T(8,128)(2,1)}, bf16[1536,2048]{1,0:T(8,128)(2,1)}, bf16[1536,1408]{1,0:T(8,128)(2,1)}, bf16[1536,1408]{1,0:T(8,128)(2,1)}, bf...) custom-call(s32[3]{0:T(128)} %pad_add_fusion.spot, ...), custom_call_target="tpu_custom_call" | custom-call | flops 2126008811520 | bytes 1698693120 | tf_op jit(solution)/shard_map/ffn_all/pallas_call | solution.py:744
  332.0 14.9 %down_grads.1 = (bf16[4,176,2048]{2,1,0:T(8,128)(2,1)}, bf16[4,176,2048]{2,1,0:T(8,128)(2,1)}) custom-call(s32[3]{0:T(128)} %pad_add_fusion.spot, bf16[1536,1408]{1,0:T(8,128)(2,1)} %get-tuple-element.192.refs_0_, bf16[1536,2048]{1,0:T(8,128)(2,1)} %get-tuple-element.193.refs_1_), custom_call_target="tpu_custom_call" | custom-call | flops 354334801920 | bytes 655360000 | tf_op jit(solution)/shard_map/down_grads/pallas_call | solution.py:1065
  346.8 15.5 %unit_grads.2 = (bf16[4,4,64,1408]{3,2,1,0:T(8,128)(2,1)}, bf16[4,4,64,1408]{3,2,1,0:T(8,128)(2,1)}) custom-call(s32[3]{0:T(128)} %pad_add_fusion.spot, bf16[1536,2048]{1,0:T(8,128)(2,1)} %get-tuple-element.204.refs_0_, bf16[1536,1408]{1,0:T(8,128)(2,1)} %get-tuple-element.197.refs_1_), custom_call_target="tpu_custom_call" | custom-call | flops 354334801920 | bytes 655360000 | tf_op jit(solution)/shard_map/unit_grads/pallas_call | solution.py:1042
  362.9 4.9 add.58
  367.8 3.2 add.59
  372.4 15.5 %unit_grads.3 = (bf16[4,4,64,1408]{3,2,1,0:T(8,128)(2,1)}, bf16[4,4,64,1408]{3,2,1,0:T(8,128)(2,1)}) custom-call(s32[3]{0:T(128)} %pad_add_fusion.spot, bf16[1536,2048]{1,0:T(8,128)(2,1)} %get-tuple-element.204.refs_0_, bf16[1536,1408]{1,0:T(8,128)(2,1)} %get-tuple-element.205.refs_1_), custom_call_target="tpu_custom_call" | custom-call | flops 354334801920 | bytes 655360000 | tf_op jit(solution)/shard_map/unit_grads/pallas_call | solution.py:1042
  387.9 2.8 collective-permute-done.38.refs_2_
  391.0 8.7 %branch.1 = (f32[384,2048]{1,0:T(8,128)}, bf16[384,2048]{1,0:T(8,128)(2,1)}, f32[8,2048]{1,0:T(8,128)}) custom-call(f32[384,2048]{1,0:T(8,128)} %get-tuple-element.207.resid, bf16[384,2048]{1,0:T(8,128)(2,1)} %cot.1, f32[8,2048]{1,0:T(8,128)} %get-tuple-element.177.gains, bf16[8,192,2048]{2,1,0:T(8,128)(2,1)} %bitcast.61, ...), custom_call_target="tpu_custom_call" | custom-call | bytes 566231040 | tf_op jit(solution)/shard_map/branch/pallas_call | solution.py:871
  401.8 9.4 %row_grads.2 = (bf16[2,4,2,64,2048]{4,3,2,1,0:T(8,128)(2,1)}, bf16[2,4,2,64,2048]{4,3,2,1,0:T(8,128)(2,1)}) custom-call(s32[3]{0:T(128)} %pad_add_fusion.spot, bf16[384,2048]{1,0:T(8,128)(2,1)} %get-tuple-element.176.attended.left, bf16[384,2048]{1,0:T(8,128)(2,1)} %get-tuple-element.215.right.grads), custom_call_target="tpu_custom_call" | custom-call | flops 128849018880 | bytes 461373440 | tf_op jit(solution)/shard_map/row_grads/pallas_call | solution.py:940
  411.2 8.4 %leave_back.1.grad_ref = bf16[384,2048]{1,0:T(8,128)(2,1)} custom-call(s32[3]{0:T(128)} %pad_add_fusion.spot, bf16[384,2048]{1,0:T(8,128)(2,1)} %get-tuple-element.215.right.grads, bf16[4,64,2048]{2,1,0:T(8,128)(2,1)} %pad_maximum_fusion.1.refs_0_, bf16[4,64,2048]{2,1,0:T(8,128)(2,1)} %collective-permute-done.20.whole.refs_1_, ...), custom_call_target="tpu_custom_call" | custom-call | flops 128849018880 | bytes 335544320 | tf_op jit(solution)/shard_map/leave_back/pallas_call | solution.py:569
  419.6 3.4 add.60
  424.9 4.9 add.61
  429.9 19.9 %attend_back.1.grads.right = bf16[384,2432]{1,0:T(8,128)(2,1)} custom-call(bf16[384,2048]{1,0:T(8,128)(2,1)} %get-tuple-element.219.query_ref, bf16[384,2048]{1,0:T(8,128)(2,1)} %leave_back.1.grad_ref, bf16[384,256]{1,0:T(8,128)(2,1)} %get-tuple-element.222.shared, bf16[384,256]{1,0:T(8,128)(2,1)} %kv_next.1, f32[384,128]{1,0:T(8,128)} %get-tuple-element.402.cosine, ...), custom_call_target="tpu_custom_call" | custom-call | flops 169114337280 | bytes 251658240 | tf_op jit(solution)/shard_map/attend_back/pallas_call | solution.py:180
  449.8 13.0 %enter_back.1 = (f32[384,2048]{1,0:T(8,128)}, f32[8,2048]{1,0:T(8,128)}) custom-call(s32[3]{0:T(128)} %pad_add_fusion.spot, bf16[384,2432]{1,0:T(8,128)(2,1)} %attend_back.1.grads.right, bf16[384,2048]{1,0:T(8,128)(2,1)} %tokens.4, f32[8,2048]{1,0:T(8,128)} %get-tuple-element.177.gains, f32[384,2048]{1,0:T(8,128)} %get-tuple-element.223.grad_resid, ...), custom_call_target="tpu_custom_call" | custom-call | flops 128849018880 | bytes 335544320 | tf_op jit(solution)/shard_map/enter_back/pallas_call | solution.py:594
  462.9 2.8 add.62
  465.6 10.4 %row_grads.3 = (bf16[2,4,2,64,2432]{4,3,2,1,0:T(8,128)(2,1)}, bf16[2,4,2,64,2432]{4,3,2,1,0:T(8,128)(2,1)}) custom-call(s32[3]{0:T(128)} %pad_add_fusion.spot, bf16[384,2048]{1,0:T(8,128)(2,1)} %get-tuple-element.232.left, bf16[384,2432]{1,0:T(8,128)(2,1)} %attend_back.1.grads.right, f32[8,2048]{1,0:T(8,128)} %get-tuple-element.233.refs_0_, ...), custom_call_target="tpu_custom_call" | custom-call | flops 153008209920 | bytes 536084480 | tf_op jit(solution)/shard_map/row_grads/pallas_call | solution.py:940
  476.1 4.9 add.63
  484.1 12.2 %collective-permute-done.47.refs_3_ = bf16[2,64,2048]{2,1,0:T(8,128)(2,1)S(1)} collective-permute-done((bf16[2,64,2048]{2,1,0:T(8,128)(2,1)S(1)}, bf16[2,64,2048]{2,1,0:T(8,128)(2,1)S(1)}, u32[]{:S(2)}, u32[]{:S(2)}) %collective-permute-start.47) | collective-permute-done | bytes 524320 | tf_op jit(solution)/shard_map/ppermute | solution.py:248
  498.4 2.3 add.64
  500.7 3.7 add.65
  505.6 3.2 add.66
  508.7 4.9 update_rows.3
  513.6 19.6 %collective-permute-done.52.refs_2_ = bf16[4,64,2432]{2,1,0:T(8,128)(2,1)S(1)} collective-permute-done((bf16[4,64,2432]{2,1,0:T(8,128)(2,1)}, bf16[4,64,2432]{2,1,0:T(8,128)(2,1)S(1)}, u32[]{:S(2)}, u32[]{:S(2)}) %collective-permute-start.52) | collective-permute-done | bytes 1245216 | tf_op jit(solution)/shard_map/ppermute | solution.py:248
  534.7 3.0 add.67
  542.3 12.6 %collective-permute-done.55.refs_3_ = bf16[2,64,2432]{2,1,0:T(8,128)(2,1)S(1)} collective-permute-done((bf16[2,64,2432]{2,1,0:T(8,128)(2,1)}, bf16[2,64,2432]{2,1,0:T(8,128)(2,1)S(1)}, u32[]{:S(2)}, u32[]{:S(2)}) %collective-permute-start.55) | collective-permute-done | bytes 622624 | tf_op jit(solution)/shard_map/ppermute | solution.py:248
  555.7 2.6 add.68
  563.3 2.1 add.69
  567.0 4.6 collective-permute-done.56.refs_4_
  571.6 3.9 collective-permute-start.62
  576.7 2.3 add.70
  583.0 5.8 collective-permute-done.60.refs_2_
  588.8 2.7 collective-permute-done.62.refs_5_
  591.6 6.6 %layer_out.1 = f32[384,2048]{1,0:T(8,128)} custom-call(f32[384,2048]{1,0:T(8,128)} %get-tuple-element.207.resid, bf16[8,192,2048]{2,1,0:T(8,128)(2,1)} %bitcast.57, bf16[2,192,2048]{2,1,0:T(8,128)(2,1)} %collective-permute-done.40.refs_1_, bf16[1,192,2048]{2,1,0:T(8,128)(2,1)} %copy-done.18, bf16[8,192,2048]{2,1,0:T(8,128)(2,1)} %bitcast.58, ...), custom_call_target="tpu_custom_call" | custom-call | bytes 440401920 | tf_op jit(solution)/shard_map/layer_out/pallas_call | solution.py:899
  598.2 4.9 update_units.2
  603.1 4.9 update_units.3
  608.1 3.3 update_rows.5
  612.1 3.4 update_rows.4
  (235 shorter events, 81.6 us)
Async XLA Ops:
  7.2 247.9 %all-gather.3.cloned.1.call-start = ((), (), s32[]{:S(2)}) async-start(), calls=%async_computation.6 | async-start | bytes 19869696 | tf_op jit(solution)/shard_map/all_gather | solution.py:1346
  11.7 22.6 %collective-permute-start.6 = (bf16[2,64,1408]{2,1,0:T(8,128)(2,1)}, bf16[2,64,1408]{2,1,0:T(8,128)(2,1)S(1)}, u32[]{:S(2)}, u32[]{:S(2)}) collective-permute-start(bf16[2,64,1408]{2,1,0:T(8,128)(2,1)} %get-tuple-element.166), channel_id=1, source_target_pairs={{0,8},{8,0},{16,24},{24,16},{1,9},{9,1},{17,25},{25,17},{2,10},{10... | collective-permute-start | bytes 1081352 | tf_op jit(solution)/shard_map/ppermute | solution.py:248
  16.9 16.8 %collective-permute-start = (bf16[64,2432]{1,0:T(8,128)(2,1)}, bf16[64,2432]{1,0:T(8,128)(2,1)}, u32[]{:S(2)}, u32[]{:S(2)}) collective-permute-start(bf16[64,2432]{1,0:T(8,128)(2,1)} %get-tuple-element.398), channel_id=1, source_target_pairs={{0,4},{1,5},{2,6},{3,7},{4,0},{5,1},{6,2},{7,3},{8,12},{9,13},{10,... | collective-permute-start | bytes 933896 | tf_op jit(solution)/shard_map/ppermute | solution.py:253
  19.5 19.1 %collective-permute-start.1 = (bf16[64,2432]{1,0:T(8,128)(2,1)}, bf16[64,2432]{1,0:T(8,128)(2,1)}, u32[]{:S(2)}, u32[]{:S(2)}) collective-permute-start(bf16[64,2432]{1,0:T(8,128)(2,1)} %get-tuple-element.398), channel_id=1, source_target_pairs={{0,2},{1,3},{2,0},{3,1},{4,6},{5,7},{6,4},{7,5},{8,10},{9,11},{10,... | collective-permute-start | bytes 933896 | tf_op jit(solution)/shard_map/ppermute | solution.py:253
  21.1 17.2 %collective-permute-start.7 = (bf16[2,64,1408]{2,1,0:T(8,128)(2,1)}, bf16[2,64,1408]{2,1,0:T(8,128)(2,1)S(1)}, u32[]{:S(2)}, u32[]{:S(2)}) collective-permute-start(bf16[2,64,1408]{2,1,0:T(8,128)(2,1)} %get-tuple-element.167), channel_id=1, source_target_pairs={{0,16},{8,24},{16,0},{24,8},{1,17},{9,25},{17,1},{25,9},{2,18},{10... | collective-permute-start | bytes 1081352 | tf_op jit(solution)/shard_map/ppermute | solution.py:248
  22.6 15.8 %collective-permute-start.8 = (bf16[2,64,1408]{2,1,0:T(8,128)(2,1)}, bf16[2,64,1408]{2,1,0:T(8,128)(2,1)S(1)}, u32[]{:S(2)}, u32[]{:S(2)}) collective-permute-start(bf16[2,64,1408]{2,1,0:T(8,128)(2,1)} %get-tuple-element.168), channel_id=1, source_target_pairs={{0,24},{8,16},{16,8},{24,0},{1,25},{9,17},{17,9},{25,1},{2,26},{10... | collective-permute-start | bytes 1081352 | tf_op jit(solution)/shard_map/ppermute | solution.py:248
  33.7 8.4 %collective-permute-start.2 = (bf16[64,2432]{1,0:T(8,128)(2,1)}, bf16[64,2432]{1,0:T(8,128)(2,1)S(1)}, u32[]{:S(2)}, u32[]{:S(2)}) collective-permute-start(bf16[64,2432]{1,0:T(8,128)(2,1)} %collective-permute-done), channel_id=1, source_target_pairs={{0,2},{1,3},{2,0},{3,1},{4,6},{5,7},{6,4},{7,5},{8,10},{9,11},{10,... | collective-permute-start | bytes 933896 | tf_op jit(solution)/shard_map/ppermute | solution.py:253
  43.3 27.8 %collective-permute-start.9 = (bf16[4,64,2432]{2,1,0:T(8,128)(2,1)S(1)}, bf16[4,64,2432]{2,1,0:T(8,128)(2,1)S(1)}, u32[]{:S(2)}, u32[]{:S(2)}) collective-permute-start(bf16[4,64,2432]{2,1,0:T(8,128)(2,1)S(1)} %pad_maximum_fusion.refs_0_), channel_id=1, source_target_pairs={{0,8},{8,0},{16,24},{24,16},{1,9},{9,1},{17,25},{25,17},{2,10},{10... | collective-permute-start | bytes 3735560 | tf_op jit(solution)/shard_map/ppermute | solution.py:248
  43.9 28.3 %collective-permute-start.10 = (bf16[4,64,2432]{2,1,0:T(8,128)(2,1)S(1)}, bf16[4,64,2432]{2,1,0:T(8,128)(2,1)}, u32[]{:S(2)}, u32[]{:S(2)}) collective-permute-start(bf16[4,64,2432]{2,1,0:T(8,128)(2,1)S(1)} %pad_maximum_fusion.refs_0_), channel_id=1, source_target_pairs={{0,16},{8,24},{16,0},{24,8},{1,17},{9,25},{17,1},{25,9},{2,18},{10... | collective-permute-start | bytes 3735560 | tf_op jit(solution)/shard_map/ppermute | solution.py:248
  45.5 14.4 %collective-permute-start.3 = (bf16[64,2048]{1,0:T(8,128)(2,1)S(1)}, bf16[64,2048]{1,0:T(8,128)(2,1)S(1)}, u32[]{:S(2)}, u32[]{:S(2)}) collective-permute-start(bf16[64,2048]{1,0:T(8,128)(2,1)S(1)} %convert_element_type.22), channel_id=1, source_target_pairs={{0,4},{1,5},{2,6},{3,7},{4,0},{5,1},{6,2},{7,3},{8,12},{9,13},{10,... | collective-permute-start | bytes 786440 | tf_op jit(solution)/shard_map/ppermute | solution.py:253
  59.9 9.3 %collective-permute-start.5 = (bf16[64,2048]{1,0:T(8,128)(2,1)S(1)}, bf16[64,2048]{1,0:T(8,128)(2,1)S(1)}, u32[]{:S(2)}, u32[]{:S(2)}) collective-permute-start(bf16[64,2048]{1,0:T(8,128)(2,1)S(1)} %collective-permute-done.3), channel_id=1, source_target_pairs={{0,2},{1,3},{2,0},{3,1},{4,6},{5,7},{6,4},{7,5},{8,10},{9,11},{10,... | collective-permute-start | bytes 786440 | tf_op jit(solution)/shard_map/ppermute | solution.py:253
  60.6 18.2 %collective-permute-start.4 = (bf16[64,2048]{1,0:T(8,128)(2,1)S(1)}, bf16[64,2048]{1,0:T(8,128)(2,1)S(1)}, u32[]{:S(2)}, u32[]{:S(2)}) collective-permute-start(bf16[64,2048]{1,0:T(8,128)(2,1)S(1)} %convert_element_type.22), channel_id=1, source_target_pairs={{0,2},{1,3},{2,0},{3,1},{4,6},{5,7},{6,4},{7,5},{8,10},{9,11},{10,... | collective-permute-start | bytes 786440 | tf_op jit(solution)/shard_map/ppermute | solution.py:253
  74.1 13.9 %collective-permute-start.11 = (bf16[2,64,2432]{2,1,0:T(8,128)(2,1)}, bf16[2,64,2432]{2,1,0:T(8,128)(2,1)}, u32[]{:S(2)}, u32[]{:S(2)}) collective-permute-start(bf16[2,64,2432]{2,1,0:T(8,128)(2,1)} %cut.8), channel_id=1, source_target_pairs={{0,16},{8,24},{16,0},{24,8},{1,17},{9,25},{17,1},{25,9},{2,18},{10... | collective-permute-start | bytes 1867784 | tf_op jit(solution)/shard_map/ppermute | solution.py:248
  77.5 13.6 %collective-permute-start.12 = (bf16[2,64,2432]{2,1,0:T(8,128)(2,1)}, bf16[2,64,2432]{2,1,0:T(8,128)(2,1)}, u32[]{:S(2)}, u32[]{:S(2)}) collective-permute-start(bf16[2,64,2432]{2,1,0:T(8,128)(2,1)} %cut.9), channel_id=1, source_target_pairs={{0,8},{8,0},{16,24},{24,16},{1,9},{9,1},{17,25},{25,17},{2,10},{10... | collective-permute-start | bytes 1867784 | tf_op jit(solution)/shard_map/ppermute | solution.py:248
  78.3 18.2 %collective-permute-start.13 = (bf16[4,64,2432]{2,1,0:T(8,128)(2,1)S(1)}, bf16[4,64,2432]{2,1,0:T(8,128)(2,1)}, u32[]{:S(2)}, u32[]{:S(2)}) collective-permute-start(bf16[4,64,2432]{2,1,0:T(8,128)(2,1)S(1)} %copy-done.15), channel_id=1, source_target_pairs={{0,1},{1,0},{2,3},{3,2},{4,5},{5,4},{6,7},{7,6},{8,9},{9,8},{10,11... | collective-permute-start | bytes 3735560 | tf_op jit(solution)/shard_map/ppermute | solution.py:258
  78.3 19.7 %collective-permute-start.14 = (bf16[4,64,2432]{2,1,0:T(8,128)(2,1)S(1)}, bf16[4,64,2432]{2,1,0:T(8,128)(2,1)}, u32[]{:S(2)}, u32[]{:S(2)}) collective-permute-start(bf16[4,64,2432]{2,1,0:T(8,128)(2,1)S(1)} %copy-done.17), channel_id=1, source_target_pairs={{0,1},{1,0},{2,3},{3,2},{4,5},{5,4},{6,7},{7,6},{8,9},{9,8},{10,11... | collective-permute-start | bytes 3735560 | tf_op jit(solution)/shard_map/ppermute | solution.py:258
  79.5 20.0 %collective-permute-start.15 = (bf16[4,64,2432]{2,1,0:T(8,128)(2,1)}, bf16[4,64,2432]{2,1,0:T(8,128)(2,1)}, u32[]{:S(2)}, u32[]{:S(2)}) collective-permute-start(bf16[4,64,2432]{2,1,0:T(8,128)(2,1)} %collective-permute-done.10.whole.refs_2_), channel_id=1, source_target_pairs={{0,1},{1,0},{2,3},{3,2},{4,5},{5,4},{6,7},{7,6},{8,9},{9,8},{10,11... | collective-permute-start | bytes 3735560 | tf_op jit(solution)/shard_map/ppermute | solution.py:258
  88.1 7.3 %collective-permute-start.16 = (bf16[2,64,2432]{2,1,0:T(8,128)(2,1)}, bf16[2,64,2432]{2,1,0:T(8,128)(2,1)}, u32[]{:S(2)}, u32[]{:S(2)}) collective-permute-start(bf16[2,64,2432]{2,1,0:T(8,128)(2,1)} %collective-permute-done.11.refs_3_), channel_id=1, source_target_pairs={{0,1},{1,0},{2,3},{3,2},{4,5},{5,4},{6,7},{7,6},{8,9},{9,8},{10,11... | collective-permute-start | bytes 1867784 | tf_op jit(solution)/shard_map/ppermute | solution.py:258
  94.8 370.9 %reduce-scatter.4.cloned.1.call-start = ((), (), s32[]{:S(2)}) async-start(), calls=%async_computation.3 | async-start | bytes 3604480 | tf_op jit(solution)/shard_map/reduce_scatter | solution.py:1004
  95.4 29.9 %collective-permute-start.20 = (bf16[4,64,2048]{2,1,0:T(8,128)(2,1)}, bf16[4,64,2048]{2,1,0:T(8,128)(2,1)}, u32[]{:S(2)}, u32[]{:S(2)}) collective-permute-start(bf16[4,64,2048]{2,1,0:T(8,128)(2,1)} %pad_maximum_fusion.1.refs_0_), channel_id=1, source_target_pairs={{0,8},{8,0},{16,24},{24,16},{1,9},{9,1},{17,25},{25,17},{2,10},{10... | collective-permute-start | bytes 3145736 | tf_op jit(solution)/shard_map/ppermute | solution.py:248
  96.0 29.4 %collective-permute-start.21 = (bf16[4,64,2048]{2,1,0:T(8,128)(2,1)}, bf16[4,64,2048]{2,1,0:T(8,128)(2,1)}, u32[]{:S(2)}, u32[]{:S(2)}) collective-permute-start(bf16[4,64,2048]{2,1,0:T(8,128)(2,1)} %pad_maximum_fusion.1.refs_0_), channel_id=1, source_target_pairs={{0,16},{8,24},{16,0},{24,8},{1,17},{9,25},{17,1},{25,9},{2,18},{10... | collective-permute-start | bytes 3145736 | tf_op jit(solution)/shard_map/ppermute | solution.py:248
  96.5 70.5 %collective-permute-start.18 = (bf16[384,2048]{1,0:T(8,128)(2,1)}, bf16[384,2048]{1,0:T(8,128)(2,1)}, u32[]{:S(2)}, u32[]{:S(2)}) collective-permute-start(bf16[384,2048]{1,0:T(8,128)(2,1)} %cot.1), channel_id=1, source_target_pairs={{0,8},{8,0},{16,24},{24,16},{1,9},{9,1},{17,25},{25,17},{2,10},{10... | collective-permute-start | bytes 4718600 | tf_op jit(solution)/shard_map/ppermute | solution.py:248
  98.0 69.1 %collective-permute-start.19 = (bf16[384,2048]{1,0:T(8,128)(2,1)}, bf16[384,2048]{1,0:T(8,128)(2,1)}, u32[]{:S(2)}, u32[]{:S(2)}) collective-permute-start(bf16[384,2048]{1,0:T(8,128)(2,1)} %cot.1), channel_id=1, source_target_pairs={{0,16},{8,24},{16,0},{24,8},{1,17},{9,25},{17,1},{25,9},{2,18},{10... | collective-permute-start | bytes 4718600 | tf_op jit(solution)/shard_map/ppermute | solution.py:248
  127.1 39.4 %collective-permute-start.22 = (bf16[2,64,2048]{2,1,0:T(8,128)(2,1)}, bf16[2,64,2048]{2,1,0:T(8,128)(2,1)}, u32[]{:S(2)}, u32[]{:S(2)}) collective-permute-start(bf16[2,64,2048]{2,1,0:T(8,128)(2,1)} %cut.12), channel_id=1, source_target_pairs={{0,16},{8,24},{16,0},{24,8},{1,17},{9,25},{17,1},{25,9},{2,18},{10... | collective-permute-start | bytes 1572872 | tf_op jit(solution)/shard_map/ppermute | solution.py:248
  129.4 37.2 %collective-permute-start.23 = (bf16[2,64,2048]{2,1,0:T(8,128)(2,1)}, bf16[2,64,2048]{2,1,0:T(8,128)(2,1)}, u32[]{:S(2)}, u32[]{:S(2)}) collective-permute-start(bf16[2,64,2048]{2,1,0:T(8,128)(2,1)} %cut.13), channel_id=1, source_target_pairs={{0,8},{8,0},{16,24},{24,16},{1,9},{9,1},{17,25},{25,17},{2,10},{10... | collective-permute-start | bytes 1572872 | tf_op jit(solution)/shard_map/ppermute | solution.py:248
  130.0 41.5 %collective-permute-start.24 = (bf16[4,64,2048]{2,1,0:T(8,128)(2,1)}, bf16[4,64,2048]{2,1,0:T(8,128)(2,1)S(1)}, u32[]{:S(2)}, u32[]{:S(2)}) collective-permute-start(bf16[4,64,2048]{2,1,0:T(8,128)(2,1)} %pad_maximum_fusion.1.refs_0_), channel_id=1, source_target_pairs={{0,1},{1,0},{2,3},{3,2},{4,5},{5,4},{6,7},{7,6},{8,9},{9,8},{10,11... | collective-permute-start | bytes 3145736 | tf_op jit(solution)/shard_map/ppermute | solution.py:258
  166.5 7.0 %collective-permute-start.25 = (bf16[4,64,2048]{2,1,0:T(8,128)(2,1)}, bf16[4,64,2048]{2,1,0:T(8,128)(2,1)S(1)}, u32[]{:S(2)}, u32[]{:S(2)}) collective-permute-start(bf16[4,64,2048]{2,1,0:T(8,128)(2,1)} %collective-permute-done.20.whole.refs_1_), channel_id=1, source_target_pairs={{0,1},{1,0},{2,3},{3,2},{4,5},{5,4},{6,7},{7,6},{8,9},{9,8},{10,11... | collective-permute-start | bytes 3145736 | tf_op jit(solution)/shard_map/ppermute | solution.py:258
  166.5 7.0 %collective-permute-start.26 = (bf16[4,64,2048]{2,1,0:T(8,128)(2,1)}, bf16[4,64,2048]{2,1,0:T(8,128)(2,1)S(1)}, u32[]{:S(2)}, u32[]{:S(2)}) collective-permute-start(bf16[4,64,2048]{2,1,0:T(8,128)(2,1)} %collective-permute-done.21.whole.refs_2_), channel_id=1, source_target_pairs={{0,1},{1,0},{2,3},{3,2},{4,5},{5,4},{6,7},{7,6},{8,9},{9,8},{10,11... | collective-permute-start | bytes 3145736 | tf_op jit(solution)/shard_map/ppermute | solution.py:258
  171.4 19.7 %collective-permute-start.29 = (bf16[192,2048]{1,0:T(8,128)(2,1)S(1)}, bf16[192,2048]{1,0:T(8,128)(2,1)}, u32[]{:S(2)}, u32[]{:S(2)}) collective-permute-start(bf16[192,2048]{1,0:T(8,128)(2,1)S(1)} %copy-done.19), channel_id=1, source_target_pairs={{0,16},{8,24},{16,0},{24,8},{1,17},{9,25},{17,1},{25,9},{2,18},{10... | collective-permute-start | bytes 2359304 | tf_op jit(solution)/shard_map/ppermute | solution.py:248
  172.0 19.6 %collective-permute-start.30 = (bf16[192,2048]{1,0:T(8,128)(2,1)}, bf16[192,2048]{1,0:T(8,128)(2,1)}, u32[]{:S(2)}, u32[]{:S(2)}) collective-permute-start(bf16[192,2048]{1,0:T(8,128)(2,1)} %cut.11), channel_id=1, source_target_pairs={{0,8},{8,0},{16,24},{24,16},{1,9},{9,1},{17,25},{25,17},{2,10},{10... | collective-permute-start | bytes 2359304 | tf_op jit(solution)/shard_map/ppermute | solution.py:248
  191.6 35.4 %collective-permute-start.31 = (bf16[384,2048]{1,0:T(8,128)(2,1)}, bf16[384,2048]{1,0:T(8,128)(2,1)S(1)}, u32[]{:S(2)}, u32[]{:S(2)}) collective-permute-start(bf16[384,2048]{1,0:T(8,128)(2,1)} %get-tuple-element.183.refs_0_), channel_id=1, source_target_pairs={{0,8},{8,0},{16,24},{24,16},{1,9},{9,1},{17,25},{25,17},{2,10},{10... | collective-permute-start | bytes 4718600 | tf_op jit(solution)/shard_map/ppermute | solution.py:248
  193.1 38.6 %collective-permute-start.32 = (bf16[384,2048]{1,0:T(8,128)(2,1)}, bf16[384,2048]{1,0:T(8,128)(2,1)S(1)}, u32[]{:S(2)}, u32[]{:S(2)}) collective-permute-start(bf16[384,2048]{1,0:T(8,128)(2,1)} %get-tuple-element.183.refs_0_), channel_id=1, source_target_pairs={{0,16},{8,24},{16,0},{24,8},{1,17},{9,25},{17,1},{25,9},{2,18},{10... | collective-permute-start | bytes 4718600 | tf_op jit(solution)/shard_map/ppermute | solution.py:248
  230.1 17.8 %collective-permute-start.33 = (bf16[192,2048]{1,0:T(8,128)(2,1)}, bf16[192,2048]{1,0:T(8,128)(2,1)S(1)}, u32[]{:S(2)}, u32[]{:S(2)}) collective-permute-start(bf16[192,2048]{1,0:T(8,128)(2,1)} %cut.14), channel_id=1, source_target_pairs={{0,16},{8,24},{16,0},{24,8},{1,17},{9,25},{17,1},{25,9},{2,18},{10... | collective-permute-start | bytes 2359304 | tf_op jit(solution)/shard_map/ppermute | solution.py:248
  234.7 17.5 %collective-permute-start.34 = (bf16[192,2048]{1,0:T(8,128)(2,1)}, bf16[192,2048]{1,0:T(8,128)(2,1)S(1)}, u32[]{:S(2)}, u32[]{:S(2)}) collective-permute-start(bf16[192,2048]{1,0:T(8,128)(2,1)} %cut.15), channel_id=1, source_target_pairs={{0,8},{8,0},{16,24},{24,16},{1,9},{9,1},{17,25},{25,17},{2,10},{10... | collective-permute-start | bytes 2359304 | tf_op jit(solution)/shard_map/ppermute | solution.py:248
  329.0 38.8 %collective-permute-start.35 = (bf16[2,192,2048]{2,1,0:T(8,128)(2,1)}, bf16[2,192,2048]{2,1,0:T(8,128)(2,1)}, u32[]{:S(2)}, u32[]{:S(2)}) collective-permute-start(bf16[2,192,2048]{2,1,0:T(8,128)(2,1)} %get-tuple-element.190), channel_id=1, source_target_pairs={{0,8},{8,0},{16,24},{24,16},{1,9},{9,1},{17,25},{25,17},{2,10},{10... | collective-permute-start | bytes 4718600 | tf_op jit(solution)/shard_map/ppermute | solution.py:248
  330.5 37.3 %collective-permute-start.36 = (bf16[2,192,2048]{2,1,0:T(8,128)(2,1)}, bf16[2,192,2048]{2,1,0:T(8,128)(2,1)}, u32[]{:S(2)}, u32[]{:S(2)}) collective-permute-start(bf16[2,192,2048]{2,1,0:T(8,128)(2,1)} %get-tuple-element.191), channel_id=1, source_target_pairs={{0,16},{8,24},{16,0},{24,8},{1,17},{9,25},{17,1},{25,9},{2,18},{10... | collective-permute-start | bytes 4718600 | tf_op jit(solution)/shard_map/ppermute | solution.py:248
  346.8 16.0 %collective-permute-start.37 = (bf16[4,176,2048]{2,1,0:T(8,128)(2,1)}, bf16[4,176,2048]{2,1,0:T(8,128)(2,1)}, u32[]{:S(2)}, u32[]{:S(2)}) collective-permute-start(bf16[4,176,2048]{2,1,0:T(8,128)(2,1)} %get-tuple-element.195), channel_id=1, source_target_pairs={{0,1},{1,0},{2,3},{3,2},{4,5},{5,4},{6,7},{7,6},{8,9},{9,8},{10,11... | collective-permute-start | bytes 8650760 | tf_op jit(solution)/shard_map/ppermute | solution.py:258
  362.4 57.2 %collective-permute-start.42 = (bf16[4,4,64,1408]{3,2,1,0:T(8,128)(2,1)}, bf16[4,4,64,1408]{3,2,1,0:T(8,128)(2,1)}, u32[]{:S(2)}, u32[]{:S(2)}) collective-permute-start(bf16[4,4,64,1408]{3,2,1,0:T(8,128)(2,1)} %get-tuple-element.213), channel_id=1, source_target_pairs={{0,1},{1,0},{2,3},{3,2},{4,5},{5,4},{6,7},{7,6},{8,9},{9,8},{10,11... | collective-permute-start | bytes 8650760 | tf_op jit(solution)/shard_map/ppermute | solution.py:258
  370.9 19.8 %collective-permute-start.38 = (bf16[1,192,2048]{2,1,0:T(8,128)(2,1)}, bf16[1,192,2048]{2,1,0:T(8,128)(2,1)}, u32[]{:S(2)}, u32[]{:S(2)}) collective-permute-start(bf16[1,192,2048]{2,1,0:T(8,128)(2,1)} %get-tuple-element.202), channel_id=1, source_target_pairs={{0,16},{8,24},{16,0},{24,8},{1,17},{9,25},{17,1},{25,9},{2,18},{10... | collective-permute-start | bytes 2359304 | tf_op jit(solution)/shard_map/ppermute | solution.py:248
  371.7 19.3 %collective-permute-start.39 = (bf16[1,192,2048]{2,1,0:T(8,128)(2,1)}, bf16[1,192,2048]{2,1,0:T(8,128)(2,1)}, u32[]{:S(2)}, u32[]{:S(2)}) collective-permute-start(bf16[1,192,2048]{2,1,0:T(8,128)(2,1)} %get-tuple-element.203), channel_id=1, source_target_pairs={{0,8},{8,0},{16,24},{24,16},{1,9},{9,1},{17,25},{25,17},{2,10},{10... | collective-permute-start | bytes 2359304 | tf_op jit(solution)/shard_map/ppermute | solution.py:248
  372.3 128.4 %reduce-scatter.6.cloned.1.call-start = ((), (), s32[]{:S(2)}) async-start(), calls=%async_computation.4 | async-start | bytes 3604480 | tf_op jit(solution)/shard_map/reduce_scatter | solution.py:1004
  387.9 88.2 %collective-permute-start.49 = (bf16[4,4,64,1408]{3,2,1,0:T(8,128)(2,1)}, bf16[4,4,64,1408]{3,2,1,0:T(8,128)(2,1)}, u32[]{:S(2)}, u32[]{:S(2)}) collective-permute-start(bf16[4,4,64,1408]{3,2,1,0:T(8,128)(2,1)} %get-tuple-element.237), channel_id=1, source_target_pairs={{0,1},{1,0},{2,3},{3,2},{4,5},{5,4},{6,7},{7,6},{8,9},{9,8},{10,11... | collective-permute-start | bytes 8650760 | tf_op jit(solution)/shard_map/ppermute | solution.py:258
  399.7 63.2 %collective-permute-start.40 = (bf16[2,192,2048]{2,1,0:T(8,128)(2,1)}, bf16[2,192,2048]{2,1,0:T(8,128)(2,1)}, u32[]{:S(2)}, u32[]{:S(2)}) collective-permute-start(bf16[2,192,2048]{2,1,0:T(8,128)(2,1)} %get-tuple-element.209), channel_id=1, source_target_pairs={{0,8},{8,0},{16,24},{24,16},{1,9},{9,1},{17,25},{25,17},{2,10},{10... | collective-permute-start | bytes 4718600 | tf_op jit(solution)/shard_map/ppermute | solution.py:248
  400.3 62.6 %collective-permute-start.41 = (bf16[2,192,2048]{2,1,0:T(8,128)(2,1)}, bf16[2,192,2048]{2,1,0:T(8,128)(2,1)}, u32[]{:S(2)}, u32[]{:S(2)}) collective-permute-start(bf16[2,192,2048]{2,1,0:T(8,128)(2,1)} %get-tuple-element.210), channel_id=1, source_target_pairs={{0,16},{8,24},{16,0},{24,8},{1,17},{9,25},{17,1},{25,9},{2,18},{10... | collective-permute-start | bytes 4718600 | tf_op jit(solution)/shard_map/ppermute | solution.py:248
  411.2 8.5 %collective-permute-start.43 = (bf16[2,4,2,64,2048]{4,3,2,1,0:T(8,128)(2,1)}, bf16[2,4,2,64,2048]{4,3,2,1,0:T(8,128)(2,1)}, u32[]{:S(2)}, u32[]{:S(2)}) collective-permute-start(bf16[2,4,2,64,2048]{4,3,2,1,0:T(8,128)(2,1)} %get-tuple-element.214), channel_id=1, source_target_pairs={{0,1},{1,0},{2,3},{3,2},{4,5},{5,4},{6,7},{7,6},{8,9},{9,8},{10,11... | collective-permute-start | bytes 12582920 | tf_op jit(solution)/shard_map/ppermute | solution.py:258
  423.0 39.9 %collective-permute-start.44 = (bf16[4,64,2048]{2,1,0:T(8,128)(2,1)}, bf16[4,64,2048]{2,1,0:T(8,128)(2,1)}, u32[]{:S(2)}, u32[]{:S(2)}) collective-permute-start(bf16[4,64,2048]{2,1,0:T(8,128)(2,1)} %get-tuple-element.217), channel_id=1, source_target_pairs={{0,8},{8,0},{16,24},{24,16},{1,9},{9,1},{17,25},{25,17},{2,10},{10... | collective-permute-start | bytes 3145736 | tf_op jit(solution)/shard_map/ppermute | solution.py:248
  424.5 38.4 %collective-permute-start.45 = (bf16[4,64,2048]{2,1,0:T(8,128)(2,1)}, bf16[4,64,2048]{2,1,0:T(8,128)(2,1)}, u32[]{:S(2)}, u32[]{:S(2)}) collective-permute-start(bf16[4,64,2048]{2,1,0:T(8,128)(2,1)} %get-tuple-element.218), channel_id=1, source_target_pairs={{0,16},{8,24},{16,0},{24,8},{1,17},{9,25},{17,1},{25,9},{2,18},{10... | collective-permute-start | bytes 3145736 | tf_op jit(solution)/shard_map/ppermute | solution.py:248
  429.9 129.1 %reduce-scatter.8.cloned.1.call-start = ((), (), s32[]{:S(2)}) async-start(), calls=%async_computation.5 | async-start | bytes 3604480 | tf_op jit(solution)/shard_map/reduce_scatter | solution.py:1004
  476.0 24.7 %collective-permute-start.46 = (bf16[2,4,2,64,2432]{4,3,2,1,0:T(8,128)(2,1)}, bf16[2,4,2,64,2432]{4,3,2,1,0:T(8,128)(2,1)}, u32[]{:S(2)}, u32[]{:S(2)}) collective-permute-start(bf16[2,4,2,64,2432]{4,3,2,1,0:T(8,128)(2,1)} %get-tuple-element.236), channel_id=1, source_target_pairs={{0,1},{1,0},{2,3},{3,2},{4,5},{5,4},{6,7},{7,6},{8,9},{9,8},{10,11... | collective-permute-start | bytes 14942216 | tf_op jit(solution)/shard_map/ppermute | solution.py:258
  482.0 14.3 %collective-permute-start.47 = (bf16[2,64,2048]{2,1,0:T(8,128)(2,1)S(1)}, bf16[2,64,2048]{2,1,0:T(8,128)(2,1)S(1)}, u32[]{:S(2)}, u32[]{:S(2)}) collective-permute-start(bf16[2,64,2048]{2,1,0:T(8,128)(2,1)S(1)} %copy-done.40), channel_id=1, source_target_pairs={{0,16},{8,24},{16,0},{24,8},{1,17},{9,25},{17,1},{25,9},{2,18},{10... | collective-permute-start | bytes 1572872 | tf_op jit(solution)/shard_map/ppermute | solution.py:248
  483.6 14.0 %collective-permute-start.48 = (bf16[2,64,2048]{2,1,0:T(8,128)(2,1)S(1)}, bf16[2,64,2048]{2,1,0:T(8,128)(2,1)S(1)}, u32[]{:S(2)}, u32[]{:S(2)}) collective-permute-start(bf16[2,64,2048]{2,1,0:T(8,128)(2,1)S(1)} %copy-done.39), channel_id=1, source_target_pairs={{0,8},{8,0},{16,24},{24,16},{1,9},{9,1},{17,25},{25,17},{2,10},{10... | collective-permute-start | bytes 1572872 | tf_op jit(solution)/shard_map/ppermute | solution.py:248
  504.4 28.9 %collective-permute-start.52 = (bf16[4,64,2432]{2,1,0:T(8,128)(2,1)}, bf16[4,64,2432]{2,1,0:T(8,128)(2,1)S(1)}, u32[]{:S(2)}, u32[]{:S(2)}) collective-permute-start(bf16[4,64,2432]{2,1,0:T(8,128)(2,1)} %get-tuple-element.242), channel_id=1, source_target_pairs={{0,8},{8,0},{16,24},{24,16},{1,9},{9,1},{17,25},{25,17},{2,10},{10... | collective-permute-start | bytes 3735560 | tf_op jit(solution)/shard_map/ppermute | solution.py:248
  505.0 28.6 %collective-permute-start.53 = (bf16[4,64,2432]{2,1,0:T(8,128)(2,1)}, bf16[4,64,2432]{2,1,0:T(8,128)(2,1)S(1)}, u32[]{:S(2)}, u32[]{:S(2)}) collective-permute-start(bf16[4,64,2432]{2,1,0:T(8,128)(2,1)} %get-tuple-element.243), channel_id=1, source_target_pairs={{0,16},{8,24},{16,0},{24,8},{1,17},{9,25},{17,1},{25,9},{2,18},{10... | collective-permute-start | bytes 3735560 | tf_op jit(solution)/shard_map/ppermute | solution.py:248
  537.7 17.2 %collective-permute-start.55 = (bf16[2,64,2432]{2,1,0:T(8,128)(2,1)}, bf16[2,64,2432]{2,1,0:T(8,128)(2,1)S(1)}, u32[]{:S(2)}, u32[]{:S(2)}) collective-permute-start(bf16[2,64,2432]{2,1,0:T(8,128)(2,1)} %get-tuple-element.253), channel_id=1, source_target_pairs={{0,8},{8,0},{16,24},{24,16},{1,9},{9,1},{17,25},{25,17},{2,10},{10... | collective-permute-start | bytes 1867784 | tf_op jit(solution)/shard_map/ppermute | solution.py:248
  539.0 22.4 %collective-permute-start.57 = (bf16[2,64,2048]{2,1,0:T(8,128)(2,1)}, bf16[2,64,2048]{2,1,0:T(8,128)(2,1)S(1)}, u32[]{:S(2)}, u32[]{:S(2)}) collective-permute-start(bf16[2,64,2048]{2,1,0:T(8,128)(2,1)} %add.64), channel_id=1, source_target_pairs={{0,2},{1,3},{2,0},{3,1},{4,6},{5,7},{6,4},{7,5},{8,10},{9,11},{10,... | collective-permute-start | bytes 1572872 | tf_op jit(solution)/shard_map/ppermute | solution.py:253
  539.3 39.7 %collective-permute-start.50 = (bf16[1,192,2048]{2,1,0:T(8,128)(2,1)}, bf16[1,192,2048]{2,1,0:T(8,128)(2,1)S(1)}, u32[]{:S(2)}, u32[]{:S(2)}) collective-permute-start(bf16[1,192,2048]{2,1,0:T(8,128)(2,1)} %get-tuple-element.246), channel_id=1, source_target_pairs={{0,16},{8,24},{16,0},{24,8},{1,17},{9,25},{17,1},{25,9},{2,18},{10... | collective-permute-start | bytes 2359304 | tf_op jit(solution)/shard_map/ppermute | solution.py:248
  540.7 39.4 %collective-permute-start.51 = (bf16[1,192,2048]{2,1,0:T(8,128)(2,1)}, bf16[1,192,2048]{2,1,0:T(8,128)(2,1)}, u32[]{:S(2)}, u32[]{:S(2)}) collective-permute-start(bf16[1,192,2048]{2,1,0:T(8,128)(2,1)} %get-tuple-element.247), channel_id=1, source_target_pairs={{0,8},{8,0},{16,24},{24,16},{1,9},{9,1},{17,25},{25,17},{2,10},{10... | collective-permute-start | bytes 2359304 | tf_op jit(solution)/shard_map/ppermute | solution.py:248
  541.6 33.9 %collective-permute-start.54 = (bf16[2,64,2432]{2,1,0:T(8,128)(2,1)}, bf16[2,64,2432]{2,1,0:T(8,128)(2,1)S(1)}, u32[]{:S(2)}, u32[]{:S(2)}) collective-permute-start(bf16[2,64,2432]{2,1,0:T(8,128)(2,1)} %get-tuple-element.252), channel_id=1, source_target_pairs={{0,16},{8,24},{16,0},{24,8},{1,17},{9,25},{17,1},{25,9},{2,18},{10... | collective-permute-start | bytes 1867784 | tf_op jit(solution)/shard_map/ppermute | solution.py:248
  558.3 13.3 %collective-permute-start.56 = (bf16[2,64,2432]{2,1,0:T(8,128)(2,1)}, bf16[2,64,2432]{2,1,0:T(8,128)(2,1)S(1)}, u32[]{:S(2)}, u32[]{:S(2)}) collective-permute-start(bf16[2,64,2432]{2,1,0:T(8,128)(2,1)} %add.68), channel_id=1, source_target_pairs={{0,2},{1,3},{2,0},{3,1},{4,6},{5,7},{6,4},{7,5},{8,10},{9,11},{10,... | collective-permute-start | bytes 1867784 | tf_op jit(solution)/shard_map/ppermute | solution.py:253
  562.3 20.7 %collective-permute-start.59 = (bf16[2,64,1408]{2,1,0:T(8,128)(2,1)}, bf16[2,64,1408]{2,1,0:T(8,128)(2,1)S(1)}, u32[]{:S(2)}, u32[]{:S(2)}) collective-permute-start(bf16[2,64,1408]{2,1,0:T(8,128)(2,1)} %pad_maximum_fusion.3), channel_id=1, source_target_pairs={{0,8},{8,0},{16,24},{24,16},{1,9},{9,1},{17,25},{25,17},{2,10},{10... | collective-permute-start | bytes 1081352 | tf_op jit(solution)/shard_map/ppermute | solution.py:248
  571.6 19.9 %collective-permute-start.62 = (bf16[1,64,2048]{2,1,0:T(8,128)(2,1)}, bf16[1,64,2048]{2,1,0:T(8,128)(2,1)S(1)}, u32[]{:S(2)}, u32[]{:S(2)}) collective-permute-start(bf16[1,64,2048]{2,1,0:T(8,128)(2,1)} %add.69), channel_id=1, source_target_pairs={{0,4},{1,5},{2,6},{3,7},{4,0},{5,1},{6,2},{7,3},{8,12},{9,13},{10,... | collective-permute-start | bytes 786440 | tf_op jit(solution)/shard_map/ppermute | solution.py:253
  575.6 13.3 %collective-permute-start.60 = (bf16[2,64,1408]{2,1,0:T(8,128)(2,1)}, bf16[2,64,1408]{2,1,0:T(8,128)(2,1)S(1)}, u32[]{:S(2)}, u32[]{:S(2)}) collective-permute-start(bf16[2,64,1408]{2,1,0:T(8,128)(2,1)} %pad_maximum_fusion.4), channel_id=1, source_target_pairs={{0,16},{8,24},{16,0},{24,8},{1,17},{9,25},{17,1},{25,9},{2,18},{10... | collective-permute-start | bytes 1081352 | tf_op jit(solution)/shard_map/ppermute | solution.py:248
  578.9 9.9 %collective-permute-start.61 = (bf16[2,64,1408]{2,1,0:T(8,128)(2,1)}, bf16[2,64,1408]{2,1,0:T(8,128)(2,1)S(1)}, u32[]{:S(2)}, u32[]{:S(2)}) collective-permute-start(bf16[2,64,1408]{2,1,0:T(8,128)(2,1)} %pad_maximum_fusion.5), channel_id=1, source_target_pairs={{0,24},{8,16},{16,8},{24,0},{1,25},{9,17},{17,9},{25,1},{2,26},{10... | collective-permute-start | bytes 1081352 | tf_op jit(solution)/shard_map/ppermute | solution.py:248
  580.1 31.2 %collective-permute-start.58 = (bf16[1,64,2432]{2,1,0:T(8,128)(2,1)}, bf16[1,64,2432]{2,1,0:T(8,128)(2,1)S(1)}, u32[]{:S(2)}, u32[]{:S(2)}) collective-permute-start(bf16[1,64,2432]{2,1,0:T(8,128)(2,1)} %add.70), channel_id=1, source_target_pairs={{0,4},{1,5},{2,6},{3,7},{4,0},{5,1},{6,2},{7,3},{8,12},{9,13},{10,... | collective-permute-start | bytes 933896 | tf_op jit(solution)/shard_map/ppermute | solution.py:253
  (44 other events, 277.5 us)
Sparse Core Ops, SparseCore 0:
  94.9 160.1 all-gather.2
  372.4 56.4 reduce-scatter.3
  431.2 56.0 reduce-scatter.5
  490.0 57.6 reduce-scatter.7
